TPU v7x, 32 devices: a whole 2x2x4 slice. The times are simulated.
32 devices in a mesh: dp: 16 (over z, y, core), seq: 2 (over x).
Axes of the slice: x: 2, y: 2, z: 4, core: 2. Of those that a mesh axis runs over, the one named last changes fastest.
Arguments:
- tokens: bfloat16 [16, 1024, 768], P('dp', 'seq'), may hold values from -6 to 6
- cotangent: bfloat16 [16, 1024, 768], P('dp', 'seq'), may hold values from -6 to 6
- time_index: int32 [16], P('dp'), may hold values from 0 to 999
- step_table: float32 [1000, 128], replicated, may hold values from -6 to 6
- first_gain: bfloat16 [768], replicated, may hold values from 0.5 to 1.5
- attn_qkv: bfloat16 [768, 2304], replicated, may hold values from -0.21875 to 0.21875
- attn_out: bfloat16 [768, 768], replicated, may hold values from -2.5 to 2.5
- second_gain: bfloat16 [768], replicated, may hold values from 0.5 to 1.5
- mlp_up: bfloat16 [768, 3072], replicated, may hold values from -0.21875 to 0.21875
- up_bias: bfloat16 [3072], replicated, may hold values from -3 to 3
- mlp_down: bfloat16 [3072, 768], replicated, may hold values from -0.109375 to 0.109375
- down_bias: bfloat16 [768], replicated, may hold values from -3 to 3
- ada_weight: bfloat16 [128, 4608], replicated, may hold values from -0.5 to 0.5
- ada_bias: bfloat16 [4608], replicated, may hold values from -3 to 3
Outputs:
- mixed: bfloat16 [16, 1024, 768], P('dp', 'seq')
- tokens_grad: float32 [16, 1024, 768], P('dp', 'seq')
- cond_grad: float32 [16, 128], P('dp')
- first_gain_grad: float32 [768], replicated
- attn_qkv_grad: float32 [768, 2304], P('dp')
- attn_out_grad: float32 [768, 768], P('dp')
- second_gain_grad: float32 [768], replicated
- mlp_up_grad: float32 [768, 3072], P('dp')
- up_bias_grad: float32 [3072], replicated
- mlp_down_grad: float32 [3072, 768], P('dp')
- down_bias_grad: float32 [768], replicated
- ada_weight_grad: float32 [128, 4608], P(None, 'dp')
- ada_bias_grad: float32 [4608], replicated
All inputs are finite; a program needn't handle non-finite values.
Results may differ from a plain program's by a relative error of at most 0.014.
The roundings to bfloat16 on the way count: a program that leaves them out, or rounds other values in their place, can miss the bound.
Values may be sent and summed in bfloat16 or wider, within the bound.
No kernel may reach another device: no remote copies, remote signals or barrier semaphores. Data moves between devices by JAX's collectives and lax.ppermute only.
A program may use at most 192 MiB of HBM per device.

v0:
```python
import functools

import jax
import jax.numpy as jnp
from jax import lax
from jax.experimental import pallas as pl
from jax.experimental.pallas import tpu as pltpu
from jax.sharding import PartitionSpec as P

HD = 64
LOG2E = 1.4426950408889634


highest = lax.Precision.HIGHEST


def tables(positions):
    half_dim = HD // 2
    frequency = jnp.exp(
        -jnp.log(10000.0) * (2.0 * jnp.arange(half_dim, dtype=jnp.float32) / HD)
    )
    angles = positions.astype(jnp.float32)[:, None] * frequency[None, :]
    cosine, sine = jnp.cos(angles), jnp.sin(angles)
    return (
        jnp.concatenate([cosine] * 4, axis=1),
        jnp.concatenate([-sine, sine, -sine, sine], axis=1),
    )


def full(shape):
    return pl.BlockSpec(shape, lambda step: (0,) * len(shape))


def columns(rows, width, first=0):
    return pl.BlockSpec((rows, width), lambda step: (0, step + first))


def shaped(shape, kind):
    return jax.ShapeDtypeStruct(shape, kind)


def far(shape, kind):
    return pltpu.VMEM(shape, kind)


def far(shape, kind):
    return pltpu.HBM(shape, kind)


def store_split(low, core, own, keep, send):
    pairs = low.shape[0] // (2 * own)

    def store(kept):
        for pair in range(pairs):
            rows = slice(pair * own, (pair + 1) * own)
            for parity, target in ((kept, keep), (1 - kept, send)):
                start = (2 * pair + parity) * own
                target[rows, :] = low[start : start + own, :]

    @pl.when(core[0] == 0)
    def _():
        store(0)

    @pl.when(core[0] == 1)
    def _():
        store(1)


def zero_shape():
    return jax.ShapeDtypeStruct((1, 1), jnp.float32)


def scalar_spec():
    return pl.BlockSpec(memory_space=pltpu.SMEM)


def kernel_call(body, steps, in_specs, out_specs, out_shape, scratch, grant):
    call = pl.pallas_call(
        body,
        grid=(steps,),
        in_specs=in_specs,
        out_specs=out_specs,
        out_shape=out_shape,
        scratch_shapes=scratch,
        compiler_params=pltpu.CompilerParams(
            dimension_semantics=("arbitrary",), vmem_limit_bytes=grant * 1024 * 1024
        ),
        cost_estimate=pl.CostEstimate(flops=1, bytes_accessed=1, transcendentals=0),
    )

    def run(*args, free=()):
        placed = []
        for arg in args:
            if arg.size > 4096 and not any(arg is other for other in free):
                arg = pltpu.with_memory_space_constraint(arg, pltpu.HBM)
            placed.append(arg)
        return call(*placed)

    return run


def dot(left, right, left_axis=1, right_axis=0):
    return lax.dot_general(
        left,
        right,
        (((left_axis,), (right_axis,)), ((), ())),
        preferred_element_type=jnp.float32,
    )


def normalized(inputs):
    center = inputs - jnp.mean(inputs, axis=-1, keepdims=True)
    inverse = lax.rsqrt(jnp.mean(center * center, axis=-1, keepdims=True) + 1e-05)
    return center * inverse, inverse


def norm_back(back, hat, inverse, factor):
    scaled = back * factor
    return inverse * (
        scaled
        - jnp.mean(scaled, axis=-1, keepdims=True)
        - hat * jnp.mean(scaled * hat, axis=-1, keepdims=True)
    )


def column_sum(values):
    return jnp.sum(values, axis=0, keepdims=True)


SHIFT1, SCALE1, GATE1, SHIFT2, SCALE2, GATE2, GAIN1, GAIN2, COND = range(9)


def row(ref, index):
    return ref[index : index + 1, :]


def rotate_lanes(values, cosine, sine):
    lane = lax.broadcasted_iota(jnp.int32, cosine.shape, 1)
    lower = (lane % HD) < HD // 2
    parts = []
    for start in range(0, values.shape[1], 128):
        part = values[:, start : start + 128]
        other = jnp.where(lower, pltpu.roll(part, 128 - HD // 2, 1), pltpu.roll(part, HD // 2, 1))
        parts.append(part * cosine + other * sine)
    return jnp.concatenate(parts, axis=1)


COLUMNS = 768


def key_value_body(tokens, mods, weight, cosine, sine, cotangent, normed, out):
    step = pl.program_id(0)
    turned_steps = pl.num_programs(0) // 2

    @pl.when(step == 0)
    def _():
        hat, _ = normalized(tokens[...].astype(jnp.float32))
        value = hat * row(mods, GAIN1) * (1.0 + row(mods, SCALE1)) + row(mods, SHIFT1)
        normed[...] = value.astype(jnp.bfloat16)

    @pl.when(step < turned_steps)
    def _():
        value = dot(normed[...], weight[...])
        out[...] = rotate_lanes(value, cosine[...], sine[...]).astype(jnp.bfloat16)

    @pl.when(step >= turned_steps)
    def _():
        out[...] = dot(normed[...], weight[...]).astype(jnp.bfloat16)


def project_key_value(tokens, mods, weight, cosine, sine, after):
    rows, width = tokens.shape
    first = width // COLUMNS
    return kernel_call(
        key_value_body,
        2 * first,
        [
            full((rows, width)),
            full((16, width)),
            columns(width, COLUMNS, first),
            full((rows, 128)),
            full((rows, 128)),
            pl.BlockSpec(memory_space=pl.ANY),
        ],
        [full((rows, width)), columns(rows, COLUMNS)],
        [far((rows, width), jnp.bfloat16), far((rows, 2 * width), jnp.bfloat16)],
        [],
        18,
    )(tokens, mods, weight, cosine, sine, after, free=(tokens, after))


def head_mask(shape, head):
    lane = lax.broadcasted_iota(jnp.int32, shape, 1)
    return jnp.where(lane // HD == head, 1.0, 0.0).astype(jnp.bfloat16)


HEADS = 4


def head_lanes(head):
    pair, place = divmod(head, 2)
    return slice(pair * 128, (pair + 1) * 128), place, slice(place * HD, (place + 1) * HD)


def in_turn(count, first, rest):
    results = []
    ahead = first(0)
    for index in range(count):
        now = ahead
        if index + 1 < count:
            ahead = first(index + 1)
        results.append(rest(index, now))
    return results


def attend_heads(query, keys1, values1, keys2, values2, log_total):
    rows = query.shape[0]

    def first(head):
        lanes, place, _ = head_lanes(head)
        own = query[:, lanes] * head_mask((rows, 128), place)
        return dot(keys1[:, lanes], own, 1, 1), dot(keys2[:, lanes], own, 1, 1)

    def rest(head, scores):
        lanes, place, turned = head_lanes(head)
        scores1, scores2 = scores
        top = jnp.maximum(
            jnp.max(scores1, axis=0, keepdims=True), jnp.max(scores2, axis=0, keepdims=True)
        )
        exps1 = jnp.exp2(scores1 - top)
        exps2 = jnp.exp2(scores2 - top)
        total = column_sum(exps1) + column_sum(exps2)
        mixed = dot(values1[:, lanes].T[turned], exps1.astype(jnp.bfloat16)) + dot(
            values2[:, lanes].T[turned], exps2.astype(jnp.bfloat16)
        )
        log_total[0, head : head + 1, :] = top + jnp.log2(total)
        return mixed * (1.0 / total)

    parts = in_turn(HEADS, first, rest)
    return jnp.concatenate(
        [
            jnp.concatenate(parts[head : head + 2], axis=0).T.astype(jnp.bfloat16)
            for head in range(0, HEADS, 2)
        ],
        axis=1,
    )


def attend_back_body(second, query, keys, values, grad, attended, log_total, *refs):
    if second:
        before, cosine, sine = refs[:3]
    d_query, d_pair, zero = refs[-3:]
    zero[0, 0] = 0.0
    rows = query.shape[0]
    products = {}

    def first(head):
        lanes, place, _ = head_lanes(head)
        if place == 0:
            product = grad[:, lanes].astype(jnp.float32) * attended[:, lanes].astype(jnp.float32)
            products[head] = products[head + 1] = product.T
        own = query[:, lanes] * head_mask((rows, 128), place)
        own_grad = grad[:, lanes] * head_mask((rows, 128), place)
        scores = dot(keys[:, lanes], own, 1, 1)
        d_probs = dot(values[:, lanes], own_grad, 1, 1)
        return own, own_grad, scores, d_probs

    def rest(head, given):
        own, own_grad, scores, d_probs = given
        lanes, place, turned = head_lanes(head)
        delta = column_sum(products[head][turned])
        probs = jnp.exp2(scores - log_total[0, head : head + 1, :])
        d_scores = (probs * (d_probs - delta)).astype(jnp.bfloat16)
        return (
            dot(keys[:, lanes].T[turned], d_scores),
            dot(d_scores, own),
            dot(probs.astype(jnp.bfloat16), own_grad),
        )

    parts = in_turn(HEADS, first, rest)
    width = HEADS * HD
    for head in range(0, HEADS, 2):
        lanes = head_lanes(head)[0]
        value_lanes = slice(width + lanes.start, width + lanes.stop)
        one, two = parts[head : head + 2]
        turned = jnp.concatenate([one[0], two[0]], axis=0).T * HD ** (-0.5)
        if second:
            turned = rotate_lanes(turned + before[:, lanes], cosine[...], -sine[...])
        d_query[:, lanes] = turned.astype(d_query.dtype)
        d_pair[:, lanes] = ((one[1] + two[1]) * (1.0 / LOG2E)).astype(jnp.bfloat16)
        d_pair[:, value_lanes] = (one[2] + two[2]).astype(jnp.bfloat16)


def attend_back(query, pair, grad, attended, log_total, before=None, after=(), free=()):
    rows, width = query.shape
    lanes = HEADS * HD
    steps = width // lanes
    block = columns(rows, lanes)
    second = before is not None
    extra = list(before) if second else []
    extra_specs = [block, full((rows, 128)), full((rows, 128))] if second else []
    return kernel_call(
        functools.partial(attend_back_body, second),
        steps,
        [
            block,
            block,
            columns(rows, lanes, steps),
            block,
            block,
            pl.BlockSpec((1, HEADS, rows), lambda step: (step, 0, 0)),
        ]
        + extra_specs
        + [pl.BlockSpec(memory_space=pl.ANY)] * len(after),
        [block, columns(rows, 2 * lanes), scalar_spec()],
        [
            far((rows, width), jnp.bfloat16 if second else jnp.float32),
            far((rows, 2 * width), jnp.bfloat16),
            zero_shape(),
        ],
        [],
        28,
    )(query, pair, pair, grad, attended, log_total, *extra, *after, free=(*free, *after))


def block_body(
    own_up, own_down, attend_steps, hidden_steps,
    core, normed1, query_weight, cosine, sine, keys1, values1, keys2, values2, mods,
    up_bias, down_bias, tokens_far, cotangent_far, out_far, up_far, down_far,
    query, attended, log_total, mixed, d_middle, d_attended, up_keep, up_send,
    down_keep, down_send, bias_grad, sums,
    tokens, cotangent, out_weight, up_weight, down_weight, arrived,
    all_attended, normed, d_ffn, branch, middle, forward, back,
):
    step = pl.program_id(0)
    tile = up_bias.shape[1]
    arrivals = [
        pltpu.make_async_copy(source, target, arrived.at[index])
        for index, (source, target) in enumerate(
            (
                (tokens_far, tokens),
                (cotangent_far, cotangent),
                (out_far, out_weight),
                (up_far, up_weight),
                (down_far, down_weight),
            )
        )
    ]

    @pl.when(step == 0)
    def _():
        for arrival in arrivals:
            arrival.start()

    @pl.when(step < attend_steps)
    def _():
        value = rotate_lanes(dot(normed1[...], query_weight[...]), cosine[...], sine[...])
        query[...] = (value * (LOG2E * HD ** (-0.5))).astype(jnp.bfloat16)
        found = attend_heads(query, keys1, values1, keys2, values2, log_total)
        attended[...] = found
        for index in range(attend_steps):

            @pl.when(step == index)
            def _(index=index):
                lanes = HEADS * HD
                all_attended[:, index * lanes : (index + 1) * lanes] = found

    @pl.when(step == attend_steps)
    def _():
        for arrival in arrivals:
            arrival.wait()
        turned = dot(all_attended[...], out_weight[...])
        branch[...] = turned.astype(jnp.bfloat16)
        value = tokens[...].astype(jnp.float32) + row(mods, GATE1) * turned
        middle[...] = value
        hat, _ = normalized(value)
        value = hat * row(mods, GAIN2) * (1.0 + row(mods, SCALE2)) + row(mods, SHIFT2)
        normed[...] = value.astype(jnp.bfloat16)
        low = (row(mods, GATE2) * cotangent[...].astype(jnp.float32)).astype(jnp.bfloat16)
        d_ffn[...] = low
        sums[4:5, :] = column_sum(low.astype(jnp.float32))
        forward[...] = jnp.zeros_like(forward)
        back[...] = jnp.zeros_like(back)

    @pl.when((step >= attend_steps) & (step < attend_steps + hidden_steps))
    def _():
        place = pl.ds(pl.multiple_of((step - attend_steps) * tile, tile), tile)
        pre = dot(normed[...], up_weight[:, place]) + up_bias[...]
        d_activated = dot(d_ffn[...], down_weight[place, :], 1, 1)
        root = 0.7978845608028654
        square = pre * pre
        bent = jnp.tanh(root * pre * (1.0 + 0.044715 * square))
        half = 0.5 + 0.5 * bent
        slope = half + (0.5 * root) * pre * (1.0 - bent * bent) * (1.0 + 0.134145 * square)
        low = (pre * half).astype(jnp.bfloat16)
        d_pre = d_activated * slope
        d_low = d_pre.astype(jnp.bfloat16)
        bias_grad[...] = column_sum(d_pre)
        down_grad = dot(low, d_ffn[...], 0, 0).astype(jnp.bfloat16)
        store_split(down_grad, core, own_down, down_keep, down_send)
        up_grad = dot(normed[...], d_low, 0, 0).astype(jnp.bfloat16)
        store_split(up_grad, core, own_up, up_keep, up_send)
        forward[...] += dot(low, down_weight[place, :])
        back[...] += dot(d_low, up_weight[:, place], 1, 1)

    @pl.when(step == attend_steps + hidden_steps)
    def _():
        grad = cotangent[...].astype(jnp.float32)
        held = middle[...]
        hat, inverse = normalized(held)
        factor = row(mods, GAIN2) * (1.0 + row(mods, SCALE2))
        value = back[...]
        d_value = grad + norm_back(value, hat, inverse, factor)
        d_middle[...] = d_value
        d_branch = (row(mods, GATE1) * d_value).astype(jnp.bfloat16)
        d_attended[...] = dot(d_branch, out_weight[...], 1, 1).astype(jnp.bfloat16)
        out_grad = dot(all_attended[...], d_branch, 0, 0).astype(jnp.bfloat16)
        store_split(out_grad, core, own_up, up_keep, up_send)
        ffn = forward[...] + down_bias[...]
        mixed[...] = (held + row(mods, GATE2) * ffn).astype(jnp.bfloat16)
        sums[0:1, :] = column_sum(value)
        sums[1:2, :] = column_sum(value * hat)
        sums[2:3, :] = column_sum(d_value * branch[...].astype(jnp.float32))
        sums[3:4, :] = column_sum(grad * ffn)
        sums[5:8, :] = jnp.zeros_like(sums[5:8, :])


def split_rows(rows):
    own = rows // lax.axis_size("dp")
    return own if own % 16 == 0 else rows // 2


def block_layer(
    core, normed1, qkv_weight, cosine, sine, own, peer, mods, up_bias, down_bias,
    tokens, cotangent, out_weight, up_weight, down_weight,
):
    rows, width = tokens.shape
    hidden = up_weight.shape[1]
    tile = width
    lanes = HEADS * HD
    attend_steps = width // lanes
    hidden_steps = hidden // tile
    own_down = hidden // lax.axis_size("dp")
    if own_down % 16 > 0:
        own_down = tile // 2

    def heads(first=0):
        return pl.BlockSpec(
            (rows, lanes), lambda step: (0, jnp.minimum(step, attend_steps - 1) + first)
        )

    def tiles(step):
        return jnp.clip(step - attend_steps, 0, hidden_steps - 1)

    def up_tiles(step):
        return jnp.clip(step - attend_steps, 0, hidden_steps)

    block = full((rows, width))
    far_spec = pl.BlockSpec(memory_space=pl.ANY)
    low = jnp.bfloat16
    up_spec = pl.BlockSpec((width // 2, tile), lambda step: (0, up_tiles(step)))
    down_spec = pl.BlockSpec((tile // 2, width), lambda step: (tiles(step), 0))
    return kernel_call(
        functools.partial(
            block_body, split_rows(width), own_down, attend_steps, hidden_steps
        ),
        attend_steps + hidden_steps + 1,
        [
            scalar_spec(),
            block,
            pl.BlockSpec((width, lanes), lambda step: (0, jnp.minimum(step, attend_steps - 1))),
            full((rows, 128)),
            full((rows, 128)),
            heads(),
            heads(attend_steps),
            heads(),
            heads(attend_steps),
            full((16, width)),
            pl.BlockSpec((1, tile), lambda step: (0, tiles(step))),
            full((1, width)),
        ]
        + [far_spec] * 5,
        [
            heads(),
            heads(),
            pl.BlockSpec(
                (1, HEADS, rows), lambda step: (jnp.minimum(step, attend_steps - 1), 0, 0)
            ),
            block,
            block,
            block,
            up_spec,
            up_spec,
            down_spec,
            down_spec,
            pl.BlockSpec((1, tile), lambda step: (0, tiles(step))),
            full((8, width)),
        ],
        [
            far((rows, width), low),
            far((rows, width), low),
            far((attend_steps, HEADS, rows), jnp.float32),
            far((rows, width), low),
            far((rows, width), jnp.float32),
            far((rows, width), low),
            far((width // 2, hidden + width), low),
            far((width // 2, hidden + width), low),
            far((hidden // 2, width), low),
            far((hidden // 2, width), low),
            far((1, hidden), jnp.float32),
            far((8, width), jnp.float32),
        ],
        [
            pltpu.VMEM((rows, width), low),
            pltpu.VMEM((rows, width), low),
            pltpu.VMEM((width, width), low),
            pltpu.VMEM((width, hidden), low),
            pltpu.VMEM((hidden, width), low),
            pltpu.SemaphoreType.DMA((5,)),
            pltpu.VMEM((rows, width), low),
            pltpu.VMEM((rows, width), low),
            pltpu.VMEM((rows, width), low),
            pltpu.VMEM((rows, width), low),
            pltpu.VMEM((rows, width), jnp.float32),
            pltpu.VMEM((rows, width), jnp.float32),
            pltpu.VMEM((rows, width), jnp.float32),
        ],
        58,
    )(
        core, normed1, qkv_weight, cosine, sine, own, own, peer, peer, mods, up_bias, down_bias,
        tokens, cotangent, out_weight, up_weight, down_weight, free=(peer, cotangent, tokens),
    )


def projected_back_body(
    own, core, d_query, d_pair, peer_pair, normed, cosine, sine, d_projected, keep, send, zero
):
    zero[0, 0] = 0.0
    lanes = HEADS * HD
    pair = d_pair[...].astype(jnp.float32) + peer_pair[...].astype(jnp.float32)
    keys = rotate_lanes(pair[:, :lanes], cosine[...], -sine[...]).astype(jnp.bfloat16)
    low = jnp.concatenate([d_query[...], keys, pair[:, lanes:].astype(jnp.bfloat16)], axis=1)
    d_projected[...] = low
    store_split(dot(normed[...], low, 0, 0).astype(jnp.bfloat16), core, own, keep, send)


def projected_back(core, d_query, d_pair, peer_pair, normed, cosine, sine):
    rows, width = normed.shape
    lanes = HEADS * HD
    return kernel_call(
        functools.partial(projected_back_body, split_rows(width)),
        width // lanes,
        [
            scalar_spec(),
            columns(rows, lanes),
            columns(rows, 2 * lanes),
            columns(rows, 2 * lanes),
            full((rows, width)),
            full((rows, 128)),
            full((rows, 128)),
        ],
        [
            columns(rows, 3 * lanes),
            columns(width // 2, 3 * lanes),
            columns(width // 2, 3 * lanes),
            scalar_spec(),
        ],
        [
            far((rows, 3 * width), jnp.bfloat16),
            far((width // 2, 3 * width), jnp.bfloat16),
            far((width // 2, 3 * width), jnp.bfloat16),
            zero_shape(),
        ],
        [],
        32,
    )(core, d_query, d_pair, peer_pair, normed, cosine, sine, free=(peer_pair,))


def tokens_back_body(
    d_projected, weight1, weight2, weight3, tokens, d_middle, mods, sums, bias_grad, *refs
):
    out, small, zero, total = refs[-4:]
    zero[0, 0] = 0.0
    step = pl.program_id(0)
    width = tokens.shape[1]
    lanes = HEADS * HD
    part = sum(
        dot(d_projected[:, index * lanes : (index + 1) * lanes], weight[...], 1, 1)
        for index, weight in enumerate((weight1, weight2, weight3))
    )

    @pl.when(step == 0)
    def _():
        total[...] = part

    @pl.when(step > 0)
    def _():
        total[...] += part

    @pl.when(step == pl.num_programs(0) - 1)
    def _():
        back = total[...]
        hat, inverse = normalized(tokens[...].astype(jnp.float32))
        scale1 = 1.0 + row(mods, SCALE1)
        gain1 = row(mods, GAIN1)
        out[...] = (d_middle[...] + norm_back(back, hat, inverse, gain1 * scale1)).astype(
            jnp.bfloat16
        )
        hat_sum1 = column_sum(back * hat)
        hat_sum2 = row(sums, 1)
        rows = [
            column_sum(back),
            hat_sum1 * gain1,
            row(sums, 2),
            row(sums, 0),
            hat_sum2 * row(mods, GAIN2),
            row(sums, 3),
            row(mods, COND) * 0.5,
            jnp.zeros_like(hat_sum1),
            hat_sum1 * scale1,
            hat_sum2 * (1.0 + row(mods, SCALE2)),
            row(sums, 4),
        ]
        for index in range(bias_grad.shape[1] // width):
            rows.append(bias_grad[:, index * width : (index + 1) * width])
        for index, value in enumerate(rows):
            small[index : index + 1, :] = value
        small[len(rows) :, :] = jnp.zeros_like(small[len(rows) :, :])


def tokens_back(d_projected, weight, tokens, d_middle, mods, sums, bias_grad, after):
    rows, width = tokens.shape
    block = full((rows, width))
    lanes = HEADS * HD
    steps = width // lanes
    return kernel_call(
        tokens_back_body,
        steps,
        [
            columns(rows, 3 * lanes),
            columns(width, lanes),
            columns(width, lanes, steps),
            columns(width, lanes, 2 * steps),
            block,
            block,
            full((16, width)),
            full((8, width)),
            full(bias_grad.shape),
        ]
        + [pl.BlockSpec(memory_space=pl.ANY)] * len(after),
        [block, full((16, width)), scalar_spec()],
        [far((rows, width), jnp.bfloat16), far((16, width), jnp.float32), zero_shape()],
        [pltpu.VMEM((rows, width), jnp.float32)],
        32,
    )(d_projected, weight, weight, weight, tokens, d_middle, mods, sums, bias_grad, *after, free=after)


def swap_halves(block):
    count = lax.axis_size("dp") * lax.axis_size("seq")
    target = {1: 2, 2: 1}
    perm = [(i, i - i % 4 + target.get(i % 4, i % 4)) for i in range(count)]
    return lax.ppermute(block, ("dp", "seq"), perm)


def swap_bit(block, bit):
    return lax.ppermute(block, "dp", [(i, i ^ bit) for i in range(lax.axis_size("dp"))])


def swap_cores(block):
    return swap_bit(block, 1)


def swap_seq(block):
    return lax.ppermute(block, "seq", [(0, 1), (1, 0)])


def dp_bits():
    bits, bit = [], 1
    while bit < lax.axis_size("dp"):
        bits.append(bit)
        bit *= 2
    return bits


def pick(block, axis, index):
    return lax.dynamic_index_in_dim(block, index, axis, keepdims=False)


class Flow:
    def __init__(self, got, kept, lanes=None):
        self.got, self.kept = got, kept
        self.lanes = lanes or (0, kept.shape[2])
        self.count, self.rest = kept.shape[:2]
        self.width = self.lanes[1] - self.lanes[0]


def stage_body(jobs, counts, mine, *refs):
    inputs = refs[: counts[0]]
    outputs = refs[counts[0] + counts[1] :]
    for place, (half, sources, target) in enumerate(jobs):
        sent, kept = outputs[target], outputs[target + 1]

        def store(out, which, half=half, sources=sources):
            at = 0
            for one, two, start, stop, rows in sources:
                if half:
                    middle = (start + stop) // 2
                    lanes = slice(middle, stop) if which else slice(start, middle)
                    total = inputs[one][:, :, lanes].astype(jnp.float32)
                    total = total + inputs[two][:, :, lanes].astype(jnp.float32)
                    out[...] = total.astype(jnp.bfloat16)
                    continue
                for pair in range(out.shape[0]):
                    block = 2 * pair + which
                    total = inputs[one][block, :, start:stop].astype(jnp.float32)
                    total = total + inputs[two][block, :, start:stop].astype(jnp.float32)
                    total = total.astype(jnp.bfloat16)
                    column = at
                    for first in range(0, total.shape[0], rows):
                        out[pair, :, column : column + stop - start] = total[first : first + rows]
                        column += stop - start
                at = column

        for which in range(2):

            @pl.when(mine[place] == which)
            def _(which=which, sent=sent, kept=kept, store=store):
                store(kept, which)
                store(sent, 1 - which)


def small_body(steps, first, one, two, out):
    rows = one.shape[0] - 8

    @pl.when(pl.program_id(0) == 0)
    def _():
        if first:
            out[...] = one[...] + two[...]
        else:
            out[:rows, :] = one[:rows, :]
            out[rows : 2 * rows, :] = two[:rows, :]
            out[2 * rows :, :] = one[rows:, :] + two[rows:, :]


def stage(steps, jobs, after=(), small=None):
    seq_rank, dp_rank = lax.axis_index("seq"), lax.axis_index("dp")
    inputs, in_specs, specs, out_specs, out_shape, mine = [], [], [], [], [], []

    def place_of(array):
        for index, other in enumerate(inputs):
            if other is array:
                return index
        inputs.append(array)
        each = array.shape[0] // steps
        in_specs.append(pl.BlockSpec((each,) + array.shape[1:], lambda at: (at, 0, 0)))
        return len(inputs) - 1

    for flows, step in jobs:
        half = step == "half"
        rest, count = flows[0].rest, flows[0].count
        sources = [
            (place_of(flow.got), place_of(flow.kept), *flow.lanes, rest) for flow in flows
        ]
        if half:
            shape = (count, rest, flows[0].width // 2)
            mine.append(seq_rank)
        else:
            width = sum(flow.width * flow.rest // rest for flow in flows)
            shape = (count // 2, rest, width)
            mine.append((dp_rank // step) % 2)
        specs.append((half, sources, len(out_shape)))
        out_shape += [far(shape, jnp.bfloat16)] * 2
        block = (shape[0] // steps,) + shape[1:]
        out_specs += [pl.BlockSpec(block, lambda at: (at, 0, 0))] * 2
    counts = (len(inputs), len(after))
    extra = []
    if small is not None:
        got, kept, first = small
        extra = [kept, got]
        rows = kept.shape[0] if first else 2 * kept.shape[0] - 8
        out_shape.append(far((rows, kept.shape[1]), jnp.float32))
        out_specs.append(full((rows, kept.shape[1])))

    def body(mine, *refs):
        if small is None:
            stage_body(specs, counts, mine, *refs)
            return
        main, ends = refs[: sum(counts)], refs[sum(counts) :]
        small_body(steps, first, ends[0], ends[1], ends[-1])
        stage_body(specs, counts, mine, *main, *ends[2:-1])

    results = kernel_call(
        body,
        steps,
        [scalar_spec()]
        + in_specs
        + [pl.BlockSpec(memory_space=pl.ANY)] * len(after)
        + [full(array.shape) for array in extra],
        out_specs,
        out_shape,
        [],
        40,
    )(jnp.stack(mine), *inputs, *after, *extra, free=(*inputs, *after, *extra))
    new = []
    for (flows, step), (_, _, target) in zip(jobs, specs):
        sent = results[target]
        got = swap_seq(sent) if step == "half" else swap_bit(sent, step)
        new.append(Flow(got, results[target + 1]))
    if small is not None:
        new.append(results[-1])
    return new, results[0]


def from_tiles(kept, sent, tile):
    rows, width = 2 * kept.shape[0], kept.shape[1]
    core = lax.axis_index("dp") % 2
    first = jnp.where(core == 0, kept, sent).reshape(rows // tile, 1, tile // 2, width)
    second = jnp.where(core == 0, sent, kept).reshape(rows // tile, 1, tile // 2, width)
    return jnp.concatenate([first, second], axis=1).reshape(rows, width)


def plain_sum(kept, sent, tile):
    matrix = from_tiles(kept, sent, tile)
    return lax.psum(
        lax.psum_scatter(matrix, "dp", scatter_dimension=0, tiled=True).astype(jnp.float32), "seq"
    )


def joined(terms, size, widths):
    block = terms.got[0].astype(jnp.float32) + terms.kept[0].astype(jnp.float32)
    got = swap_seq(block.astype(jnp.bfloat16)).astype(jnp.float32)
    here = lax.axis_index("seq") == 0
    first, second = jnp.where(here, block, got), jnp.where(here, got, block)
    parts, at = [], 0
    for index, width in enumerate(widths):
        rows = []
        for _ in range(size if index == len(widths) - 1 else 1):
            rows.append(
                jnp.concatenate([first[:, at : at + width], second[:, at : at + width]], axis=1)
            )
            at += width
        parts.append(jnp.concatenate(rows, axis=0))
    return parts


def per_device(
    tokens,
    cotangent,
    time_index,
    step_table,
    first_gain,
    attn_qkv,
    attn_out,
    second_gain,
    mlp_up,
    up_bias,
    mlp_down,
    down_bias,
    ada_weight,
    ada_bias,
):
    rows, width = tokens.shape[1:]
    dp_rank = lax.axis_index("dp")
    core = dp_rank % 2
    own_cond, silu_back = jax.vjp(
        jax.nn.silu, lax.dynamic_slice_in_dim(step_table, time_index[0], 1, axis=0)
    )
    positions = core * rows + jnp.arange(rows, dtype=jnp.int32)
    cosine, sine = tables(positions)
    tokens = swap_halves(tokens[0])
    time_index = swap_halves(time_index)
    cotangent = swap_halves(cotangent[0])
    cond = jax.nn.silu(lax.dynamic_slice_in_dim(step_table, time_index[0], 1, axis=0))
    ada_float = ada_weight.astype(jnp.float32)
    modulation = jnp.dot(cond, ada_float, precision=highest) + ada_bias.astype(jnp.float32)
    gain1 = first_gain.astype(jnp.float32)
    gain2 = second_gain.astype(jnp.float32)
    cond_row = jnp.pad(cond, ((0, 0), (0, width - cond.shape[1])))
    mods = jnp.concatenate(
        [modulation.reshape(6, width), gain1[None], gain2[None], cond_row, jnp.zeros((7, width))]
    )
    normed1, own_pair = project_key_value(tokens, mods, attn_qkv, cosine, sine, cotangent)
    peer_pair = swap_cores(own_pair)
    core_ref = core[None]
    (
        query, attended, log_total, mixed, d_middle, d_attended, up_keep, up_send,
        down_keep, down_send, up_bias_grad, sums2,
    ) = block_layer(
        core_ref, normed1, attn_qkv, cosine, sine, own_pair, peer_pair, mods,
        up_bias.astype(jnp.float32)[None], down_bias.astype(jnp.float32)[None],
        tokens, cotangent, attn_out, mlp_up, mlp_down,
    )
    hidden = mlp_up.shape[1]
    dp_size = lax.axis_size("dp")
    bits = dp_bits()
    by_steps = split_rows(width) == width // dp_size
    mixed = swap_halves(mixed)

    def blocks(part):
        return part.reshape(dp_size // 2, -1, part.shape[1])

    if by_steps:
        up = Flow(swap_cores(blocks(up_send)), blocks(up_keep))
        down = Flow(swap_cores(blocks(down_send)), blocks(down_keep))
    d_query, away_pair, _ = attend_back(
        query, peer_pair, d_attended, attended, log_total, free=(peer_pair,)
    )
    after = (mixed,)
    if by_steps:
        (down, up), sent = stage(4, [([down], "half"), ([up], bits[1])], (away_pair,))
        after = (sent, mixed)
    back_pair = swap_cores(away_pair)
    d_query, d_pair, _ = attend_back(
        query, own_pair, d_attended, attended, log_total, (d_query, cosine, sine), after
    )
    d_projected, qkv_keep, qkv_send, _ = projected_back(
        core_ref, d_query, d_pair, back_pair, normed1, cosine, sine
    )
    after = ()
    cut = (3 * width // 256 - 1) // 2 * 256
    if by_steps:
        got, kept = swap_cores(blocks(qkv_send)), blocks(qkv_keep)
        one, two = Flow(got, kept, (0, cut)), Flow(got, kept, (cut, 3 * width))
        (one, two), sent = stage(4, [([one], "half"), ([two], bits[1])])
        after = (sent,)
    tokens_grad, small, _ = tokens_back(
        d_projected, attn_qkv, tokens, d_middle, mods, sums2, up_bias_grad, after
    )
    got = swap_cores(small)
    if by_steps:
        (down, up, small), sent = stage(
            4, [([down], bits[1]), ([up], "half")], (), (got, small, True)
        )
        got = swap_seq(small)
        (one, two, small), sent = stage(
            4, [([one], bits[1]), ([two], "half")], (sent,), (got, small, False)
        )
        early, late = [up, down], [one, two]
        for bit, small_bit in zip(bits[2:], bits[1:]):
            early, sent = stage(early[0].count // 2, [(early, bit)], (sent,))
            got = swap_bit(small, small_bit)
            (*late, small), sent = stage(
                late[0].count // 2, [(late, bit)], (sent,), (got, small, False)
            )
        got = swap_bit(small, bits[-1])
        small = jnp.concatenate([small[:-8], got[:-8], small[-8:] + got[-8:]], axis=0)
        up_half, down_half = (hidden + width) // 2, width // 2
        up_rows, down_rows = joined(early[0], hidden // width, (up_half, down_half))
        grouped = jnp.concatenate(joined(late[0], 1, (cut // 2, (3 * width - cut) // 2)), axis=1)
    else:
        small = small + got
        moves = [swap_seq] + [functools.partial(swap_bit, bit=bit) for bit in bits[1:]]
        for move in moves:
            got = move(small)
            small = jnp.concatenate([small[:-8], got[:-8], small[-8:] + got[-8:]], axis=0)
        up_rows = plain_sum(up_keep, up_send, width)
        down_rows = plain_sum(down_keep, down_send, width)
        grouped = plain_sum(qkv_keep, qkv_send, width)
    per_sequence, sums = small[:-8].reshape(-1, 8, width), small[-8:]
    d_mod_all = per_sequence[:, :6].reshape(per_sequence.shape[0], 6 * width)
    cond_all = per_sequence[:, 6, : cond.shape[1]]
    ada_bias_grad = jnp.sum(d_mod_all, axis=0)
    own_columns = d_mod_all.shape[1] // lax.axis_size("dp")
    mine = lax.dynamic_slice_in_dim(d_mod_all, dp_rank * own_columns, own_columns, axis=1)
    ada_weight_grad = lax.dot_general(
        cond_all, mine, (((0,), (0,)), ((), ())), precision=highest
    )
    d_mod_own = jnp.where(lax.axis_index("seq") == core, d_mod_all[:1], d_mod_all[1:2])
    (cond_grad,) = silu_back(jnp.dot(d_mod_own, ada_float.T, precision=highest))
    parts = []
    for index in range(3):
        for start in range(index * HEADS * HD, 3 * width, 3 * HEADS * HD):
            parts.append(grouped[:, start : start + HEADS * HD])
    qkv_rows = jnp.concatenate(parts, axis=1)
    return (
        mixed[None],
        swap_halves(tokens_grad).astype(jnp.float32)[None],
        cond_grad,
        sums[0],
        qkv_rows,
        up_rows[:, hidden:],
        sums[1],
        up_rows[:, :hidden],
        sums[3:7].reshape(-1),
        down_rows,
        sums[2],
        ada_weight_grad,
        ada_bias_grad,
    )


def solution(mesh):
    placed = (
        P("dp", "seq", None),
        P("dp", "seq", None),
        P("dp"),
        P(),
        P(),
        P(),
        P(),
        P(),
        P(),
        P(),
        P(),
        P(),
        P(),
        P(),
    )
    return jax.shard_map(
        per_device,
        mesh=mesh,
        in_specs=placed,
        out_specs=(
            P("dp", "seq", None),
            P("dp", "seq", None),
            P("dp", None),
            P(),
            P("dp", None),
            P("dp", None),
            P(),
            P("dp", None),
            P(),
            P("dp", None),
            P(),
            P(None, "dp"),
            P(),
        ),
        check_vma=False,
    )
```

profile of v0, /device:TPU:0, one launch (start us, length us, event | category | flops | bytes accessed | tf_op | source)
XLA Modules:
  0.0 277.2 jit_solution(6613204603082552898)
XLA Ops:
  0.7 2.0 collective-permute-start.1
  2.7 1.8 collective-permute-start
  4.5 1.8 collective-permute-start.2
  7.6 1.0 fusion
  8.6 1.3 pad_maximum_fusion.1
  13.4 1.3 concatenate.37.mods
  14.7 5.8 %shard_map.237 = (bf16[512,768]{1,0:T(8,128)(2,1)}, bf16[512,1536]{1,0:T(8,128)(2,1)}) custom-call(bf16[512,768]{1,0:T(8,128)(2,1)S(1)} %collective-permute-done.tokens.tokens_far, f32[16,768]{1,0:T(8,128)} %concatenate.37.mods, bf16[768,2304]{1,0:T(8,128)(2,1)} %weight3.1, f32[512,128]{1,0:T(8,128)} %get-tuple-element.135.cosine.refs_1_, ...), custom_call_target="tpu_custom_call" | custom-call | flops 1 | bytes 1 | tf_op jit(solution)/shard_map/pallas_call | solution.py:97
  20.5 12.9 %collective-permute-start.3 = (bf16[512,1536]{1,0:T(8,128)(2,1)}, bf16[512,1536]{1,0:T(8,128)(2,1)S(1)}, u32[]{:S(2)}, u32[]{:S(2)}) collective-permute-start(bf16[512,1536]{1,0:T(8,128)(2,1)} %get-tuple-element.65.keys1.values1.keys.values), channel_id=1, source_target_pairs={{0,2},{2,0},{4,6},{6,4},{8,10},{10,8},{12,14},{14,12},{16,18},{18,... | collective-permute-start | bytes 4718600 | tf_op jit(solution)/shard_map/ppermute | solution.py:666
  34.5 2.1 collective-permute-done.3.keys2.values2.keys.values
  36.6 1.2 copy-done.1
  37.9 41.6 %shard_map.238 = (bf16[512,768]{1,0:T(8,128)(2,1)}, bf16[512,768]{1,0:T(8,128)(2,1)}, f32[3,4,512]{2,1,0:T(4,128)}, bf16[512,768]{1,0:T(8,128)(2,1)}, f32[512,76...) custom-call(s32[1]{0:T(128)} %bitcast.core, ...), custom_call_target="tpu_custom_call" | custom-call | flops 1 | bytes 1 | tf_op jit(solution)/shard_map/pallas_call | solution.py:97
  80.0 1.4 copy-done.2
  81.4 10.9 %shard_map.239 = (f32[512,768]{1,0:T(8,128)}, bf16[512,1536]{1,0:T(8,128)(2,1)}, f32[1,1]{1,0:T(1,128)}) custom-call(bf16[512,768]{1,0:T(8,128)(2,1)} %get-tuple-element.67.query, bf16[512,1536]{1,0:T(8,128)(2,1)S(1)} %copy-done.2, bf16[512,1536]{1,0:T(8,128)(2,1)S(1)} %copy-done.2, bf16[512,768]{1,0:T(8,128)(2,1)} %get-tuple-element.68.grad, ...), custom_call_target="tpu_custom_call" | custom-call | flops 1 | bytes 1 | tf_op jit(solution)/shard_map/pallas_call | solution.py:97
  92.7 1.8 collective-permute-start.4
  94.6 1.8 copy-done.5
  96.4 1.7 copy-done.6
  98.1 1.4 copy-done.8
  99.5 5.8 %shard_map.240 = (bf16[8,192,384]{2,1,0:T(8,128)(2,1)}, bf16[8,192,384]{2,1,0:T(8,128)(2,1)}, bf16[4,48,3840]{2,1,0:T(8,128)(2,1)}, bf16[4,48,3840]{2,1,0:T(8,128)(2,1)}) custom-call(s32[2]{0:T(128)S(1)} %pad_add_fusion.mine, bf16[8,192,768]{2,1,0:T(8,128)(2,1)} %collective-permute-done.5.refs_0_, bf16[8,192,768]{2,1,0:T(8,128)(2,1)S(1)} %bitcast.51, ...), custom_call_target="tpu_custom_call" | custom-call | flops 1 | bytes 1 | tf_op jit(solution)/shard_map/pallas_call | solution.py:97
  105.3 1.3 copy-done.11
  106.6 11.6 %shard_map.241 = (bf16[512,768]{1,0:T(8,128)(2,1)}, bf16[512,1536]{1,0:T(8,128)(2,1)}, f32[1,1]{1,0:T(1,128)}) custom-call(bf16[512,768]{1,0:T(8,128)(2,1)} %get-tuple-element.67.query, bf16[512,1536]{1,0:T(8,128)(2,1)} %get-tuple-element.65.keys1.values1.keys.values, bf16[512,1536]{1,0:T(8,128)(2,1)} %get-tuple-element.65.keys1.values1.keys.values, ...), custom_call_target="tpu_custom_call" | custom-call | flops 1 | bytes 1 | tf_op jit(solution)/shard_map/pallas_call | solution.py:97
  118.2 7.1 %shard_map.242 = (bf16[512,2304]{1,0:T(8,128)(2,1)}, bf16[384,2304]{1,0:T(8,128)(2,1)}, bf16[384,2304]{1,0:T(8,128)(2,1)}, f32[1,1]{1,0:T(1,128)}) custom-call(s32[1]{0:T(128)} %bitcast.core, bf16[512,768]{1,0:T(8,128)(2,1)} %get-tuple-element.78.d_query, bf16[512,1536]{1,0:T(8,128)(2,1)} %get-tuple-element.79.d_pair, ...), custom_call_target="tpu_custom_call" | custom-call | flops 1 | bytes 1 | tf_op jit(solution)/shard_map/pallas_call | solution.py:97
  125.3 1.0 collective-permute-start.8
  126.3 1.5 collective-permute-start.13
  127.8 1.0 collective-permute-start.12
  128.8 1.0 collective-permute-done.8.refs_0_
  129.8 1.5 copy-done.7
  131.3 2.5 shard_map.243
  133.8 8.0 %shard_map.244 = (bf16[512,768]{1,0:T(8,128)(2,1)}, f32[16,768]{1,0:T(8,128)}, f32[1,1]{1,0:T(1,128)}) custom-call(bf16[512,2304]{1,0:T(8,128)(2,1)} %get-tuple-element.80.d_projected, bf16[768,2304]{1,0:T(8,128)(2,1)} %weight3.1, bf16[768,2304]{1,0:T(8,128)(2,1)} %weight3.1, bf16[768,2304]{1,0:T(8,128)(2,1)} %weight3.1, bf16[512,768]{1,0:T(8,128)(2,1)} %copy-done.3, ...), custom_call_target="tpu_custom_call" | custom-call | flops 1 | bytes 1 | tf_op jit(solution)/shard_map/pallas_call | solution.py:97
  142.3 13.1 %collective-permute-done.12.refs_0_ = bf16[8,192,384]{2,1,0:T(8,128)(2,1)S(1)} collective-permute-done((bf16[8,192,384]{2,1,0:T(8,128)(2,1)S(1)}, bf16[8,192,384]{2,1,0:T(8,128)(2,1)S(1)}, u32[]{:S(2)}, u32[]{:S(2)}) %collective-permute-start.12) | collective-permute-done | bytes 1179680 | tf_op jit(solution)/shard_map/ppermute | solution.py:674
  155.5 5.1 %collective-permute-done.13.refs_2_ = bf16[4,48,3840]{2,1,0:T(8,128)(2,1)S(1)} collective-permute-done((bf16[4,48,3840]{2,1,0:T(8,128)(2,1)S(1)}, bf16[4,48,3840]{2,1,0:T(8,128)(2,1)S(1)}, u32[]{:S(2)}, u32[]{:S(2)}) %collective-permute-start.13) | collective-permute-done | bytes 1474592 | tf_op jit(solution)/shard_map/ppermute | solution.py:666
  161.4 2.9 %shard_map.245 = (bf16[4,192,384]{2,1,0:T(8,128)(2,1)}, bf16[4,192,384]{2,1,0:T(8,128)(2,1)}, bf16[4,48,1920]{2,1,0:T(8,128)(2,1)}, bf16[4,48,1920]{2,1,0:T(8,128)(2,1)}, f32[16,768]{1,0:T(8,128)}) custom-call(s32[2]{0:T(128)S(1)} %pad_add_fusion.1.mine, bf16[8,192,384]{2,1,0:T(8,128)(2,1)S(1)} %collective-permute-done.12.refs_0_, ...), custom_call_target="tpu_custom_call" | custom-call | flops 1 | bytes 1 | tf_op jit(solution)/shard_map/pallas_call | solution.py:97
  164.2 1.5 collective-permute-start.18
  165.7 1.5 collective-permute-start.19
  168.4 1.4 collective-permute-start.15
  169.7 21.9 %collective-permute-done.15.refs_6_ = f32[16,768]{1,0:T(8,128)S(1)} collective-permute-done((f32[16,768]{1,0:T(8,128)}, f32[16,768]{1,0:T(8,128)S(1)}, u32[]{:S(2)}, u32[]{:S(2)}) %collective-permute-start.15) | collective-permute-done | bytes 49184 | tf_op jit(solution)/shard_map/ppermute | solution.py:674
  191.7 1.1 copy-done.17
  192.8 1.0 copy-done.18
  193.8 1.0 copy-done.19
  195.6 3.5 %shard_map.246 = (bf16[4,48,512]{2,1,0:T(8,128)(2,1)}, bf16[4,48,512]{2,1,0:T(8,128)(2,1)}, bf16[4,48,640]{2,1,0:T(8,128)(2,1)}, bf16[4,48,640]{2,1,0:T(8,128)(2,1)}, f32[24,768]{1,0:T(8,128)}) custom-call(s32[2]{0:T(128)S(1)} %pad_add_fusion.1.mine, bf16[8,48,512]{2,1,0:T(8,128)(2,1)} %collective-permute-done.10.refs_0_, ...), custom_call_target="tpu_custom_call" | custom-call | flops 1 | bytes 1 | tf_op jit(solution)/shard_map/pallas_call | solution.py:97
  199.2 1.0 copy-done.26
  200.2 2.2 shard_map.247
  202.4 1.6 collective-permute-start.22
  204.0 1.7 collective-permute-start.17
  205.7 1.5 collective-permute-start.16
  207.8 4.7 %collective-permute-done.20.refs_6_ = f32[24,768]{1,0:T(8,128)S(1)} collective-permute-done((f32[24,768]{1,0:T(8,128)S(1)}, f32[24,768]{1,0:T(8,128)S(1)}, u32[]{:S(2)}, u32[]{:S(2)}) %collective-permute-start.20) | collective-permute-done | bytes 73760 | tf_op jit(solution)/shard_map/ppermute | solution.py:666
  212.5 1.1 copy-done.15
  215.0 7.4 %collective-permute-start.9 = (bf16[512,768]{1,0:T(8,128)(2,1)}, bf16[512,768]{1,0:T(8,128)(2,1)}, u32[]{:S(2)}, u32[]{:S(2)}) collective-permute-start(bf16[512,768]{1,0:T(8,128)(2,1)} %get-tuple-element.87), channel_id=1, source_target_pairs={{0,0},{1,2},{2,1},{3,3},{4,4},{5,6},{6,5},{7,7},{8,8},{9,10},{10,9... | collective-permute-start | bytes 2359304 | tf_op jit(solution)/shard_map/ppermute | solution.py:662
  222.4 1.6 collective-permute-start.23
  223.9 0.9 copy-done.24
  224.9 1.0 shard_map.249
  225.9 1.7 collective-permute-done.23.refs_4_
  227.6 1.0 copy-done.20
  228.6 1.8 shard_map.250
  230.4 2.6 collective-permute-start.25
  233.7 3.8 %collective-permute-done.25 = bf16[1,48,1152]{2,1,0:T(8,128)(2,1)S(1)} collective-permute-done((bf16[1,48,1152]{2,1,0:T(8,128)(2,1)}, bf16[1,48,1152]{2,1,0:T(8,128)(2,1)S(1)}, u32[]{:S(2)}, u32[]{:S(2)}) %collective-permute-start.25) | collective-permute-done | bytes 110624 | tf_op jit(solution)/shard_map/ppermute | solution.py:666
  237.5 0.9 bitcast_convert_fusion.2
  238.5 2.4 bitcast_convert_fusion
  240.9 1.5 collective-permute-start.24
  242.4 1.5 collective-permute-start.27
  244.2 14.4 %collective-permute-done.24 = f32[72,768]{1,0:T(8,128)S(1)} collective-permute-done((f32[72,768]{1,0:T(8,128)S(1)}, f32[72,768]{1,0:T(8,128)S(1)}, u32[]{:S(2)}, u32[]{:S(2)}) %collective-permute-start.24) | collective-permute-done | bytes 221216 | tf_op jit(solution)/shard_map/ppermute | solution.py:666
  260.1 1.2 fusion.3
  261.3 3.4 %collective-permute-done.27 = bf16[1,48,3456]{2,1,0:T(8,128)(2,1)S(1)} collective-permute-done((bf16[1,48,3456]{2,1,0:T(8,128)(2,1)S(1)}, bf16[1,48,3456]{2,1,0:T(8,128)(2,1)S(1)}, u32[]{:S(2)}, u32[]{:S(2)}) %collective-permute-start.27) | collective-permute-done | bytes 331808 | tf_op jit(solution)/shard_map/ppermute | solution.py:666
  265.8 2.2 fusion.7
  268.0 5.7 %collective-permute-done.28 = bf16[48,3456]{1,0:T(8,128)(2,1)S(1)} collective-permute-done((bf16[48,3456]{1,0:T(8,128)(2,1)S(1)}, bf16[48,3456]{1,0:T(8,128)(2,1)S(1)}, u32[]{:S(2)}, u32[]{:S(2)}) %collective-permute-start.28) | collective-permute-done | bytes 331808 | tf_op jit(solution)/shard_map/ppermute | solution.py:674
  (147 shorter events, 16.5 us)
Async XLA Ops:
  0.6 12.1 %copy-start = (bf16[128,4608]{1,0:T(8,128)(2,1)S(1)}, bf16[128,4608]{1,0:T(8,128)(2,1)}, u32[]{:S(2)}) copy-start(bf16[128,4608]{1,0:T(8,128)(2,1)} %param.26) | copy-start | bytes 3538948
  0.7 9.3 %collective-permute-start.1 = (s32[1]{0:T(128)}, s32[1]{0:T(128)}, u32[]{:S(2)}, u32[]{:S(2)}) collective-permute-start(s32[1]{0:T(128)} %param.16), channel_id=1, source_target_pairs={{0,0},{1,2},{2,1},{3,3},{4,4},{5,6},{6,5},{7,7},{8,8},{9,10},{10,9... | collective-permute-start | bytes 20 | tf_op jit(solution)/shard_map/ppermute | solution.py:662
  2.7 11.9 %collective-permute-start = (bf16[512,768]{1,0:T(8,128)(2,1)}, bf16[512,768]{1,0:T(8,128)(2,1)S(1)}, u32[]{:S(2)}, u32[]{:S(2)}) collective-permute-start(bf16[512,768]{1,0:T(8,128)(2,1)} %bitcast.61), channel_id=1, source_target_pairs={{0,0},{1,2},{2,1},{3,3},{4,4},{5,6},{6,5},{7,7},{8,8},{9,10},{10,9... | collective-permute-start | bytes 2359304 | tf_op jit(solution)/shard_map/ppermute | solution.py:662
  4.5 10.1 %collective-permute-start.2 = (bf16[512,768]{1,0:T(8,128)(2,1)}, bf16[512,768]{1,0:T(8,128)(2,1)S(1)}, u32[]{:S(2)}, u32[]{:S(2)}) collective-permute-start(bf16[512,768]{1,0:T(8,128)(2,1)} %bitcast.62), channel_id=1, source_target_pairs={{0,0},{1,2},{2,1},{3,3},{4,4},{5,6},{6,5},{7,7},{8,8},{9,10},{10,9... | collective-permute-start | bytes 2359304 | tf_op jit(solution)/shard_map/ppermute | solution.py:662
  7.6 5.6 %copy-start.36 = (bf16[4608]{0:T(1024)(128)(2,1)S(1)}, bf16[4608]{0:T(1024)(128)(2,1)}, u32[]{:S(2)}) copy-start(bf16[4608]{0:T(1024)(128)(2,1)} %param.27) | copy-start | bytes 27652
  14.6 5.9 %copy-start.3 = (bf16[512,768]{1,0:T(8,128)(2,1)}, bf16[512,768]{1,0:T(8,128)(2,1)S(1)}, u32[]{:S(2)}) copy-start(bf16[512,768]{1,0:T(8,128)(2,1)S(1)} %collective-permute-done.tokens.tokens_far) | copy-start | bytes 2359300
  14.6 5.9 %copy-start.4 = (bf16[512,768]{1,0:T(8,128)(2,1)}, bf16[512,768]{1,0:T(8,128)(2,1)S(1)}, u32[]{:S(2)}) copy-start(bf16[512,768]{1,0:T(8,128)(2,1)S(1)} %collective-permute-done.2.cotangent.cotangent_far) | copy-start | bytes 2359300
  14.6 18.7 %copy-start.37 = (bf16[3072]{0:T(1024)(128)(2,1)S(1)}, bf16[3072]{0:T(1024)(128)(2,1)}, u32[]{:S(2)}) copy-start(bf16[3072]{0:T(1024)(128)(2,1)} %param.23) | copy-start | bytes 18436
  14.6 19.3 %copy-start.39 = (bf16[768]{0:T(1024)(128)(2,1)S(1)}, bf16[768]{0:T(1024)(128)(2,1)}, u32[]{:S(2)}) copy-start(bf16[768]{0:T(1024)(128)(2,1)} %param.25) | copy-start | bytes 4612
  20.5 16.1 %collective-permute-start.3 = (bf16[512,1536]{1,0:T(8,128)(2,1)}, bf16[512,1536]{1,0:T(8,128)(2,1)S(1)}, u32[]{:S(2)}, u32[]{:S(2)}) collective-permute-start(bf16[512,1536]{1,0:T(8,128)(2,1)} %get-tuple-element.65.keys1.values1.keys.values), channel_id=1, source_target_pairs={{0,2},{2,0},{4,6},{6,4},{8,10},{10,8},{12,14},{14,12},{16,18},{18,... | collective-permute-start | bytes 4718600 | tf_op jit(solution)/shard_map/ppermute | solution.py:666
  36.6 1.2 copy-start.1
  79.5 15.1 %collective-permute-start.6 = (bf16[8,48,3840]{2,1,0:T(8,128)(2,1)}, bf16[8,48,3840]{2,1,0:T(8,128)(2,1)}, u32[]{:S(2)}, u32[]{:S(2)}) collective-permute-start(bf16[8,48,3840]{2,1,0:T(8,128)(2,1)} %bitcast.58), channel_id=1, source_target_pairs={{0,2},{2,0},{4,6},{6,4},{8,10},{10,8},{12,14},{14,12},{16,18},{18,... | collective-permute-start | bytes 8847368 | tf_op jit(solution)/shard_map/ppermute | solution.py:666
  79.9 14.7 %collective-permute-start.5 = (bf16[8,192,768]{2,1,0:T(8,128)(2,1)}, bf16[8,192,768]{2,1,0:T(8,128)(2,1)}, u32[]{:S(2)}, u32[]{:S(2)}) collective-permute-start(bf16[8,192,768]{2,1,0:T(8,128)(2,1)} %bitcast.59), channel_id=1, source_target_pairs={{0,2},{2,0},{4,6},{6,4},{8,10},{10,8},{12,14},{14,12},{16,18},{18,... | collective-permute-start | bytes 7077896 | tf_op jit(solution)/shard_map/ppermute | solution.py:666
  80.0 1.4 copy-start.2
  92.3 25.9 %collective-permute-start.7 = (bf16[512,1536]{1,0:T(8,128)(2,1)}, bf16[512,1536]{1,0:T(8,128)(2,1)S(1)}, u32[]{:S(2)}, u32[]{:S(2)}) collective-permute-start(bf16[512,1536]{1,0:T(8,128)(2,1)} %get-tuple-element.76.refs_4_), channel_id=1, source_target_pairs={{0,2},{2,0},{4,6},{6,4},{8,10},{10,8},{12,14},{14,12},{16,18},{18,... | collective-permute-start | bytes 4718600 | tf_op jit(solution)/shard_map/ppermute | solution.py:666
  92.7 12.6 %collective-permute-start.4 = (bf16[512,768]{1,0:T(8,128)(2,1)}, bf16[512,768]{1,0:T(8,128)(2,1)S(1)}, u32[]{:S(2)}, u32[]{:S(2)}) collective-permute-start(bf16[512,768]{1,0:T(8,128)(2,1)} %get-tuple-element.66), channel_id=1, source_target_pairs={{0,0},{1,2},{2,1},{3,3},{4,4},{5,6},{6,5},{7,7},{8,8},{9,10},{10,9... | collective-permute-start | bytes 2359304 | tf_op jit(solution)/shard_map/ppermute | solution.py:662
  94.6 1.8 copy-start.5
  96.4 1.7 copy-start.6
  98.1 1.4 copy-start.8
  105.3 1.3 copy-start.11
  118.2 8.1 %copy-start.40 = (bf16[4,48,3840]{2,1,0:T(8,128)(2,1)S(1)}, bf16[4,48,3840]{2,1,0:T(8,128)(2,1)}, u32[]{:S(2)}) copy-start(bf16[4,48,3840]{2,1,0:T(8,128)(2,1)} %get-tuple-element.92) | copy-start | bytes 4423684
  118.2 9.6 %copy-start.12 = (bf16[8,192,384]{2,1,0:T(8,128)(2,1)S(1)}, bf16[8,192,384]{2,1,0:T(8,128)(2,1)}, u32[]{:S(2)}) copy-start(bf16[8,192,384]{2,1,0:T(8,128)(2,1)} %get-tuple-element.77.refs_3_) | copy-start | bytes 3538948
  125.3 4.5 %collective-permute-start.8 = (bf16[8,48,2304]{2,1,0:T(8,128)(2,1)}, bf16[8,48,2304]{2,1,0:T(8,128)(2,1)S(1)}, u32[]{:S(2)}, u32[]{:S(2)}) collective-permute-start(bf16[8,48,2304]{2,1,0:T(8,128)(2,1)} %bitcast.60), channel_id=1, source_target_pairs={{0,2},{2,0},{4,6},{6,4},{8,10},{10,8},{12,14},{14,12},{16,18},{18,... | collective-permute-start | bytes 5308424 | tf_op jit(solution)/shard_map/ppermute | solution.py:666
  126.3 34.3 %collective-permute-start.13 = (bf16[4,48,3840]{2,1,0:T(8,128)(2,1)S(1)}, bf16[4,48,3840]{2,1,0:T(8,128)(2,1)S(1)}, u32[]{:S(2)}, u32[]{:S(2)}) collective-permute-start(bf16[4,48,3840]{2,1,0:T(8,128)(2,1)S(1)} %copy-done.40), channel_id=1, source_target_pairs={{0,4},{2,6},{4,0},{6,2},{8,12},{10,14},{12,8},{14,10},{16,20},{18,... | collective-permute-start | bytes 4423688 | tf_op jit(solution)/shard_map/ppermute | solution.py:666
  127.8 27.7 %collective-permute-start.12 = (bf16[8,192,384]{2,1,0:T(8,128)(2,1)S(1)}, bf16[8,192,384]{2,1,0:T(8,128)(2,1)S(1)}, u32[]{:S(2)}, u32[]{:S(2)}) collective-permute-start(bf16[8,192,384]{2,1,0:T(8,128)(2,1)S(1)} %copy-done.12), channel_id=1, source_target_pairs={{0,1},{1,0},{2,3},{3,2},{4,5},{5,4},{6,7},{7,6},{8,9},{9,8},{10,11... | collective-permute-start | bytes 3538952 | tf_op jit(solution)/shard_map/ppermute | solution.py:674
  129.8 1.5 copy-start.7
  131.3 2.5 copy-start.32
  133.8 26.8 %copy-start.9 = (bf16[4,48,3840]{2,1,0:T(8,128)(2,1)S(1)}, bf16[4,48,3840]{2,1,0:T(8,128)(2,1)}, u32[]{:S(2)}) copy-start(bf16[4,48,3840]{2,1,0:T(8,128)(2,1)} %get-tuple-element.93.refs_3_) | copy-start | bytes 4423684
  133.8 26.8 %copy-start.10 = (bf16[8,192,384]{2,1,0:T(8,128)(2,1)S(1)}, bf16[8,192,384]{2,1,0:T(8,128)(2,1)}, u32[]{:S(2)}) copy-start(bf16[8,192,384]{2,1,0:T(8,128)(2,1)} %get-tuple-element.91.refs_1_) | copy-start | bytes 3538948
  141.8 18.7 %collective-permute-start.14 = (f32[16,768]{1,0:T(8,128)}, f32[16,768]{1,0:T(8,128)S(1)}, u32[]{:S(2)}, u32[]{:S(2)}) collective-permute-start(f32[16,768]{1,0:T(8,128)} %get-tuple-element.94.refs_4_), channel_id=1, source_target_pairs={{0,2},{2,0},{4,6},{6,4},{8,10},{10,8},{12,14},{14,12},{16,18},{18,... | collective-permute-start | bytes 147464 | tf_op jit(solution)/shard_map/ppermute | solution.py:666
  164.2 34.9 %copy-start.13 = (bf16[4,48,1920]{2,1,0:T(8,128)(2,1)S(1)}, bf16[4,48,1920]{2,1,0:T(8,128)(2,1)}, u32[]{:S(2)}) copy-start(bf16[4,48,1920]{2,1,0:T(8,128)(2,1)} %get-tuple-element.102.refs_1_) | copy-start | bytes 2211844
  164.2 34.9 %collective-permute-start.18 = (bf16[4,48,1920]{2,1,0:T(8,128)(2,1)}, bf16[4,48,1920]{2,1,0:T(8,128)(2,1)S(1)}, u32[]{:S(2)}, u32[]{:S(2)}) collective-permute-start(bf16[4,48,1920]{2,1,0:T(8,128)(2,1)} %get-tuple-element.101), channel_id=1, source_target_pairs={{0,1},{1,0},{2,3},{3,2},{4,5},{5,4},{6,7},{7,6},{8,9},{9,8},{10,11... | collective-permute-start | bytes 2211848 | tf_op jit(solution)/shard_map/ppermute | solution.py:674
  165.7 33.4 %collective-permute-start.19 = (bf16[4,192,384]{2,1,0:T(8,128)(2,1)}, bf16[4,192,384]{2,1,0:T(8,128)(2,1)}, u32[]{:S(2)}, u32[]{:S(2)}) collective-permute-start(bf16[4,192,384]{2,1,0:T(8,128)(2,1)} %get-tuple-element.95.refs_4_), channel_id=1, source_target_pairs={{0,4},{2,6},{4,0},{6,2},{8,12},{10,14},{12,8},{14,10},{16,20},{18,... | collective-permute-start | bytes 1769480 | tf_op jit(solution)/shard_map/ppermute | solution.py:666
  167.2 24.5 %collective-permute-start.11 = (bf16[4,48,1280]{2,1,0:T(8,128)(2,1)}, bf16[4,48,1280]{2,1,0:T(8,128)(2,1)}, u32[]{:S(2)}, u32[]{:S(2)}) collective-permute-start(bf16[4,48,1280]{2,1,0:T(8,128)(2,1)} %get-tuple-element.89), channel_id=1, source_target_pairs={{0,4},{2,6},{4,0},{6,2},{8,12},{10,14},{12,8},{14,10},{16,20},{18,... | collective-permute-start | bytes 1474568 | tf_op jit(solution)/shard_map/ppermute | solution.py:666
  167.7 24.0 %collective-permute-start.10 = (bf16[8,48,512]{2,1,0:T(8,128)(2,1)}, bf16[8,48,512]{2,1,0:T(8,128)(2,1)}, u32[]{:S(2)}, u32[]{:S(2)}) collective-permute-start(bf16[8,48,512]{2,1,0:T(8,128)(2,1)} %get-tuple-element.86.refs_0_), channel_id=1, source_target_pairs={{0,1},{1,0},{2,3},{3,2},{4,5},{5,4},{6,7},{7,6},{8,9},{9,8},{10,11... | collective-permute-start | bytes 1179656 | tf_op jit(solution)/shard_map/ppermute | solution.py:674
  168.4 23.3 %collective-permute-start.15 = (f32[16,768]{1,0:T(8,128)}, f32[16,768]{1,0:T(8,128)S(1)}, u32[]{:S(2)}, u32[]{:S(2)}) collective-permute-start(f32[16,768]{1,0:T(8,128)} %get-tuple-element.96.refs_5_), channel_id=1, source_target_pairs={{0,1},{1,0},{2,3},{3,2},{4,5},{5,4},{6,7},{7,6},{8,9},{9,8},{10,11... | collective-permute-start | bytes 147464 | tf_op jit(solution)/shard_map/ppermute | solution.py:674
  169.7 29.4 %copy-start.16 = (bf16[4,192,384]{2,1,0:T(8,128)(2,1)S(1)}, bf16[4,192,384]{2,1,0:T(8,128)(2,1)}, u32[]{:S(2)}) copy-start(bf16[4,192,384]{2,1,0:T(8,128)(2,1)} %get-tuple-element.103.refs_3_) | copy-start | bytes 1769476
  191.7 1.1 copy-start.17
  199.1 13.3 %copy-start.22 = (bf16[4,48,640]{2,1,0:T(8,128)(2,1)S(1)}, bf16[4,48,640]{2,1,0:T(8,128)(2,1)}, u32[]{:S(2)}) copy-start(bf16[4,48,640]{2,1,0:T(8,128)(2,1)} %get-tuple-element.100.refs_3_) | copy-start | bytes 737284
  199.1 13.3 %copy-start.25 = (bf16[4,48,512]{2,1,0:T(8,128)(2,1)S(1)}, bf16[4,48,512]{2,1,0:T(8,128)(2,1)}, u32[]{:S(2)}) copy-start(bf16[4,48,512]{2,1,0:T(8,128)(2,1)} %get-tuple-element.98.refs_1_) | copy-start | bytes 589828
  200.2 3.8 %copy-start.41 = (bf16[4,48,640]{2,1,0:T(8,128)(2,1)S(1)}, bf16[4,48,640]{2,1,0:T(8,128)(2,1)}, u32[]{:S(2)}) copy-start(bf16[4,48,640]{2,1,0:T(8,128)(2,1)} %get-tuple-element.99) | copy-start | bytes 737284
  200.2 5.6 %copy-start.27 = (bf16[4,48,512]{2,1,0:T(8,128)(2,1)S(1)}, bf16[4,48,512]{2,1,0:T(8,128)(2,1)}, u32[]{:S(2)}) copy-start(bf16[4,48,512]{2,1,0:T(8,128)(2,1)} %get-tuple-element.97.refs_4_) | copy-start | bytes 589828
  200.2 7.1 %copy-start.29 = (f32[24,768]{1,0:T(8,128)S(1)}, f32[24,768]{1,0:T(8,128)}, u32[]{:S(2)}) copy-start(f32[24,768]{1,0:T(8,128)} %get-tuple-element.105.refs_5_) | copy-start | bytes 221188
  202.4 21.5 %copy-start.14 = (bf16[2,48,3456]{2,1,0:T(8,128)(2,1)S(1)}, bf16[2,48,3456]{2,1,0:T(8,128)(2,1)}, u32[]{:S(2)}) copy-start(bf16[2,48,3456]{2,1,0:T(8,128)(2,1)} %get-tuple-element.108.refs_1_) | copy-start | bytes 1990660
  202.4 21.5 %collective-permute-start.22 = (bf16[2,48,3456]{2,1,0:T(8,128)(2,1)}, bf16[2,48,3456]{2,1,0:T(8,128)(2,1)S(1)}, u32[]{:S(2)}, u32[]{:S(2)}) collective-permute-start(bf16[2,48,3456]{2,1,0:T(8,128)(2,1)} %get-tuple-element.104.refs_4_), channel_id=1, source_target_pairs={{0,8},{2,10},{4,12},{6,14},{8,0},{10,2},{12,4},{14,6},{16,24},{18,... | collective-permute-start | bytes 1990664 | tf_op jit(solution)/shard_map/ppermute | solution.py:666
  204.0 8.4 %collective-permute-start.17 = (bf16[4,48,640]{2,1,0:T(8,128)(2,1)S(1)}, bf16[4,48,640]{2,1,0:T(8,128)(2,1)S(1)}, u32[]{:S(2)}, u32[]{:S(2)}) collective-permute-start(bf16[4,48,640]{2,1,0:T(8,128)(2,1)S(1)} %copy-done.41), channel_id=1, source_target_pairs={{0,1},{1,0},{2,3},{3,2},{4,5},{5,4},{6,7},{7,6},{8,9},{9,8},{10,11... | collective-permute-start | bytes 737288 | tf_op jit(solution)/shard_map/ppermute | solution.py:674
  205.7 6.7 %collective-permute-start.16 = (bf16[4,48,512]{2,1,0:T(8,128)(2,1)S(1)}, bf16[4,48,512]{2,1,0:T(8,128)(2,1)S(1)}, u32[]{:S(2)}, u32[]{:S(2)}) collective-permute-start(bf16[4,48,512]{2,1,0:T(8,128)(2,1)S(1)} %copy-done.27), channel_id=1, source_target_pairs={{0,4},{2,6},{4,0},{6,2},{8,12},{10,14},{12,8},{14,10},{16,20},{18,... | collective-permute-start | bytes 589832 | tf_op jit(solution)/shard_map/ppermute | solution.py:666
  207.3 5.2 %collective-permute-start.20 = (f32[24,768]{1,0:T(8,128)S(1)}, f32[24,768]{1,0:T(8,128)S(1)}, u32[]{:S(2)}, u32[]{:S(2)}) collective-permute-start(f32[24,768]{1,0:T(8,128)S(1)} %copy-done.29), channel_id=1, source_target_pairs={{0,4},{2,6},{4,0},{6,2},{8,12},{10,14},{12,8},{14,10},{16,20},{18,... | collective-permute-start | bytes 221192 | tf_op jit(solution)/shard_map/ppermute | solution.py:666
  212.5 1.1 copy-start.15
  214.4 13.1 %copy-start.23 = (bf16[2,48,1152]{2,1,0:T(8,128)(2,1)S(1)}, bf16[2,48,1152]{2,1,0:T(8,128)(2,1)}, u32[]{:S(2)}) copy-start(bf16[2,48,1152]{2,1,0:T(8,128)(2,1)} %get-tuple-element.107.refs_1_) | copy-start | bytes 663556
  214.4 13.1 %collective-permute-start.21 = (bf16[2,48,1152]{2,1,0:T(8,128)(2,1)}, bf16[2,48,1152]{2,1,0:T(8,128)(2,1)}, u32[]{:S(2)}, u32[]{:S(2)}) collective-permute-start(bf16[2,48,1152]{2,1,0:T(8,128)(2,1)} %get-tuple-element.106.refs_2_), channel_id=1, source_target_pairs={{0,8},{2,10},{4,12},{6,14},{8,0},{10,2},{12,4},{14,6},{16,24},{18,... | collective-permute-start | bytes 663560 | tf_op jit(solution)/shard_map/ppermute | solution.py:666
  215.0 23.5 %collective-permute-start.9 = (bf16[512,768]{1,0:T(8,128)(2,1)}, bf16[512,768]{1,0:T(8,128)(2,1)}, u32[]{:S(2)}, u32[]{:S(2)}) collective-permute-start(bf16[512,768]{1,0:T(8,128)(2,1)} %get-tuple-element.87), channel_id=1, source_target_pairs={{0,0},{1,2},{2,1},{3,3},{4,4},{5,6},{6,5},{7,7},{8,8},{9,10},{10,9... | collective-permute-start | bytes 2359304 | tf_op jit(solution)/shard_map/ppermute | solution.py:662
  222.4 5.2 %collective-permute-start.23 = (f32[40,768]{1,0:T(8,128)}, f32[40,768]{1,0:T(8,128)}, u32[]{:S(2)}, u32[]{:S(2)}) collective-permute-start(f32[40,768]{1,0:T(8,128)} %get-tuple-element.110.refs_3_), channel_id=1, source_target_pairs={{0,8},{2,10},{4,12},{6,14},{8,0},{10,2},{12,4},{14,6},{16,24},{18,... | collective-permute-start | bytes 368648 | tf_op jit(solution)/shard_map/ppermute | solution.py:666
  224.9 2.7 copy-start.28
  230.4 10.5 %copy-start.35 = (f32[72,768]{1,0:T(8,128)S(1)}, f32[72,768]{1,0:T(8,128)}, u32[]{:S(2)}) copy-start(f32[72,768]{1,0:T(8,128)} %get-tuple-element.111) | copy-start | bytes 663556
  230.4 12.0 %copy-start.21 = (bf16[1,48,3456]{2,1,0:T(8,128)(2,1)S(1)}, bf16[1,48,3456]{2,1,0:T(8,128)(2,1)}, u32[]{:S(2)}) copy-start(bf16[1,48,3456]{2,1,0:T(8,128)(2,1)} %get-tuple-element.109.refs_2_) | copy-start | bytes 995332
  230.4 13.5 %copy-start.34 = (bf16[1,48,1152]{2,1,0:T(8,128)(2,1)S(1)}, bf16[1,48,1152]{2,1,0:T(8,128)(2,1)}, u32[]{:S(2)}) copy-start(bf16[1,48,1152]{2,1,0:T(8,128)(2,1)} %get-tuple-element.113) | copy-start | bytes 331780
  230.4 7.1 %collective-permute-start.25 = (bf16[1,48,1152]{2,1,0:T(8,128)(2,1)}, bf16[1,48,1152]{2,1,0:T(8,128)(2,1)S(1)}, u32[]{:S(2)}, u32[]{:S(2)}) collective-permute-start(bf16[1,48,1152]{2,1,0:T(8,128)(2,1)} %get-tuple-element.112), channel_id=1, source_target_pairs={{0,16},{2,18},{4,20},{6,22},{8,24},{10,26},{12,28},{14,30},{16,0},... | collective-permute-start | bytes 331784 | tf_op jit(solution)/shard_map/ppermute | solution.py:666
  238.4 5.5 %collective-permute-start.26 = (bf16[48,1152]{1,0:T(8,128)(2,1)S(1)}, bf16[48,1152]{1,0:T(8,128)(2,1)S(1)}, u32[]{:S(2)}, u32[]{:S(2)}) collective-permute-start(bf16[48,1152]{1,0:T(8,128)(2,1)S(1)} %bitcast_convert_fusion.2), channel_id=1, source_target_pairs={{0,1},{1,0},{2,3},{3,2},{4,5},{5,4},{6,7},{7,6},{8,9},{9,8},{10,11... | collective-permute-start | bytes 331784 | tf_op jit(solution)/shard_map/ppermute | solution.py:674
  240.9 17.7 %collective-permute-start.24 = (f32[72,768]{1,0:T(8,128)S(1)}, f32[72,768]{1,0:T(8,128)S(1)}, u32[]{:S(2)}, u32[]{:S(2)}) collective-permute-start(f32[72,768]{1,0:T(8,128)S(1)} %copy-done.35), channel_id=1, source_target_pairs={{0,16},{2,18},{4,20},{6,22},{8,24},{10,26},{12,28},{14,30},{16,0},... | collective-permute-start | bytes 663560 | tf_op jit(solution)/shard_map/ppermute | solution.py:666
  242.4 22.3 %collective-permute-start.27 = (bf16[1,48,3456]{2,1,0:T(8,128)(2,1)S(1)}, bf16[1,48,3456]{2,1,0:T(8,128)(2,1)S(1)}, u32[]{:S(2)}, u32[]{:S(2)}) collective-permute-start(bf16[1,48,3456]{2,1,0:T(8,128)(2,1)S(1)} %copy-done.21), channel_id=1, source_target_pairs={{0,16},{2,18},{4,20},{6,22},{8,24},{10,26},{12,28},{14,30},{16,0},... | collective-permute-start | bytes 995336 | tf_op jit(solution)/shard_map/ppermute | solution.py:666
  244.1 14.4 %copy-start.38 = (f32[48,2304]{1,0:T(8,128)}, f32[48,2304]{1,0:T(8,128)S(1)}, u32[]{:S(2)}) copy-start(f32[48,2304]{1,0:T(8,128)S(1)} %slice_dynamic-update-slice_fusion.1) | copy-start | bytes 1327108
  244.2 20.5 %copy-start.33 = (bf16[1,48,3456]{2,1,0:T(8,128)(2,1)S(1)}, bf16[1,48,3456]{2,1,0:T(8,128)(2,1)}, u32[]{:S(2)}) copy-start(bf16[1,48,3456]{2,1,0:T(8,128)(2,1)} %get-tuple-element.114) | copy-start | bytes 995332
  264.8 8.9 %collective-permute-start.28 = (bf16[48,3456]{1,0:T(8,128)(2,1)S(1)}, bf16[48,3456]{1,0:T(8,128)(2,1)S(1)}, u32[]{:S(2)}, u32[]{:S(2)}) collective-permute-start(bf16[48,3456]{1,0:T(8,128)(2,1)S(1)} %bitcast_convert_fusion.1), channel_id=1, source_target_pairs={{0,1},{1,0},{2,3},{3,2},{4,5},{5,4},{6,7},{7,6},{8,9},{9,8},{10,11... | collective-permute-start | bytes 995336 | tf_op jit(solution)/shard_map/ppermute | solution.py:674
  (7 other events, 6.6 us)
where the time goes:
time: 279 us; the launch traced here: 277 us
  Pallas kernels  106 us (38%)
  waiting for transfers between devices  76.9 us (28%)
  starting transfers between devices  51.5 us (18%)
  local copies, waits for them, and re-layouts  26 us (9%)
  other arithmetic  9.13 us (3%)
  matrix products  3.98 us (1%)
  between operations  3.94 us (1%)
    pallas_call x14, Pallas kernels, run(): return call(*placed)  106 us
    ppermute x7, waiting for transfers between devices, swap_seq(): return lax.ppermute(block, 'seq', [(0, 1), (1, 0)])  40.7 us
    ppermute x17, waiting for transfers between devices, swap_bit(): lax.ppermute(block, 'dp', [(i, i ^ bit) for i in range(lax.axis_size('dp'...  36.2 us
    ppermute x17, starting transfers between devices, swap_bit(): lax.ppermute(block, 'dp', [(i, i ^ bit) for i in range(lax.axis_size('dp'...  30.1 us
    unnamed x93, local copies, waits for them, and re-layouts  20.1 us
    ppermute x5, starting transfers between devices, swap_halves(): return lax.ppermute(block, ('dp', 'seq'), perm)  14.8 us
    ppermute x7, starting transfers between devices, swap_seq(): return lax.ppermute(block, 'seq', [(0, 1), (1, 0)])  6.67 us
  transfers between devices with their start and end apart: 29, of which 11 were waited for; matrix products, arithmetic and copies ran while one was open for 6% of the time, Pallas kernels for 17%

commit v1 on v0

--- a/solution.py
+++ b/solution.py
@@ -145,12 +145,13 @@
     return jnp.concatenate(parts, axis=1)
 
 
-COLUMNS = 768
-
-
-def key_value_body(tokens, mods, weight, cosine, sine, cotangent, normed, out):
+HEADS = 4
+
+
+def key_value_body(
+    tokens, mods, key_weight, value_weight, cosine, sine, normed, every, *parts
+):
     step = pl.program_id(0)
-    turned_steps = pl.num_programs(0) // 2
 
     @pl.when(step == 0)
     def _():
@@ -158,35 +159,39 @@
         value = hat * row(mods, GAIN1) * (1.0 + row(mods, SCALE1)) + row(mods, SHIFT1)
         normed[...] = value.astype(jnp.bfloat16)
 
-    @pl.when(step < turned_steps)
-    def _():
-        value = dot(normed[...], weight[...])
-        out[...] = rotate_lanes(value, cosine[...], sine[...]).astype(jnp.bfloat16)
-
-    @pl.when(step >= turned_steps)
-    def _():
-        out[...] = dot(normed[...], weight[...]).astype(jnp.bfloat16)
-
-
-def project_key_value(tokens, mods, weight, cosine, sine, after):
+    keys = rotate_lanes(dot(normed[...], key_weight[...]), cosine[...], sine[...])
+    values = dot(normed[...], value_weight[...])
+    both = jnp.concatenate([keys, values], axis=1).astype(jnp.bfloat16)
+    every[...] = both
+    for index, part in enumerate(parts):
+
+        @pl.when(step == index)
+        def _(part=part):
+            part[...] = both
+
+
+def project_key_value(tokens, mods, weight, cosine, sine):
     rows, width = tokens.shape
-    first = width // COLUMNS
+    lanes = HEADS * HD
+    steps = width // lanes
+    low = jnp.bfloat16
     return kernel_call(
         key_value_body,
-        2 * first,
+        steps,
         [
             full((rows, width)),
             full((16, width)),
-            columns(width, COLUMNS, first),
+            columns(width, lanes, steps),
+            columns(width, lanes, 2 * steps),
             full((rows, 128)),
             full((rows, 128)),
-            pl.BlockSpec(memory_space=pl.ANY),
         ],
-        [full((rows, width)), columns(rows, COLUMNS)],
-        [far((rows, width), jnp.bfloat16), far((rows, 2 * width), jnp.bfloat16)],
+        [full((rows, width)), columns(rows, 2 * lanes)] + [full((rows, 2 * lanes))] * steps,
+        [far((rows, width), low), far((rows, 2 * width), low)]
+        + [far((rows, 2 * lanes), low)] * steps,
         [],
-        18,
-    )(tokens, mods, weight, cosine, sine, after, free=(tokens, after))
+        24,
+    )(tokens, mods, weight, weight, cosine, sine, free=(tokens,))
 
 
 def head_mask(shape, head):
@@ -194,12 +199,13 @@
     return jnp.where(lane // HD == head, 1.0, 0.0).astype(jnp.bfloat16)
 
 
-HEADS = 4
-
-
 def head_lanes(head):
     pair, place = divmod(head, 2)
     return slice(pair * 128, (pair + 1) * 128), place, slice(place * HD, (place + 1) * HD)
+
+
+def value_lanes(lanes):
+    return slice(HEADS * HD + lanes.start, HEADS * HD + lanes.stop)
 
 
 def in_turn(count, first, rest):
@@ -213,13 +219,13 @@
     return results
 
 
-def attend_heads(query, keys1, values1, keys2, values2, log_total):
+def attend_heads(query, pair1, pair2, log_total):
     rows = query.shape[0]
 
     def first(head):
         lanes, place, _ = head_lanes(head)
         own = query[:, lanes] * head_mask((rows, 128), place)
-        return dot(keys1[:, lanes], own, 1, 1), dot(keys2[:, lanes], own, 1, 1)
+        return dot(pair1[:, lanes], own, 1, 1), dot(pair2[:, lanes], own, 1, 1)
 
     def rest(head, scores):
         lanes, place, turned = head_lanes(head)
@@ -230,8 +236,9 @@
         exps1 = jnp.exp2(scores1 - top)
         exps2 = jnp.exp2(scores2 - top)
         total = column_sum(exps1) + column_sum(exps2)
-        mixed = dot(values1[:, lanes].T[turned], exps1.astype(jnp.bfloat16)) + dot(
-            values2[:, lanes].T[turned], exps2.astype(jnp.bfloat16)
+        lanes = value_lanes(lanes)
+        mixed = dot(pair1[:, lanes].T[turned], exps1.astype(jnp.bfloat16)) + dot(
+            pair2[:, lanes].T[turned], exps2.astype(jnp.bfloat16)
         )
         log_total[0, head : head + 1, :] = top + jnp.log2(total)
         return mixed * (1.0 / total)
@@ -246,7 +253,7 @@
     )
 
 
-def attend_back_body(second, query, keys, values, grad, attended, log_total, *refs):
+def attend_back_body(second, query, pair, grad, attended, log_total, *refs):
     if second:
         before, cosine, sine = refs[:3]
     d_query, d_pair, zero = refs[-3:]
@@ -261,8 +268,8 @@
             products[head] = products[head + 1] = product.T
         own = query[:, lanes] * head_mask((rows, 128), place)
         own_grad = grad[:, lanes] * head_mask((rows, 128), place)
-        scores = dot(keys[:, lanes], own, 1, 1)
-        d_probs = dot(values[:, lanes], own_grad, 1, 1)
+        scores = dot(pair[:, lanes], own, 1, 1)
+        d_probs = dot(pair[:, value_lanes(lanes)], own_grad, 1, 1)
         return own, own_grad, scores, d_probs
 
     def rest(head, given):
@@ -272,23 +279,21 @@
         probs = jnp.exp2(scores - log_total[0, head : head + 1, :])
         d_scores = (probs * (d_probs - delta)).astype(jnp.bfloat16)
         return (
-            dot(keys[:, lanes].T[turned], d_scores),
+            dot(pair[:, lanes].T[turned], d_scores),
             dot(d_scores, own),
             dot(probs.astype(jnp.bfloat16), own_grad),
         )
 
     parts = in_turn(HEADS, first, rest)
-    width = HEADS * HD
     for head in range(0, HEADS, 2):
         lanes = head_lanes(head)[0]
-        value_lanes = slice(width + lanes.start, width + lanes.stop)
         one, two = parts[head : head + 2]
         turned = jnp.concatenate([one[0], two[0]], axis=0).T * HD ** (-0.5)
         if second:
             turned = rotate_lanes(turned + before[:, lanes], cosine[...], -sine[...])
         d_query[:, lanes] = turned.astype(d_query.dtype)
         d_pair[:, lanes] = ((one[1] + two[1]) * (1.0 / LOG2E)).astype(jnp.bfloat16)
-        d_pair[:, value_lanes] = (one[2] + two[2]).astype(jnp.bfloat16)
+        d_pair[:, value_lanes(lanes)] = (one[2] + two[2]).astype(jnp.bfloat16)
 
 
 def attend_back(query, pair, grad, attended, log_total, before=None, after=(), free=()):
@@ -304,8 +309,7 @@
         steps,
         [
             block,
-            block,
-            columns(rows, lanes, steps),
+            columns(rows, 2 * lanes),
             block,
             block,
             pl.BlockSpec((1, HEADS, rows), lambda step: (step, 0, 0)),
@@ -320,20 +324,44 @@
         ],
         [],
         28,
-    )(query, pair, pair, grad, attended, log_total, *extra, *after, free=(*free, *after))
+    )(query, pair, grad, attended, log_total, *extra, *after, free=free)
 
 
 def block_body(
     own_up, own_down, attend_steps, hidden_steps,
-    core, normed1, query_weight, cosine, sine, keys1, values1, keys2, values2, mods,
-    up_bias, down_bias, tokens_far, cotangent_far, out_far, up_far, down_far,
-    query, attended, log_total, mixed, d_middle, d_attended, up_keep, up_send,
-    down_keep, down_send, bias_grad, sums,
-    tokens, cotangent, out_weight, up_weight, down_weight, arrived,
-    all_attended, normed, d_ffn, branch, middle, forward, back,
+    core, normed1, query_weight, cosine, sine, mods, up_bias, down_bias, *refs,
 ):
+    pairs_far, refs = refs[: 2 * attend_steps], refs[2 * attend_steps :]
+    (
+        tokens_far, cotangent_far, out_far, up_far, down_far,
+        query, attended, log_total, mixed, d_middle, d_attended, up_keep, up_send,
+        down_keep, down_send, bias_grad, sums, peer_far,
+        tokens, cotangent, out_weight, up_weight, down_weight, arrived,
+        own_pairs, peer_pairs, pair_arrived, left,
+        all_attended, normed, d_ffn, branch, middle, forward, back,
+    ) = refs
     step = pl.program_id(0)
     tile = up_bias.shape[1]
+    lanes = 2 * HEADS * HD
+    own_arrivals, peer_arrivals, departures = [], [], []
+    for index in range(attend_steps):
+        own_arrivals.append(
+            pltpu.make_async_copy(
+                pairs_far[index], own_pairs.at[index], pair_arrived.at[0, index]
+            )
+        )
+        peer_arrivals.append(
+            pltpu.make_async_copy(
+                pairs_far[attend_steps + index], peer_pairs.at[index], pair_arrived.at[1, index]
+            )
+        )
+        departures.append(
+            pltpu.make_async_copy(
+                peer_pairs.at[index],
+                peer_far.at[:, pl.ds(index * lanes, lanes)],
+                left.at[index],
+            )
+        )
     arrivals = [
         pltpu.make_async_copy(source, target, arrived.at[index])
         for index, (source, target) in enumerate(
@@ -349,26 +377,39 @@
 
     @pl.when(step == 0)
     def _():
+        for index in range(attend_steps):
+            own_arrivals[index].start()
+            peer_arrivals[index].start()
         for arrival in arrivals:
             arrival.start()
+
+    for index in range(attend_steps):
+
+        @pl.when(step == index)
+        def _(index=index):
+            own_arrivals[index].wait()
+            peer_arrivals[index].wait()
+            departures[index].start()
 
     @pl.when(step < attend_steps)
     def _():
         value = rotate_lanes(dot(normed1[...], query_weight[...]), cosine[...], sine[...])
         query[...] = (value * (LOG2E * HD ** (-0.5))).astype(jnp.bfloat16)
-        found = attend_heads(query, keys1, values1, keys2, values2, log_total)
+        found = attend_heads(query, own_pairs.at[step], peer_pairs.at[step], log_total)
         attended[...] = found
         for index in range(attend_steps):
 
             @pl.when(step == index)
             def _(index=index):
-                lanes = HEADS * HD
-                all_attended[:, index * lanes : (index + 1) * lanes] = found
+                heads = HEADS * HD
+                all_attended[:, index * heads : (index + 1) * heads] = found
 
     @pl.when(step == attend_steps)
     def _():
         for arrival in arrivals:
             arrival.wait()
+        for departure in departures:
+            departure.wait()
         turned = dot(all_attended[...], out_weight[...])
         branch[...] = turned.astype(jnp.bfloat16)
         value = tokens[...].astype(jnp.float32) + row(mods, GATE1) * turned
@@ -431,7 +472,7 @@
 
 
 def block_layer(
-    core, normed1, qkv_weight, cosine, sine, own, peer, mods, up_bias, down_bias,
+    core, normed1, qkv_weight, cosine, sine, mods, up_bias, down_bias, own, peer,
     tokens, cotangent, out_weight, up_weight, down_weight,
 ):
     rows, width = tokens.shape
@@ -471,15 +512,11 @@
             pl.BlockSpec((width, lanes), lambda step: (0, jnp.minimum(step, attend_steps - 1))),
             full((rows, 128)),
             full((rows, 128)),
-            heads(),
-            heads(attend_steps),
-            heads(),
-            heads(attend_steps),
             full((16, width)),
             pl.BlockSpec((1, tile), lambda step: (0, tiles(step))),
             full((1, width)),
         ]
-        + [far_spec] * 5,
+        + [far_spec] * (2 * attend_steps + 5),
         [
             heads(),
             heads(),
@@ -495,6 +532,7 @@
             down_spec,
             pl.BlockSpec((1, tile), lambda step: (0, tiles(step))),
             full((8, width)),
+            far_spec,
         ],
         [
             far((rows, width), low),
@@ -509,6 +547,7 @@
             far((hidden // 2, width), low),
             far((1, hidden), jnp.float32),
             far((8, width), jnp.float32),
+            far((rows, 2 * width), low),
         ],
         [
             pltpu.VMEM((rows, width), low),
@@ -517,6 +556,10 @@
             pltpu.VMEM((width, hidden), low),
             pltpu.VMEM((hidden, width), low),
             pltpu.SemaphoreType.DMA((5,)),
+            pltpu.VMEM((attend_steps, rows, 2 * lanes), low),
+            pltpu.VMEM((attend_steps, rows, 2 * lanes), low),
+            pltpu.SemaphoreType.DMA((2, attend_steps)),
+            pltpu.SemaphoreType.DMA((attend_steps,)),
             pltpu.VMEM((rows, width), low),
             pltpu.VMEM((rows, width), low),
             pltpu.VMEM((rows, width), low),
@@ -527,13 +570,14 @@
         ],
         58,
     )(
-        core, normed1, qkv_weight, cosine, sine, own, own, peer, peer, mods, up_bias, down_bias,
-        tokens, cotangent, out_weight, up_weight, down_weight, free=(peer, cotangent, tokens),
+        core, normed1, qkv_weight, cosine, sine, mods, up_bias, down_bias, *own, *peer,
+        tokens, cotangent, out_weight, up_weight, down_weight,
+        free=(*peer, cotangent, tokens),
     )
 
 
 def projected_back_body(
-    own, core, d_query, d_pair, peer_pair, normed, cosine, sine, d_projected, keep, send, zero
+    own, core, d_query, d_pair, peer_pair, normed, cosine, sine, d_projected, zero, *parts
 ):
     zero[0, 0] = 0.0
     lanes = HEADS * HD
@@ -541,7 +585,10 @@
     keys = rotate_lanes(pair[:, :lanes], cosine[...], -sine[...]).astype(jnp.bfloat16)
     low = jnp.concatenate([d_query[...], keys, pair[:, lanes:].astype(jnp.bfloat16)], axis=1)
     d_projected[...] = low
-    store_split(dot(normed[...], low, 0, 0).astype(jnp.bfloat16), core, own, keep, send)
+    grad = dot(normed[...], low, 0, 0).astype(jnp.bfloat16)
+    for index in range(3):
+        part = grad[:, index * lanes : (index + 1) * lanes]
+        store_split(part, core, own, parts[2 * index], parts[2 * index + 1])
 
 
 def projected_back(core, d_query, d_pair, peer_pair, normed, cosine, sine):
@@ -559,18 +606,9 @@
             full((rows, 128)),
             full((rows, 128)),
         ],
-        [
-            columns(rows, 3 * lanes),
-            columns(width // 2, 3 * lanes),
-            columns(width // 2, 3 * lanes),
-            scalar_spec(),
-        ],
-        [
-            far((rows, 3 * width), jnp.bfloat16),
-            far((width // 2, 3 * width), jnp.bfloat16),
-            far((width // 2, 3 * width), jnp.bfloat16),
-            zero_shape(),
-        ],
+        [columns(rows, 3 * lanes), scalar_spec()] + [columns(width // 2, lanes)] * 6,
+        [far((rows, 3 * width), jnp.bfloat16), zero_shape()]
+        + [far((width // 2, width), jnp.bfloat16)] * 6,
         [],
         32,
     )(core, d_query, d_pair, peer_pair, normed, cosine, sine, free=(peer_pair,))
@@ -628,7 +666,7 @@
         small[len(rows) :, :] = jnp.zeros_like(small[len(rows) :, :])
 
 
-def tokens_back(d_projected, weight, tokens, d_middle, mods, sums, bias_grad, after):
+def tokens_back(d_projected, weight, tokens, d_middle, mods, sums, bias_grad):
     rows, width = tokens.shape
     block = full((rows, width))
     lanes = HEADS * HD
@@ -646,13 +684,12 @@
             full((16, width)),
             full((8, width)),
             full(bias_grad.shape),
-        ]
-        + [pl.BlockSpec(memory_space=pl.ANY)] * len(after),
+        ],
         [block, full((16, width)), scalar_spec()],
         [far((rows, width), jnp.bfloat16), far((16, width), jnp.float32), zero_shape()],
         [pltpu.VMEM((rows, width), jnp.float32)],
         32,
-    )(d_projected, weight, weight, weight, tokens, d_middle, mods, sums, bias_grad, *after, free=after)
+    )(d_projected, weight, weight, weight, tokens, d_middle, mods, sums, bias_grad)
 
 
 def swap_halves(block):
@@ -698,6 +735,10 @@
     inputs = refs[: counts[0]]
     outputs = refs[counts[0] + counts[1] :]
     for place, (half, sources, target) in enumerate(jobs):
+        if half is None:
+            total = sum(inputs[place][...].astype(jnp.float32) for place in sources[0][:2])
+            outputs[target][...] = total.astype(jnp.bfloat16)
+            continue
         sent, kept = outputs[target], outputs[target + 1]
 
         def store(out, which, half=half, sources=sources):
@@ -708,7 +749,8 @@
                     lanes = slice(middle, stop) if which else slice(start, middle)
                     total = inputs[one][:, :, lanes].astype(jnp.float32)
                     total = total + inputs[two][:, :, lanes].astype(jnp.float32)
-                    out[...] = total.astype(jnp.bfloat16)
+                    out[:, :, at : at + stop - middle] = total.astype(jnp.bfloat16)
+                    at += stop - middle
                     continue
                 for pair in range(out.shape[0]):
                     block = 2 * pair + which
@@ -742,9 +784,10 @@
             out[2 * rows :, :] = one[rows:, :] + two[rows:, :]
 
 
-def stage(steps, jobs, after=(), small=None):
+def stage(steps, jobs, after=(), small=None, free=()):
     seq_rank, dp_rank = lax.axis_index("seq"), lax.axis_index("dp")
     inputs, in_specs, specs, out_specs, out_shape, mine = [], [], [], [], [], []
+    free = [*free] + [flow.got for flows, _ in jobs for flow in flows]
 
     def place_of(array):
         for index, other in enumerate(inputs):
@@ -756,22 +799,26 @@
         return len(inputs) - 1
 
     for flows, step in jobs:
-        half = step == "half"
+        half = None if step == "sum" else step == "half"
         rest, count = flows[0].rest, flows[0].count
         sources = [
             (place_of(flow.got), place_of(flow.kept), *flow.lanes, rest) for flow in flows
         ]
-        if half:
-            shape = (count, rest, flows[0].width // 2)
+        if half is None:
+            shape = flows[0].kept.shape
+            mine.append(seq_rank)
+        elif half:
+            shape = (count, rest, sum(flow.width for flow in flows) // 2)
             mine.append(seq_rank)
         else:
             width = sum(flow.width * flow.rest // rest for flow in flows)
             shape = (count // 2, rest, width)
             mine.append((dp_rank // step) % 2)
         specs.append((half, sources, len(out_shape)))
-        out_shape += [far(shape, jnp.bfloat16)] * 2
+        results = 1 if half is None else 2
+        out_shape += [far(shape, jnp.bfloat16)] * results
         block = (shape[0] // steps,) + shape[1:]
-        out_specs += [pl.BlockSpec(block, lambda at: (at, 0, 0))] * 2
+        out_specs += [pl.BlockSpec(block, lambda at: (at, 0, 0))] * results
     counts = (len(inputs), len(after))
     extra = []
     if small is not None:
@@ -800,12 +847,12 @@
         out_shape,
         [],
         40,
-    )(jnp.stack(mine), *inputs, *after, *extra, free=(*inputs, *after, *extra))
+    )(jnp.stack(mine), *inputs, *after, *extra, free=(*free, *extra))
     new = []
     for (flows, step), (_, _, target) in zip(jobs, specs):
         sent = results[target]
-        got = swap_seq(sent) if step == "half" else swap_bit(sent, step)
-        new.append(Flow(got, results[target + 1]))
+        got = swap_seq(sent) if isinstance(step, str) else swap_bit(sent, step)
+        new.append(Flow(got, sent if step == "sum" else results[target + 1]))
     if small is not None:
         new.append(results[-1])
     return new, results[0]
@@ -827,8 +874,7 @@
 
 
 def joined(terms, size, widths):
-    block = terms.got[0].astype(jnp.float32) + terms.kept[0].astype(jnp.float32)
-    got = swap_seq(block.astype(jnp.bfloat16)).astype(jnp.float32)
+    block, got = terms.kept[0].astype(jnp.float32), terms.got[0].astype(jnp.float32)
     here = lax.axis_index("seq") == 0
     first, second = jnp.where(here, block, got), jnp.where(here, got, block)
     parts, at = [], 0
@@ -879,15 +925,16 @@
     mods = jnp.concatenate(
         [modulation.reshape(6, width), gain1[None], gain2[None], cond_row, jnp.zeros((7, width))]
     )
-    normed1, own_pair = project_key_value(tokens, mods, attn_qkv, cosine, sine, cotangent)
-    peer_pair = swap_cores(own_pair)
+    normed1, own_pair, *own_parts = project_key_value(tokens, mods, attn_qkv, cosine, sine)
+    peer_parts = [swap_cores(part) for part in own_parts]
     core_ref = core[None]
     (
         query, attended, log_total, mixed, d_middle, d_attended, up_keep, up_send,
-        down_keep, down_send, up_bias_grad, sums2,
+        down_keep, down_send, up_bias_grad, sums2, peer_pair,
     ) = block_layer(
-        core_ref, normed1, attn_qkv, cosine, sine, own_pair, peer_pair, mods,
+        core_ref, normed1, attn_qkv, cosine, sine, mods,
         up_bias.astype(jnp.float32)[None], down_bias.astype(jnp.float32)[None],
+        own_parts, peer_parts,
         tokens, cotangent, attn_out, mlp_up, mlp_down,
     )
     hidden = mlp_up.shape[1]
@@ -902,60 +949,86 @@
     if by_steps:
         up = Flow(swap_cores(blocks(up_send)), blocks(up_keep))
         down = Flow(swap_cores(blocks(down_send)), blocks(down_keep))
-    d_query, away_pair, _ = attend_back(
-        query, peer_pair, d_attended, attended, log_total, free=(peer_pair,)
-    )
-    after = (mixed,)
+    d_query, away_pair, _ = attend_back(query, peer_pair, d_attended, attended, log_total)
+    after = ()
     if by_steps:
-        (down, up), sent = stage(4, [([down], "half"), ([up], bits[1])], (away_pair,))
-        after = (sent, mixed)
+        (down, up), sent = stage(
+            4, [([down], "half"), ([up], bits[1])], (away_pair, mixed), free=(mixed,)
+        )
+        after = (sent,)
     back_pair = swap_cores(away_pair)
     d_query, d_pair, _ = attend_back(
         query, own_pair, d_attended, attended, log_total, (d_query, cosine, sine), after
     )
-    d_projected, qkv_keep, qkv_send, _ = projected_back(
+    d_projected, _, *qkv_parts = projected_back(
         core_ref, d_query, d_pair, back_pair, normed1, cosine, sine
     )
-    after = ()
-    cut = (3 * width // 256 - 1) // 2 * 256
+    third = HEADS * HD
     if by_steps:
-        got, kept = swap_cores(blocks(qkv_send)), blocks(qkv_keep)
-        one, two = Flow(got, kept, (0, cut)), Flow(got, kept, (cut, 3 * width))
-        (one, two), sent = stage(4, [([one], "half"), ([two], bits[1])])
-        after = (sent,)
+        queries, keys, values = [
+            (swap_cores(blocks(send)), blocks(keep))
+            for keep, send in zip(qkv_parts[::2], qkv_parts[1::2])
+        ]
+        one = [Flow(*queries), Flow(*values, (0, third))]
+        two = [Flow(*keys), Flow(*values, (third, width))]
     tokens_grad, small, _ = tokens_back(
-        d_projected, attn_qkv, tokens, d_middle, mods, sums2, up_bias_grad, after
+        d_projected, attn_qkv, tokens, d_middle, mods, sums2, up_bias_grad
     )
     got = swap_cores(small)
+    def doubled(small, got):
+        return jnp.concatenate([small[:-8], got[:-8], small[-8:] + got[-8:]], axis=0)
+
     if by_steps:
-        (down, up, small), sent = stage(
-            4, [([down], bits[1]), ([up], "half")], (), (got, small, True)
-        )
-        got = swap_seq(small)
-        (one, two, small), sent = stage(
-            4, [([one], bits[1]), ([two], "half")], (sent,), (got, small, False)
-        )
-        early, late = [up, down], [one, two]
-        for bit, small_bit in zip(bits[2:], bits[1:]):
-            early, sent = stage(early[0].count // 2, [(early, bit)], (sent,))
-            got = swap_bit(small, small_bit)
-            (*late, small), sent = stage(
-                late[0].count // 2, [(late, bit)], (sent,), (got, small, False)
-            )
-        got = swap_bit(small, bits[-1])
-        small = jnp.concatenate([small[:-8], got[:-8], small[-8:] + got[-8:]], axis=0)
+        (down, up, one, two, small), sent = stage(
+            4,
+            [([down], bits[1]), ([up], "half"), (one, "half"), (two, bits[1])],
+            (),
+            (got, small, True),
+        )
+        early = [up, down]
+        two = [Flow(two.got, two.kept, lanes) for lanes in ((0, width), (width, two.width))]
+        late = [one, two]
+        moves = [functools.partial(swap_bit, bit=bit) for bit in bits[2:] + bits[1:2]]
+        moves.append(swap_seq)
+
+        def next_stage(jobs, count):
+            nonlocal small, sent
+            extra = (moves.pop(0)(small), small, False) if len(moves) > 0 else None
+            flows, sent = stage(count, jobs, (sent,), extra)
+            if extra is not None:
+                small = flows.pop()
+            return flows
+
+        early = next_stage([(early, bits[2])], early[0].count // 2)
+        late = next_stage([([one], bits[1]), (two, "half")], 4)
+        for index, bit in enumerate(bits[3:]):
+            early = next_stage([(early, bit)], early[0].count // 2)
+            late = next_stage([(late, bits[2 + index])], late[0].count // 2)
+        early = next_stage([(early, "sum")], 1)
+        late = next_stage([(late, bits[-1])], late[0].count // 2)
+        late = next_stage([(late, "sum")], 1)
+        while len(moves) > 0:
+            small = doubled(small, moves.pop(0)(small))
         up_half, down_half = (hidden + width) // 2, width // 2
         up_rows, down_rows = joined(early[0], hidden // width, (up_half, down_half))
-        grouped = jnp.concatenate(joined(late[0], 1, (cut // 2, (3 * width - cut) // 2)), axis=1)
+        query_rows, value_rows1, key_rows, value_rows2 = joined(
+            late[0], 1, (width // 2, third // 2, width // 2, (width - third) // 2)
+        )
+        qkv_rows = jnp.concatenate([query_rows, key_rows, value_rows1, value_rows2], axis=1)
     else:
         small = small + got
-        moves = [swap_seq] + [functools.partial(swap_bit, bit=bit) for bit in bits[1:]]
-        for move in moves:
-            got = move(small)
-            small = jnp.concatenate([small[:-8], got[:-8], small[-8:] + got[-8:]], axis=0)
+        moves = [functools.partial(swap_bit, bit=bit) for bit in bits[2:] + bits[1:2]]
+        for move in moves + [swap_seq]:
+            small = doubled(small, move(small))
         up_rows = plain_sum(up_keep, up_send, width)
         down_rows = plain_sum(down_keep, down_send, width)
-        grouped = plain_sum(qkv_keep, qkv_send, width)
+        qkv_rows = jnp.concatenate(
+            [
+                plain_sum(keep, send, width)
+                for keep, send in zip(qkv_parts[::2], qkv_parts[1::2])
+            ],
+            axis=1,
+        )
     per_sequence, sums = small[:-8].reshape(-1, 8, width), small[-8:]
     d_mod_all = per_sequence[:, :6].reshape(per_sequence.shape[0], 6 * width)
     cond_all = per_sequence[:, 6, : cond.shape[1]]
@@ -965,13 +1038,11 @@
     ada_weight_grad = lax.dot_general(
         cond_all, mine, (((0,), (0,)), ((), ())), precision=highest
     )
-    d_mod_own = jnp.where(lax.axis_index("seq") == core, d_mod_all[:1], d_mod_all[1:2])
+    other = d_mod_all.shape[0] // 2
+    d_mod_own = jnp.where(
+        lax.axis_index("seq") == core, d_mod_all[:1], d_mod_all[other : other + 1]
+    )
     (cond_grad,) = silu_back(jnp.dot(d_mod_own, ada_float.T, precision=highest))
-    parts = []
-    for index in range(3):
-        for start in range(index * HEADS * HD, 3 * width, 3 * HEADS * HD):
-            parts.append(grouped[:, start : start + HEADS * HD])
-    qkv_rows = jnp.concatenate(parts, axis=1)
     return (
         mixed[None],
         swap_halves(tokens_grad).astype(jnp.float32)[None],

time: 279 us -> 227 us (0.81)
  waiting for transfers between devices: 76.9 us -> 29.8 us
  local copies, waits for them, and re-layouts: 26 us -> 13.8 us
  Pallas kernels: 106 us -> 115 us
    ppermute x7, waiting for transfers between devices: 40.7 us -> 10.1 us  [swap_seq(): return lax.ppermute(block, 'seq', [(0, 1), (1, 0)])]
    ppermute x17 -> x21, waiting for transfers between devices: 36.2 us -> 19.7 us  [swap_bit(): lax.ppermute(block, 'dp', [(i, i ^ bit) for i in range(lax.axis_size('dp'...]
    unnamed x93 -> x60, local copies, waits for them, and re-layouts: 20.1 us -> 5.31 us
    pallas_call x14 -> x15, Pallas kernels: 106 us -> 115 us  [run(): return call(*placed)]
    ppermute x7, starting transfers between devices: 6.67 us -> 10.4 us  [swap_seq(): return lax.ppermute(block, 'seq', [(0, 1), (1, 0)])]
    ppermute x17 -> x21, starting transfers between devices: 30.1 us -> 26.5 us  [swap_bit(): lax.ppermute(block, 'dp', [(i, i ^ bit) for i in range(lax.axis_size('dp'...]
  transfers between devices with their start and end apart: 29 -> 33, of which waited for: 11 -> 15; matrix products, arithmetic and copies ran while one was open for 6% -> 8% of each run, Pallas kernels for 17% -> 30%
where the time goes in v1:
time: 227 us; the launch traced here: 226 us
  Pallas kernels  115 us (51%)
  starting transfers between devices  51.6 us (23%)
  waiting for transfers between devices  29.8 us (13%)
  local copies, waits for them, and re-layouts  13.8 us (6%)
  other arithmetic  8.18 us (4%)
  matrix products  3.97 us (2%)
  between operations  3.39 us (1%)
    pallas_call x15, Pallas kernels, run(): return call(*placed)  115 us
    ppermute x21, starting transfers between devices, swap_bit(): lax.ppermute(block, 'dp', [(i, i ^ bit) for i in range(lax.axis_size('dp'...  26.5 us
    ppermute x21, waiting for transfers between devices, swap_bit(): lax.ppermute(block, 'dp', [(i, i ^ bit) for i in range(lax.axis_size('dp'...  19.7 us
    ppermute x5, starting transfers between devices, swap_halves(): return lax.ppermute(block, ('dp', 'seq'), perm)  14.7 us
    ppermute x7, starting transfers between devices, swap_seq(): return lax.ppermute(block, 'seq', [(0, 1), (1, 0)])  10.4 us
    ppermute x7, waiting for transfers between devices, swap_seq(): return lax.ppermute(block, 'seq', [(0, 1), (1, 0)])  10.1 us
    unnamed x60, local copies, waits for them, and re-layouts  5.31 us
  transfers between devices with their start and end apart: 33, of which 15 were waited for; matrix products, arithmetic and copies ran while one was open for 8% of the time, Pallas kernels for 30%

profile of v1, /device:TPU:0, one launch (start us, length us, event | category | flops | bytes accessed | tf_op | source)
XLA Modules:
  0.0 225.5 jit_solution(6559546650062397429)
XLA Ops:
  0.7 2.0 collective-permute-start.1
  2.6 1.8 collective-permute-start
  4.4 1.8 collective-permute-start.5
  7.6 1.0 fusion.4
  8.6 1.3 pad_maximum_fusion.1
  12.9 1.3 concatenate.30.mods
  14.1 6.8 %shard_map.237 = (bf16[512,768]{1,0:T(8,128)(2,1)}, bf16[512,1536]{1,0:T(8,128)(2,1)}, bf16[512,512]{1,0:T(8,128)(2,1)}, bf16[512,512]{1,0:T(8,128)(2,1)}, bf16[512,512]{1,0:T(8,128)(2,1)}) custom-call(bf16[512,768]{1,0:T(8,128)(2,1)S(1)} %collective-permute-done.tokens.refs_6_, f32[16,768]{1,0:T(8,128)} %concatenate.30.mods, bf16[768,2304]{1,0:T(8,128)(2,1)} %weight3.1, ...), custom_call_target="tpu_custom_call" | custom-call | flops 1 | bytes 1 | tf_op jit(solution)/shard_map/pallas_call | solution.py:97
  20.9 5.3 %collective-permute-start.2 = (bf16[512,512]{1,0:T(8,128)(2,1)}, bf16[512,512]{1,0:T(8,128)(2,1)S(1)}, u32[]{:S(2)}, u32[]{:S(2)}) collective-permute-start(bf16[512,512]{1,0:T(8,128)(2,1)} %get-tuple-element.74.refs_0_), channel_id=1, source_target_pairs={{0,2},{2,0},{4,6},{6,4},{8,10},{10,8},{12,14},{14,12},{16,18},{18,... | collective-permute-start | bytes 1572872 | tf_op jit(solution)/shard_map/ppermute | solution.py:703
  30.2 42.6 %shard_map.238 = (bf16[512,768]{1,0:T(8,128)(2,1)}, bf16[512,768]{1,0:T(8,128)(2,1)}, f32[3,4,512]{2,1,0:T(4,128)}, bf16[512,768]{1,0:T(8,128)(2,1)}, f32[512,76...) custom-call(s32[1]{0:T(128)} %bitcast.core, ...), custom_call_target="tpu_custom_call" | custom-call | flops 1 | bytes 1 | tf_op jit(solution)/shard_map/pallas_call | solution.py:97
  73.4 1.8 collective-permute-start.6
  75.2 11.1 %shard_map.239 = (f32[512,768]{1,0:T(8,128)}, bf16[512,1536]{1,0:T(8,128)(2,1)}, f32[1,1]{1,0:T(1,128)}) custom-call(bf16[512,768]{1,0:T(8,128)(2,1)} %get-tuple-element.78.query, bf16[512,1536]{1,0:T(8,128)(2,1)} %get-tuple-element.83.pair, bf16[512,768]{1,0:T(8,128)(2,1)} %get-tuple-element.80.grad, bf16[512,768]{1,0:T(8,128)(2,1)} %get-tuple-element.81.attended, ...), custom_call_target="tpu_custom_call" | custom-call | flops 1 | bytes 1 | tf_op jit(solution)/shard_map/pallas_call | solution.py:97
  86.9 7.0 %shard_map.240 = (bf16[8,192,384]{2,1,0:T(8,128)(2,1)}, bf16[8,192,384]{2,1,0:T(8,128)(2,1)}, bf16[4,48,3840]{2,1,0:T(8,128)(2,1)}, bf16[4,48,3840]{2,1,0:T(8,128)(2,1)}) custom-call(s32[2]{0:T(128)S(1)} %pad_add_fusion.mine, bf16[8,192,768]{2,1,0:T(8,128)(2,1)} %collective-permute-done.7.refs_0_, bf16[8,192,768]{2,1,0:T(8,128)(2,1)} %bitcast.55, ...), custom_call_target="tpu_custom_call" | custom-call | flops 1 | bytes 1 | tf_op jit(solution)/shard_map/pallas_call | solution.py:97
  94.0 1.5 collective-permute-start.12
  95.5 1.7 collective-permute-start.11
  97.2 11.7 %shard_map.241 = (bf16[512,768]{1,0:T(8,128)(2,1)}, bf16[512,1536]{1,0:T(8,128)(2,1)}, f32[1,1]{1,0:T(1,128)}) custom-call(bf16[512,768]{1,0:T(8,128)(2,1)} %get-tuple-element.78.query, bf16[512,1536]{1,0:T(8,128)(2,1)} %get-tuple-element.79.pair, bf16[512,768]{1,0:T(8,128)(2,1)} %get-tuple-element.80.grad, bf16[512,768]{1,0:T(8,128)(2,1)} %get-tuple-element.81.attended, ...), custom_call_target="tpu_custom_call" | custom-call | flops 1 | bytes 1 | tf_op jit(solution)/shard_map/pallas_call | solution.py:97
  108.9 6.9 %shard_map.242 = (bf16[512,2304]{1,0:T(8,128)(2,1)}, f32[1,1]{1,0:T(1,128)}, bf16[384,768]{1,0:T(8,128)(2,1)}, bf16[384,768]{1,0:T(8,128)(2,1)}, bf16[384,768]{1...) custom-call(s32[1]{0:T(128)} %bitcast.core, ...), custom_call_target="tpu_custom_call" | custom-call | flops 1 | bytes 1 | tf_op jit(solution)/shard_map/pallas_call | solution.py:97
  115.8 8.0 %shard_map.243 = (bf16[512,768]{1,0:T(8,128)(2,1)}, f32[16,768]{1,0:T(8,128)}, f32[1,1]{1,0:T(1,128)}) custom-call(bf16[512,2304]{1,0:T(8,128)(2,1)} %get-tuple-element.93.d_projected, bf16[768,2304]{1,0:T(8,128)(2,1)} %weight3.1, bf16[768,2304]{1,0:T(8,128)(2,1)} %weight3.1, bf16[768,2304]{1,0:T(8,128)(2,1)} %weight3.1, bf16[512,768]{1,0:T(8,128)(2,1)} %copy-done.1, ...), custom_call_target="tpu_custom_call" | custom-call | flops 1 | bytes 1 | tf_op jit(solution)/shard_map/pallas_call | solution.py:97
  124.5 0.8 collective-permute-done.16.refs_11_
  126.0 0.8 collective-permute-done.14.refs_6_
  126.9 0.8 collective-permute-done.15.refs_8_
  127.7 1.1 collective-permute-done.12.refs_2_
  128.8 0.8 copy-done.5
  129.6 5.4 %shard_map.244 = (bf16[4,192,384]{2,1,0:T(8,128)(2,1)}, bf16[4,192,384]{2,1,0:T(8,128)(2,1)}, bf16[4,48,1920]{2,1,0:T(8,128)(2,1)}, bf16[4,48,1920]{2,1,0:T(8,12...) custom-call(s32[4]{0:T(128)S(1)} %pad_add_fusion.2.mine, ...), custom_call_target="tpu_custom_call" | custom-call | flops 1 | bytes 1 | tf_op jit(solution)/shard_map/pallas_call | solution.py:97
  135.0 1.8 collective-permute-start.19
  136.8 1.5 collective-permute-start.20
  138.3 7.4 %collective-permute-start.10 = (bf16[512,768]{1,0:T(8,128)(2,1)}, bf16[512,768]{1,0:T(8,128)(2,1)}, u32[]{:S(2)}, u32[]{:S(2)}) collective-permute-start(bf16[512,768]{1,0:T(8,128)(2,1)} %get-tuple-element.97), channel_id=1, source_target_pairs={{0,0},{1,2},{2,1},{3,3},{4,4},{5,6},{6,5},{7,7},{8,8},{9,10},{10,9... | collective-permute-start | bytes 2359304 | tf_op jit(solution)/shard_map/ppermute | solution.py:699
  145.7 1.6 collective-permute-start.21
  147.3 2.7 %collective-permute-done.21.refs_6_ = f32[16,768]{1,0:T(8,128)S(1)} collective-permute-done((f32[16,768]{1,0:T(8,128)}, f32[16,768]{1,0:T(8,128)S(1)}, u32[]{:S(2)}, u32[]{:S(2)}) %collective-permute-start.21) | collective-permute-done | bytes 49184 | tf_op jit(solution)/shard_map/ppermute | solution.py:703
  150.0 1.6 collective-permute-done.20.refs_2_
  151.6 2.4 %collective-permute-done.19.refs_0_ = bf16[4,48,1920]{2,1,0:T(8,128)(2,1)S(1)} collective-permute-done((bf16[4,48,1920]{2,1,0:T(8,128)(2,1)}, bf16[4,48,1920]{2,1,0:T(8,128)(2,1)S(1)}, u32[]{:S(2)}, u32[]{:S(2)}) %collective-permute-start.19) | collective-permute-done | bytes 737312 | tf_op jit(solution)/shard_map/ppermute | solution.py:711
  154.0 0.8 copy-done.6
  154.8 2.6 %shard_map.245 = (bf16[2,48,3456]{2,1,0:T(8,128)(2,1)}, bf16[2,48,3456]{2,1,0:T(8,128)(2,1)}, f32[24,768]{1,0:T(8,128)}) custom-call(s32[1]{0:T(128)} %bitcast.15.mine, bf16[4,48,1920]{2,1,0:T(8,128)(2,1)S(1)} %collective-permute-done.19.refs_0_, bf16[4,48,1920]{2,1,0:T(8,128)(2,1)} %get-tuple-element.113.refs_1_, ...), custom_call_target="tpu_custom_call" | custom-call | flops 1 | bytes 1 | tf_op jit(solution)/shard_map/pallas_call | solution.py:97
  157.4 1.6 collective-permute-start.25
  159.0 1.5 collective-permute-start.18
  160.5 2.4 %collective-permute-start.17 = (bf16[8,48,512]{2,1,0:T(8,128)(2,1)S(1)}, bf16[8,48,512]{2,1,0:T(8,128)(2,1)S(1)}, u32[]{:S(2)}, u32[]{:S(2)}) collective-permute-start(bf16[8,48,512]{2,1,0:T(8,128)(2,1)S(1)} %copy-done.24), channel_id=1, source_target_pairs={{0,1},{1,0},{2,3},{3,2},{4,5},{5,4},{6,7},{7,6},{8,9},{9,8},{10,11... | collective-permute-start | bytes 1179656 | tf_op jit(solution)/shard_map/ppermute | solution.py:711
  162.9 2.6 %collective-permute-start.22 = (f32[24,768]{1,0:T(8,128)}, f32[24,768]{1,0:T(8,128)S(1)}, u32[]{:S(2)}, u32[]{:S(2)}) collective-permute-start(f32[24,768]{1,0:T(8,128)} %get-tuple-element.118.refs_5_), channel_id=1, source_target_pairs={{0,16},{2,18},{4,20},{6,22},{8,24},{10,26},{12,28},{14,30},{16,0},... | collective-permute-start | bytes 221192 | tf_op jit(solution)/shard_map/ppermute | solution.py:703
  165.6 4.6 %collective-permute-done.17.refs_0_ = bf16[8,48,512]{2,1,0:T(8,128)(2,1)S(1)} collective-permute-done((bf16[8,48,512]{2,1,0:T(8,128)(2,1)S(1)}, bf16[8,48,512]{2,1,0:T(8,128)(2,1)S(1)}, u32[]{:S(2)}, u32[]{:S(2)}) %collective-permute-start.17) | collective-permute-done | bytes 393248 | tf_op jit(solution)/shard_map/ppermute | solution.py:711
  170.2 3.2 %collective-permute-done.22.refs_6_ = f32[24,768]{1,0:T(8,128)S(1)} collective-permute-done((f32[24,768]{1,0:T(8,128)}, f32[24,768]{1,0:T(8,128)S(1)}, u32[]{:S(2)}, u32[]{:S(2)}) %collective-permute-start.22) | collective-permute-done | bytes 73760 | tf_op jit(solution)/shard_map/ppermute | solution.py:703
  173.3 0.9 copy-done.4
  174.2 3.5 %shard_map.246 = (bf16[4,48,512]{2,1,0:T(8,128)(2,1)}, bf16[4,48,512]{2,1,0:T(8,128)(2,1)}, bf16[4,48,640]{2,1,0:T(8,128)(2,1)}, bf16[4,48,640]{2,1,0:T(8,128)(2,1)}, f32[40,768]{1,0:T(8,128)}) custom-call(s32[2]{0:T(128)S(1)} %pad_add_fusion.1.mine, bf16[8,48,512]{2,1,0:T(8,128)(2,1)S(1)} %collective-permute-done.17.refs_0_, ...), custom_call_target="tpu_custom_call" | custom-call | flops 1 | bytes 1 | tf_op jit(solution)/shard_map/pallas_call | solution.py:97
  177.7 1.6 collective-permute-start.26
  180.0 1.8 collective-permute-start.24
  182.3 1.7 collective-permute-done.26.refs_4_
  184.1 0.9 copy-done.3
  185.0 2.2 shard_map.247
  187.1 0.9 collective-permute-start.27
  188.0 2.4 %bitcast_convert_fusion = f32[1,512,768]{2,1,0:T(8,128)} fusion(bf16[512,768]{1,0:T(8,128)(2,1)} %collective-permute-done.10), kind=kLoop, calls=%fused_computation.3 | loop fusion | flops 393216 | bytes 2359296 | tf_op jit(solution)/shard_map/broadcast_in_dim | solution.py:1048
  190.4 3.1 %collective-permute-start.29 = (bf16[1,48,3456]{2,1,0:T(8,128)(2,1)S(1)}, bf16[1,48,3456]{2,1,0:T(8,128)(2,1)S(1)}, u32[]{:S(2)}, u32[]{:S(2)}) collective-permute-start(bf16[1,48,3456]{2,1,0:T(8,128)(2,1)S(1)} %copy-done.14), channel_id=1, source_target_pairs={{0,16},{2,18},{4,20},{6,22},{8,24},{10,26},{12,28},{14,30},{16,0},... | collective-permute-start | bytes 995336 | tf_op jit(solution)/shard_map/ppermute | solution.py:703
  193.4 2.0 shard_map.248
  195.5 1.1 slice_bitcast_fusion
  196.7 3.0 %collective-permute-start.28 = (bf16[2,48,1152]{2,1,0:T(8,128)(2,1)S(1)}, bf16[2,48,1152]{2,1,0:T(8,128)(2,1)S(1)}, u32[]{:S(2)}, u32[]{:S(2)}) collective-permute-start(bf16[2,48,1152]{2,1,0:T(8,128)(2,1)S(1)} %copy-done.15), channel_id=1, source_target_pairs={{0,8},{2,10},{4,12},{6,14},{8,0},{10,2},{12,4},{14,6},{16,24},{18,... | collective-permute-start | bytes 663560 | tf_op jit(solution)/shard_map/ppermute | solution.py:703
  201.7 2.2 fusion.10
  203.9 1.8 shard_map.249.refs_2_
  205.7 0.9 collective-permute-start.32
  206.6 1.2 fusion.6
  207.8 1.7 shard_map.250
  209.7 1.5 slice_reduce_fusion
  211.2 4.9 %collective-permute-done.30.refs_0_ = bf16[1,48,1152]{2,1,0:T(8,128)(2,1)S(1)} collective-permute-done((bf16[1,48,1152]{2,1,0:T(8,128)(2,1)}, bf16[1,48,1152]{2,1,0:T(8,128)(2,1)S(1)}, u32[]{:S(2)}, u32[]{:S(2)}) %collective-permute-start.30) | collective-permute-done | bytes 110624 | tf_op jit(solution)/shard_map/ppermute | solution.py:703
  216.1 1.6 shard_map.251
  217.7 0.9 collective-permute-start.31
  219.6 3.1 %collective-permute-done.31 = bf16[1,48,1152]{2,1,0:T(8,128)(2,1)S(1)} collective-permute-done((bf16[1,48,1152]{2,1,0:T(8,128)(2,1)}, bf16[1,48,1152]{2,1,0:T(8,128)(2,1)S(1)}, u32[]{:S(2)}, u32[]{:S(2)}) %collective-permute-start.31) | collective-permute-done | bytes 110624 | tf_op jit(solution)/shard_map/ppermute | solution.py:711
  222.8 1.0 pad_maximum_fusion
  223.8 0.9 maximum_maximum_fusion
  224.6 0.9 copy.39
  (116 shorter events, 13.4 us)
Async XLA Ops:
  0.6 11.6 %copy-start = (bf16[128,4608]{1,0:T(8,128)(2,1)S(1)}, bf16[128,4608]{1,0:T(8,128)(2,1)}, u32[]{:S(2)}) copy-start(bf16[128,4608]{1,0:T(8,128)(2,1)} %param.26) | copy-start | bytes 3538948
  0.7 9.2 %collective-permute-start.1 = (s32[1]{0:T(128)}, s32[1]{0:T(128)}, u32[]{:S(2)}, u32[]{:S(2)}) collective-permute-start(s32[1]{0:T(128)} %param.16), channel_id=1, source_target_pairs={{0,0},{1,2},{2,1},{3,3},{4,4},{5,6},{6,5},{7,7},{8,8},{9,10},{10,9... | collective-permute-start | bytes 20 | tf_op jit(solution)/shard_map/ppermute | solution.py:699
  2.6 11.5 %collective-permute-start = (bf16[512,768]{1,0:T(8,128)(2,1)}, bf16[512,768]{1,0:T(8,128)(2,1)S(1)}, u32[]{:S(2)}, u32[]{:S(2)}) collective-permute-start(bf16[512,768]{1,0:T(8,128)(2,1)} %bitcast.66), channel_id=1, source_target_pairs={{0,0},{1,2},{2,1},{3,3},{4,4},{5,6},{6,5},{7,7},{8,8},{9,10},{10,9... | collective-permute-start | bytes 2359304 | tf_op jit(solution)/shard_map/ppermute | solution.py:699
  4.4 23.5 %collective-permute-start.5 = (bf16[512,768]{1,0:T(8,128)(2,1)}, bf16[512,768]{1,0:T(8,128)(2,1)S(1)}, u32[]{:S(2)}, u32[]{:S(2)}) collective-permute-start(bf16[512,768]{1,0:T(8,128)(2,1)} %bitcast.67), channel_id=1, source_target_pairs={{0,0},{1,2},{2,1},{3,3},{4,4},{5,6},{6,5},{7,7},{8,8},{9,10},{10,9... | collective-permute-start | bytes 2359304 | tf_op jit(solution)/shard_map/ppermute | solution.py:699
  7.6 5.2 %copy-start.17 = (bf16[4608]{0:T(1024)(128)(2,1)S(1)}, bf16[4608]{0:T(1024)(128)(2,1)}, u32[]{:S(2)}) copy-start(bf16[4608]{0:T(1024)(128)(2,1)} %param.27) | copy-start | bytes 27652
  14.1 6.8 %copy-start.1 = (bf16[512,768]{1,0:T(8,128)(2,1)}, bf16[512,768]{1,0:T(8,128)(2,1)S(1)}, u32[]{:S(2)}) copy-start(bf16[512,768]{1,0:T(8,128)(2,1)S(1)} %collective-permute-done.tokens.refs_6_) | copy-start | bytes 2359300
  14.1 12.6 %copy-start.18 = (bf16[3072]{0:T(1024)(128)(2,1)S(1)}, bf16[3072]{0:T(1024)(128)(2,1)}, u32[]{:S(2)}) copy-start(bf16[3072]{0:T(1024)(128)(2,1)} %param.23) | copy-start | bytes 18436
  14.1 13.2 %copy-start.19 = (bf16[768]{0:T(1024)(128)(2,1)S(1)}, bf16[768]{0:T(1024)(128)(2,1)}, u32[]{:S(2)}) copy-start(bf16[768]{0:T(1024)(128)(2,1)} %param.25) | copy-start | bytes 4612
  20.9 7.0 %collective-permute-start.2 = (bf16[512,512]{1,0:T(8,128)(2,1)}, bf16[512,512]{1,0:T(8,128)(2,1)S(1)}, u32[]{:S(2)}, u32[]{:S(2)}) collective-permute-start(bf16[512,512]{1,0:T(8,128)(2,1)} %get-tuple-element.74.refs_0_), channel_id=1, source_target_pairs={{0,2},{2,0},{4,6},{6,4},{8,10},{10,8},{12,14},{14,12},{16,18},{18,... | collective-permute-start | bytes 1572872 | tf_op jit(solution)/shard_map/ppermute | solution.py:703
  26.2 2.5 %collective-permute-start.3 = (bf16[512,512]{1,0:T(8,128)(2,1)}, bf16[512,512]{1,0:T(8,128)(2,1)S(1)}, u32[]{:S(2)}, u32[]{:S(2)}) collective-permute-start(bf16[512,512]{1,0:T(8,128)(2,1)} %get-tuple-element.75.refs_1_), channel_id=1, source_target_pairs={{0,2},{2,0},{4,6},{6,4},{8,10},{10,8},{12,14},{14,12},{16,18},{18,... | collective-permute-start | bytes 1572872 | tf_op jit(solution)/shard_map/ppermute | solution.py:703
  26.3 3.2 %collective-permute-start.4 = (bf16[512,512]{1,0:T(8,128)(2,1)}, bf16[512,512]{1,0:T(8,128)(2,1)S(1)}, u32[]{:S(2)}, u32[]{:S(2)}) collective-permute-start(bf16[512,512]{1,0:T(8,128)(2,1)} %get-tuple-element.76.refs_2_), channel_id=1, source_target_pairs={{0,2},{2,0},{4,6},{6,4},{8,10},{10,8},{12,14},{14,12},{16,18},{18,... | collective-permute-start | bytes 1572872 | tf_op jit(solution)/shard_map/ppermute | solution.py:703
  27.9 1.5 copy-start.9
  27.9 1.5 copy-start.10
  28.7 0.8 copy-start.11
  29.4 0.8 copy-start.12
  72.9 14.1 %collective-permute-start.8 = (bf16[8,48,3840]{2,1,0:T(8,128)(2,1)}, bf16[8,48,3840]{2,1,0:T(8,128)(2,1)}, u32[]{:S(2)}, u32[]{:S(2)}) collective-permute-start(bf16[8,48,3840]{2,1,0:T(8,128)(2,1)} %bitcast.64), channel_id=1, source_target_pairs={{0,2},{2,0},{4,6},{6,4},{8,10},{10,8},{12,14},{14,12},{16,18},{18,... | collective-permute-start | bytes 8847368 | tf_op jit(solution)/shard_map/ppermute | solution.py:703
  73.3 13.6 %collective-permute-start.7 = (bf16[8,192,768]{2,1,0:T(8,128)(2,1)}, bf16[8,192,768]{2,1,0:T(8,128)(2,1)}, u32[]{:S(2)}, u32[]{:S(2)}) collective-permute-start(bf16[8,192,768]{2,1,0:T(8,128)(2,1)} %bitcast.65), channel_id=1, source_target_pairs={{0,2},{2,0},{4,6},{6,4},{8,10},{10,8},{12,14},{14,12},{16,18},{18,... | collective-permute-start | bytes 7077896 | tf_op jit(solution)/shard_map/ppermute | solution.py:703
  73.4 13.5 %collective-permute-start.6 = (bf16[512,768]{1,0:T(8,128)(2,1)}, bf16[512,768]{1,0:T(8,128)(2,1)S(1)}, u32[]{:S(2)}, u32[]{:S(2)}) collective-permute-start(bf16[512,768]{1,0:T(8,128)(2,1)} %get-tuple-element.77), channel_id=1, source_target_pairs={{0,0},{1,2},{2,1},{3,3},{4,4},{5,6},{6,5},{7,7},{8,8},{9,10},{10,9... | collective-permute-start | bytes 2359304 | tf_op jit(solution)/shard_map/ppermute | solution.py:699
  86.3 22.6 %collective-permute-start.9 = (bf16[512,1536]{1,0:T(8,128)(2,1)}, bf16[512,1536]{1,0:T(8,128)(2,1)S(1)}, u32[]{:S(2)}, u32[]{:S(2)}) collective-permute-start(bf16[512,1536]{1,0:T(8,128)(2,1)} %get-tuple-element.89.refs_4_), channel_id=1, source_target_pairs={{0,2},{2,0},{4,6},{6,4},{8,10},{10,8},{12,14},{14,12},{16,18},{18,... | collective-permute-start | bytes 4718600 | tf_op jit(solution)/shard_map/ppermute | solution.py:703
  94.0 34.8 %collective-permute-start.12 = (bf16[4,48,3840]{2,1,0:T(8,128)(2,1)}, bf16[4,48,3840]{2,1,0:T(8,128)(2,1)S(1)}, u32[]{:S(2)}, u32[]{:S(2)}) collective-permute-start(bf16[4,48,3840]{2,1,0:T(8,128)(2,1)} %get-tuple-element.99), channel_id=1, source_target_pairs={{0,4},{2,6},{4,0},{6,2},{8,12},{10,14},{12,8},{14,10},{16,20},{18,... | collective-permute-start | bytes 4423688 | tf_op jit(solution)/shard_map/ppermute | solution.py:703
  95.5 32.2 %collective-permute-start.11 = (bf16[8,192,384]{2,1,0:T(8,128)(2,1)}, bf16[8,192,384]{2,1,0:T(8,128)(2,1)S(1)}, u32[]{:S(2)}, u32[]{:S(2)}) collective-permute-start(bf16[8,192,384]{2,1,0:T(8,128)(2,1)} %get-tuple-element.90.refs_3_), channel_id=1, source_target_pairs={{0,1},{1,0},{2,3},{3,2},{4,5},{5,4},{6,7},{7,6},{8,9},{9,8},{10,11... | collective-permute-start | bytes 3538952 | tf_op jit(solution)/shard_map/ppermute | solution.py:711
  108.9 6.9 %copy-start.7 = (f32[1,3072]{1,0:T(1,128)S(1)}, f32[1,3072]{1,0:T(1,128)}, u32[]{:S(2)}) copy-start(f32[1,3072]{1,0:T(1,128)} %get-tuple-element.96.bias_grad) | copy-start | bytes 36868
  115.8 8.1 %copy-start.22 = (bf16[384,768]{1,0:T(8,128)(2,1)S(1)}, bf16[384,768]{1,0:T(8,128)(2,1)}, u32[]{:S(2)}) copy-start(bf16[384,768]{1,0:T(8,128)(2,1)} %get-tuple-element.101) | copy-start | bytes 1769476
  115.8 8.6 %copy-start.21 = (bf16[384,768]{1,0:T(8,128)(2,1)S(1)}, bf16[384,768]{1,0:T(8,128)(2,1)}, u32[]{:S(2)}) copy-start(bf16[384,768]{1,0:T(8,128)(2,1)} %get-tuple-element.103) | copy-start | bytes 1769476
  115.8 9.5 %copy-start.20 = (bf16[384,768]{1,0:T(8,128)(2,1)S(1)}, bf16[384,768]{1,0:T(8,128)(2,1)}, u32[]{:S(2)}) copy-start(bf16[384,768]{1,0:T(8,128)(2,1)} %get-tuple-element.105) | copy-start | bytes 1769476
  123.8 1.5 collective-permute-start.16
  123.9 2.1 collective-permute-start.13
  124.4 2.5 %collective-permute-start.14 = (bf16[8,48,768]{2,1,0:T(8,128)(2,1)S(1)}, bf16[8,48,768]{2,1,0:T(8,128)(2,1)S(1)}, u32[]{:S(2)}, u32[]{:S(2)}) collective-permute-start(bf16[8,48,768]{2,1,0:T(8,128)(2,1)S(1)} %bitcast.69), channel_id=1, source_target_pairs={{0,2},{2,0},{4,6},{6,4},{8,10},{10,8},{12,14},{14,12},{16,18},{18,... | collective-permute-start | bytes 1769480 | tf_op jit(solution)/shard_map/ppermute | solution.py:703
  125.3 2.4 %collective-permute-start.15 = (bf16[8,48,768]{2,1,0:T(8,128)(2,1)S(1)}, bf16[8,48,768]{2,1,0:T(8,128)(2,1)S(1)}, u32[]{:S(2)}, u32[]{:S(2)}) collective-permute-start(bf16[8,48,768]{2,1,0:T(8,128)(2,1)S(1)} %bitcast.68), channel_id=1, source_target_pairs={{0,2},{2,0},{4,6},{6,4},{8,10},{10,8},{12,14},{14,12},{16,18},{18,... | collective-permute-start | bytes 1769480 | tf_op jit(solution)/shard_map/ppermute | solution.py:703
  128.8 0.8 copy-start.5
  135.0 19.0 %collective-permute-start.19 = (bf16[4,48,1920]{2,1,0:T(8,128)(2,1)}, bf16[4,48,1920]{2,1,0:T(8,128)(2,1)S(1)}, u32[]{:S(2)}, u32[]{:S(2)}) collective-permute-start(bf16[4,48,1920]{2,1,0:T(8,128)(2,1)} %get-tuple-element.112), channel_id=1, source_target_pairs={{0,1},{1,0},{2,3},{3,2},{4,5},{5,4},{6,7},{7,6},{8,9},{9,8},{10,11... | collective-permute-start | bytes 2211848 | tf_op jit(solution)/shard_map/ppermute | solution.py:711
  136.8 14.8 %collective-permute-start.20 = (bf16[4,192,384]{2,1,0:T(8,128)(2,1)}, bf16[4,192,384]{2,1,0:T(8,128)(2,1)S(1)}, u32[]{:S(2)}, u32[]{:S(2)}) collective-permute-start(bf16[4,192,384]{2,1,0:T(8,128)(2,1)} %get-tuple-element.114.refs_4_), channel_id=1, source_target_pairs={{0,4},{2,6},{4,0},{6,2},{8,12},{10,14},{12,8},{14,10},{16,20},{18,... | collective-permute-start | bytes 1769480 | tf_op jit(solution)/shard_map/ppermute | solution.py:703
  138.3 49.7 %collective-permute-start.10 = (bf16[512,768]{1,0:T(8,128)(2,1)}, bf16[512,768]{1,0:T(8,128)(2,1)}, u32[]{:S(2)}, u32[]{:S(2)}) collective-permute-start(bf16[512,768]{1,0:T(8,128)(2,1)} %get-tuple-element.97), channel_id=1, source_target_pairs={{0,0},{1,2},{2,1},{3,3},{4,4},{5,6},{6,5},{7,7},{8,8},{9,10},{10,9... | collective-permute-start | bytes 2359304 | tf_op jit(solution)/shard_map/ppermute | solution.py:699
  145.7 4.3 %collective-permute-start.21 = (f32[16,768]{1,0:T(8,128)}, f32[16,768]{1,0:T(8,128)S(1)}, u32[]{:S(2)}, u32[]{:S(2)}) collective-permute-start(f32[16,768]{1,0:T(8,128)} %get-tuple-element.116.refs_5_), channel_id=1, source_target_pairs={{0,8},{2,10},{4,12},{6,14},{8,0},{10,2},{12,4},{14,6},{16,24},{18,... | collective-permute-start | bytes 147464 | tf_op jit(solution)/shard_map/ppermute | solution.py:703
  154.0 0.8 copy-start.6
  154.8 4.2 %copy-start.23 = (bf16[4,48,1280]{2,1,0:T(8,128)(2,1)S(1)}, bf16[4,48,1280]{2,1,0:T(8,128)(2,1)}, u32[]{:S(2)}) copy-start(bf16[4,48,1280]{2,1,0:T(8,128)(2,1)} %get-tuple-element.110) | copy-start | bytes 1474564
  154.8 5.8 %copy-start.24 = (bf16[8,48,512]{2,1,0:T(8,128)(2,1)S(1)}, bf16[8,48,512]{2,1,0:T(8,128)(2,1)}, u32[]{:S(2)}) copy-start(bf16[8,48,512]{2,1,0:T(8,128)(2,1)} %get-tuple-element.108) | copy-start | bytes 1179652
  157.4 26.7 %collective-permute-start.25 = (bf16[2,48,3456]{2,1,0:T(8,128)(2,1)}, bf16[2,48,3456]{2,1,0:T(8,128)(2,1)S(1)}, u32[]{:S(2)}, u32[]{:S(2)}) collective-permute-start(bf16[2,48,3456]{2,1,0:T(8,128)(2,1)} %get-tuple-element.117.refs_4_), channel_id=1, source_target_pairs={{0,8},{2,10},{4,12},{6,14},{8,0},{10,2},{12,4},{14,6},{16,24},{18,... | collective-permute-start | bytes 1990664 | tf_op jit(solution)/shard_map/ppermute | solution.py:703
  159.0 11.1 %collective-permute-start.18 = (bf16[4,48,1280]{2,1,0:T(8,128)(2,1)S(1)}, bf16[4,48,1280]{2,1,0:T(8,128)(2,1)S(1)}, u32[]{:S(2)}, u32[]{:S(2)}) collective-permute-start(bf16[4,48,1280]{2,1,0:T(8,128)(2,1)S(1)} %copy-done.23), channel_id=1, source_target_pairs={{0,4},{2,6},{4,0},{6,2},{8,12},{10,14},{12,8},{14,10},{16,20},{18,... | collective-permute-start | bytes 1474568 | tf_op jit(solution)/shard_map/ppermute | solution.py:703
  160.5 9.6 %collective-permute-start.17 = (bf16[8,48,512]{2,1,0:T(8,128)(2,1)S(1)}, bf16[8,48,512]{2,1,0:T(8,128)(2,1)S(1)}, u32[]{:S(2)}, u32[]{:S(2)}) collective-permute-start(bf16[8,48,512]{2,1,0:T(8,128)(2,1)S(1)} %copy-done.24), channel_id=1, source_target_pairs={{0,1},{1,0},{2,3},{3,2},{4,5},{5,4},{6,7},{7,6},{8,9},{9,8},{10,11... | collective-permute-start | bytes 1179656 | tf_op jit(solution)/shard_map/ppermute | solution.py:711
  162.9 10.4 %collective-permute-start.22 = (f32[24,768]{1,0:T(8,128)}, f32[24,768]{1,0:T(8,128)S(1)}, u32[]{:S(2)}, u32[]{:S(2)}) collective-permute-start(f32[24,768]{1,0:T(8,128)} %get-tuple-element.118.refs_5_), channel_id=1, source_target_pairs={{0,16},{2,18},{4,20},{6,22},{8,24},{10,26},{12,28},{14,30},{16,0},... | collective-permute-start | bytes 221192 | tf_op jit(solution)/shard_map/ppermute | solution.py:703
  173.3 0.9 copy-start.4
  177.7 6.3 %collective-permute-start.26 = (f32[40,768]{1,0:T(8,128)}, f32[40,768]{1,0:T(8,128)S(1)}, u32[]{:S(2)}, u32[]{:S(2)}) collective-permute-start(f32[40,768]{1,0:T(8,128)} %get-tuple-element.124.refs_3_), channel_id=1, source_target_pairs={{0,4},{2,6},{4,0},{6,2},{8,12},{10,14},{12,8},{14,10},{16,20},{18,... | collective-permute-start | bytes 368648 | tf_op jit(solution)/shard_map/ppermute | solution.py:703
  180.0 13.4 %collective-permute-start.24 = (bf16[4,48,640]{2,1,0:T(8,128)(2,1)}, bf16[4,48,640]{2,1,0:T(8,128)(2,1)S(1)}, u32[]{:S(2)}, u32[]{:S(2)}) collective-permute-start(bf16[4,48,640]{2,1,0:T(8,128)(2,1)} %get-tuple-element.121), channel_id=1, source_target_pairs={{0,1},{1,0},{2,3},{3,2},{4,5},{5,4},{6,7},{7,6},{8,9},{9,8},{10,11... | collective-permute-start | bytes 737288 | tf_op jit(solution)/shard_map/ppermute | solution.py:711
  181.8 11.6 %collective-permute-start.23 = (bf16[4,48,512]{2,1,0:T(8,128)(2,1)}, bf16[4,48,512]{2,1,0:T(8,128)(2,1)S(1)}, u32[]{:S(2)}, u32[]{:S(2)}) collective-permute-start(bf16[4,48,512]{2,1,0:T(8,128)(2,1)} %get-tuple-element.119.refs_2_), channel_id=1, source_target_pairs={{0,4},{2,6},{4,0},{6,2},{8,12},{10,14},{12,8},{14,10},{16,20},{18,... | collective-permute-start | bytes 589832 | tf_op jit(solution)/shard_map/ppermute | solution.py:703
  184.0 0.9 copy-start.3
  187.1 3.3 %copy-start.14 = (bf16[1,48,3456]{2,1,0:T(8,128)(2,1)S(1)}, bf16[1,48,3456]{2,1,0:T(8,128)(2,1)}, u32[]{:S(2)}) copy-start(bf16[1,48,3456]{2,1,0:T(8,128)(2,1)} %get-tuple-element.125.refs_4_) | copy-start | bytes 995332
  187.1 6.3 %copy-start.2 = (f32[72,768]{1,0:T(8,128)S(1)}, f32[72,768]{1,0:T(8,128)}, u32[]{:S(2)}) copy-start(f32[72,768]{1,0:T(8,128)} %get-tuple-element.126.refs_5_) | copy-start | bytes 663556
  187.1 6.3 %collective-permute-start.27 = (f32[72,768]{1,0:T(8,128)}, f32[72,768]{1,0:T(8,128)S(1)}, u32[]{:S(2)}, u32[]{:S(2)}) collective-permute-start(f32[72,768]{1,0:T(8,128)} %get-tuple-element.126.refs_5_), channel_id=1, source_target_pairs={{0,1},{1,0},{2,3},{3,2},{4,5},{5,4},{6,7},{7,6},{8,9},{9,8},{10,11... | collective-permute-start | bytes 663560 | tf_op jit(solution)/shard_map/ppermute | solution.py:711
  190.4 13.5 %collective-permute-start.29 = (bf16[1,48,3456]{2,1,0:T(8,128)(2,1)S(1)}, bf16[1,48,3456]{2,1,0:T(8,128)(2,1)S(1)}, u32[]{:S(2)}, u32[]{:S(2)}) collective-permute-start(bf16[1,48,3456]{2,1,0:T(8,128)(2,1)S(1)} %copy-done.14), channel_id=1, source_target_pairs={{0,16},{2,18},{4,20},{6,22},{8,24},{10,26},{12,28},{14,30},{16,0},... | collective-permute-start | bytes 995336 | tf_op jit(solution)/shard_map/ppermute | solution.py:703
  195.5 1.2 copy-start.15
  196.7 11.1 %collective-permute-start.28 = (bf16[2,48,1152]{2,1,0:T(8,128)(2,1)S(1)}, bf16[2,48,1152]{2,1,0:T(8,128)(2,1)S(1)}, u32[]{:S(2)}, u32[]{:S(2)}) collective-permute-start(bf16[2,48,1152]{2,1,0:T(8,128)(2,1)S(1)} %copy-done.15), channel_id=1, source_target_pairs={{0,8},{2,10},{4,12},{6,14},{8,0},{10,2},{12,4},{14,6},{16,24},{18,... | collective-permute-start | bytes 663560 | tf_op jit(solution)/shard_map/ppermute | solution.py:703
  205.7 13.0 %copy-start.8 = (bf16[1,48,3456]{2,1,0:T(8,128)(2,1)S(1)}, bf16[1,48,3456]{2,1,0:T(8,128)(2,1)}, u32[]{:S(2)}) copy-start(bf16[1,48,3456]{2,1,0:T(8,128)(2,1)} %shard_map.249.refs_2_) | copy-start | bytes 995332
  205.7 12.9 %collective-permute-start.32 = (bf16[1,48,3456]{2,1,0:T(8,128)(2,1)}, bf16[1,48,3456]{2,1,0:T(8,128)(2,1)S(1)}, u32[]{:S(2)}, u32[]{:S(2)}) collective-permute-start(bf16[1,48,3456]{2,1,0:T(8,128)(2,1)} %shard_map.249.refs_2_), channel_id=1, source_target_pairs={{0,1},{1,0},{2,3},{3,2},{4,5},{5,4},{6,7},{7,6},{8,9},{9,8},{10,11... | collective-permute-start | bytes 995336 | tf_op jit(solution)/shard_map/ppermute | solution.py:711
  209.5 6.7 %collective-permute-start.30 = (bf16[1,48,1152]{2,1,0:T(8,128)(2,1)}, bf16[1,48,1152]{2,1,0:T(8,128)(2,1)S(1)}, u32[]{:S(2)}, u32[]{:S(2)}) collective-permute-start(bf16[1,48,1152]{2,1,0:T(8,128)(2,1)} %get-tuple-element.131.refs_2_), channel_id=1, source_target_pairs={{0,16},{2,18},{4,20},{6,22},{8,24},{10,26},{12,28},{14,30},{16,0},... | collective-permute-start | bytes 331784 | tf_op jit(solution)/shard_map/ppermute | solution.py:703
  217.7 5.0 %collective-permute-start.31 = (bf16[1,48,1152]{2,1,0:T(8,128)(2,1)}, bf16[1,48,1152]{2,1,0:T(8,128)(2,1)S(1)}, u32[]{:S(2)}, u32[]{:S(2)}) collective-permute-start(bf16[1,48,1152]{2,1,0:T(8,128)(2,1)} %shard_map.251), channel_id=1, source_target_pairs={{0,1},{1,0},{2,3},{3,2},{4,5},{5,4},{6,7},{7,6},{8,9},{9,8},{10,11... | collective-permute-start | bytes 331784 | tf_op jit(solution)/shard_map/ppermute | solution.py:711
  218.8 3.9 %copy-start.13 = (bf16[1,48,1152]{2,1,0:T(8,128)(2,1)S(1)}, bf16[1,48,1152]{2,1,0:T(8,128)(2,1)}, u32[]{:S(2)}) copy-start(bf16[1,48,1152]{2,1,0:T(8,128)(2,1)} %shard_map.251) | copy-start | bytes 331780
  222.8 2.7 %copy-start.16 = (f32[48,2304]{1,0:T(8,128)}, f32[48,2304]{1,0:T(8,128)S(1)}, u32[]{:S(2)}) copy-start(f32[48,2304]{1,0:T(8,128)S(1)} %slice_dynamic-update-slice_fusion.4) | copy-start | bytes 1327108

commit v2 on v1

--- a/solution.py
+++ b/solution.py
@@ -256,8 +256,7 @@
 def attend_back_body(second, query, pair, grad, attended, log_total, *refs):
     if second:
         before, cosine, sine = refs[:3]
-    d_query, d_pair, zero = refs[-3:]
-    zero[0, 0] = 0.0
+    d_query, d_keys, d_values = refs[-3:]
     rows = query.shape[0]
     products = {}
 
@@ -292,8 +291,8 @@
         if second:
             turned = rotate_lanes(turned + before[:, lanes], cosine[...], -sine[...])
         d_query[:, lanes] = turned.astype(d_query.dtype)
-        d_pair[:, lanes] = ((one[1] + two[1]) * (1.0 / LOG2E)).astype(jnp.bfloat16)
-        d_pair[:, value_lanes(lanes)] = (one[2] + two[2]).astype(jnp.bfloat16)
+        d_keys[:, lanes] = ((one[1] + two[1]) * (1.0 / LOG2E)).astype(jnp.bfloat16)
+        d_values[:, lanes] = (one[2] + two[2]).astype(jnp.bfloat16)
 
 
 def attend_back(query, pair, grad, attended, log_total, before=None, after=(), free=()):
@@ -316,11 +315,11 @@
         ]
         + extra_specs
         + [pl.BlockSpec(memory_space=pl.ANY)] * len(after),
-        [block, columns(rows, 2 * lanes), scalar_spec()],
+        [block, block, block],
         [
             far((rows, width), jnp.bfloat16 if second else jnp.float32),
-            far((rows, 2 * width), jnp.bfloat16),
-            zero_shape(),
+            far((rows, width), jnp.bfloat16),
+            far((rows, width), jnp.bfloat16),
         ],
         [],
         28,
@@ -328,13 +327,13 @@
 
 
 def block_body(
-    own_up, own_down, attend_steps, hidden_steps,
+    own_down, attend_steps, hidden_steps,
     core, normed1, query_weight, cosine, sine, mods, up_bias, down_bias, *refs,
 ):
     pairs_far, refs = refs[: 2 * attend_steps], refs[2 * attend_steps :]
     (
         tokens_far, cotangent_far, out_far, up_far, down_far,
-        query, attended, log_total, mixed, d_middle, d_attended, up_keep, up_send,
+        query, attended, log_total, mixed, d_middle, d_attended, up_grad,
         down_keep, down_send, bias_grad, sums, peer_far,
         tokens, cotangent, out_weight, up_weight, down_weight, arrived,
         own_pairs, peer_pairs, pair_arrived, left,
@@ -439,8 +438,7 @@
         bias_grad[...] = column_sum(d_pre)
         down_grad = dot(low, d_ffn[...], 0, 0).astype(jnp.bfloat16)
         store_split(down_grad, core, own_down, down_keep, down_send)
-        up_grad = dot(normed[...], d_low, 0, 0).astype(jnp.bfloat16)
-        store_split(up_grad, core, own_up, up_keep, up_send)
+        up_grad[...] = dot(normed[...], d_low, 0, 0).astype(jnp.bfloat16)
         forward[...] += dot(low, down_weight[place, :])
         back[...] += dot(d_low, up_weight[:, place], 1, 1)
 
@@ -455,8 +453,7 @@
         d_middle[...] = d_value
         d_branch = (row(mods, GATE1) * d_value).astype(jnp.bfloat16)
         d_attended[...] = dot(d_branch, out_weight[...], 1, 1).astype(jnp.bfloat16)
-        out_grad = dot(all_attended[...], d_branch, 0, 0).astype(jnp.bfloat16)
-        store_split(out_grad, core, own_up, up_keep, up_send)
+        up_grad[...] = dot(all_attended[...], d_branch, 0, 0).astype(jnp.bfloat16)
         ffn = forward[...] + down_bias[...]
         mixed[...] = (held + row(mods, GATE2) * ffn).astype(jnp.bfloat16)
         sums[0:1, :] = column_sum(value)
@@ -499,12 +496,10 @@
     block = full((rows, width))
     far_spec = pl.BlockSpec(memory_space=pl.ANY)
     low = jnp.bfloat16
-    up_spec = pl.BlockSpec((width // 2, tile), lambda step: (0, up_tiles(step)))
+    up_spec = pl.BlockSpec((width, tile), lambda step: (0, up_tiles(step)))
     down_spec = pl.BlockSpec((tile // 2, width), lambda step: (tiles(step), 0))
     return kernel_call(
-        functools.partial(
-            block_body, split_rows(width), own_down, attend_steps, hidden_steps
-        ),
+        functools.partial(block_body, own_down, attend_steps, hidden_steps),
         attend_steps + hidden_steps + 1,
         [
             scalar_spec(),
@@ -527,7 +522,6 @@
             block,
             block,
             up_spec,
-            up_spec,
             down_spec,
             down_spec,
             pl.BlockSpec((1, tile), lambda step: (0, tiles(step))),
@@ -541,8 +535,7 @@
             far((rows, width), low),
             far((rows, width), jnp.float32),
             far((rows, width), low),
-            far((width // 2, hidden + width), low),
-            far((width // 2, hidden + width), low),
+            far((width, hidden + width), low),
             far((hidden // 2, width), low),
             far((hidden // 2, width), low),
             far((1, hidden), jnp.float32),
@@ -576,55 +569,27 @@
     )
 
 
-def projected_back_body(
-    own, core, d_query, d_pair, peer_pair, normed, cosine, sine, d_projected, zero, *parts
+def tokens_back_body(
+    own, core, d_query, d_keys, d_values, peer_keys, peer_values, normed, cosine, sine,
+    weight1, weight2, weight3, tokens, d_middle, mods, sums, bias_grad, *refs,
 ):
-    zero[0, 0] = 0.0
-    lanes = HEADS * HD
-    pair = d_pair[...].astype(jnp.float32) + peer_pair[...].astype(jnp.float32)
-    keys = rotate_lanes(pair[:, :lanes], cosine[...], -sine[...]).astype(jnp.bfloat16)
-    low = jnp.concatenate([d_query[...], keys, pair[:, lanes:].astype(jnp.bfloat16)], axis=1)
-    d_projected[...] = low
-    grad = dot(normed[...], low, 0, 0).astype(jnp.bfloat16)
-    for index in range(3):
-        part = grad[:, index * lanes : (index + 1) * lanes]
-        store_split(part, core, own, parts[2 * index], parts[2 * index + 1])
-
-
-def projected_back(core, d_query, d_pair, peer_pair, normed, cosine, sine):
-    rows, width = normed.shape
-    lanes = HEADS * HD
-    return kernel_call(
-        functools.partial(projected_back_body, split_rows(width)),
-        width // lanes,
-        [
-            scalar_spec(),
-            columns(rows, lanes),
-            columns(rows, 2 * lanes),
-            columns(rows, 2 * lanes),
-            full((rows, width)),
-            full((rows, 128)),
-            full((rows, 128)),
-        ],
-        [columns(rows, 3 * lanes), scalar_spec()] + [columns(width // 2, lanes)] * 6,
-        [far((rows, 3 * width), jnp.bfloat16), zero_shape()]
-        + [far((width // 2, width), jnp.bfloat16)] * 6,
-        [],
-        32,
-    )(core, d_query, d_pair, peer_pair, normed, cosine, sine, free=(peer_pair,))
-
-
-def tokens_back_body(
-    d_projected, weight1, weight2, weight3, tokens, d_middle, mods, sums, bias_grad, *refs
-):
-    out, small, zero, total = refs[-4:]
-    zero[0, 0] = 0.0
+    parts, (out, small, total) = refs[:6], refs[6:]
     step = pl.program_id(0)
     width = tokens.shape[1]
     lanes = HEADS * HD
-    part = sum(
-        dot(d_projected[:, index * lanes : (index + 1) * lanes], weight[...], 1, 1)
-        for index, weight in enumerate((weight1, weight2, weight3))
+    keys = d_keys[...].astype(jnp.float32) + peer_keys[...].astype(jnp.float32)
+    keys = rotate_lanes(keys, cosine[...], -sine[...]).astype(jnp.bfloat16)
+    values = d_values[...].astype(jnp.float32) + peer_values[...].astype(jnp.float32)
+    values = values.astype(jnp.bfloat16)
+    low = jnp.concatenate([d_query[...], keys, values], axis=1)
+    grad = dot(normed[...], low, 0, 0).astype(jnp.bfloat16)
+    for index in range(3):
+        third = grad[:, index * lanes : (index + 1) * lanes]
+        store_split(third, core, own, parts[2 * index], parts[2 * index + 1])
+    part = (
+        dot(d_query[...], weight1[...], 1, 1)
+        + dot(keys, weight2[...], 1, 1)
+        + dot(values, weight3[...], 1, 1)
     )
 
     @pl.when(step == 0)
@@ -666,16 +631,27 @@
         small[len(rows) :, :] = jnp.zeros_like(small[len(rows) :, :])
 
 
-def tokens_back(d_projected, weight, tokens, d_middle, mods, sums, bias_grad):
-    rows, width = tokens.shape
-    block = full((rows, width))
+def tokens_back(
+    core, d_query, d_keys, d_values, peer_keys, peer_values, normed, cosine, sine, weight,
+    tokens, d_middle, mods, sums, bias_grad,
+):
+    rows, width = normed.shape
     lanes = HEADS * HD
     steps = width // lanes
+    block = full((rows, width))
     return kernel_call(
-        tokens_back_body,
+        functools.partial(tokens_back_body, split_rows(width)),
         steps,
         [
-            columns(rows, 3 * lanes),
+            scalar_spec(),
+            columns(rows, lanes),
+            columns(rows, lanes),
+            columns(rows, lanes),
+            columns(rows, lanes),
+            columns(rows, lanes),
+            block,
+            full((rows, 128)),
+            full((rows, 128)),
             columns(width, lanes),
             columns(width, lanes, steps),
             columns(width, lanes, 2 * steps),
@@ -685,11 +661,19 @@
             full((8, width)),
             full(bias_grad.shape),
         ],
-        [block, full((16, width)), scalar_spec()],
-        [far((rows, width), jnp.bfloat16), far((16, width), jnp.float32), zero_shape()],
+        [columns(width // 2, lanes)] * 6 + [block, full((16, width))],
+        [far((width // 2, width), jnp.bfloat16)] * 6
+        + [
+            far((rows, width), jnp.bfloat16),
+            far((16, width), jnp.float32),
+        ],
         [pltpu.VMEM((rows, width), jnp.float32)],
-        32,
-    )(d_projected, weight, weight, weight, tokens, d_middle, mods, sums, bias_grad)
+        40,
+    )(
+        core, d_query, d_keys, d_values, peer_keys, peer_values, normed, cosine, sine,
+        weight, weight, weight, tokens, d_middle, mods, sums, bias_grad,
+        free=(peer_keys, peer_values),
+    )
 
 
 def swap_halves(block):
@@ -734,44 +718,61 @@
 def stage_body(jobs, counts, mine, *refs):
     inputs = refs[: counts[0]]
     outputs = refs[counts[0] + counts[1] :]
-    for place, (half, sources, target) in enumerate(jobs):
-        if half is None:
-            total = sum(inputs[place][...].astype(jnp.float32) for place in sources[0][:2])
-            outputs[target][...] = total.astype(jnp.bfloat16)
-            continue
-        sent, kept = outputs[target], outputs[target + 1]
-
-        def store(out, which, half=half, sources=sources):
-            at = 0
-            for one, two, start, stop, rows in sources:
-                if half:
-                    middle = (start + stop) // 2
-                    lanes = slice(middle, stop) if which else slice(start, middle)
-                    total = inputs[one][:, :, lanes].astype(jnp.float32)
-                    total = total + inputs[two][:, :, lanes].astype(jnp.float32)
-                    out[:, :, at : at + stop - middle] = total.astype(jnp.bfloat16)
-                    at += stop - middle
-                    continue
-                for pair in range(out.shape[0]):
-                    block = 2 * pair + which
-                    total = inputs[one][block, :, start:stop].astype(jnp.float32)
-                    total = total + inputs[two][block, :, start:stop].astype(jnp.float32)
-                    total = total.astype(jnp.bfloat16)
-                    column = at
-                    for first in range(0, total.shape[0], rows):
-                        out[pair, :, column : column + stop - start] = total[first : first + rows]
-                        column += stop - start
-                at = column
+
+    def terms(sources, place):
+        for one, two, lanes, rows in sources:
+            total = inputs[one][place + (slice(None), lanes)].astype(jnp.float32)
+            total = total + inputs[two][place + (slice(None), lanes)].astype(jnp.float32)
+            total = total.astype(jnp.bfloat16)
+            height = total.shape[-2]
+            for start in range(0, height, rows):
+                yield total if height == rows else total[..., start : start + rows, :]
+
+    def store(out, place, values):
+        at = 0
+        for value in values:
+            width = value.shape[-1]
+            out[place + (slice(None), slice(at, at + width))] = value
+            at += width
+
+    def run(index, kind, stride, sources, target):
+        if kind == "sum":
+            store(outputs[target], (slice(None),), terms(sources, (slice(None),)))
+            return
+
+        def part(out, which):
+            if kind == "half":
+                halves = []
+                for one, two, lanes, rows in sources:
+                    middle = (lanes.start + lanes.stop) // 2
+                    first, second = slice(lanes.start, middle), slice(middle, lanes.stop)
+                    halves.append((one, two, second if which else first, rows))
+                store(out, (slice(None),), terms(halves, (slice(None),)))
+                return
+            for block in range(out.shape[0]):
+                high, low = divmod(block, stride)
+                place = (2 * high + which) * stride + low
+                store(out, (block,), terms(sources, (place,)))
 
         for which in range(2):
 
-            @pl.when(mine[place] == which)
-            def _(which=which, sent=sent, kept=kept, store=store):
-                store(kept, which)
-                store(sent, 1 - which)
-
-
-def small_body(steps, first, one, two, out):
+            @pl.when(mine[index] == which)
+            def _(which=which):
+                part(outputs[target + 1], which)
+                part(outputs[target], 1 - which)
+
+    for index, (kind, stride, sources, target, whole) in enumerate(jobs):
+        if whole:
+
+            @pl.when(pl.program_id(0) == 0)
+            def _(args=(index, kind, stride, sources, target)):
+                run(*args)
+
+        else:
+            run(index, kind, stride, sources, target)
+
+
+def small_body(first, one, two, out):
     rows = one.shape[0] - 8
 
     @pl.when(pl.program_id(0) == 0)
@@ -789,36 +790,39 @@
     inputs, in_specs, specs, out_specs, out_shape, mine = [], [], [], [], [], []
     free = [*free] + [flow.got for flows, _ in jobs for flow in flows]
 
-    def place_of(array):
+    def spec(shape, whole):
+        if whole:
+            return full(shape)
+        return pl.BlockSpec((shape[0] // steps,) + shape[1:], lambda at: (at, 0, 0))
+
+    def place_of(array, whole):
         for index, other in enumerate(inputs):
             if other is array:
                 return index
         inputs.append(array)
-        each = array.shape[0] // steps
-        in_specs.append(pl.BlockSpec((each,) + array.shape[1:], lambda at: (at, 0, 0)))
+        in_specs.append(spec(array.shape, whole))
         return len(inputs) - 1
 
     for flows, step in jobs:
-        half = None if step == "sum" else step == "half"
+        bit, stride = step if isinstance(step, tuple) else (None, 1)
         rest, count = flows[0].rest, flows[0].count
+        smallest = 1 if bit is None else 2 * stride
+        whole = count % steps > 0 or (count // steps) % smallest > 0
         sources = [
-            (place_of(flow.got), place_of(flow.kept), *flow.lanes, rest) for flow in flows
+            (place_of(flow.got, whole), place_of(flow.kept, whole), slice(*flow.lanes), rest)
+            for flow in flows
         ]
-        if half is None:
-            shape = flows[0].kept.shape
+        width = sum(flow.width * flow.rest // rest for flow in flows)
+        if bit is not None:
+            shape = (count // 2, rest, width)
+            mine.append((dp_rank // bit) % 2)
+        else:
+            shape = (count, rest, width // 2 if step == "half" else width)
             mine.append(seq_rank)
-        elif half:
-            shape = (count, rest, sum(flow.width for flow in flows) // 2)
-            mine.append(seq_rank)
-        else:
-            width = sum(flow.width * flow.rest // rest for flow in flows)
-            shape = (count // 2, rest, width)
-            mine.append((dp_rank // step) % 2)
-        specs.append((half, sources, len(out_shape)))
-        results = 1 if half is None else 2
+        specs.append((step if bit is None else "bit", stride, sources, len(out_shape), whole))
+        results = 1 if step == "sum" else 2
         out_shape += [far(shape, jnp.bfloat16)] * results
-        block = (shape[0] // steps,) + shape[1:]
-        out_specs += [pl.BlockSpec(block, lambda at: (at, 0, 0))] * results
+        out_specs += [spec(shape, whole)] * results
     counts = (len(inputs), len(after))
     extra = []
     if small is not None:
@@ -833,7 +837,7 @@
             stage_body(specs, counts, mine, *refs)
             return
         main, ends = refs[: sum(counts)], refs[sum(counts) :]
-        small_body(steps, first, ends[0], ends[1], ends[-1])
+        small_body(first, ends[0], ends[1], ends[-1])
         stage_body(specs, counts, mine, *main, *ends[2:-1])
 
     results = kernel_call(
@@ -847,11 +851,11 @@
         out_shape,
         [],
         40,
-    )(jnp.stack(mine), *inputs, *after, *extra, free=(*free, *extra))
+    )(jnp.stack(mine), *inputs, *after, *extra, free=(*free, *extra[1:]))
     new = []
-    for (flows, step), (_, _, target) in zip(jobs, specs):
+    for (flows, step), (_, _, _, target, _) in zip(jobs, specs):
         sent = results[target]
-        got = swap_seq(sent) if isinstance(step, str) else swap_bit(sent, step)
+        got = swap_seq(sent) if isinstance(step, str) else swap_bit(sent, step[0])
         new.append(Flow(got, sent if step == "sum" else results[target + 1]))
     if small is not None:
         new.append(results[-1])
@@ -873,19 +877,16 @@
     )
 
 
-def joined(terms, size, widths):
-    block, got = terms.kept[0].astype(jnp.float32), terms.got[0].astype(jnp.float32)
+def joined(flow, widths):
+    block, got = flow.kept[0].astype(jnp.float32), flow.got[0].astype(jnp.float32)
     here = lax.axis_index("seq") == 0
     first, second = jnp.where(here, block, got), jnp.where(here, got, block)
     parts, at = [], 0
-    for index, width in enumerate(widths):
-        rows = []
-        for _ in range(size if index == len(widths) - 1 else 1):
-            rows.append(
-                jnp.concatenate([first[:, at : at + width], second[:, at : at + width]], axis=1)
-            )
-            at += width
-        parts.append(jnp.concatenate(rows, axis=0))
+    for width in widths:
+        parts.append(
+            jnp.concatenate([first[:, at : at + width], second[:, at : at + width]], axis=1)
+        )
+        at += width
     return parts
 
 
@@ -929,7 +930,7 @@
     peer_parts = [swap_cores(part) for part in own_parts]
     core_ref = core[None]
     (
-        query, attended, log_total, mixed, d_middle, d_attended, up_keep, up_send,
+        query, attended, log_total, mixed, d_middle, d_attended, up_grad,
         down_keep, down_send, up_bias_grad, sums2, peer_pair,
     ) = block_layer(
         core_ref, normed1, attn_qkv, cosine, sine, mods,
@@ -940,87 +941,67 @@
     hidden = mlp_up.shape[1]
     dp_size = lax.axis_size("dp")
     bits = dp_bits()
-    by_steps = split_rows(width) == width // dp_size
+    by_steps = split_rows(width) == width // dp_size and len(bits) == 4
     mixed = swap_halves(mixed)
+    up_rows = lax.psum_scatter(up_grad, "dp", scatter_dimension=0, tiled=True)
+    up_got = swap_seq(up_rows)
 
     def blocks(part):
         return part.reshape(dp_size // 2, -1, part.shape[1])
 
     if by_steps:
-        up = Flow(swap_cores(blocks(up_send)), blocks(up_keep))
         down = Flow(swap_cores(blocks(down_send)), blocks(down_keep))
-    d_query, away_pair, _ = attend_back(query, peer_pair, d_attended, attended, log_total)
+    d_query, away_keys, away_values = attend_back(query, peer_pair, d_attended, attended, log_total)
     after = ()
     if by_steps:
-        (down, up), sent = stage(
-            4, [([down], "half"), ([up], bits[1])], (away_pair, mixed), free=(mixed,)
-        )
+        (down,), sent = stage(4, [([down], "half")], (away_keys, mixed), free=(mixed,))
         after = (sent,)
-    back_pair = swap_cores(away_pair)
-    d_query, d_pair, _ = attend_back(
+    peer_keys, peer_values = swap_cores(away_keys), swap_cores(away_values)
+    d_query, d_keys, d_values = attend_back(
         query, own_pair, d_attended, attended, log_total, (d_query, cosine, sine), after
     )
-    d_projected, _, *qkv_parts = projected_back(
-        core_ref, d_query, d_pair, back_pair, normed1, cosine, sine
-    )
-    third = HEADS * HD
-    if by_steps:
-        queries, keys, values = [
-            (swap_cores(blocks(send)), blocks(keep))
-            for keep, send in zip(qkv_parts[::2], qkv_parts[1::2])
-        ]
-        one = [Flow(*queries), Flow(*values, (0, third))]
-        two = [Flow(*keys), Flow(*values, (third, width))]
-    tokens_grad, small, _ = tokens_back(
-        d_projected, attn_qkv, tokens, d_middle, mods, sums2, up_bias_grad
+    *qkv_parts, tokens_grad, small = tokens_back(
+        core_ref, d_query, d_keys, d_values, peer_keys, peer_values, normed1, cosine, sine, attn_qkv, tokens,
+        d_middle, mods, sums2, up_bias_grad,
     )
     got = swap_cores(small)
     def doubled(small, got):
         return jnp.concatenate([small[:-8], got[:-8], small[-8:] + got[-8:]], axis=0)
 
     if by_steps:
-        (down, up, one, two, small), sent = stage(
-            4,
-            [([down], bits[1]), ([up], "half"), (one, "half"), (two, bits[1])],
-            (),
-            (got, small, True),
-        )
-        early = [up, down]
-        two = [Flow(two.got, two.kept, lanes) for lanes in ((0, width), (width, two.width))]
-        late = [one, two]
+        late = [
+            Flow(swap_cores(blocks(send)), blocks(keep))
+            for keep, send in zip(qkv_parts[::2], qkv_parts[1::2])
+        ]
         moves = [functools.partial(swap_bit, bit=bit) for bit in bits[2:] + bits[1:2]]
         moves.append(swap_seq)
-
-        def next_stage(jobs, count):
+        (down, late, small), sent = stage(
+            4, [([down], (bits[1], 1)), (late, "half")], (), (got, small, True)
+        )
+
+        small = doubled(small, moves.pop(0)(small))
+
+        def next_stage(jobs, count, after=()):
             nonlocal small, sent
             extra = (moves.pop(0)(small), small, False) if len(moves) > 0 else None
-            flows, sent = stage(count, jobs, (sent,), extra)
+            flows, sent = stage(count, jobs, (sent, *after), extra, after)
             if extra is not None:
                 small = flows.pop()
             return flows
 
-        early = next_stage([(early, bits[2])], early[0].count // 2)
-        late = next_stage([([one], bits[1]), (two, "half")], 4)
-        for index, bit in enumerate(bits[3:]):
-            early = next_stage([(early, bit)], early[0].count // 2)
-            late = next_stage([(late, bits[2 + index])], late[0].count // 2)
-        early = next_stage([(early, "sum")], 1)
-        late = next_stage([(late, bits[-1])], late[0].count // 2)
-        late = next_stage([(late, "sum")], 1)
+        down, late = next_stage([([down], (bits[2], 1)), ([late], (bits[1], 1))], 2)
+        down, late = next_stage([([down], (bits[3], 1)), ([late], (bits[2], 1))], 2)
+        down, late = next_stage([([down], "sum"), ([late], (bits[3], 1))], 1, (up_got,))
+        (late,) = next_stage([([late], "sum")], 1)
         while len(moves) > 0:
             small = doubled(small, moves.pop(0)(small))
-        up_half, down_half = (hidden + width) // 2, width // 2
-        up_rows, down_rows = joined(early[0], hidden // width, (up_half, down_half))
-        query_rows, value_rows1, key_rows, value_rows2 = joined(
-            late[0], 1, (width // 2, third // 2, width // 2, (width - third) // 2)
-        )
-        qkv_rows = jnp.concatenate([query_rows, key_rows, value_rows1, value_rows2], axis=1)
+        (down_rows,) = joined(down, (width // 2,))
+        qkv_rows = jnp.concatenate(joined(late, (width // 2,) * 3), axis=1)
     else:
         small = small + got
-        moves = [functools.partial(swap_bit, bit=bit) for bit in bits[2:] + bits[1:2]]
-        for move in moves + [swap_seq]:
+        moves = [functools.partial(swap_bit, bit=bit) for bit in bits[1:]] + [swap_seq]
+        for move in moves:
             small = doubled(small, move(small))
-        up_rows = plain_sum(up_keep, up_send, width)
         down_rows = plain_sum(down_keep, down_send, width)
         qkv_rows = jnp.concatenate(
             [
@@ -1029,6 +1010,7 @@
             ],
             axis=1,
         )
+    up_rows = up_rows.astype(jnp.float32) + up_got.astype(jnp.float32)
     per_sequence, sums = small[:-8].reshape(-1, 8, width), small[-8:]
     d_mod_all = per_sequence[:, :6].reshape(per_sequence.shape[0], 6 * width)
     cond_all = per_sequence[:, 6, : cond.shape[1]]

time: 227 us -> 217 us (0.956)
  between operations: 3.39 us -> 16.7 us
  Pallas kernels: 115 us -> 104 us
  starting transfers between devices: 51.6 us -> 45.2 us
  waiting for transfers between devices: 29.8 us -> 24.6 us
    pallas_call x15 -> x11, Pallas kernels: 115 us -> 104 us  [run(): return call(*placed)]
    ppermute x7 -> x6, waiting for transfers between devices: 10.1 us -> 4.26 us  [swap_seq(): return lax.ppermute(block, 'seq', [(0, 1), (1, 0)])]
    ppermute x21 -> x19, starting transfers between devices: 26.5 us -> 23.5 us  [swap_bit(): lax.ppermute(block, 'dp', [(i, i ^ bit) for i in range(lax.axis_size('dp'...]
    unnamed x60 -> x40, local copies, waits for them, and re-layouts: 5.31 us -> 2.68 us
    ppermute x7 -> x6, starting transfers between devices: 10.4 us -> 8.05 us  [swap_seq(): return lax.ppermute(block, 'seq', [(0, 1), (1, 0)])]
    ppermute x21 -> x19, waiting for transfers between devices: 19.7 us -> 20 us  [swap_bit(): lax.ppermute(block, 'dp', [(i, i ^ bit) for i in range(lax.axis_size('dp'...]
  transfers between devices with their start and end apart: 33 -> 31, of which waited for: 15 -> 12; matrix products, arithmetic and copies ran while one was open for 8% -> 10% of each run, Pallas kernels for 30% -> 28%
where the time goes in v2:
time: 217 us; the launch traced here: 215 us
  Pallas kernels  104 us (48%)
  starting transfers between devices  45.2 us (21%)
  waiting for transfers between devices  24.6 us (11%)
  between operations  16.7 us (8%)
  local copies, waits for them, and re-layouts  11.9 us (5%)
  other arithmetic  9 us (4%)
  matrix products  3.99 us (2%)
    pallas_call x11, Pallas kernels, run(): return call(*placed)  104 us
    ppermute x19, starting transfers between devices, swap_bit(): lax.ppermute(block, 'dp', [(i, i ^ bit) for i in range(lax.axis_size('dp'...  23.5 us
    ppermute x19, waiting for transfers between devices, swap_bit(): lax.ppermute(block, 'dp', [(i, i ^ bit) for i in range(lax.axis_size('dp'...  20 us
    ppermute x5, starting transfers between devices, swap_halves(): return lax.ppermute(block, ('dp', 'seq'), perm)  13.6 us
    ppermute x6, starting transfers between devices, swap_seq(): return lax.ppermute(block, 'seq', [(0, 1), (1, 0)])  8.05 us
  transfers between devices with their start and end apart: 31, of which 12 were waited for; matrix products, arithmetic and copies ran while one was open for 10% of the time, Pallas kernels for 28%

profile of v2, /device:TPU:0, one launch (start us, length us, event | category | flops | bytes accessed | tf_op | source)
XLA Modules:
  0.0 215.4 jit_solution(6984236061832406500)
XLA Ops:
  7.2 1.9 collective-permute-start.1
  9.2 1.8 collective-permute-start
  10.9 1.8 collective-permute-start.5
  12.7 0.7 reshape.117
  13.4 0.7 reshape.118
  14.1 1.0 fusion.4
  15.1 1.3 pad_maximum_fusion.1
  18.0 0.7 divide_multiply_fusion
  18.7 0.6 convolution_reduce_fusion
  19.4 1.3 concatenate.18.mods
  20.7 6.7 %shard_map.237 = (bf16[512,768]{1,0:T(8,128)(2,1)}, bf16[512,1536]{1,0:T(8,128)(2,1)}, bf16[512,512]{1,0:T(8,128)(2,1)}, bf16[512,512]{1,0:T(8,128)(2,1)}, bf16[512,512]{1,0:T(8,128)(2,1)}) custom-call(bf16[512,768]{1,0:T(8,128)(2,1)S(1)} %collective-permute-done.tokens.refs_6_, f32[16,768]{1,0:T(8,128)} %concatenate.18.mods, bf16[768,2304]{1,0:T(8,128)(2,1)} %weight3.1, ...), custom_call_target="tpu_custom_call" | custom-call | flops 1 | bytes 1 | tf_op jit(solution)/shard_map/pallas_call | solution.py:97
  27.4 5.3 %collective-permute-start.2 = (bf16[512,512]{1,0:T(8,128)(2,1)}, bf16[512,512]{1,0:T(8,128)(2,1)S(1)}, u32[]{:S(2)}, u32[]{:S(2)}) collective-permute-start(bf16[512,512]{1,0:T(8,128)(2,1)} %get-tuple-element.66.refs_0_), channel_id=1, source_target_pairs={{0,2},{2,0},{4,6},{6,4},{8,10},{10,8},{12,14},{14,12},{16,18},{18,... | collective-permute-start | bytes 1572872 | tf_op jit(solution)/shard_map/ppermute | solution.py:687
  33.2 0.6 broadcast_in_dim.55
  33.8 0.6 reshape.120.down_bias
  34.5 0.7 collective-permute-done.3.refs_4_
  35.2 0.7 collective-permute-done.4.refs_5_
  36.0 0.8 copy-done.6
  36.8 40.8 %shard_map.238 = (bf16[512,768]{1,0:T(8,128)(2,1)}, bf16[512,768]{1,0:T(8,128)(2,1)}, f32[3,4,512]{2,1,0:T(4,128)}, bf16[512,768]{1,0:T(8,128)(2,1)}, f32[512,76...) custom-call(s32[1]{0:T(128)} %bitcast.core, ...), custom_call_target="tpu_custom_call" | custom-call | flops 1 | bytes 1 | tf_op jit(solution)/shard_map/pallas_call | solution.py:97
  78.1 0.6 copy-done.14
  78.7 0.7 collective-permute-start.6
  79.4 11.3 %shard_map.239 = (f32[512,768]{1,0:T(8,128)}, bf16[512,768]{1,0:T(8,128)(2,1)}, bf16[512,768]{1,0:T(8,128)(2,1)}) custom-call(bf16[512,768]{1,0:T(8,128)(2,1)} %get-tuple-element.70.query, bf16[512,1536]{1,0:T(8,128)(2,1)} %get-tuple-element.75.pair, bf16[512,768]{1,0:T(8,128)(2,1)} %get-tuple-element.72.grad, bf16[512,768]{1,0:T(8,128)(2,1)} %get-tuple-element.73.attended, ...), custom_call_target="tpu_custom_call" | custom-call | flops 1 | bytes 1 | tf_op jit(solution)/shard_map/pallas_call | solution.py:97
  90.7 1.6 collective-permute-start.8
  92.4 4.6 %shard_map.240 = (bf16[8,192,384]{2,1,0:T(8,128)(2,1)}, bf16[8,192,384]{2,1,0:T(8,128)(2,1)}) custom-call(s32[1]{0:T(128)} %bitcast.8.mine, bf16[8,192,768]{2,1,0:T(8,128)(2,1)} %collective-permute-done.7.refs_0_, bf16[8,192,768]{2,1,0:T(8,128)(2,1)} %bitcast.52, bf16[512,768]{1,0:T(8,128)(2,1)} %get-tuple-element.79.refs_2_, ...), custom_call_target="tpu_custom_call" | custom-call | flops 1 | bytes 1 | tf_op jit(solution)/shard_map/pallas_call | solution.py:97
  97.0 2.1 collective-permute-start.11
  99.1 11.8 %shard_map.241 = (bf16[512,768]{1,0:T(8,128)(2,1)}, bf16[512,768]{1,0:T(8,128)(2,1)}, bf16[512,768]{1,0:T(8,128)(2,1)}) custom-call(bf16[512,768]{1,0:T(8,128)(2,1)} %get-tuple-element.70.query, bf16[512,1536]{1,0:T(8,128)(2,1)} %get-tuple-element.71.pair, bf16[512,768]{1,0:T(8,128)(2,1)} %get-tuple-element.72.grad, ...), custom_call_target="tpu_custom_call" | custom-call | flops 1 | bytes 1 | tf_op jit(solution)/shard_map/pallas_call | solution.py:97
  110.9 15.0 %shard_map.242 = (bf16[384,768]{1,0:T(8,128)(2,1)}, bf16[384,768]{1,0:T(8,128)(2,1)}, bf16[384,768]{1,0:T(8,128)(2,1)}, bf16[384,768]{1,0:T(8,128)(2,1)}, bf16[3...) custom-call(s32[1]{0:T(128)} %bitcast.core, ...), custom_call_target="tpu_custom_call" | custom-call | flops 1 | bytes 1 | tf_op jit(solution)/shard_map/pallas_call | solution.py:97
  127.1 1.7 collective-permute-done.15.refs_9_
  129.3 0.8 collective-permute-done.14.refs_6_
  130.1 5.0 %shard_map.243 = (bf16[4,192,384]{2,1,0:T(8,128)(2,1)}, bf16[4,192,384]{2,1,0:T(8,128)(2,1)}, bf16[8,48,1152]{2,1,0:T(8,128)(2,1)}, bf16[8,48,1152]{2,1,0:T(8,128)(2,1)}, f32[16,768]{1,0:T(8,128)}) custom-call(s32[2]{0:T(128)S(1)} %pad_add_fusion.3.mine, bf16[8,192,384]{2,1,0:T(8,128)(2,1)S(1)} %collective-permute-done.11.refs_0_, ...), custom_call_target="tpu_custom_call" | custom-call | flops 1 | bytes 1 | tf_op jit(solution)/shard_map/pallas_call | solution.py:97
  135.5 1.4 collective-permute-start.16
  136.9 1.6 collective-permute-start.18
  138.5 7.4 %collective-permute-start.10 = (bf16[512,768]{1,0:T(8,128)(2,1)}, bf16[512,768]{1,0:T(8,128)(2,1)}, u32[]{:S(2)}, u32[]{:S(2)}) collective-permute-start(bf16[512,768]{1,0:T(8,128)(2,1)} %get-tuple-element.88), channel_id=1, source_target_pairs={{0,0},{1,2},{2,1},{3,3},{4,4},{5,6},{6,5},{7,7},{8,8},{9,10},{10,9... | collective-permute-start | bytes 2359304 | tf_op jit(solution)/shard_map/ppermute | solution.py:683
  145.9 0.8 fusion.12
  146.7 2.6 %collective-permute-start.19 = (f32[24,768]{1,0:T(8,128)S(1)}, f32[24,768]{1,0:T(8,128)S(1)}, u32[]{:S(2)}, u32[]{:S(2)}) collective-permute-start(f32[24,768]{1,0:T(8,128)S(1)} %pad_maximum_fusion.3.refs_5_), channel_id=1, source_target_pairs={{0,16},{2,18},{4,20},{6,22},{8,24},{10,26},{12,28},{14,30},{16,0},... | collective-permute-start | bytes 221192 | tf_op jit(solution)/shard_map/ppermute | solution.py:687
  149.4 5.1 %collective-permute-done.19.refs_6_ = f32[24,768]{1,0:T(8,128)S(1)} collective-permute-done((f32[24,768]{1,0:T(8,128)S(1)}, f32[24,768]{1,0:T(8,128)S(1)}, u32[]{:S(2)}, u32[]{:S(2)}) %collective-permute-start.19) | collective-permute-done | bytes 73760 | tf_op jit(solution)/shard_map/ppermute | solution.py:687
  154.8 2.3 %collective-permute-done.17.refs_2_ = bf16[8,48,1152]{2,1,0:T(8,128)(2,1)S(1)} collective-permute-done((bf16[8,48,1152]{2,1,0:T(8,128)(2,1)}, bf16[8,48,1152]{2,1,0:T(8,128)(2,1)S(1)}, u32[]{:S(2)}, u32[]{:S(2)}) %collective-permute-start.17) | collective-permute-done | bytes 884768 | tf_op jit(solution)/shard_map/ppermute | solution.py:695
  157.1 2.8 %shard_map.244 = (bf16[2,192,384]{2,1,0:T(8,128)(2,1)}, bf16[2,192,384]{2,1,0:T(8,128)(2,1)}, bf16[4,48,1152]{2,1,0:T(8,128)(2,1)}, bf16[4,48,1152]{2,1,0:T(8,128)(2,1)}, f32[40,768]{1,0:T(8,128)}) custom-call(s32[2]{0:T(128)S(1)} %pad_add_fusion.2.mine, bf16[4,192,384]{2,1,0:T(8,128)(2,1)S(1)} %collective-permute-done.16.refs_0_, ...), custom_call_target="tpu_custom_call" | custom-call | flops 1 | bytes 1 | tf_op jit(solution)/shard_map/pallas_call | solution.py:97
  159.8 1.7 collective-permute-start.21
  161.5 1.6 collective-permute-start.20
  164.5 1.6 collective-permute-start.25
  166.2 7.9 %collective-permute-done.22.refs_6_ = f32[40,768]{1,0:T(8,128)S(1)} collective-permute-done((f32[40,768]{1,0:T(8,128)}, f32[40,768]{1,0:T(8,128)S(1)}, u32[]{:S(2)}, u32[]{:S(2)}) %collective-permute-start.22) | collective-permute-done | bytes 122912 | tf_op jit(solution)/shard_map/ppermute | solution.py:687
  174.2 2.3 %shard_map.245 = (bf16[1,192,384]{2,1,0:T(8,128)(2,1)}, bf16[1,192,384]{2,1,0:T(8,128)(2,1)}, bf16[2,48,1152]{2,1,0:T(8,128)(2,1)}, bf16[2,48,1152]{2,1,0:T(8,128)(2,1)}, f32[72,768]{1,0:T(8,128)}) custom-call(s32[2]{0:T(128)S(1)} %pad_add_fusion.1.mine, bf16[2,192,384]{2,1,0:T(8,128)(2,1)S(1)} %collective-permute-done.20.refs_0_, ...), custom_call_target="tpu_custom_call" | custom-call | flops 1 | bytes 1 | tf_op jit(solution)/shard_map/pallas_call | solution.py:97
  176.5 1.5 collective-permute-start.24
  178.5 2.7 %collective-permute-start.23 = (bf16[1,192,384]{2,1,0:T(8,128)(2,1)}, bf16[1,192,384]{2,1,0:T(8,128)(2,1)S(1)}, u32[]{:S(2)}, u32[]{:S(2)}) collective-permute-start(bf16[1,192,384]{2,1,0:T(8,128)(2,1)} %get-tuple-element.107.refs_4_), channel_id=1, source_target_pairs={{0,16},{2,18},{4,20},{6,22},{8,24},{10,26},{12,28},{14,30},{16,0},... | collective-permute-start | bytes 442376 | tf_op jit(solution)/shard_map/ppermute | solution.py:687
  181.1 2.4 %bitcast_convert_fusion = f32[1,512,768]{2,1,0:T(8,128)} fusion(bf16[512,768]{1,0:T(8,128)(2,1)} %collective-permute-done.10), kind=kLoop, calls=%fused_computation.1 | loop fusion | flops 393216 | bytes 2359296 | tf_op jit(solution)/shard_map/broadcast_in_dim | solution.py:1030
  183.5 2.2 collective-permute-done.23.refs_0_
  185.7 2.1 shard_map.246
  187.8 1.1 slice_bitcast_fusion
  189.0 2.3 %collective-permute-start.29 = (bf16[1,192,384]{2,1,0:T(8,128)(2,1)}, bf16[1,192,384]{2,1,0:T(8,128)(2,1)S(1)}, u32[]{:S(2)}, u32[]{:S(2)}) collective-permute-start(bf16[1,192,384]{2,1,0:T(8,128)(2,1)} %get-tuple-element.116.refs_2_), channel_id=1, source_target_pairs={{0,1},{1,0},{2,3},{3,2},{4,5},{5,4},{6,7},{7,6},{8,9},{9,8},{10,11... | collective-permute-start | bytes 442376 | tf_op jit(solution)/shard_map/ppermute | solution.py:695
  191.3 1.0 collective-permute-start.27
  192.4 2.2 %fusion.10 = f32[1,128]{1,0:T(1,128)} fusion(f32[1000,128]{1,0:T(8,128)} %param.17, s32[]{:T(128)S(6)} %select_n.108, f32[4608,1]{0,1:T(1,128)S(1)} %bitcast.58, bf16[128,4608]{1,0:T(8,128)(2,1)S(1)} %copy-done), kind=kOutput, calls=%fused_computation.41 | convolution fusion | flops 7079040 | bytes 1199108 | tf_op jit(solution)/shard_map/dot_general | solution.py:1027
  194.7 1.2 fusion.6
  195.9 0.7 slice.89
  196.6 0.9 slice.104
  197.5 0.7 slice.103
  198.2 0.6 reduce_sum.12
  198.8 0.6 reshape.115
  199.4 1.5 slice_reduce_fusion
  200.9 1.6 shard_map.247
  202.4 1.2 collective-permute-start.28
  203.6 1.0 fusion
  204.6 0.9 pad_maximum_fusion
  205.4 2.0 collective-permute-done.28
  207.5 0.9 copy.37
  (89 shorter events, 5.4 us)
Async XLA Ops:
  7.2 11.6 %copy-start = (bf16[128,4608]{1,0:T(8,128)(2,1)S(1)}, bf16[128,4608]{1,0:T(8,128)(2,1)}, u32[]{:S(2)}) copy-start(bf16[128,4608]{1,0:T(8,128)(2,1)} %param.26) | copy-start | bytes 3538948
  7.2 157.3 %reduce-scatter.2.cloned.1.call-start = ((), (), s32[]{:S(2)}) async-start(), calls=%async_computation.1 | async-start | bytes 6266880 | tf_op jit(solution)/shard_map/reduce_scatter | solution.py:946
  7.2 9.2 %collective-permute-start.1 = (s32[1]{0:T(128)}, s32[1]{0:T(128)}, u32[]{:S(2)}, u32[]{:S(2)}) collective-permute-start(s32[1]{0:T(128)} %param.16), channel_id=1, source_target_pairs={{0,0},{1,2},{2,1},{3,3},{4,4},{5,6},{6,5},{7,7},{8,8},{9,10},{10,9... | collective-permute-start | bytes 20 | tf_op jit(solution)/shard_map/ppermute | solution.py:683
  9.2 11.5 %collective-permute-start = (bf16[512,768]{1,0:T(8,128)(2,1)}, bf16[512,768]{1,0:T(8,128)(2,1)S(1)}, u32[]{:S(2)}, u32[]{:S(2)}) collective-permute-start(bf16[512,768]{1,0:T(8,128)(2,1)} %bitcast.62), channel_id=1, source_target_pairs={{0,0},{1,2},{2,1},{3,3},{4,4},{5,6},{6,5},{7,7},{8,8},{9,10},{10,9... | collective-permute-start | bytes 2359304 | tf_op jit(solution)/shard_map/ppermute | solution.py:683
  10.9 23.5 %collective-permute-start.5 = (bf16[512,768]{1,0:T(8,128)(2,1)}, bf16[512,768]{1,0:T(8,128)(2,1)S(1)}, u32[]{:S(2)}, u32[]{:S(2)}) collective-permute-start(bf16[512,768]{1,0:T(8,128)(2,1)} %bitcast.63), channel_id=1, source_target_pairs={{0,0},{1,2},{2,1},{3,3},{4,4},{5,6},{6,5},{7,7},{8,8},{9,10},{10,9... | collective-permute-start | bytes 2359304 | tf_op jit(solution)/shard_map/ppermute | solution.py:683
  14.1 5.2 %copy-start.11 = (bf16[4608]{0:T(1024)(128)(2,1)S(1)}, bf16[4608]{0:T(1024)(128)(2,1)}, u32[]{:S(2)}) copy-start(bf16[4608]{0:T(1024)(128)(2,1)} %param.27) | copy-start | bytes 27652
  20.7 6.8 %copy-start.1 = (bf16[512,768]{1,0:T(8,128)(2,1)}, bf16[512,768]{1,0:T(8,128)(2,1)S(1)}, u32[]{:S(2)}) copy-start(bf16[512,768]{1,0:T(8,128)(2,1)S(1)} %collective-permute-done.tokens.refs_6_) | copy-start | bytes 2359300
  20.7 12.6 %copy-start.12 = (bf16[3072]{0:T(1024)(128)(2,1)S(1)}, bf16[3072]{0:T(1024)(128)(2,1)}, u32[]{:S(2)}) copy-start(bf16[3072]{0:T(1024)(128)(2,1)} %param.23) | copy-start | bytes 18436
  20.7 13.2 %copy-start.13 = (bf16[768]{0:T(1024)(128)(2,1)S(1)}, bf16[768]{0:T(1024)(128)(2,1)}, u32[]{:S(2)}) copy-start(bf16[768]{0:T(1024)(128)(2,1)} %param.25) | copy-start | bytes 4612
  27.4 7.0 %collective-permute-start.2 = (bf16[512,512]{1,0:T(8,128)(2,1)}, bf16[512,512]{1,0:T(8,128)(2,1)S(1)}, u32[]{:S(2)}, u32[]{:S(2)}) collective-permute-start(bf16[512,512]{1,0:T(8,128)(2,1)} %get-tuple-element.66.refs_0_), channel_id=1, source_target_pairs={{0,2},{2,0},{4,6},{6,4},{8,10},{10,8},{12,14},{14,12},{16,18},{18,... | collective-permute-start | bytes 1572872 | tf_op jit(solution)/shard_map/ppermute | solution.py:687
  32.7 2.5 %collective-permute-start.3 = (bf16[512,512]{1,0:T(8,128)(2,1)}, bf16[512,512]{1,0:T(8,128)(2,1)S(1)}, u32[]{:S(2)}, u32[]{:S(2)}) collective-permute-start(bf16[512,512]{1,0:T(8,128)(2,1)} %get-tuple-element.67.refs_1_), channel_id=1, source_target_pairs={{0,2},{2,0},{4,6},{6,4},{8,10},{10,8},{12,14},{14,12},{16,18},{18,... | collective-permute-start | bytes 1572872 | tf_op jit(solution)/shard_map/ppermute | solution.py:687
  32.8 3.2 %collective-permute-start.4 = (bf16[512,512]{1,0:T(8,128)(2,1)}, bf16[512,512]{1,0:T(8,128)(2,1)S(1)}, u32[]{:S(2)}, u32[]{:S(2)}) collective-permute-start(bf16[512,512]{1,0:T(8,128)(2,1)} %get-tuple-element.68.refs_2_), channel_id=1, source_target_pairs={{0,2},{2,0},{4,6},{6,4},{8,10},{10,8},{12,14},{14,12},{16,18},{18,... | collective-permute-start | bytes 1572872 | tf_op jit(solution)/shard_map/ppermute | solution.py:687
  34.4 1.5 copy-start.3
  34.5 1.5 copy-start.4
  35.2 0.8 copy-start.5
  36.0 0.8 copy-start.6
  77.6 1.1 copy-start.14
  77.6 14.8 %collective-permute-start.7 = (bf16[8,192,768]{2,1,0:T(8,128)(2,1)}, bf16[8,192,768]{2,1,0:T(8,128)(2,1)}, u32[]{:S(2)}, u32[]{:S(2)}) collective-permute-start(bf16[8,192,768]{2,1,0:T(8,128)(2,1)} %bitcast.61), channel_id=1, source_target_pairs={{0,2},{2,0},{4,6},{6,4},{8,10},{10,8},{12,14},{14,12},{16,18},{18,... | collective-permute-start | bytes 7077896 | tf_op jit(solution)/shard_map/ppermute | solution.py:687
  78.7 13.7 %collective-permute-start.6 = (bf16[512,768]{1,0:T(8,128)(2,1)S(1)}, bf16[512,768]{1,0:T(8,128)(2,1)S(1)}, u32[]{:S(2)}, u32[]{:S(2)}) collective-permute-start(bf16[512,768]{1,0:T(8,128)(2,1)S(1)} %copy-done.14), channel_id=1, source_target_pairs={{0,0},{1,2},{2,1},{3,3},{4,4},{5,6},{6,5},{7,7},{8,8},{9,10},{10,9... | collective-permute-start | bytes 2359304 | tf_op jit(solution)/shard_map/ppermute | solution.py:683
  90.7 20.1 %collective-permute-start.8 = (bf16[512,768]{1,0:T(8,128)(2,1)}, bf16[512,768]{1,0:T(8,128)(2,1)}, u32[]{:S(2)}, u32[]{:S(2)}) collective-permute-start(bf16[512,768]{1,0:T(8,128)(2,1)} %get-tuple-element.79.refs_2_), channel_id=1, source_target_pairs={{0,2},{2,0},{4,6},{6,4},{8,10},{10,8},{12,14},{14,12},{16,18},{18,... | collective-permute-start | bytes 2359304 | tf_op jit(solution)/shard_map/ppermute | solution.py:687
  92.4 18.5 %collective-permute-start.9 = (bf16[512,768]{1,0:T(8,128)(2,1)}, bf16[512,768]{1,0:T(8,128)(2,1)}, u32[]{:S(2)}, u32[]{:S(2)}) collective-permute-start(bf16[512,768]{1,0:T(8,128)(2,1)} %get-tuple-element.84), channel_id=1, source_target_pairs={{0,2},{2,0},{4,6},{6,4},{8,10},{10,8},{12,14},{14,12},{16,18},{18,... | collective-permute-start | bytes 2359304 | tf_op jit(solution)/shard_map/ppermute | solution.py:687
  97.0 33.1 %collective-permute-start.11 = (bf16[8,192,384]{2,1,0:T(8,128)(2,1)}, bf16[8,192,384]{2,1,0:T(8,128)(2,1)S(1)}, u32[]{:S(2)}, u32[]{:S(2)}) collective-permute-start(bf16[8,192,384]{2,1,0:T(8,128)(2,1)} %get-tuple-element.80.refs_3_), channel_id=1, source_target_pairs={{0,1},{1,0},{2,3},{3,2},{4,5},{5,4},{6,7},{7,6},{8,9},{9,8},{10,11... | collective-permute-start | bytes 3538952 | tf_op jit(solution)/shard_map/ppermute | solution.py:695
  99.1 11.8 %copy-start.2 = (f32[1,3072]{1,0:T(1,128)S(1)}, f32[1,3072]{1,0:T(1,128)}, u32[]{:S(2)}) copy-start(f32[1,3072]{1,0:T(1,128)} %get-tuple-element.87.bias_grad) | copy-start | bytes 36868
  125.9 2.9 %collective-permute-start.12 = (bf16[8,48,768]{2,1,0:T(8,128)(2,1)}, bf16[8,48,768]{2,1,0:T(8,128)(2,1)}, u32[]{:S(2)}, u32[]{:S(2)}) collective-permute-start(bf16[8,48,768]{2,1,0:T(8,128)(2,1)} %bitcast.66), channel_id=1, source_target_pairs={{0,2},{2,0},{4,6},{6,4},{8,10},{10,8},{12,14},{14,12},{16,18},{18,... | collective-permute-start | bytes 1769480 | tf_op jit(solution)/shard_map/ppermute | solution.py:687
  126.0 3.2 %collective-permute-start.13 = (bf16[8,48,768]{2,1,0:T(8,128)(2,1)}, bf16[8,48,768]{2,1,0:T(8,128)(2,1)}, u32[]{:S(2)}, u32[]{:S(2)}) collective-permute-start(bf16[8,48,768]{2,1,0:T(8,128)(2,1)} %bitcast.65), channel_id=1, source_target_pairs={{0,2},{2,0},{4,6},{6,4},{8,10},{10,8},{12,14},{14,12},{16,18},{18,... | collective-permute-start | bytes 1769480 | tf_op jit(solution)/shard_map/ppermute | solution.py:687
  126.5 3.6 %collective-permute-start.14 = (bf16[8,48,768]{2,1,0:T(8,128)(2,1)}, bf16[8,48,768]{2,1,0:T(8,128)(2,1)}, u32[]{:S(2)}, u32[]{:S(2)}) collective-permute-start(bf16[8,48,768]{2,1,0:T(8,128)(2,1)} %bitcast.64), channel_id=1, source_target_pairs={{0,2},{2,0},{4,6},{6,4},{8,10},{10,8},{12,14},{14,12},{16,18},{18,... | collective-permute-start | bytes 1769480 | tf_op jit(solution)/shard_map/ppermute | solution.py:687
  126.6 2.2 %collective-permute-start.15 = (f32[16,768]{1,0:T(8,128)}, f32[16,768]{1,0:T(8,128)S(1)}, u32[]{:S(2)}, u32[]{:S(2)}) collective-permute-start(f32[16,768]{1,0:T(8,128)} %get-tuple-element.96.refs_8_), channel_id=1, source_target_pairs={{0,2},{2,0},{4,6},{6,4},{8,10},{10,8},{12,14},{14,12},{16,18},{18,... | collective-permute-start | bytes 147464 | tf_op jit(solution)/shard_map/ppermute | solution.py:687
  135.1 22.0 %collective-permute-start.17 = (bf16[8,48,1152]{2,1,0:T(8,128)(2,1)}, bf16[8,48,1152]{2,1,0:T(8,128)(2,1)S(1)}, u32[]{:S(2)}, u32[]{:S(2)}) collective-permute-start(bf16[8,48,1152]{2,1,0:T(8,128)(2,1)} %get-tuple-element.99), channel_id=1, source_target_pairs={{0,1},{1,0},{2,3},{3,2},{4,5},{5,4},{6,7},{7,6},{8,9},{9,8},{10,11... | collective-permute-start | bytes 2654216 | tf_op jit(solution)/shard_map/ppermute | solution.py:695
  135.5 19.3 %collective-permute-start.16 = (bf16[4,192,384]{2,1,0:T(8,128)(2,1)}, bf16[4,192,384]{2,1,0:T(8,128)(2,1)S(1)}, u32[]{:S(2)}, u32[]{:S(2)}) collective-permute-start(bf16[4,192,384]{2,1,0:T(8,128)(2,1)} %get-tuple-element.97.refs_4_), channel_id=1, source_target_pairs={{0,4},{2,6},{4,0},{6,2},{8,12},{10,14},{12,8},{14,10},{16,20},{18,... | collective-permute-start | bytes 1769480 | tf_op jit(solution)/shard_map/ppermute | solution.py:687
  136.9 9.0 %collective-permute-start.18 = (f32[16,768]{1,0:T(8,128)}, f32[16,768]{1,0:T(8,128)S(1)}, u32[]{:S(2)}, u32[]{:S(2)}) collective-permute-start(f32[16,768]{1,0:T(8,128)} %get-tuple-element.101), channel_id=1, source_target_pairs={{0,8},{2,10},{4,12},{6,14},{8,0},{10,2},{12,4},{14,6},{16,24},{18,... | collective-permute-start | bytes 147464 | tf_op jit(solution)/shard_map/ppermute | solution.py:687
  138.5 42.6 %collective-permute-start.10 = (bf16[512,768]{1,0:T(8,128)(2,1)}, bf16[512,768]{1,0:T(8,128)(2,1)}, u32[]{:S(2)}, u32[]{:S(2)}) collective-permute-start(bf16[512,768]{1,0:T(8,128)(2,1)} %get-tuple-element.88), channel_id=1, source_target_pairs={{0,0},{1,2},{2,1},{3,3},{4,4},{5,6},{6,5},{7,7},{8,8},{9,10},{10,9... | collective-permute-start | bytes 2359304 | tf_op jit(solution)/shard_map/ppermute | solution.py:683
  146.7 10.3 %copy-start.9 = (f32[24,768]{1,0:T(8,128)}, f32[24,768]{1,0:T(8,128)S(1)}, u32[]{:S(2)}) copy-start(f32[24,768]{1,0:T(8,128)S(1)} %pad_maximum_fusion.3.refs_5_) | copy-start | bytes 221188
  146.7 7.8 %collective-permute-start.19 = (f32[24,768]{1,0:T(8,128)S(1)}, f32[24,768]{1,0:T(8,128)S(1)}, u32[]{:S(2)}, u32[]{:S(2)}) collective-permute-start(f32[24,768]{1,0:T(8,128)S(1)} %pad_maximum_fusion.3.refs_5_), channel_id=1, source_target_pairs={{0,16},{2,18},{4,20},{6,22},{8,24},{10,26},{12,28},{14,30},{16,0},... | collective-permute-start | bytes 221192 | tf_op jit(solution)/shard_map/ppermute | solution.py:687
  159.8 14.3 %collective-permute-start.21 = (bf16[4,48,1152]{2,1,0:T(8,128)(2,1)}, bf16[4,48,1152]{2,1,0:T(8,128)(2,1)S(1)}, u32[]{:S(2)}, u32[]{:S(2)}) collective-permute-start(bf16[4,48,1152]{2,1,0:T(8,128)(2,1)} %get-tuple-element.104), channel_id=1, source_target_pairs={{0,4},{2,6},{4,0},{6,2},{8,12},{10,14},{12,8},{14,10},{16,20},{18,... | collective-permute-start | bytes 1327112 | tf_op jit(solution)/shard_map/ppermute | solution.py:687
  161.5 12.7 %collective-permute-start.20 = (bf16[2,192,384]{2,1,0:T(8,128)(2,1)}, bf16[2,192,384]{2,1,0:T(8,128)(2,1)S(1)}, u32[]{:S(2)}, u32[]{:S(2)}) collective-permute-start(bf16[2,192,384]{2,1,0:T(8,128)(2,1)} %get-tuple-element.102.refs_4_), channel_id=1, source_target_pairs={{0,8},{2,10},{4,12},{6,14},{8,0},{10,2},{12,4},{14,6},{16,24},{18,... | collective-permute-start | bytes 884744 | tf_op jit(solution)/shard_map/ppermute | solution.py:687
  163.1 11.1 %collective-permute-start.22 = (f32[40,768]{1,0:T(8,128)}, f32[40,768]{1,0:T(8,128)S(1)}, u32[]{:S(2)}, u32[]{:S(2)}) collective-permute-start(f32[40,768]{1,0:T(8,128)} %get-tuple-element.106.refs_5_), channel_id=1, source_target_pairs={{0,4},{2,6},{4,0},{6,2},{8,12},{10,14},{12,8},{14,10},{16,20},{18,... | collective-permute-start | bytes 368648 | tf_op jit(solution)/shard_map/ppermute | solution.py:687
  164.5 21.1 %collective-permute-start.25 = (bf16[48,3840]{1,0:T(8,128)(2,1)}, bf16[48,3840]{1,0:T(8,128)(2,1)S(1)}, u32[]{:S(2)}, u32[]{:S(2)}) collective-permute-start(bf16[48,3840]{1,0:T(8,128)(2,1)} %reduce-scatter.2.cloned.1.call-done), channel_id=1, source_target_pairs={{0,1},{1,0},{2,3},{3,2},{4,5},{5,4},{6,7},{7,6},{8,9},{9,8},{10,11... | collective-permute-start | bytes 1105928 | tf_op jit(solution)/shard_map/ppermute | solution.py:695
  176.5 9.2 %collective-permute-start.24 = (bf16[2,48,1152]{2,1,0:T(8,128)(2,1)}, bf16[2,48,1152]{2,1,0:T(8,128)(2,1)S(1)}, u32[]{:S(2)}, u32[]{:S(2)}) collective-permute-start(bf16[2,48,1152]{2,1,0:T(8,128)(2,1)} %get-tuple-element.109), channel_id=1, source_target_pairs={{0,8},{2,10},{4,12},{6,14},{8,0},{10,2},{12,4},{14,6},{16,24},{18,... | collective-permute-start | bytes 663560 | tf_op jit(solution)/shard_map/ppermute | solution.py:687
  178.0 7.6 %collective-permute-start.26 = (f32[72,768]{1,0:T(8,128)}, f32[72,768]{1,0:T(8,128)S(1)}, u32[]{:S(2)}, u32[]{:S(2)}) collective-permute-start(f32[72,768]{1,0:T(8,128)} %get-tuple-element.112.refs_6_), channel_id=1, source_target_pairs={{0,1},{1,0},{2,3},{3,2},{4,5},{5,4},{6,7},{7,6},{8,9},{9,8},{10,11... | collective-permute-start | bytes 663560 | tf_op jit(solution)/shard_map/ppermute | solution.py:695
  178.5 7.2 %collective-permute-start.23 = (bf16[1,192,384]{2,1,0:T(8,128)(2,1)}, bf16[1,192,384]{2,1,0:T(8,128)(2,1)S(1)}, u32[]{:S(2)}, u32[]{:S(2)}) collective-permute-start(bf16[1,192,384]{2,1,0:T(8,128)(2,1)} %get-tuple-element.107.refs_4_), channel_id=1, source_target_pairs={{0,16},{2,18},{4,20},{6,22},{8,24},{10,26},{12,28},{14,30},{16,0},... | collective-permute-start | bytes 442376 | tf_op jit(solution)/shard_map/ppermute | solution.py:687
  187.8 3.5 %copy-start.15 = (bf16[1,48,1152]{2,1,0:T(8,128)(2,1)S(1)}, bf16[1,48,1152]{2,1,0:T(8,128)(2,1)}, u32[]{:S(2)}) copy-start(bf16[1,48,1152]{2,1,0:T(8,128)(2,1)} %get-tuple-element.114) | copy-start | bytes 331780
  188.9 5.8 %copy-start.8 = (bf16[48,3840]{1,0:T(8,128)(2,1)S(1)}, bf16[48,3840]{1,0:T(8,128)(2,1)}, u32[]{:S(2)}) copy-start(bf16[48,3840]{1,0:T(8,128)(2,1)} %reduce-scatter.2.cloned.1.call-done) | copy-start | bytes 1105924
  189.0 14.6 %collective-permute-start.29 = (bf16[1,192,384]{2,1,0:T(8,128)(2,1)}, bf16[1,192,384]{2,1,0:T(8,128)(2,1)S(1)}, u32[]{:S(2)}, u32[]{:S(2)}) collective-permute-start(bf16[1,192,384]{2,1,0:T(8,128)(2,1)} %get-tuple-element.116.refs_2_), channel_id=1, source_target_pairs={{0,1},{1,0},{2,3},{3,2},{4,5},{5,4},{6,7},{7,6},{8,9},{9,8},{10,11... | collective-permute-start | bytes 442376 | tf_op jit(solution)/shard_map/ppermute | solution.py:695
  191.3 9.5 %collective-permute-start.27 = (bf16[1,48,1152]{2,1,0:T(8,128)(2,1)S(1)}, bf16[1,48,1152]{2,1,0:T(8,128)(2,1)S(1)}, u32[]{:S(2)}, u32[]{:S(2)}) collective-permute-start(bf16[1,48,1152]{2,1,0:T(8,128)(2,1)S(1)} %copy-done.15), channel_id=1, source_target_pairs={{0,16},{2,18},{4,20},{6,22},{8,24},{10,26},{12,28},{14,30},{16,0},... | collective-permute-start | bytes 331784 | tf_op jit(solution)/shard_map/ppermute | solution.py:687
  202.4 5.0 %copy-start.7 = (bf16[1,48,1152]{2,1,0:T(8,128)(2,1)S(1)}, bf16[1,48,1152]{2,1,0:T(8,128)(2,1)}, u32[]{:S(2)}) copy-start(bf16[1,48,1152]{2,1,0:T(8,128)(2,1)} %shard_map.247) | copy-start | bytes 331780
  202.4 5.0 %collective-permute-start.28 = (bf16[1,48,1152]{2,1,0:T(8,128)(2,1)}, bf16[1,48,1152]{2,1,0:T(8,128)(2,1)S(1)}, u32[]{:S(2)}, u32[]{:S(2)}) collective-permute-start(bf16[1,48,1152]{2,1,0:T(8,128)(2,1)} %shard_map.247), channel_id=1, source_target_pairs={{0,1},{1,0},{2,3},{3,2},{4,5},{5,4},{6,7},{7,6},{8,9},{9,8},{10,11... | collective-permute-start | bytes 331784 | tf_op jit(solution)/shard_map/ppermute | solution.py:695
  207.5 1.0 copy-start.10
Sparse Core Ops, SparseCore 0:
  77.7 86.7 reduce-scatter.1

commit v3 on v2

--- a/solution.py
+++ b/solution.py
@@ -569,27 +569,60 @@
     )
 
 
-def tokens_back_body(
+def projected_back_body(
     own, core, d_query, d_keys, d_values, peer_keys, peer_values, normed, cosine, sine,
-    weight1, weight2, weight3, tokens, d_middle, mods, sums, bias_grad, *refs,
+    d_projected, *parts,
 ):
-    parts, (out, small, total) = refs[:6], refs[6:]
-    step = pl.program_id(0)
-    width = tokens.shape[1]
     lanes = HEADS * HD
     keys = d_keys[...].astype(jnp.float32) + peer_keys[...].astype(jnp.float32)
     keys = rotate_lanes(keys, cosine[...], -sine[...]).astype(jnp.bfloat16)
     values = d_values[...].astype(jnp.float32) + peer_values[...].astype(jnp.float32)
-    values = values.astype(jnp.bfloat16)
-    low = jnp.concatenate([d_query[...], keys, values], axis=1)
+    low = jnp.concatenate([d_query[...], keys, values.astype(jnp.bfloat16)], axis=1)
+    d_projected[...] = low
     grad = dot(normed[...], low, 0, 0).astype(jnp.bfloat16)
     for index in range(3):
         third = grad[:, index * lanes : (index + 1) * lanes]
         store_split(third, core, own, parts[2 * index], parts[2 * index + 1])
-    part = (
-        dot(d_query[...], weight1[...], 1, 1)
-        + dot(keys, weight2[...], 1, 1)
-        + dot(values, weight3[...], 1, 1)
+
+
+def projected_back(core, d_query, d_keys, d_values, peer_keys, peer_values, normed, cosine, sine):
+    rows, width = normed.shape
+    lanes = HEADS * HD
+    block = columns(rows, lanes)
+    return kernel_call(
+        functools.partial(projected_back_body, split_rows(width)),
+        width // lanes,
+        [
+            scalar_spec(),
+            block,
+            block,
+            block,
+            block,
+            block,
+            full((rows, width)),
+            full((rows, 128)),
+            full((rows, 128)),
+        ],
+        [columns(rows, 3 * lanes)] + [columns(width // 2, lanes)] * 6,
+        [far((rows, 3 * width), jnp.bfloat16)] + [far((width // 2, width), jnp.bfloat16)] * 6,
+        [],
+        32,
+    )(
+        core, d_query, d_keys, d_values, peer_keys, peer_values, normed, cosine, sine,
+        free=(peer_keys, peer_values),
+    )
+
+
+def tokens_back_body(
+    d_projected, weight1, weight2, weight3, tokens, d_middle, mods, sums, bias_grad, *refs
+):
+    out, small, total = refs[-3:]
+    step = pl.program_id(0)
+    width = tokens.shape[1]
+    lanes = HEADS * HD
+    part = sum(
+        dot(d_projected[:, index * lanes : (index + 1) * lanes], weight[...], 1, 1)
+        for index, weight in enumerate((weight1, weight2, weight3))
     )
 
     @pl.when(step == 0)
@@ -631,27 +664,16 @@
         small[len(rows) :, :] = jnp.zeros_like(small[len(rows) :, :])
 
 
-def tokens_back(
-    core, d_query, d_keys, d_values, peer_keys, peer_values, normed, cosine, sine, weight,
-    tokens, d_middle, mods, sums, bias_grad,
-):
-    rows, width = normed.shape
+def tokens_back(d_projected, weight, tokens, d_middle, mods, sums, bias_grad, after):
+    rows, width = tokens.shape
     lanes = HEADS * HD
     steps = width // lanes
     block = full((rows, width))
     return kernel_call(
-        functools.partial(tokens_back_body, split_rows(width)),
+        tokens_back_body,
         steps,
         [
-            scalar_spec(),
-            columns(rows, lanes),
-            columns(rows, lanes),
-            columns(rows, lanes),
-            columns(rows, lanes),
-            columns(rows, lanes),
-            block,
-            full((rows, 128)),
-            full((rows, 128)),
+            columns(rows, 3 * lanes),
             columns(width, lanes),
             columns(width, lanes, steps),
             columns(width, lanes, 2 * steps),
@@ -660,20 +682,91 @@
             full((16, width)),
             full((8, width)),
             full(bias_grad.shape),
+        ]
+        + [pl.BlockSpec(memory_space=pl.ANY)] * len(after),
+        [block, full((16, width))],
+        [far((rows, width), jnp.bfloat16), far((16, width), jnp.float32)],
+        [pltpu.VMEM((rows, width), jnp.float32)],
+        36,
+    )(d_projected, weight, weight, weight, tokens, d_middle, mods, sums, bias_grad, *after)
+
+
+def finish_body(
+    places, here, there, embedded, ada_weight,
+    first_gain, second_gain, up_bias, down_bias, ada_bias, ada_grad, cond_grad, every,
+):
+    width = here.shape[1]
+    sequences = (here.shape[0] - 8) // 8
+    own_columns = ada_grad.shape[1]
+    sums = here[8 * sequences :, :] + there[8 * sequences :, :]
+    first_gain[...] = sums[0, :]
+    second_gain[...] = sums[1, :]
+    down_bias[...] = sums[2, :]
+    for index in range(up_bias.shape[0] // width):
+        up_bias[index * width : (index + 1) * width] = sums[3 + index, :]
+    total = here[:8, :] + there[:8, :]
+    for index in range(1, sequences):
+        rows = slice(8 * index, 8 * index + 8)
+        total = total + here[rows, :] + there[rows, :]
+    conds = []
+    for side, block in enumerate((here, there)):
+        for index in range(sequences):
+            conds.append(block[8 * index + 6 : 8 * index + 7, : embedded.shape[1]])
+            for part in range(6):
+                every[
+                    side * sequences + index : side * sequences + index + 1,
+                    part * width : (part + 1) * width,
+                ] = block[8 * index + part : 8 * index + part + 1, :]
+    for part in range(6):
+        ada_bias[part * width : (part + 1) * width] = total[part, :]
+    turned = pltpu.roll(every[...], places[0], 1)[:, : -(-own_columns // 128) * 128]
+    grad = lax.dot_general(
+        jnp.concatenate(conds, axis=0),
+        turned,
+        (((0,), (0,)), ((), ())),
+        precision=highest,
+        preferred_element_type=jnp.float32,
+    )
+    ada_grad[...] = grad[:, :own_columns]
+    own = jnp.where(places[1] == 1, here[:8, :], there[:8, :])
+    products = ada_weight[:, :width].astype(jnp.float32) * own[0:1, :]
+    for part in range(1, 6):
+        columns_here = ada_weight[:, part * width : (part + 1) * width].astype(jnp.float32)
+        products = products + columns_here * own[part : part + 1, :]
+    summed = jnp.sum(products, axis=1, keepdims=True)
+    turned_sum = jnp.broadcast_to(summed, (summed.shape[0], 128)).T[0:1, :]
+    value = embedded[...]
+    sigmoid = 1.0 / (1.0 + jnp.exp(-value))
+    cond_grad[...] = turned_sum * (sigmoid * (1.0 + value * (1.0 - sigmoid)))
+
+
+def finish(here, there, embedded, ada_weight, hidden):
+    width = here.shape[1]
+    sequences = (here.shape[0] - 8) // 8
+    dp_size, dp_rank = lax.axis_size("dp"), lax.axis_index("dp")
+    all_columns = ada_weight.shape[1]
+    own_columns = all_columns // dp_size
+    turn = (all_columns - dp_rank * own_columns) % all_columns
+    same = (lax.axis_index("seq") == dp_rank % 2).astype(jnp.int32)
+    kind = jnp.float32
+    whole = pl.BlockSpec(memory_space=pltpu.VMEM)
+    return pl.pallas_call(
+        finish_body,
+        in_specs=[scalar_spec(), whole, whole, whole, whole],
+        out_specs=[whole] * 7,
+        out_shape=[
+            shaped((width,), kind),
+            shaped((width,), kind),
+            shaped((hidden,), kind),
+            shaped((width,), kind),
+            shaped((all_columns,), kind),
+            shaped((ada_weight.shape[0], own_columns), kind),
+            shaped((1, ada_weight.shape[0]), kind),
         ],
-        [columns(width // 2, lanes)] * 6 + [block, full((16, width))],
-        [far((width // 2, width), jnp.bfloat16)] * 6
-        + [
-            far((rows, width), jnp.bfloat16),
-            far((16, width), jnp.float32),
-        ],
-        [pltpu.VMEM((rows, width), jnp.float32)],
-        40,
-    )(
-        core, d_query, d_keys, d_values, peer_keys, peer_values, normed, cosine, sine,
-        weight, weight, weight, tokens, d_middle, mods, sums, bias_grad,
-        free=(peer_keys, peer_values),
-    )
+        scratch_shapes=[pltpu.VMEM((2 * sequences, all_columns), kind)],
+        compiler_params=pltpu.CompilerParams(vmem_limit_bytes=24 * 1024 * 1024),
+        cost_estimate=pl.CostEstimate(flops=1, bytes_accessed=1, transcendentals=0),
+    )(jnp.stack([turn, same]), here, there, embedded, ada_weight)
 
 
 def swap_halves(block):
@@ -785,7 +878,7 @@
             out[2 * rows :, :] = one[rows:, :] + two[rows:, :]
 
 
-def stage(steps, jobs, after=(), small=None, free=()):
+def stage(steps, jobs, after=(), small=None, free=(), relay=None):
     seq_rank, dp_rank = lax.axis_index("seq"), lax.axis_index("dp")
     inputs, in_specs, specs, out_specs, out_shape, mine = [], [], [], [], [], []
     free = [*free] + [flow.got for flows, _ in jobs for flow in flows]
@@ -832,7 +925,16 @@
         out_shape.append(far((rows, kept.shape[1]), jnp.float32))
         out_specs.append(full((rows, kept.shape[1])))
 
+    if relay is not None:
+        extra.append(relay)
+        out_shape.append(far(relay.shape, relay.dtype))
+        out_specs.append(full(relay.shape))
+
     def body(mine, *refs):
+        if relay is not None:
+            place = sum(counts) + len(extra) - 1
+            refs[-1][...] = refs[place][...]
+            refs = (*refs[:place], *refs[place + 1 : -1])
         if small is None:
             stage_body(specs, counts, mine, *refs)
             return
@@ -851,13 +953,15 @@
         out_shape,
         [],
         40,
-    )(jnp.stack(mine), *inputs, *after, *extra, free=(*free, *extra[1:]))
+    )(jnp.stack(mine), *inputs, *after, *extra, free=(*free, *extra[1:2]))
     new = []
     for (flows, step), (_, _, _, target, _) in zip(jobs, specs):
         sent = results[target]
         got = swap_seq(sent) if isinstance(step, str) else swap_bit(sent, step[0])
         new.append(Flow(got, sent if step == "sum" else results[target + 1]))
     if small is not None:
+        new.append(results[-1 if relay is None else -2])
+    if relay is not None:
         new.append(results[-1])
     return new, results[0]
 
@@ -909,9 +1013,7 @@
     rows, width = tokens.shape[1:]
     dp_rank = lax.axis_index("dp")
     core = dp_rank % 2
-    own_cond, silu_back = jax.vjp(
-        jax.nn.silu, lax.dynamic_slice_in_dim(step_table, time_index[0], 1, axis=0)
-    )
+    own_embedded = lax.dynamic_slice_in_dim(step_table, time_index[0], 1, axis=0)
     positions = core * rows + jnp.arange(rows, dtype=jnp.int32)
     cosine, sine = tables(positions)
     tokens = swap_halves(tokens[0])
@@ -960,46 +1062,52 @@
     d_query, d_keys, d_values = attend_back(
         query, own_pair, d_attended, attended, log_total, (d_query, cosine, sine), after
     )
-    *qkv_parts, tokens_grad, small = tokens_back(
-        core_ref, d_query, d_keys, d_values, peer_keys, peer_values, normed1, cosine, sine, attn_qkv, tokens,
-        d_middle, mods, sums2, up_bias_grad,
-    )
-    got = swap_cores(small)
-    def doubled(small, got):
-        return jnp.concatenate([small[:-8], got[:-8], small[-8:] + got[-8:]], axis=0)
-
+    d_projected, *qkv_parts = projected_back(
+        core_ref, d_query, d_keys, d_values, peer_keys, peer_values, normed1, cosine, sine
+    )
+    sent = ()
     if by_steps:
         late = [
             Flow(swap_cores(blocks(send)), blocks(keep))
             for keep, send in zip(qkv_parts[::2], qkv_parts[1::2])
         ]
-        moves = [functools.partial(swap_bit, bit=bit) for bit in bits[2:] + bits[1:2]]
-        moves.append(swap_seq)
-        (down, late, small), sent = stage(
-            4, [([down], (bits[1], 1)), (late, "half")], (), (got, small, True)
-        )
-
-        small = doubled(small, moves.pop(0)(small))
-
-        def next_stage(jobs, count, after=()):
+        (late,), *sent = stage(4, [(late, "half")])
+        (down,), *sent = stage(4, [([down], (bits[1], 1))], sent)
+    tokens_grad, small = tokens_back(
+        d_projected, attn_qkv, tokens, d_middle, mods, sums2, up_bias_grad, sent
+    )
+    small = small + swap_cores(small)
+    moves = [functools.partial(swap_bit, bit=bit) for bit in bits[2:] + bits[1:2]] + [swap_seq]
+
+    def doubled(small, got):
+        return jnp.concatenate([small[:-8], got[:-8], small[-8:] + got[-8:]], axis=0)
+
+    if by_steps:
+
+        def next_stage(jobs, count, moves_before, after=(), relay=None):
             nonlocal small, sent
+            for _ in range(moves_before):
+                small = doubled(small, moves.pop(0)(small))
             extra = (moves.pop(0)(small), small, False) if len(moves) > 0 else None
-            flows, sent = stage(count, jobs, (sent, *after), extra, after)
+            flows, *sent = stage(count, jobs, (*sent, *after), extra, after, relay)
             if extra is not None:
-                small = flows.pop()
+                small = flows.pop(len(jobs))
             return flows
 
-        down, late = next_stage([([down], (bits[2], 1)), ([late], (bits[1], 1))], 2)
-        down, late = next_stage([([down], (bits[3], 1)), ([late], (bits[2], 1))], 2)
-        down, late = next_stage([([down], "sum"), ([late], (bits[3], 1))], 1, (up_got,))
-        (late,) = next_stage([([late], "sum")], 1)
-        while len(moves) > 0:
-            small = doubled(small, moves.pop(0)(small))
+        down, late, tokens_grad = next_stage(
+            [([down], (bits[2], 1)), ([late], (bits[1], 1))], 2, 0, (), tokens_grad
+        )
+        down, late = next_stage([([down], (bits[3], 1)), ([late], (bits[2], 1))], 2, 0)
+        down, late = next_stage([([down], "sum"), ([late], (bits[3], 1))], 1, 0, (up_got,))
+        last = moves.pop(0)(small)
+        (late,) = next_stage([([late], "sum")], 1, 0)
+        (
+            first_gain_grad, second_gain_grad, all_up_bias_grad, down_bias_grad, ada_bias_grad,
+            ada_weight_grad, cond_grad,
+        ) = finish(small, last, own_embedded, ada_weight, hidden)
         (down_rows,) = joined(down, (width // 2,))
         qkv_rows = jnp.concatenate(joined(late, (width // 2,) * 3), axis=1)
     else:
-        small = small + got
-        moves = [functools.partial(swap_bit, bit=bit) for bit in bits[1:]] + [swap_seq]
         for move in moves:
             small = doubled(small, move(small))
         down_rows = plain_sum(down_keep, down_send, width)
@@ -1010,33 +1118,36 @@
             ],
             axis=1,
         )
+        per_sequence, sums = small[:-8].reshape(-1, 8, width), small[-8:]
+        d_mod_all = per_sequence[:, :6].reshape(per_sequence.shape[0], 6 * width)
+        cond_all = per_sequence[:, 6, : cond.shape[1]]
+        own_columns = d_mod_all.shape[1] // dp_size
+        mine = lax.dynamic_slice_in_dim(d_mod_all, dp_rank * own_columns, own_columns, axis=1)
+        ada_weight_grad = lax.dot_general(
+            cond_all, mine, (((0,), (0,)), ((), ())), precision=highest
+        )
+        other = d_mod_all.shape[0] // 2
+        d_mod_own = jnp.where(
+            lax.axis_index("seq") == core, d_mod_all[:1], d_mod_all[other : other + 1]
+        )
+        _, silu_back = jax.vjp(jax.nn.silu, own_embedded)
+        (cond_grad,) = silu_back(jnp.dot(d_mod_own, ada_float.T, precision=highest))
+        first_gain_grad, second_gain_grad, down_bias_grad = sums[0], sums[1], sums[2]
+        all_up_bias_grad = sums[3:7].reshape(-1)
+        ada_bias_grad = jnp.sum(d_mod_all, axis=0)
     up_rows = up_rows.astype(jnp.float32) + up_got.astype(jnp.float32)
-    per_sequence, sums = small[:-8].reshape(-1, 8, width), small[-8:]
-    d_mod_all = per_sequence[:, :6].reshape(per_sequence.shape[0], 6 * width)
-    cond_all = per_sequence[:, 6, : cond.shape[1]]
-    ada_bias_grad = jnp.sum(d_mod_all, axis=0)
-    own_columns = d_mod_all.shape[1] // lax.axis_size("dp")
-    mine = lax.dynamic_slice_in_dim(d_mod_all, dp_rank * own_columns, own_columns, axis=1)
-    ada_weight_grad = lax.dot_general(
-        cond_all, mine, (((0,), (0,)), ((), ())), precision=highest
-    )
-    other = d_mod_all.shape[0] // 2
-    d_mod_own = jnp.where(
-        lax.axis_index("seq") == core, d_mod_all[:1], d_mod_all[other : other + 1]
-    )
-    (cond_grad,) = silu_back(jnp.dot(d_mod_own, ada_float.T, precision=highest))
     return (
         mixed[None],
         swap_halves(tokens_grad).astype(jnp.float32)[None],
         cond_grad,
-        sums[0],
+        first_gain_grad,
         qkv_rows,
         up_rows[:, hidden:],
-        sums[1],
+        second_gain_grad,
         up_rows[:, :hidden],
-        sums[3:7].reshape(-1),
+        all_up_bias_grad,
         down_rows,
-        sums[2],
+        down_bias_grad,
         ada_weight_grad,
         ada_bias_grad,
     )

time: 217 us -> 213 us (0.982)
  Pallas kernels: 104 us -> 109 us
  local copies, waits for them, and re-layouts: 11.9 us -> 7.92 us
  starting transfers between devices: 45.2 us -> 41.5 us
  matrix products: 3.99 us -> 0.59 us
    ppermute x6, starting transfers between devices: 8.05 us -> 4.32 us  [swap_seq(): return lax.ppermute(block, 'seq', [(0, 1), (1, 0)])]
    dot_general x2 -> x0, matrix products: 3.4 us -> none  [the longest x1 2.23 us: per_device(): cond_grad, = silu_back(jnp.dot(d_mod_own, ada_float.T, precision=highest))]
    pallas_call x11 -> x13, Pallas kernels: 104 us -> 107 us  [run(): return call(*placed)]
    slice x3 -> x0, local copies, waits for them, and re-layouts: 2.23 us -> none  [the longest x1 1.48 us: per_device(): sums[2]]
  transfers between devices with their start and end apart: 31 -> 31, of which waited for: 12 -> 14; matrix products, arithmetic and copies ran while one was open for 10% -> 6% of each run, Pallas kernels for 28% -> 30%
where the time goes in v3:
time: 213 us; the launch traced here: 211 us
  Pallas kernels  109 us (51%)
  starting transfers between devices  41.5 us (19%)
  waiting for transfers between devices  26.7 us (13%)
  between operations  17.1 us (8%)
  other arithmetic  8.2 us (4%)
  local copies, waits for them, and re-layouts  7.92 us (4%)
    pallas_call x13, Pallas kernels, run(): return call(*placed)  107 us
    ppermute x19, starting transfers between devices, swap_bit(): lax.ppermute(block, 'dp', [(i, i ^ bit) for i in range(lax.axis_size('dp'...  23.3 us
    ppermute x19, waiting for transfers between devices, swap_bit(): lax.ppermute(block, 'dp', [(i, i ^ bit) for i in range(lax.axis_size('dp'...  20.3 us
    ppermute x5, starting transfers between devices, swap_halves(): return lax.ppermute(block, ('dp', 'seq'), perm)  13.8 us
    ppermute x6, waiting for transfers between devices, swap_seq(): return lax.ppermute(block, 'seq', [(0, 1), (1, 0)])  6.33 us
    ppermute x6, starting transfers between devices, swap_seq(): return lax.ppermute(block, 'seq', [(0, 1), (1, 0)])  4.32 us
  transfers between devices with their start and end apart: 31, of which 14 were waited for; matrix products, arithmetic and copies ran while one was open for 6% of the time, Pallas kernels for 30%

profile of v3, /device:TPU:0, one launch (start us, length us, event | category | flops | bytes accessed | tf_op | source)
XLA Modules:
  0.0 211.1 jit_solution(6492307728224758219)
XLA Ops:
  7.2 2.0 collective-permute-start.1
  9.3 1.8 collective-permute-start
  11.0 1.8 collective-permute-start.5
  13.5 0.7 reshape.91
  14.2 0.7 reshape.92
  14.9 1.0 fusion.4
  15.9 1.3 pad_maximum_fusion.1
  19.2 0.8 constant_dynamic-slice_fusion
  20.0 0.6 convolution_reduce_fusion
  20.7 1.3 concatenate.15.mods
  21.9 6.8 %shard_map.237 = (bf16[512,768]{1,0:T(8,128)(2,1)}, bf16[512,1536]{1,0:T(8,128)(2,1)}, bf16[512,512]{1,0:T(8,128)(2,1)}, bf16[512,512]{1,0:T(8,128)(2,1)}, bf16[512,512]{1,0:T(8,128)(2,1)}) custom-call(bf16[512,768]{1,0:T(8,128)(2,1)S(1)} %collective-permute-done.tokens.refs_6_, f32[16,768]{1,0:T(8,128)} %concatenate.15.mods, bf16[768,2304]{1,0:T(8,128)(2,1)} %weight3.1, ...), custom_call_target="tpu_custom_call" | custom-call | flops 1 | bytes 1 | tf_op jit(solution)/shard_map/pallas_call | solution.py:97
  28.7 5.1 %collective-permute-start.2 = (bf16[512,512]{1,0:T(8,128)(2,1)}, bf16[512,512]{1,0:T(8,128)(2,1)S(1)}, u32[]{:S(2)}, u32[]{:S(2)}) collective-permute-start(bf16[512,512]{1,0:T(8,128)(2,1)} %get-tuple-element.74.refs_0_), channel_id=1, source_target_pairs={{0,2},{2,0},{4,6},{6,4},{8,10},{10,8},{12,14},{14,12},{16,18},{18,... | collective-permute-start | bytes 1572872 | tf_op jit(solution)/shard_map/ppermute | solution.py:780
  34.3 0.6 broadcast_in_dim.55
  34.9 0.6 reshape.94.down_bias
  35.6 0.7 collective-permute-done.3.refs_4_
  36.3 0.7 collective-permute-done.4.refs_5_
  37.1 0.8 copy-done.8
  37.9 41.0 %shard_map.238 = (bf16[512,768]{1,0:T(8,128)(2,1)}, bf16[512,768]{1,0:T(8,128)(2,1)}, f32[3,4,512]{2,1,0:T(4,128)}, bf16[512,768]{1,0:T(8,128)(2,1)}, f32[512,76...) custom-call(s32[1]{0:T(128)} %bitcast.core, ...), custom_call_target="tpu_custom_call" | custom-call | flops 1 | bytes 1 | tf_op jit(solution)/shard_map/pallas_call | solution.py:97
  78.9 0.5 collective-permute-start.7
  79.4 0.6 copy-done.16
  80.0 0.7 collective-permute-start.6
  80.8 11.3 %shard_map.239 = (f32[512,768]{1,0:T(8,128)}, bf16[512,768]{1,0:T(8,128)(2,1)}, bf16[512,768]{1,0:T(8,128)(2,1)}) custom-call(bf16[512,768]{1,0:T(8,128)(2,1)} %get-tuple-element.80.query, bf16[512,1536]{1,0:T(8,128)(2,1)} %get-tuple-element.81.pair, bf16[512,768]{1,0:T(8,128)(2,1)} %get-tuple-element.82.grad, bf16[512,768]{1,0:T(8,128)(2,1)} %get-tuple-element.83.attended, ...), custom_call_target="tpu_custom_call" | custom-call | flops 1 | bytes 1 | tf_op jit(solution)/shard_map/pallas_call | solution.py:97
  92.0 1.6 collective-permute-start.10
  93.7 4.6 %shard_map.240 = (bf16[8,192,384]{2,1,0:T(8,128)(2,1)}, bf16[8,192,384]{2,1,0:T(8,128)(2,1)}) custom-call(s32[1]{0:T(128)} %bitcast.10.mine, bf16[8,192,768]{2,1,0:T(8,128)(2,1)} %collective-permute-done.7.refs_0_, bf16[8,192,768]{2,1,0:T(8,128)(2,1)} %bitcast.41, bf16[512,768]{1,0:T(8,128)(2,1)} %get-tuple-element.85.refs_2_, ...), custom_call_target="tpu_custom_call" | custom-call | flops 1 | bytes 1 | tf_op jit(solution)/shard_map/pallas_call | solution.py:97
  98.3 2.1 collective-permute-start.8
  100.4 11.8 %shard_map.241 = (bf16[512,768]{1,0:T(8,128)(2,1)}, bf16[512,768]{1,0:T(8,128)(2,1)}, bf16[512,768]{1,0:T(8,128)(2,1)}) custom-call(bf16[512,768]{1,0:T(8,128)(2,1)} %get-tuple-element.80.query, bf16[512,1536]{1,0:T(8,128)(2,1)} %get-tuple-element.88.pair, bf16[512,768]{1,0:T(8,128)(2,1)} %get-tuple-element.82.grad, ...), custom_call_target="tpu_custom_call" | custom-call | flops 1 | bytes 1 | tf_op jit(solution)/shard_map/pallas_call | solution.py:97
  112.2 7.4 %shard_map.242 = (bf16[512,2304]{1,0:T(8,128)(2,1)}, bf16[384,768]{1,0:T(8,128)(2,1)}, bf16[384,768]{1,0:T(8,128)(2,1)}, bf16[384,768]{1,0:T(8,128)(2,1)}, bf16[...) custom-call(s32[1]{0:T(128)} %bitcast.core, bf16[512,768]{1,0:T(8,128)(2,1)} %get-tuple-element.90.d_query, ...), custom_call_target="tpu_custom_call" | custom-call | flops 1 | bytes 1 | tf_op jit(solution)/shard_map/pallas_call | solution.py:97
  119.6 0.5 collective-permute-start.12
  120.2 1.6 collective-permute-done.11.refs_0_
  121.8 0.8 collective-permute-done.12.refs_2_
  122.7 0.8 collective-permute-done.13.refs_4_
  123.5 3.9 %shard_map.243 = (bf16[8,48,1152]{2,1,0:T(8,128)(2,1)}, bf16[8,48,1152]{2,1,0:T(8,128)(2,1)}) custom-call(s32[1]{0:T(128)} %bitcast.10.mine, bf16[8,48,768]{2,1,0:T(8,128)(2,1)S(1)} %collective-permute-done.11.refs_0_, bf16[8,48,768]{2,1,0:T(8,128)(2,1)} %bitcast.42, bf16[8,48,768]{2,1,0:T(8,128)(2,1)S(1)} %collective-permute-done.12.refs_2_, ...), custom_call_target="tpu_custom_call" | custom-call | flops 1 | bytes 1 | tf_op jit(solution)/shard_map/pallas_call | solution.py:97
  127.7 3.6 %shard_map.244 = (bf16[4,192,384]{2,1,0:T(8,128)(2,1)}, bf16[4,192,384]{2,1,0:T(8,128)(2,1)}) custom-call(s32[1]{0:T(128)} %bitcast.9.mine, bf16[8,192,384]{2,1,0:T(8,128)(2,1)S(1)} %collective-permute-done.8.refs_0_, bf16[8,192,384]{2,1,0:T(8,128)(2,1)} %get-tuple-element.87.refs_1_, bf16[8,48,1152]{2,1,0:T(8,128)(2,1)} %get-tuple-element.100.refs_2_), custom_call_target="tpu_custom_call" | custom-call | flops 1 | bytes 1 | tf_op jit(solution)/shard_map/pallas_call | solution.py:97
  131.3 1.5 collective-permute-start.14
  132.8 7.8 %shard_map.245 = (bf16[512,768]{1,0:T(8,128)(2,1)}, f32[16,768]{1,0:T(8,128)}) custom-call(bf16[512,2304]{1,0:T(8,128)(2,1)} %get-tuple-element.104.d_projected, bf16[768,2304]{1,0:T(8,128)(2,1)} %weight3.1, bf16[768,2304]{1,0:T(8,128)(2,1)} %weight3.1, bf16[768,2304]{1,0:T(8,128)(2,1)} %weight3.1, bf16[512,768]{1,0:T(8,128)(2,1)} %copy-done, ...), custom_call_target="tpu_custom_call" | custom-call | flops 1 | bytes 1 | tf_op jit(solution)/shard_map/pallas_call | solution.py:97
  140.7 1.4 collective-permute-done.16
  142.1 0.8 add.65.refs_5_
  142.9 1.6 collective-permute-start.17
  144.6 2.5 %collective-permute-done.17.refs_6_ = f32[16,768]{1,0:T(8,128)S(1)} collective-permute-done((f32[16,768]{1,0:T(8,128)S(1)}, f32[16,768]{1,0:T(8,128)S(1)}, u32[]{:S(2)}, u32[]{:S(2)}) %collective-permute-start.17) | collective-permute-done | bytes 49184 | tf_op jit(solution)/shard_map/ppermute | solution.py:780
  147.0 2.4 %collective-permute-done.15.refs_2_ = bf16[8,48,1152]{2,1,0:T(8,128)(2,1)} collective-permute-done((bf16[8,48,1152]{2,1,0:T(8,128)(2,1)}, bf16[8,48,1152]{2,1,0:T(8,128)(2,1)}, u32[]{:S(2)}, u32[]{:S(2)}) %collective-permute-start.15) | collective-permute-done | bytes 884768 | tf_op jit(solution)/shard_map/ppermute | solution.py:788
  149.4 3.4 %shard_map.246 = (bf16[2,192,384]{2,1,0:T(8,128)(2,1)}, bf16[2,192,384]{2,1,0:T(8,128)(2,1)}, bf16[4,48,1152]{2,1,0:T(8,128)(2,1)}, bf16[4,48,1152]{2,1,0:T(8,12...) custom-call(s32[2]{0:T(128)S(1)} %pad_add_fusion.mine, bf16[4,192,384]{2,1,0:T(8,128)(2,1)S(1)} %collective-permute-done.14.refs_0_, ...), custom_call_target="tpu_custom_call" | custom-call | flops 1 | bytes 1 | tf_op jit(solution)/shard_map/pallas_call | solution.py:97
  152.8 7.5 %collective-permute-start.18 = (bf16[512,768]{1,0:T(8,128)(2,1)}, bf16[512,768]{1,0:T(8,128)(2,1)}, u32[]{:S(2)}, u32[]{:S(2)}) collective-permute-start(bf16[512,768]{1,0:T(8,128)(2,1)} %get-tuple-element.110), channel_id=1, source_target_pairs={{0,0},{1,2},{2,1},{3,3},{4,4},{5,6},{6,5},{7,7},{8,8},{9,10},{10,9... | collective-permute-start | bytes 2359304 | tf_op jit(solution)/shard_map/ppermute | solution.py:776
  160.3 1.5 collective-permute-start.20
  161.8 1.6 collective-permute-start.19
  163.5 2.6 %collective-permute-start.21 = (f32[24,768]{1,0:T(8,128)}, f32[24,768]{1,0:T(8,128)S(1)}, u32[]{:S(2)}, u32[]{:S(2)}) collective-permute-start(f32[24,768]{1,0:T(8,128)} %get-tuple-element.115.refs_5_), channel_id=1, source_target_pairs={{0,16},{2,18},{4,20},{6,22},{8,24},{10,26},{12,28},{14,30},{16,0},... | collective-permute-start | bytes 221192 | tf_op jit(solution)/shard_map/ppermute | solution.py:780
  166.2 2.9 %collective-permute-done.21.refs_6_ = f32[24,768]{1,0:T(8,128)S(1)} collective-permute-done((f32[24,768]{1,0:T(8,128)}, f32[24,768]{1,0:T(8,128)S(1)}, u32[]{:S(2)}, u32[]{:S(2)}) %collective-permute-start.21) | collective-permute-done | bytes 73760 | tf_op jit(solution)/shard_map/ppermute | solution.py:780
  169.6 2.3 %shard_map.247 = (bf16[1,192,384]{2,1,0:T(8,128)(2,1)}, bf16[1,192,384]{2,1,0:T(8,128)(2,1)}, bf16[2,48,1152]{2,1,0:T(8,128)(2,1)}, bf16[2,48,1152]{2,1,0:T(8,128)(2,1)}, f32[40,768]{1,0:T(8,128)}) custom-call(s32[2]{0:T(128)S(1)} %pad_add_fusion.3.mine, bf16[2,192,384]{2,1,0:T(8,128)(2,1)S(1)} %collective-permute-done.19.refs_0_, ...), custom_call_target="tpu_custom_call" | custom-call | flops 1 | bytes 1 | tf_op jit(solution)/shard_map/pallas_call | solution.py:97
  171.8 2.8 %collective-permute-start.23 = (bf16[2,48,1152]{2,1,0:T(8,128)(2,1)}, bf16[2,48,1152]{2,1,0:T(8,128)(2,1)S(1)}, u32[]{:S(2)}, u32[]{:S(2)}) collective-permute-start(bf16[2,48,1152]{2,1,0:T(8,128)(2,1)} %get-tuple-element.118), channel_id=1, source_target_pairs={{0,8},{2,10},{4,12},{6,14},{8,0},{10,2},{12,4},{14,6},{16,24},{18,... | collective-permute-start | bytes 663560 | tf_op jit(solution)/shard_map/ppermute | solution.py:780
  174.7 2.1 %collective-permute-start.22 = (bf16[1,192,384]{2,1,0:T(8,128)(2,1)}, bf16[1,192,384]{2,1,0:T(8,128)(2,1)S(1)}, u32[]{:S(2)}, u32[]{:S(2)}) collective-permute-start(bf16[1,192,384]{2,1,0:T(8,128)(2,1)} %get-tuple-element.116.refs_4_), channel_id=1, source_target_pairs={{0,16},{2,18},{4,20},{6,22},{8,24},{10,26},{12,28},{14,30},{16,0},... | collective-permute-start | bytes 442376 | tf_op jit(solution)/shard_map/ppermute | solution.py:780
  176.8 2.4 %bitcast_convert_fusion = f32[1,512,768]{2,1,0:T(8,128)} fusion(bf16[512,768]{1,0:T(8,128)(2,1)} %collective-permute-done.18), kind=kLoop, calls=%fused_computation.1 | loop fusion | flops 393216 | bytes 2359296 | tf_op jit(solution)/shard_map/broadcast_in_dim | solution.py:1141
  179.2 2.6 %collective-permute-done.25.refs_7_ = f32[40,768]{1,0:T(8,128)S(1)} collective-permute-done((f32[40,768]{1,0:T(8,128)}, f32[40,768]{1,0:T(8,128)S(1)}, u32[]{:S(2)}, u32[]{:S(2)}) %collective-permute-start.25) | collective-permute-done | bytes 122912 | tf_op jit(solution)/shard_map/ppermute | solution.py:780
  181.9 0.6 collective-permute-done.22.refs_0_
  182.5 2.0 shard_map.248
  184.5 1.4 collective-permute-start.29
  186.0 1.2 collective-permute-start.27
  187.3 0.9 slice.39
  188.1 0.7 slice.38
  189.0 5.0 %collective-permute-done.27.refs_0_ = bf16[1,48,1152]{2,1,0:T(8,128)(2,1)S(1)} collective-permute-done((bf16[1,48,1152]{2,1,0:T(8,128)(2,1)}, bf16[1,48,1152]{2,1,0:T(8,128)(2,1)S(1)}, u32[]{:S(2)}, u32[]{:S(2)}) %collective-permute-start.27) | collective-permute-done | bytes 110624 | tf_op jit(solution)/shard_map/ppermute | solution.py:780
  193.9 1.6 shard_map.250
  195.9 0.9 pad_maximum_fusion
  196.7 4.0 %collective-permute-done.28 = bf16[1,48,1152]{2,1,0:T(8,128)(2,1)S(1)} collective-permute-done((bf16[1,48,1152]{2,1,0:T(8,128)(2,1)}, bf16[1,48,1152]{2,1,0:T(8,128)(2,1)S(1)}, u32[]{:S(2)}, u32[]{:S(2)}) %collective-permute-start.28) | collective-permute-done | bytes 110624 | tf_op jit(solution)/shard_map/ppermute | solution.py:788
  200.8 1.7 shard_map.249
  202.6 0.8 copy.29
  203.3 0.9 copy.37
  (82 shorter events, 2.7 us)
Async XLA Ops:
  7.2 12.8 %copy-start.1 = (bf16[128,4608]{1,0:T(8,128)(2,1)S(1)}, bf16[128,4608]{1,0:T(8,128)(2,1)}, u32[]{:S(2)}) copy-start(bf16[128,4608]{1,0:T(8,128)(2,1)} %ada_weight.1) | copy-start | bytes 3538948
  7.2 158.9 %reduce-scatter.2.cloned.1.call-start = ((), (), s32[]{:S(2)}) async-start(), calls=%async_computation.1 | async-start | bytes 6266880 | tf_op jit(solution)/shard_map/reduce_scatter | solution.py:1048
  7.2 9.9 %collective-permute-start.1 = (s32[1]{0:T(128)}, s32[1]{0:T(128)}, u32[]{:S(2)}, u32[]{:S(2)}) collective-permute-start(s32[1]{0:T(128)} %param.16), channel_id=1, source_target_pairs={{0,0},{1,2},{2,1},{3,3},{4,4},{5,6},{6,5},{7,7},{8,8},{9,10},{10,9... | collective-permute-start | bytes 20 | tf_op jit(solution)/shard_map/ppermute | solution.py:776
  9.3 12.7 %collective-permute-start = (bf16[512,768]{1,0:T(8,128)(2,1)}, bf16[512,768]{1,0:T(8,128)(2,1)S(1)}, u32[]{:S(2)}, u32[]{:S(2)}) collective-permute-start(bf16[512,768]{1,0:T(8,128)(2,1)} %bitcast.47), channel_id=1, source_target_pairs={{0,0},{1,2},{2,1},{3,3},{4,4},{5,6},{6,5},{7,7},{8,8},{9,10},{10,9... | collective-permute-start | bytes 2359304 | tf_op jit(solution)/shard_map/ppermute | solution.py:776
  11.0 24.5 %collective-permute-start.5 = (bf16[512,768]{1,0:T(8,128)(2,1)}, bf16[512,768]{1,0:T(8,128)(2,1)S(1)}, u32[]{:S(2)}, u32[]{:S(2)}) collective-permute-start(bf16[512,768]{1,0:T(8,128)(2,1)} %bitcast.48), channel_id=1, source_target_pairs={{0,0},{1,2},{2,1},{3,3},{4,4},{5,6},{6,5},{7,7},{8,8},{9,10},{10,9... | collective-permute-start | bytes 2359304 | tf_op jit(solution)/shard_map/ppermute | solution.py:776
  14.9 5.7 %copy-start.13 = (bf16[4608]{0:T(1024)(128)(2,1)S(1)}, bf16[4608]{0:T(1024)(128)(2,1)}, u32[]{:S(2)}) copy-start(bf16[4608]{0:T(1024)(128)(2,1)} %param.27) | copy-start | bytes 27652
  21.9 6.8 %copy-start = (bf16[512,768]{1,0:T(8,128)(2,1)}, bf16[512,768]{1,0:T(8,128)(2,1)S(1)}, u32[]{:S(2)}) copy-start(bf16[512,768]{1,0:T(8,128)(2,1)S(1)} %collective-permute-done.tokens.refs_6_) | copy-start | bytes 2359300
  21.9 12.4 %copy-start.14 = (bf16[3072]{0:T(1024)(128)(2,1)S(1)}, bf16[3072]{0:T(1024)(128)(2,1)}, u32[]{:S(2)}) copy-start(bf16[3072]{0:T(1024)(128)(2,1)} %param.23) | copy-start | bytes 18436
  21.9 13.0 %copy-start.15 = (bf16[768]{0:T(1024)(128)(2,1)S(1)}, bf16[768]{0:T(1024)(128)(2,1)}, u32[]{:S(2)}) copy-start(bf16[768]{0:T(1024)(128)(2,1)} %param.25) | copy-start | bytes 4612
  28.7 6.9 %collective-permute-start.2 = (bf16[512,512]{1,0:T(8,128)(2,1)}, bf16[512,512]{1,0:T(8,128)(2,1)S(1)}, u32[]{:S(2)}, u32[]{:S(2)}) collective-permute-start(bf16[512,512]{1,0:T(8,128)(2,1)} %get-tuple-element.74.refs_0_), channel_id=1, source_target_pairs={{0,2},{2,0},{4,6},{6,4},{8,10},{10,8},{12,14},{14,12},{16,18},{18,... | collective-permute-start | bytes 1572872 | tf_op jit(solution)/shard_map/ppermute | solution.py:780
  33.8 2.5 %collective-permute-start.3 = (bf16[512,512]{1,0:T(8,128)(2,1)}, bf16[512,512]{1,0:T(8,128)(2,1)S(1)}, u32[]{:S(2)}, u32[]{:S(2)}) collective-permute-start(bf16[512,512]{1,0:T(8,128)(2,1)} %get-tuple-element.75.refs_1_), channel_id=1, source_target_pairs={{0,2},{2,0},{4,6},{6,4},{8,10},{10,8},{12,14},{14,12},{16,18},{18,... | collective-permute-start | bytes 1572872 | tf_op jit(solution)/shard_map/ppermute | solution.py:780
  33.9 3.2 %collective-permute-start.4 = (bf16[512,512]{1,0:T(8,128)(2,1)}, bf16[512,512]{1,0:T(8,128)(2,1)S(1)}, u32[]{:S(2)}, u32[]{:S(2)}) collective-permute-start(bf16[512,512]{1,0:T(8,128)(2,1)} %get-tuple-element.76.refs_2_), channel_id=1, source_target_pairs={{0,2},{2,0},{4,6},{6,4},{8,10},{10,8},{12,14},{14,12},{16,18},{18,... | collective-permute-start | bytes 1572872 | tf_op jit(solution)/shard_map/ppermute | solution.py:780
  35.5 1.5 copy-start.4
  35.6 1.5 copy-start.6
  36.3 0.8 copy-start.7
  37.1 0.8 copy-start.8
  78.9 1.1 copy-start.16
  78.9 14.7 %collective-permute-start.7 = (bf16[8,192,768]{2,1,0:T(8,128)(2,1)}, bf16[8,192,768]{2,1,0:T(8,128)(2,1)}, u32[]{:S(2)}, u32[]{:S(2)}) collective-permute-start(bf16[8,192,768]{2,1,0:T(8,128)(2,1)} %bitcast.46), channel_id=1, source_target_pairs={{0,2},{2,0},{4,6},{6,4},{8,10},{10,8},{12,14},{14,12},{16,18},{18,... | collective-permute-start | bytes 7077896 | tf_op jit(solution)/shard_map/ppermute | solution.py:780
  80.0 13.6 %collective-permute-start.6 = (bf16[512,768]{1,0:T(8,128)(2,1)S(1)}, bf16[512,768]{1,0:T(8,128)(2,1)S(1)}, u32[]{:S(2)}, u32[]{:S(2)}) collective-permute-start(bf16[512,768]{1,0:T(8,128)(2,1)S(1)} %copy-done.16), channel_id=1, source_target_pairs={{0,0},{1,2},{2,1},{3,3},{4,4},{5,6},{6,5},{7,7},{8,8},{9,10},{10,9... | collective-permute-start | bytes 2359304 | tf_op jit(solution)/shard_map/ppermute | solution.py:776
  92.0 20.1 %collective-permute-start.10 = (bf16[512,768]{1,0:T(8,128)(2,1)}, bf16[512,768]{1,0:T(8,128)(2,1)}, u32[]{:S(2)}, u32[]{:S(2)}) collective-permute-start(bf16[512,768]{1,0:T(8,128)(2,1)} %get-tuple-element.93), channel_id=1, source_target_pairs={{0,2},{2,0},{4,6},{6,4},{8,10},{10,8},{12,14},{14,12},{16,18},{18,... | collective-permute-start | bytes 2359304 | tf_op jit(solution)/shard_map/ppermute | solution.py:780
  93.6 18.5 %collective-permute-start.9 = (bf16[512,768]{1,0:T(8,128)(2,1)}, bf16[512,768]{1,0:T(8,128)(2,1)}, u32[]{:S(2)}, u32[]{:S(2)}) collective-permute-start(bf16[512,768]{1,0:T(8,128)(2,1)} %get-tuple-element.85.refs_2_), channel_id=1, source_target_pairs={{0,2},{2,0},{4,6},{6,4},{8,10},{10,8},{12,14},{14,12},{16,18},{18,... | collective-permute-start | bytes 2359304 | tf_op jit(solution)/shard_map/ppermute | solution.py:780
  98.3 29.4 %collective-permute-start.8 = (bf16[8,192,384]{2,1,0:T(8,128)(2,1)}, bf16[8,192,384]{2,1,0:T(8,128)(2,1)S(1)}, u32[]{:S(2)}, u32[]{:S(2)}) collective-permute-start(bf16[8,192,384]{2,1,0:T(8,128)(2,1)} %get-tuple-element.86.refs_3_), channel_id=1, source_target_pairs={{0,1},{1,0},{2,3},{3,2},{4,5},{5,4},{6,7},{7,6},{8,9},{9,8},{10,11... | collective-permute-start | bytes 3538952 | tf_op jit(solution)/shard_map/ppermute | solution.py:788
  119.6 2.3 %collective-permute-start.11 = (bf16[8,48,768]{2,1,0:T(8,128)(2,1)}, bf16[8,48,768]{2,1,0:T(8,128)(2,1)S(1)}, u32[]{:S(2)}, u32[]{:S(2)}) collective-permute-start(bf16[8,48,768]{2,1,0:T(8,128)(2,1)} %bitcast.51), channel_id=1, source_target_pairs={{0,2},{2,0},{4,6},{6,4},{8,10},{10,8},{12,14},{14,12},{16,18},{18,... | collective-permute-start | bytes 1769480 | tf_op jit(solution)/shard_map/ppermute | solution.py:780
  119.6 3.0 %collective-permute-start.12 = (bf16[8,48,768]{2,1,0:T(8,128)(2,1)}, bf16[8,48,768]{2,1,0:T(8,128)(2,1)S(1)}, u32[]{:S(2)}, u32[]{:S(2)}) collective-permute-start(bf16[8,48,768]{2,1,0:T(8,128)(2,1)} %bitcast.50), channel_id=1, source_target_pairs={{0,2},{2,0},{4,6},{6,4},{8,10},{10,8},{12,14},{14,12},{16,18},{18,... | collective-permute-start | bytes 1769480 | tf_op jit(solution)/shard_map/ppermute | solution.py:780
  120.1 3.4 %collective-permute-start.13 = (bf16[8,48,768]{2,1,0:T(8,128)(2,1)}, bf16[8,48,768]{2,1,0:T(8,128)(2,1)S(1)}, u32[]{:S(2)}, u32[]{:S(2)}) collective-permute-start(bf16[8,48,768]{2,1,0:T(8,128)(2,1)} %bitcast.49), channel_id=1, source_target_pairs={{0,2},{2,0},{4,6},{6,4},{8,10},{10,8},{12,14},{14,12},{16,18},{18,... | collective-permute-start | bytes 1769480 | tf_op jit(solution)/shard_map/ppermute | solution.py:780
  127.4 22.0 %collective-permute-start.15 = (bf16[8,48,1152]{2,1,0:T(8,128)(2,1)}, bf16[8,48,1152]{2,1,0:T(8,128)(2,1)}, u32[]{:S(2)}, u32[]{:S(2)}) collective-permute-start(bf16[8,48,1152]{2,1,0:T(8,128)(2,1)} %get-tuple-element.100.refs_2_), channel_id=1, source_target_pairs={{0,1},{1,0},{2,3},{3,2},{4,5},{5,4},{6,7},{7,6},{8,9},{9,8},{10,11... | collective-permute-start | bytes 2654216 | tf_op jit(solution)/shard_map/ppermute | solution.py:788
  127.7 5.1 %copy-start.3 = (f32[1,3072]{1,0:T(1,128)S(1)}, f32[1,3072]{1,0:T(1,128)}, u32[]{:S(2)}) copy-start(f32[1,3072]{1,0:T(1,128)} %get-tuple-element.107.bias_grad) | copy-start | bytes 36868
  131.3 18.1 %collective-permute-start.14 = (bf16[4,192,384]{2,1,0:T(8,128)(2,1)}, bf16[4,192,384]{2,1,0:T(8,128)(2,1)S(1)}, u32[]{:S(2)}, u32[]{:S(2)}) collective-permute-start(bf16[4,192,384]{2,1,0:T(8,128)(2,1)} %get-tuple-element.101.refs_0_.refs_4_), channel_id=1, source_target_pairs={{0,4},{2,6},{4,0},{6,2},{8,12},{10,14},{12,8},{14,10},{16,20},{18,... | collective-permute-start | bytes 1769480 | tf_op jit(solution)/shard_map/ppermute | solution.py:780
  140.6 1.4 collective-permute-start.16
  142.9 6.5 %copy-start.11 = (f32[16,768]{1,0:T(8,128)}, f32[16,768]{1,0:T(8,128)S(1)}, u32[]{:S(2)}) copy-start(f32[16,768]{1,0:T(8,128)S(1)} %add.65.refs_5_) | copy-start | bytes 147460
  142.9 4.1 %collective-permute-start.17 = (f32[16,768]{1,0:T(8,128)S(1)}, f32[16,768]{1,0:T(8,128)S(1)}, u32[]{:S(2)}, u32[]{:S(2)}) collective-permute-start(f32[16,768]{1,0:T(8,128)S(1)} %add.65.refs_5_), channel_id=1, source_target_pairs={{0,8},{2,10},{4,12},{6,14},{8,0},{10,2},{12,4},{14,6},{16,24},{18,... | collective-permute-start | bytes 147464 | tf_op jit(solution)/shard_map/ppermute | solution.py:780
  152.8 24.0 %collective-permute-start.18 = (bf16[512,768]{1,0:T(8,128)(2,1)}, bf16[512,768]{1,0:T(8,128)(2,1)}, u32[]{:S(2)}, u32[]{:S(2)}) collective-permute-start(bf16[512,768]{1,0:T(8,128)(2,1)} %get-tuple-element.110), channel_id=1, source_target_pairs={{0,0},{1,2},{2,1},{3,3},{4,4},{5,6},{6,5},{7,7},{8,8},{9,10},{10,9... | collective-permute-start | bytes 2359304 | tf_op jit(solution)/shard_map/ppermute | solution.py:776
  160.3 9.2 %collective-permute-start.20 = (bf16[4,48,1152]{2,1,0:T(8,128)(2,1)}, bf16[4,48,1152]{2,1,0:T(8,128)(2,1)S(1)}, u32[]{:S(2)}, u32[]{:S(2)}) collective-permute-start(bf16[4,48,1152]{2,1,0:T(8,128)(2,1)} %get-tuple-element.113), channel_id=1, source_target_pairs={{0,4},{2,6},{4,0},{6,2},{8,12},{10,14},{12,8},{14,10},{16,20},{18,... | collective-permute-start | bytes 1327112 | tf_op jit(solution)/shard_map/ppermute | solution.py:780
  161.8 7.7 %collective-permute-start.19 = (bf16[2,192,384]{2,1,0:T(8,128)(2,1)}, bf16[2,192,384]{2,1,0:T(8,128)(2,1)S(1)}, u32[]{:S(2)}, u32[]{:S(2)}) collective-permute-start(bf16[2,192,384]{2,1,0:T(8,128)(2,1)} %get-tuple-element.111.refs_4_), channel_id=1, source_target_pairs={{0,8},{2,10},{4,12},{6,14},{8,0},{10,2},{12,4},{14,6},{16,24},{18,... | collective-permute-start | bytes 884744 | tf_op jit(solution)/shard_map/ppermute | solution.py:780
  163.5 5.6 %collective-permute-start.21 = (f32[24,768]{1,0:T(8,128)}, f32[24,768]{1,0:T(8,128)S(1)}, u32[]{:S(2)}, u32[]{:S(2)}) collective-permute-start(f32[24,768]{1,0:T(8,128)} %get-tuple-element.115.refs_5_), channel_id=1, source_target_pairs={{0,16},{2,18},{4,20},{6,22},{8,24},{10,26},{12,28},{14,30},{16,0},... | collective-permute-start | bytes 221192 | tf_op jit(solution)/shard_map/ppermute | solution.py:780
  166.1 16.4 %collective-permute-start.24 = (bf16[48,3840]{1,0:T(8,128)(2,1)}, bf16[48,3840]{1,0:T(8,128)(2,1)S(1)}, u32[]{:S(2)}, u32[]{:S(2)}) collective-permute-start(bf16[48,3840]{1,0:T(8,128)(2,1)} %reduce-scatter.2.cloned.1.call-done), channel_id=1, source_target_pairs={{0,1},{1,0},{2,3},{3,2},{4,5},{5,4},{6,7},{7,6},{8,9},{9,8},{10,11... | collective-permute-start | bytes 1105928 | tf_op jit(solution)/shard_map/ppermute | solution.py:788
  171.8 10.7 %collective-permute-start.23 = (bf16[2,48,1152]{2,1,0:T(8,128)(2,1)}, bf16[2,48,1152]{2,1,0:T(8,128)(2,1)S(1)}, u32[]{:S(2)}, u32[]{:S(2)}) collective-permute-start(bf16[2,48,1152]{2,1,0:T(8,128)(2,1)} %get-tuple-element.118), channel_id=1, source_target_pairs={{0,8},{2,10},{4,12},{6,14},{8,0},{10,2},{12,4},{14,6},{16,24},{18,... | collective-permute-start | bytes 663560 | tf_op jit(solution)/shard_map/ppermute | solution.py:780
  174.7 7.8 %collective-permute-start.22 = (bf16[1,192,384]{2,1,0:T(8,128)(2,1)}, bf16[1,192,384]{2,1,0:T(8,128)(2,1)S(1)}, u32[]{:S(2)}, u32[]{:S(2)}) collective-permute-start(bf16[1,192,384]{2,1,0:T(8,128)(2,1)} %get-tuple-element.116.refs_4_), channel_id=1, source_target_pairs={{0,16},{2,18},{4,20},{6,22},{8,24},{10,26},{12,28},{14,30},{16,0},... | collective-permute-start | bytes 442376 | tf_op jit(solution)/shard_map/ppermute | solution.py:780
  176.8 10.4 %copy-start.10 = (bf16[48,3840]{1,0:T(8,128)(2,1)S(1)}, bf16[48,3840]{1,0:T(8,128)(2,1)}, u32[]{:S(2)}) copy-start(bf16[48,3840]{1,0:T(8,128)(2,1)} %reduce-scatter.2.cloned.1.call-done) | copy-start | bytes 1105924
  176.8 5.1 %collective-permute-start.25 = (f32[40,768]{1,0:T(8,128)}, f32[40,768]{1,0:T(8,128)S(1)}, u32[]{:S(2)}, u32[]{:S(2)}) collective-permute-start(f32[40,768]{1,0:T(8,128)} %get-tuple-element.121.refs_6_), channel_id=1, source_target_pairs={{0,4},{2,6},{4,0},{6,2},{8,12},{10,14},{12,8},{14,10},{16,20},{18,... | collective-permute-start | bytes 368648 | tf_op jit(solution)/shard_map/ppermute | solution.py:780
  184.5 4.3 %copy-start.2 = (f32[72,768]{1,0:T(8,128)S(1)}, f32[72,768]{1,0:T(8,128)}, u32[]{:S(2)}) copy-start(f32[72,768]{1,0:T(8,128)} %get-tuple-element.122.here) | copy-start | bytes 663556
  184.5 11.3 %collective-permute-start.29 = (bf16[1,192,384]{2,1,0:T(8,128)(2,1)}, bf16[1,192,384]{2,1,0:T(8,128)(2,1)S(1)}, u32[]{:S(2)}, u32[]{:S(2)}) collective-permute-start(bf16[1,192,384]{2,1,0:T(8,128)(2,1)} %get-tuple-element.127.refs_2_), channel_id=1, source_target_pairs={{0,1},{1,0},{2,3},{3,2},{4,5},{5,4},{6,7},{7,6},{8,9},{9,8},{10,11... | collective-permute-start | bytes 442376 | tf_op jit(solution)/shard_map/ppermute | solution.py:788
  186.0 9.9 %copy-start.5 = (bf16[1,192,384]{2,1,0:T(8,128)(2,1)S(1)}, bf16[1,192,384]{2,1,0:T(8,128)(2,1)}, u32[]{:S(2)}) copy-start(bf16[1,192,384]{2,1,0:T(8,128)(2,1)} %get-tuple-element.127.refs_2_) | copy-start | bytes 442372
  186.0 8.0 %collective-permute-start.27 = (bf16[1,48,1152]{2,1,0:T(8,128)(2,1)}, bf16[1,48,1152]{2,1,0:T(8,128)(2,1)S(1)}, u32[]{:S(2)}, u32[]{:S(2)}) collective-permute-start(bf16[1,48,1152]{2,1,0:T(8,128)(2,1)} %get-tuple-element.125), channel_id=1, source_target_pairs={{0,16},{2,18},{4,20},{6,22},{8,24},{10,26},{12,28},{14,30},{16,0},... | collective-permute-start | bytes 331784 | tf_op jit(solution)/shard_map/ppermute | solution.py:780
  188.8 12.0 %collective-permute-start.26 = (f32[72,768]{1,0:T(8,128)S(1)}, f32[72,768]{1,0:T(8,128)S(1)}, u32[]{:S(2)}, u32[]{:S(2)}) collective-permute-start(f32[72,768]{1,0:T(8,128)S(1)} %copy-done.2), channel_id=1, source_target_pairs={{0,1},{1,0},{2,3},{3,2},{4,5},{5,4},{6,7},{7,6},{8,9},{9,8},{10,11... | collective-permute-start | bytes 663560 | tf_op jit(solution)/shard_map/ppermute | solution.py:788
  195.5 5.2 %copy-start.9 = (bf16[1,48,1152]{2,1,0:T(8,128)(2,1)S(1)}, bf16[1,48,1152]{2,1,0:T(8,128)(2,1)}, u32[]{:S(2)}) copy-start(bf16[1,48,1152]{2,1,0:T(8,128)(2,1)} %shard_map.250) | copy-start | bytes 331780
  195.5 5.2 %collective-permute-start.28 = (bf16[1,48,1152]{2,1,0:T(8,128)(2,1)}, bf16[1,48,1152]{2,1,0:T(8,128)(2,1)S(1)}, u32[]{:S(2)}, u32[]{:S(2)}) collective-permute-start(bf16[1,48,1152]{2,1,0:T(8,128)(2,1)} %shard_map.250), channel_id=1, source_target_pairs={{0,1},{1,0},{2,3},{3,2},{4,5},{5,4},{6,7},{7,6},{8,9},{9,8},{10,11... | collective-permute-start | bytes 331784 | tf_op jit(solution)/shard_map/ppermute | solution.py:788
  200.8 3.4 %copy-start.12 = (f32[48,2304]{1,0:T(8,128)}, f32[48,2304]{1,0:T(8,128)S(1)}, u32[]{:S(2)}) copy-start(f32[48,2304]{1,0:T(8,128)S(1)} %slice_dynamic-update-slice_fusion) | copy-start | bytes 1327108
Sparse Core Ops, SparseCore 0:
  79.1 84.9 reduce-scatter.1

commit v4 on v3

--- a/solution.py
+++ b/solution.py
@@ -37,10 +37,6 @@
 
 def shaped(shape, kind):
     return jax.ShapeDtypeStruct(shape, kind)
-
-
-def far(shape, kind):
-    return pltpu.VMEM(shape, kind)
 
 
 def far(shape, kind):
@@ -219,7 +215,7 @@
     return results
 
 
-def attend_heads(query, pair1, pair2, log_total):
+def attend_heads(query, pair1, pair2, log_total, shifted):
     rows = query.shape[0]
 
     def first(head):
@@ -230,21 +226,25 @@
     def rest(head, scores):
         lanes, place, turned = head_lanes(head)
         scores1, scores2 = scores
-        top = jnp.maximum(
-            jnp.max(scores1, axis=0, keepdims=True), jnp.max(scores2, axis=0, keepdims=True)
-        )
-        exps1 = jnp.exp2(scores1 - top)
-        exps2 = jnp.exp2(scores2 - top)
+        if shifted:
+            top = jnp.maximum(
+                jnp.max(scores1, axis=0, keepdims=True), jnp.max(scores2, axis=0, keepdims=True)
+            )
+            scores1, scores2 = scores1 - top, scores2 - top
+        exps1, exps2 = jnp.exp2(scores1), jnp.exp2(scores2)
         total = column_sum(exps1) + column_sum(exps2)
         lanes = value_lanes(lanes)
         mixed = dot(pair1[:, lanes].T[turned], exps1.astype(jnp.bfloat16)) + dot(
             pair2[:, lanes].T[turned], exps2.astype(jnp.bfloat16)
         )
-        log_total[0, head : head + 1, :] = top + jnp.log2(total)
+        log_sum = jnp.log2(total)
+        log_total[0, head : head + 1, :] = top + log_sum if shifted else log_sum
         return mixed * (1.0 / total)
 
     parts = in_turn(HEADS, first, rest)
-    return jnp.concatenate(
+    logs = log_total[0]
+    in_range = (jnp.min(logs) > -60.0) & (jnp.max(logs) < 60.0)
+    return in_range, jnp.concatenate(
         [
             jnp.concatenate(parts[head : head + 2], axis=0).T.astype(jnp.bfloat16)
             for head in range(0, HEADS, 2)
@@ -316,8 +316,10 @@
         + extra_specs
         + [pl.BlockSpec(memory_space=pl.ANY)] * len(after),
         [block, block, block],
-        [
-            far((rows, width), jnp.bfloat16 if second else jnp.float32),
+        [shaped((rows, width), jnp.bfloat16)] * 3
+        if second
+        else [
+            far((rows, width), jnp.float32),
             far((rows, width), jnp.bfloat16),
             far((rows, width), jnp.bfloat16),
         ],
@@ -394,14 +396,20 @@
     def _():
         value = rotate_lanes(dot(normed1[...], query_weight[...]), cosine[...], sine[...])
         query[...] = (value * (LOG2E * HD ** (-0.5))).astype(jnp.bfloat16)
-        found = attend_heads(query, own_pairs.at[step], peer_pairs.at[step], log_total)
+        pairs = own_pairs.at[step], peer_pairs.at[step]
+        in_range, found = attend_heads(query, *pairs, log_total, False)
         attended[...] = found
+
+        @pl.when(jnp.logical_not(in_range))
+        def _():
+            attended[...] = attend_heads(query, *pairs, log_total, True)[1]
+
         for index in range(attend_steps):
 
             @pl.when(step == index)
             def _(index=index):
                 heads = HEADS * HD
-                all_attended[:, index * heads : (index + 1) * heads] = found
+                all_attended[:, index * heads : (index + 1) * heads] = attended[...]
 
     @pl.when(step == attend_steps)
     def _():
@@ -609,7 +617,7 @@
         32,
     )(
         core, d_query, d_keys, d_values, peer_keys, peer_values, normed, cosine, sine,
-        free=(peer_keys, peer_values),
+        free=(d_query, d_keys, d_values, peer_keys, peer_values),
     )
 
 
@@ -1044,7 +1052,6 @@
     dp_size = lax.axis_size("dp")
     bits = dp_bits()
     by_steps = split_rows(width) == width // dp_size and len(bits) == 4
-    mixed = swap_halves(mixed)
     up_rows = lax.psum_scatter(up_grad, "dp", scatter_dimension=0, tiled=True)
     up_got = swap_seq(up_rows)
 
@@ -1056,7 +1063,7 @@
     d_query, away_keys, away_values = attend_back(query, peer_pair, d_attended, attended, log_total)
     after = ()
     if by_steps:
-        (down,), sent = stage(4, [([down], "half")], (away_keys, mixed), free=(mixed,))
+        (down,), sent = stage(4, [([down], "half")], (away_keys,))
         after = (sent,)
     peer_keys, peer_values = swap_cores(away_keys), swap_cores(away_values)
     d_query, d_keys, d_values = attend_back(
@@ -1072,7 +1079,7 @@
             for keep, send in zip(qkv_parts[::2], qkv_parts[1::2])
         ]
         (late,), *sent = stage(4, [(late, "half")])
-        (down,), *sent = stage(4, [([down], (bits[1], 1))], sent)
+        (down, mixed), *sent = stage(4, [([down], (bits[1], 1))], sent, relay=mixed)
     tokens_grad, small = tokens_back(
         d_projected, attn_qkv, tokens, d_middle, mods, sums2, up_bias_grad, sent
     )
@@ -1137,7 +1144,7 @@
         ada_bias_grad = jnp.sum(d_mod_all, axis=0)
     up_rows = up_rows.astype(jnp.float32) + up_got.astype(jnp.float32)
     return (
-        mixed[None],
+        swap_halves(mixed)[None],
         swap_halves(tokens_grad).astype(jnp.float32)[None],
         cond_grad,
         first_gain_grad,

time: 213 us -> 210 us (0.986)
  Pallas kernels: 109 us -> 106 us
    reduce_scatter x1, waiting for transfers between devices: 0.01 us -> 6.1 us  [per_device(): up_rows = lax.psum_scatter(up_grad, 'dp', scatter_dimension=0, tiled=True)]
    ppermute x19, waiting for transfers between devices: 20.3 us -> 16.3 us  [swap_bit(): lax.ppermute(block, 'dp', [(i, i ^ bit) for i in range(lax.axis_size('dp'...]
    pallas_call x13, Pallas kernels: 107 us -> 105 us  [run(): return call(*placed)]
    ppermute x19, starting transfers between devices: 23.3 us -> 20.7 us  [swap_bit(): lax.ppermute(block, 'dp', [(i, i ^ bit) for i in range(lax.axis_size('dp'...]
    ppermute x6, starting transfers between devices: 4.32 us -> 6.91 us  [swap_seq(): return lax.ppermute(block, 'seq', [(0, 1), (1, 0)])]
where the time goes in v4:
time: 210 us; the launch traced here: 209 us
  Pallas kernels  106 us (50%)
  starting transfers between devices  42.4 us (20%)
  waiting for transfers between devices  27.1 us (13%)
  between operations  16.7 us (8%)
  other arithmetic  8.18 us (4%)
  local copies, waits for them, and re-layouts  7.29 us (3%)
    pallas_call x13, Pallas kernels, run(): return call(*placed)  105 us
    ppermute x19, starting transfers between devices, swap_bit(): lax.ppermute(block, 'dp', [(i, i ^ bit) for i in range(lax.axis_size('dp'...  20.7 us
    ppermute x19, waiting for transfers between devices, swap_bit(): lax.ppermute(block, 'dp', [(i, i ^ bit) for i in range(lax.axis_size('dp'...  16.3 us
    ppermute x5, starting transfers between devices, swap_halves(): return lax.ppermute(block, ('dp', 'seq'), perm)  14.7 us
    ppermute x6, starting transfers between devices, swap_seq(): return lax.ppermute(block, 'seq', [(0, 1), (1, 0)])  6.91 us
    reduce_scatter x1, waiting for transfers between devices, per_device(): up_rows = lax.psum_scatter(up_grad, 'dp', scatter_dimension=0, tiled=True)  6.1 us
    ppermute x6, waiting for transfers between devices, swap_seq(): return lax.ppermute(block, 'seq', [(0, 1), (1, 0)])  4.65 us
  transfers between devices with their start and end apart: 31, of which 14 were waited for; matrix products, arithmetic and copies ran while one was open for 6% of the time, Pallas kernels for 30%

profile of v4, /device:TPU:0, one launch (start us, length us, event | category | flops | bytes accessed | tf_op | source)
XLA Modules:
  0.0 208.7 jit_solution(7894033899323626910)
XLA Ops:
  7.2 2.0 collective-permute-start.1
  9.2 1.8 collective-permute-start
  11.0 1.8 collective-permute-start.5
  13.4 0.7 reshape.91
  14.1 0.7 reshape.92
  14.8 1.0 fusion.4
  15.8 1.3 pad_maximum_fusion.1
  18.8 0.8 constant_dynamic-slice_fusion
  19.6 0.6 convolution_reduce_fusion
  20.2 1.3 concatenate.15.mods
  21.5 6.8 %shard_map.237 = (bf16[512,768]{1,0:T(8,128)(2,1)}, bf16[512,1536]{1,0:T(8,128)(2,1)}, bf16[512,512]{1,0:T(8,128)(2,1)}, bf16[512,512]{1,0:T(8,128)(2,1)}, bf16[512,512]{1,0:T(8,128)(2,1)}) custom-call(bf16[512,768]{1,0:T(8,128)(2,1)S(1)} %collective-permute-done.tokens.refs_6_, f32[16,768]{1,0:T(8,128)} %concatenate.15.mods, bf16[768,2304]{1,0:T(8,128)(2,1)} %weight3.1, ...), custom_call_target="tpu_custom_call" | custom-call | flops 1 | bytes 1 | tf_op jit(solution)/shard_map/pallas_call | solution.py:93
  28.3 5.2 %collective-permute-start.2 = (bf16[512,512]{1,0:T(8,128)(2,1)}, bf16[512,512]{1,0:T(8,128)(2,1)S(1)}, u32[]{:S(2)}, u32[]{:S(2)}) collective-permute-start(bf16[512,512]{1,0:T(8,128)(2,1)} %get-tuple-element.75.refs_0_), channel_id=1, source_target_pairs={{0,2},{2,0},{4,6},{6,4},{8,10},{10,8},{12,14},{14,12},{16,18},{18,... | collective-permute-start | bytes 1572872 | tf_op jit(solution)/shard_map/ppermute | solution.py:788
  34.0 0.6 broadcast_in_dim.55
  34.6 0.6 reshape.94.down_bias
  35.2 0.7 collective-permute-done.3.refs_4_
  35.9 0.7 collective-permute-done.4.refs_5_
  36.7 0.8 copy-done.8
  37.5 39.4 %shard_map.238 = (bf16[512,768]{1,0:T(8,128)(2,1)}, bf16[512,768]{1,0:T(8,128)(2,1)}, f32[3,4,512]{2,1,0:T(4,128)}, bf16[512,768]{1,0:T(8,128)(2,1)}, f32[512,76...) custom-call(s32[1]{0:T(128)} %bitcast.2.core, ...), custom_call_target="tpu_custom_call" | custom-call | flops 1 | bytes 1 | tf_op jit(solution)/shard_map/pallas_call | solution.py:93
  77.4 11.1 %shard_map.239 = (f32[512,768]{1,0:T(8,128)}, bf16[512,768]{1,0:T(8,128)(2,1)}, bf16[512,768]{1,0:T(8,128)(2,1)}) custom-call(bf16[512,768]{1,0:T(8,128)(2,1)} %get-tuple-element.80.query, bf16[512,1536]{1,0:T(8,128)(2,1)} %get-tuple-element.81.pair, bf16[512,768]{1,0:T(8,128)(2,1)} %get-tuple-element.82.grad, bf16[512,768]{1,0:T(8,128)(2,1)} %get-tuple-element.83.attended, ...), custom_call_target="tpu_custom_call" | custom-call | flops 1 | bytes 1 | tf_op jit(solution)/shard_map/pallas_call | solution.py:93
  89.0 4.6 %shard_map.240 = (bf16[8,192,384]{2,1,0:T(8,128)(2,1)}, bf16[8,192,384]{2,1,0:T(8,128)(2,1)}) custom-call(s32[1]{0:T(128)} %bitcast.1.mine, bf16[8,192,768]{2,1,0:T(8,128)(2,1)} %collective-permute-done.6.refs_0_, bf16[8,192,768]{2,1,0:T(8,128)(2,1)} %bitcast.40, bf16[512,768]{1,0:T(8,128)(2,1)} %get-tuple-element.85.refs_2_), custom_call_target="tpu_custom_call" | custom-call | flops 1 | bytes 1 | tf_op jit(solution)/shard_map/pallas_call | solution.py:93
  93.6 11.2 %shard_map.241 = (bf16[512,768]{1,0:T(8,128)(2,1)S(1)}, bf16[512,768]{1,0:T(8,128)(2,1)S(1)}, bf16[512,768]{1,0:T(8,128)(2,1)S(1)}) custom-call(bf16[512,768]{1,0:T(8,128)(2,1)} %get-tuple-element.80.query, bf16[512,1536]{1,0:T(8,128)(2,1)} %get-tuple-element.88.pair, bf16[512,768]{1,0:T(8,128)(2,1)} %get-tuple-element.82.grad, ...), custom_call_target="tpu_custom_call" | custom-call | flops 1 | bytes 1 | tf_op jit(solution)/shard_map/pallas_call | solution.py:93
  104.8 6.3 %shard_map.242 = (bf16[512,2304]{1,0:T(8,128)(2,1)}, bf16[384,768]{1,0:T(8,128)(2,1)}, bf16[384,768]{1,0:T(8,128)(2,1)}, bf16[384,768]{1,0:T(8,128)(2,1)}, bf16[...) custom-call(s32[1]{0:T(128)} %bitcast.2.core, ...), custom_call_target="tpu_custom_call" | custom-call | flops 1 | bytes 1 | tf_op jit(solution)/shard_map/pallas_call | solution.py:93
  111.1 0.5 collective-permute-start.11
  111.7 1.6 collective-permute-done.10.refs_0_
  113.3 0.8 collective-permute-done.11.refs_2_
  114.2 0.8 collective-permute-done.12.refs_4_
  115.0 3.9 %shard_map.243 = (bf16[8,48,1152]{2,1,0:T(8,128)(2,1)}, bf16[8,48,1152]{2,1,0:T(8,128)(2,1)}) custom-call(s32[1]{0:T(128)} %bitcast.1.mine, bf16[8,48,768]{2,1,0:T(8,128)(2,1)S(1)} %collective-permute-done.10.refs_0_, bf16[8,48,768]{2,1,0:T(8,128)(2,1)} %bitcast.42, bf16[8,48,768]{2,1,0:T(8,128)(2,1)S(1)} %collective-permute-done.11.refs_2_, ...), custom_call_target="tpu_custom_call" | custom-call | flops 1 | bytes 1 | tf_op jit(solution)/shard_map/pallas_call | solution.py:93
  118.9 2.0 collective-permute-start.15
  120.9 0.9 collective-permute-done.7.refs_0_
  121.9 4.2 %shard_map.244 = (bf16[4,192,384]{2,1,0:T(8,128)(2,1)}, bf16[4,192,384]{2,1,0:T(8,128)(2,1)}, bf16[512,768]{1,0:T(8,128)(2,1)}) custom-call(s32[1]{0:T(128)} %bitcast.mine, bf16[8,192,384]{2,1,0:T(8,128)(2,1)S(1)} %collective-permute-done.7.refs_0_, bf16[8,192,384]{2,1,0:T(8,128)(2,1)} %get-tuple-element.87.refs_1_, ...), custom_call_target="tpu_custom_call" | custom-call | flops 1 | bytes 1 | tf_op jit(solution)/shard_map/pallas_call | solution.py:93
  126.1 1.5 collective-permute-start.14
  127.6 8.0 %shard_map.245 = (bf16[512,768]{1,0:T(8,128)(2,1)}, f32[16,768]{1,0:T(8,128)}) custom-call(bf16[512,2304]{1,0:T(8,128)(2,1)} %get-tuple-element.106.d_projected, bf16[768,2304]{1,0:T(8,128)(2,1)} %weight3.1, bf16[768,2304]{1,0:T(8,128)(2,1)} %weight3.1, bf16[768,2304]{1,0:T(8,128)(2,1)} %weight3.1, bf16[512,768]{1,0:T(8,128)(2,1)} %copy-done, ...), custom_call_target="tpu_custom_call" | custom-call | flops 1 | bytes 1 | tf_op jit(solution)/shard_map/pallas_call | solution.py:93
  135.6 1.8 collective-permute-start.13
  137.4 0.8 add.65.refs_5_
  138.3 1.6 collective-permute-start.17
  139.9 2.7 %collective-permute-done.17.refs_6_ = f32[16,768]{1,0:T(8,128)S(1)} collective-permute-done((f32[16,768]{1,0:T(8,128)S(1)}, f32[16,768]{1,0:T(8,128)S(1)}, u32[]{:S(2)}, u32[]{:S(2)}) %collective-permute-start.17) | collective-permute-done | bytes 49184 | tf_op jit(solution)/shard_map/ppermute | solution.py:788
  142.6 3.4 %shard_map.246 = (bf16[2,192,384]{2,1,0:T(8,128)(2,1)}, bf16[2,192,384]{2,1,0:T(8,128)(2,1)}, bf16[4,48,1152]{2,1,0:T(8,128)(2,1)}, bf16[4,48,1152]{2,1,0:T(8,12...) custom-call(s32[2]{0:T(128)S(1)} %pad_add_fusion.mine, bf16[4,192,384]{2,1,0:T(8,128)(2,1)S(1)} %collective-permute-done.14.refs_0_, ...), custom_call_target="tpu_custom_call" | custom-call | flops 1 | bytes 1 | tf_op jit(solution)/shard_map/pallas_call | solution.py:93
  146.0 7.4 %collective-permute-start.18 = (bf16[512,768]{1,0:T(8,128)(2,1)}, bf16[512,768]{1,0:T(8,128)(2,1)}, u32[]{:S(2)}, u32[]{:S(2)}) collective-permute-start(bf16[512,768]{1,0:T(8,128)(2,1)} %get-tuple-element.112), channel_id=1, source_target_pairs={{0,0},{1,2},{2,1},{3,3},{4,4},{5,6},{6,5},{7,7},{8,8},{9,10},{10,9... | collective-permute-start | bytes 2359304 | tf_op jit(solution)/shard_map/ppermute | solution.py:784
  153.5 0.5 collective-permute-start.20
  154.0 1.5 collective-permute-start.19
  155.7 2.6 %collective-permute-start.21 = (f32[24,768]{1,0:T(8,128)}, f32[24,768]{1,0:T(8,128)S(1)}, u32[]{:S(2)}, u32[]{:S(2)}) collective-permute-start(f32[24,768]{1,0:T(8,128)} %get-tuple-element.117.refs_5_), channel_id=1, source_target_pairs={{0,16},{2,18},{4,20},{6,22},{8,24},{10,26},{12,28},{14,30},{16,0},... | collective-permute-start | bytes 221192 | tf_op jit(solution)/shard_map/ppermute | solution.py:788
  158.3 6.1 %reduce-scatter.2.cloned.1.call-done = bf16[48,3840]{1,0:T(8,128)(2,1)} async-done(((bf16[768,3840]{1,0:T(8,128)(2,1)}), bf16[48,3840]{1,0:T(8,128)(2,1)}) %reduce-scatter.2.cloned.1.call-update) | async-done | bytes 368656 | tf_op jit(solution)/shard_map/reduce_scatter | solution.py:1055
  164.4 1.7 collective-permute-start.24
  166.2 1.1 collective-permute-done.19.refs_0_
  167.2 2.3 %shard_map.247 = (bf16[1,192,384]{2,1,0:T(8,128)(2,1)}, bf16[1,192,384]{2,1,0:T(8,128)(2,1)}, bf16[2,48,1152]{2,1,0:T(8,128)(2,1)}, bf16[2,48,1152]{2,1,0:T(8,128)(2,1)}, f32[40,768]{1,0:T(8,128)}) custom-call(s32[2]{0:T(128)S(1)} %pad_add_fusion.3.mine, bf16[2,192,384]{2,1,0:T(8,128)(2,1)S(1)} %collective-permute-done.19.refs_0_, ...), custom_call_target="tpu_custom_call" | custom-call | flops 1 | bytes 1 | tf_op jit(solution)/shard_map/pallas_call | solution.py:93
  169.5 1.9 collective-permute-start.23
  171.4 0.6 collective-permute-start.22
  172.0 1.4 collective-permute-start.25
  173.4 2.4 %bitcast_convert_fusion = f32[1,512,768]{2,1,0:T(8,128)} fusion(bf16[512,768]{1,0:T(8,128)(2,1)} %collective-permute-done.18), kind=kLoop, calls=%fused_computation.1 | loop fusion | flops 393216 | bytes 2359296 | tf_op jit(solution)/shard_map/broadcast_in_dim | solution.py:1148
  175.8 1.3 collective-permute-done.25.refs_7_
  177.1 1.3 collective-permute-done.22.refs_0_
  178.4 1.3 collective-permute-done.23.refs_2_
  179.7 2.0 shard_map.248
  181.7 2.7 %collective-permute-start.29 = (bf16[1,192,384]{2,1,0:T(8,128)(2,1)}, bf16[1,192,384]{2,1,0:T(8,128)(2,1)S(1)}, u32[]{:S(2)}, u32[]{:S(2)}) collective-permute-start(bf16[1,192,384]{2,1,0:T(8,128)(2,1)} %get-tuple-element.129.refs_2_), channel_id=1, source_target_pairs={{0,1},{1,0},{2,3},{3,2},{4,5},{5,4},{6,7},{7,6},{8,9},{9,8},{10,11... | collective-permute-start | bytes 442376 | tf_op jit(solution)/shard_map/ppermute | solution.py:796
  184.5 1.8 collective-permute-start.27
  186.4 0.9 slice.39
  187.2 0.7 slice.38
  188.0 3.8 %collective-permute-done.27.refs_0_ = bf16[1,48,1152]{2,1,0:T(8,128)(2,1)S(1)} collective-permute-done((bf16[1,48,1152]{2,1,0:T(8,128)(2,1)}, bf16[1,48,1152]{2,1,0:T(8,128)(2,1)S(1)}, u32[]{:S(2)}, u32[]{:S(2)}) %collective-permute-start.27) | collective-permute-done | bytes 110624 | tf_op jit(solution)/shard_map/ppermute | solution.py:788
  191.8 1.6 shard_map.250
  193.8 0.9 pad_maximum_fusion
  194.6 3.7 %collective-permute-done.28 = bf16[1,48,1152]{2,1,0:T(8,128)(2,1)S(1)} collective-permute-done((bf16[1,48,1152]{2,1,0:T(8,128)(2,1)}, bf16[1,48,1152]{2,1,0:T(8,128)(2,1)S(1)}, u32[]{:S(2)}, u32[]{:S(2)}) %collective-permute-start.28) | collective-permute-done | bytes 110624 | tf_op jit(solution)/shard_map/ppermute | solution.py:796
  198.5 1.7 shard_map.249
  200.2 0.8 copy.29
  201.0 0.9 copy.37
  (80 shorter events, 2.8 us)
Async XLA Ops:
  7.2 12.4 %copy-start.1 = (bf16[128,4608]{1,0:T(8,128)(2,1)S(1)}, bf16[128,4608]{1,0:T(8,128)(2,1)}, u32[]{:S(2)}) copy-start(bf16[128,4608]{1,0:T(8,128)(2,1)} %ada_weight.1) | copy-start | bytes 3538948
  7.2 157.2 %reduce-scatter.2.cloned.1.call-start = ((), (), s32[]{:S(2)}) async-start(), calls=%async_computation.1 | async-start | bytes 6266880 | tf_op jit(solution)/shard_map/reduce_scatter | solution.py:1055
  7.2 9.9 %collective-permute-start.1 = (s32[1]{0:T(128)}, s32[1]{0:T(128)}, u32[]{:S(2)}, u32[]{:S(2)}) collective-permute-start(s32[1]{0:T(128)} %param.16), channel_id=1, source_target_pairs={{0,0},{1,2},{2,1},{3,3},{4,4},{5,6},{6,5},{7,7},{8,8},{9,10},{10,9... | collective-permute-start | bytes 20 | tf_op jit(solution)/shard_map/ppermute | solution.py:784
  9.2 12.3 %collective-permute-start = (bf16[512,768]{1,0:T(8,128)(2,1)}, bf16[512,768]{1,0:T(8,128)(2,1)S(1)}, u32[]{:S(2)}, u32[]{:S(2)}) collective-permute-start(bf16[512,768]{1,0:T(8,128)(2,1)} %bitcast.46), channel_id=1, source_target_pairs={{0,0},{1,2},{2,1},{3,3},{4,4},{5,6},{6,5},{7,7},{8,8},{9,10},{10,9... | collective-permute-start | bytes 2359304 | tf_op jit(solution)/shard_map/ppermute | solution.py:784
  11.0 24.2 %collective-permute-start.5 = (bf16[512,768]{1,0:T(8,128)(2,1)}, bf16[512,768]{1,0:T(8,128)(2,1)S(1)}, u32[]{:S(2)}, u32[]{:S(2)}) collective-permute-start(bf16[512,768]{1,0:T(8,128)(2,1)} %bitcast.47), channel_id=1, source_target_pairs={{0,0},{1,2},{2,1},{3,3},{4,4},{5,6},{6,5},{7,7},{8,8},{9,10},{10,9... | collective-permute-start | bytes 2359304 | tf_op jit(solution)/shard_map/ppermute | solution.py:784
  14.8 5.3 %copy-start.13 = (bf16[4608]{0:T(1024)(128)(2,1)S(1)}, bf16[4608]{0:T(1024)(128)(2,1)}, u32[]{:S(2)}) copy-start(bf16[4608]{0:T(1024)(128)(2,1)} %param.27) | copy-start | bytes 27652
  21.5 6.8 %copy-start = (bf16[512,768]{1,0:T(8,128)(2,1)}, bf16[512,768]{1,0:T(8,128)(2,1)S(1)}, u32[]{:S(2)}) copy-start(bf16[512,768]{1,0:T(8,128)(2,1)S(1)} %collective-permute-done.tokens.refs_6_) | copy-start | bytes 2359300
  21.5 12.5 %copy-start.14 = (bf16[3072]{0:T(1024)(128)(2,1)S(1)}, bf16[3072]{0:T(1024)(128)(2,1)}, u32[]{:S(2)}) copy-start(bf16[3072]{0:T(1024)(128)(2,1)} %param.23) | copy-start | bytes 18436
  21.5 13.1 %copy-start.15 = (bf16[768]{0:T(1024)(128)(2,1)S(1)}, bf16[768]{0:T(1024)(128)(2,1)}, u32[]{:S(2)}) copy-start(bf16[768]{0:T(1024)(128)(2,1)} %param.25) | copy-start | bytes 4612
  28.3 6.9 %collective-permute-start.2 = (bf16[512,512]{1,0:T(8,128)(2,1)}, bf16[512,512]{1,0:T(8,128)(2,1)S(1)}, u32[]{:S(2)}, u32[]{:S(2)}) collective-permute-start(bf16[512,512]{1,0:T(8,128)(2,1)} %get-tuple-element.75.refs_0_), channel_id=1, source_target_pairs={{0,2},{2,0},{4,6},{6,4},{8,10},{10,8},{12,14},{14,12},{16,18},{18,... | collective-permute-start | bytes 1572872 | tf_op jit(solution)/shard_map/ppermute | solution.py:788
  33.4 2.5 %collective-permute-start.3 = (bf16[512,512]{1,0:T(8,128)(2,1)}, bf16[512,512]{1,0:T(8,128)(2,1)S(1)}, u32[]{:S(2)}, u32[]{:S(2)}) collective-permute-start(bf16[512,512]{1,0:T(8,128)(2,1)} %get-tuple-element.76.refs_1_), channel_id=1, source_target_pairs={{0,2},{2,0},{4,6},{6,4},{8,10},{10,8},{12,14},{14,12},{16,18},{18,... | collective-permute-start | bytes 1572872 | tf_op jit(solution)/shard_map/ppermute | solution.py:788
  33.5 3.2 %collective-permute-start.4 = (bf16[512,512]{1,0:T(8,128)(2,1)}, bf16[512,512]{1,0:T(8,128)(2,1)S(1)}, u32[]{:S(2)}, u32[]{:S(2)}) collective-permute-start(bf16[512,512]{1,0:T(8,128)(2,1)} %get-tuple-element.77.refs_2_), channel_id=1, source_target_pairs={{0,2},{2,0},{4,6},{6,4},{8,10},{10,8},{12,14},{14,12},{16,18},{18,... | collective-permute-start | bytes 1572872 | tf_op jit(solution)/shard_map/ppermute | solution.py:788
  35.1 1.5 copy-start.4
  35.2 1.5 copy-start.6
  35.9 0.8 copy-start.7
  36.7 0.8 copy-start.8
  76.9 12.1 %collective-permute-start.6 = (bf16[8,192,768]{2,1,0:T(8,128)(2,1)}, bf16[8,192,768]{2,1,0:T(8,128)(2,1)}, u32[]{:S(2)}, u32[]{:S(2)}) collective-permute-start(bf16[8,192,768]{2,1,0:T(8,128)(2,1)} %bitcast.9), channel_id=1, source_target_pairs={{0,2},{2,0},{4,6},{6,4},{8,10},{10,8},{12,14},{14,12},{16,18},{18,... | collective-permute-start | bytes 7077896 | tf_op jit(solution)/shard_map/ppermute | solution.py:788
  88.5 16.4 %collective-permute-start.8 = (bf16[512,768]{1,0:T(8,128)(2,1)}, bf16[512,768]{1,0:T(8,128)(2,1)S(1)}, u32[]{:S(2)}, u32[]{:S(2)}) collective-permute-start(bf16[512,768]{1,0:T(8,128)(2,1)} %get-tuple-element.85.refs_2_), channel_id=1, source_target_pairs={{0,2},{2,0},{4,6},{6,4},{8,10},{10,8},{12,14},{14,12},{16,18},{18,... | collective-permute-start | bytes 2359304 | tf_op jit(solution)/shard_map/ppermute | solution.py:788
  88.6 16.3 %collective-permute-start.9 = (bf16[512,768]{1,0:T(8,128)(2,1)}, bf16[512,768]{1,0:T(8,128)(2,1)}, u32[]{:S(2)}, u32[]{:S(2)}) collective-permute-start(bf16[512,768]{1,0:T(8,128)(2,1)} %get-tuple-element.93), channel_id=1, source_target_pairs={{0,2},{2,0},{4,6},{6,4},{8,10},{10,8},{12,14},{14,12},{16,18},{18,... | collective-permute-start | bytes 2359304 | tf_op jit(solution)/shard_map/ppermute | solution.py:788
  93.6 28.3 %collective-permute-start.7 = (bf16[8,192,384]{2,1,0:T(8,128)(2,1)}, bf16[8,192,384]{2,1,0:T(8,128)(2,1)S(1)}, u32[]{:S(2)}, u32[]{:S(2)}) collective-permute-start(bf16[8,192,384]{2,1,0:T(8,128)(2,1)} %get-tuple-element.86.refs_3_), channel_id=1, source_target_pairs={{0,1},{1,0},{2,3},{3,2},{4,5},{5,4},{6,7},{7,6},{8,9},{9,8},{10,11... | collective-permute-start | bytes 3538952 | tf_op jit(solution)/shard_map/ppermute | solution.py:796
  111.1 2.2 %collective-permute-start.10 = (bf16[8,48,768]{2,1,0:T(8,128)(2,1)}, bf16[8,48,768]{2,1,0:T(8,128)(2,1)S(1)}, u32[]{:S(2)}, u32[]{:S(2)}) collective-permute-start(bf16[8,48,768]{2,1,0:T(8,128)(2,1)} %bitcast.50), channel_id=1, source_target_pairs={{0,2},{2,0},{4,6},{6,4},{8,10},{10,8},{12,14},{14,12},{16,18},{18,... | collective-permute-start | bytes 1769480 | tf_op jit(solution)/shard_map/ppermute | solution.py:788
  111.1 3.0 %collective-permute-start.11 = (bf16[8,48,768]{2,1,0:T(8,128)(2,1)}, bf16[8,48,768]{2,1,0:T(8,128)(2,1)S(1)}, u32[]{:S(2)}, u32[]{:S(2)}) collective-permute-start(bf16[8,48,768]{2,1,0:T(8,128)(2,1)} %bitcast.49), channel_id=1, source_target_pairs={{0,2},{2,0},{4,6},{6,4},{8,10},{10,8},{12,14},{14,12},{16,18},{18,... | collective-permute-start | bytes 1769480 | tf_op jit(solution)/shard_map/ppermute | solution.py:788
  111.6 3.4 %collective-permute-start.12 = (bf16[8,48,768]{2,1,0:T(8,128)(2,1)}, bf16[8,48,768]{2,1,0:T(8,128)(2,1)S(1)}, u32[]{:S(2)}, u32[]{:S(2)}) collective-permute-start(bf16[8,48,768]{2,1,0:T(8,128)(2,1)} %bitcast.48), channel_id=1, source_target_pairs={{0,2},{2,0},{4,6},{6,4},{8,10},{10,8},{12,14},{14,12},{16,18},{18,... | collective-permute-start | bytes 1769480 | tf_op jit(solution)/shard_map/ppermute | solution.py:788
  118.9 23.7 %collective-permute-start.15 = (bf16[8,48,1152]{2,1,0:T(8,128)(2,1)}, bf16[8,48,1152]{2,1,0:T(8,128)(2,1)}, u32[]{:S(2)}, u32[]{:S(2)}) collective-permute-start(bf16[8,48,1152]{2,1,0:T(8,128)(2,1)} %get-tuple-element.100.refs_2_), channel_id=1, source_target_pairs={{0,1},{1,0},{2,3},{3,2},{4,5},{5,4},{6,7},{7,6},{8,9},{9,8},{10,11... | collective-permute-start | bytes 2654216 | tf_op jit(solution)/shard_map/ppermute | solution.py:796
  121.9 5.7 %copy-start.3 = (f32[1,3072]{1,0:T(1,128)S(1)}, f32[1,3072]{1,0:T(1,128)}, u32[]{:S(2)}) copy-start(f32[1,3072]{1,0:T(1,128)} %get-tuple-element.109.bias_grad) | copy-start | bytes 36868
  126.1 16.5 %collective-permute-start.14 = (bf16[4,192,384]{2,1,0:T(8,128)(2,1)}, bf16[4,192,384]{2,1,0:T(8,128)(2,1)S(1)}, u32[]{:S(2)}, u32[]{:S(2)}) collective-permute-start(bf16[4,192,384]{2,1,0:T(8,128)(2,1)} %get-tuple-element.103.refs_0_.refs_4_), channel_id=1, source_target_pairs={{0,4},{2,6},{4,0},{6,2},{8,12},{10,14},{12,8},{14,10},{16,20},{18,... | collective-permute-start | bytes 1769480 | tf_op jit(solution)/shard_map/ppermute | solution.py:788
  135.6 1.8 collective-permute-start.16
  135.6 22.6 %collective-permute-start.13 = (bf16[512,768]{1,0:T(8,128)(2,1)}, bf16[512,768]{1,0:T(8,128)(2,1)S(1)}, u32[]{:S(2)}, u32[]{:S(2)}) collective-permute-start(bf16[512,768]{1,0:T(8,128)(2,1)} %get-tuple-element.102), channel_id=1, source_target_pairs={{0,0},{1,2},{2,1},{3,3},{4,4},{5,6},{6,5},{7,7},{8,8},{9,10},{10,9... | collective-permute-start | bytes 2359304 | tf_op jit(solution)/shard_map/ppermute | solution.py:784
  138.3 4.3 %copy-start.11 = (f32[16,768]{1,0:T(8,128)}, f32[16,768]{1,0:T(8,128)S(1)}, u32[]{:S(2)}) copy-start(f32[16,768]{1,0:T(8,128)S(1)} %add.65.refs_5_) | copy-start | bytes 147460
  138.3 4.3 %collective-permute-start.17 = (f32[16,768]{1,0:T(8,128)S(1)}, f32[16,768]{1,0:T(8,128)S(1)}, u32[]{:S(2)}, u32[]{:S(2)}) collective-permute-start(f32[16,768]{1,0:T(8,128)S(1)} %add.65.refs_5_), channel_id=1, source_target_pairs={{0,8},{2,10},{4,12},{6,14},{8,0},{10,2},{12,4},{14,6},{16,24},{18,... | collective-permute-start | bytes 147464 | tf_op jit(solution)/shard_map/ppermute | solution.py:788
  146.0 27.4 %collective-permute-start.18 = (bf16[512,768]{1,0:T(8,128)(2,1)}, bf16[512,768]{1,0:T(8,128)(2,1)}, u32[]{:S(2)}, u32[]{:S(2)}) collective-permute-start(bf16[512,768]{1,0:T(8,128)(2,1)} %get-tuple-element.112), channel_id=1, source_target_pairs={{0,0},{1,2},{2,1},{3,3},{4,4},{5,6},{6,5},{7,7},{8,8},{9,10},{10,9... | collective-permute-start | bytes 2359304 | tf_op jit(solution)/shard_map/ppermute | solution.py:784
  153.5 13.8 %collective-permute-start.20 = (bf16[4,48,1152]{2,1,0:T(8,128)(2,1)}, bf16[4,48,1152]{2,1,0:T(8,128)(2,1)S(1)}, u32[]{:S(2)}, u32[]{:S(2)}) collective-permute-start(bf16[4,48,1152]{2,1,0:T(8,128)(2,1)} %get-tuple-element.115), channel_id=1, source_target_pairs={{0,4},{2,6},{4,0},{6,2},{8,12},{10,14},{12,8},{14,10},{16,20},{18,... | collective-permute-start | bytes 1327112 | tf_op jit(solution)/shard_map/ppermute | solution.py:788
  154.0 13.2 %collective-permute-start.19 = (bf16[2,192,384]{2,1,0:T(8,128)(2,1)}, bf16[2,192,384]{2,1,0:T(8,128)(2,1)S(1)}, u32[]{:S(2)}, u32[]{:S(2)}) collective-permute-start(bf16[2,192,384]{2,1,0:T(8,128)(2,1)} %get-tuple-element.113.refs_4_), channel_id=1, source_target_pairs={{0,8},{2,10},{4,12},{6,14},{8,0},{10,2},{12,4},{14,6},{16,24},{18,... | collective-permute-start | bytes 884744 | tf_op jit(solution)/shard_map/ppermute | solution.py:788
  155.7 10.5 %collective-permute-start.21 = (f32[24,768]{1,0:T(8,128)}, f32[24,768]{1,0:T(8,128)S(1)}, u32[]{:S(2)}, u32[]{:S(2)}) collective-permute-start(f32[24,768]{1,0:T(8,128)} %get-tuple-element.117.refs_5_), channel_id=1, source_target_pairs={{0,16},{2,18},{4,20},{6,22},{8,24},{10,26},{12,28},{14,30},{16,0},... | collective-permute-start | bytes 221192 | tf_op jit(solution)/shard_map/ppermute | solution.py:788
  164.4 15.3 %collective-permute-start.24 = (bf16[48,3840]{1,0:T(8,128)(2,1)}, bf16[48,3840]{1,0:T(8,128)(2,1)S(1)}, u32[]{:S(2)}, u32[]{:S(2)}) collective-permute-start(bf16[48,3840]{1,0:T(8,128)(2,1)} %reduce-scatter.2.cloned.1.call-done), channel_id=1, source_target_pairs={{0,1},{1,0},{2,3},{3,2},{4,5},{5,4},{6,7},{7,6},{8,9},{9,8},{10,11... | collective-permute-start | bytes 1105928 | tf_op jit(solution)/shard_map/ppermute | solution.py:796
  169.5 10.2 %collective-permute-start.23 = (bf16[2,48,1152]{2,1,0:T(8,128)(2,1)}, bf16[2,48,1152]{2,1,0:T(8,128)(2,1)S(1)}, u32[]{:S(2)}, u32[]{:S(2)}) collective-permute-start(bf16[2,48,1152]{2,1,0:T(8,128)(2,1)} %get-tuple-element.120), channel_id=1, source_target_pairs={{0,8},{2,10},{4,12},{6,14},{8,0},{10,2},{12,4},{14,6},{16,24},{18,... | collective-permute-start | bytes 663560 | tf_op jit(solution)/shard_map/ppermute | solution.py:788
  171.4 7.0 %collective-permute-start.22 = (bf16[1,192,384]{2,1,0:T(8,128)(2,1)}, bf16[1,192,384]{2,1,0:T(8,128)(2,1)S(1)}, u32[]{:S(2)}, u32[]{:S(2)}) collective-permute-start(bf16[1,192,384]{2,1,0:T(8,128)(2,1)} %get-tuple-element.118.refs_4_), channel_id=1, source_target_pairs={{0,16},{2,18},{4,20},{6,22},{8,24},{10,26},{12,28},{14,30},{16,0},... | collective-permute-start | bytes 442376 | tf_op jit(solution)/shard_map/ppermute | solution.py:788
  172.0 14.3 %copy-start.10 = (bf16[48,3840]{1,0:T(8,128)(2,1)S(1)}, bf16[48,3840]{1,0:T(8,128)(2,1)}, u32[]{:S(2)}) copy-start(bf16[48,3840]{1,0:T(8,128)(2,1)} %reduce-scatter.2.cloned.1.call-done) | copy-start | bytes 1105924
  172.0 5.1 %collective-permute-start.25 = (f32[40,768]{1,0:T(8,128)}, f32[40,768]{1,0:T(8,128)S(1)}, u32[]{:S(2)}, u32[]{:S(2)}) collective-permute-start(f32[40,768]{1,0:T(8,128)} %get-tuple-element.123.refs_6_), channel_id=1, source_target_pairs={{0,4},{2,6},{4,0},{6,2},{8,12},{10,14},{12,8},{14,10},{16,20},{18,... | collective-permute-start | bytes 368648 | tf_op jit(solution)/shard_map/ppermute | solution.py:788
  181.7 6.2 %copy-start.2 = (f32[72,768]{1,0:T(8,128)S(1)}, f32[72,768]{1,0:T(8,128)}, u32[]{:S(2)}) copy-start(f32[72,768]{1,0:T(8,128)} %get-tuple-element.124.here) | copy-start | bytes 663556
  181.7 12.0 %collective-permute-start.29 = (bf16[1,192,384]{2,1,0:T(8,128)(2,1)}, bf16[1,192,384]{2,1,0:T(8,128)(2,1)S(1)}, u32[]{:S(2)}, u32[]{:S(2)}) collective-permute-start(bf16[1,192,384]{2,1,0:T(8,128)(2,1)} %get-tuple-element.129.refs_2_), channel_id=1, source_target_pairs={{0,1},{1,0},{2,3},{3,2},{4,5},{5,4},{6,7},{7,6},{8,9},{9,8},{10,11... | collective-permute-start | bytes 442376 | tf_op jit(solution)/shard_map/ppermute | solution.py:796
  184.5 9.2 %copy-start.5 = (bf16[1,192,384]{2,1,0:T(8,128)(2,1)S(1)}, bf16[1,192,384]{2,1,0:T(8,128)(2,1)}, u32[]{:S(2)}) copy-start(bf16[1,192,384]{2,1,0:T(8,128)(2,1)} %get-tuple-element.129.refs_2_) | copy-start | bytes 442372
  184.5 7.3 %collective-permute-start.27 = (bf16[1,48,1152]{2,1,0:T(8,128)(2,1)}, bf16[1,48,1152]{2,1,0:T(8,128)(2,1)S(1)}, u32[]{:S(2)}, u32[]{:S(2)}) collective-permute-start(bf16[1,48,1152]{2,1,0:T(8,128)(2,1)} %get-tuple-element.127), channel_id=1, source_target_pairs={{0,16},{2,18},{4,20},{6,22},{8,24},{10,26},{12,28},{14,30},{16,0},... | collective-permute-start | bytes 331784 | tf_op jit(solution)/shard_map/ppermute | solution.py:788
  187.9 10.6 %collective-permute-start.26 = (f32[72,768]{1,0:T(8,128)S(1)}, f32[72,768]{1,0:T(8,128)S(1)}, u32[]{:S(2)}, u32[]{:S(2)}) collective-permute-start(f32[72,768]{1,0:T(8,128)S(1)} %copy-done.2), channel_id=1, source_target_pairs={{0,1},{1,0},{2,3},{3,2},{4,5},{5,4},{6,7},{7,6},{8,9},{9,8},{10,11... | collective-permute-start | bytes 663560 | tf_op jit(solution)/shard_map/ppermute | solution.py:796
  193.3 5.0 %copy-start.9 = (bf16[1,48,1152]{2,1,0:T(8,128)(2,1)S(1)}, bf16[1,48,1152]{2,1,0:T(8,128)(2,1)}, u32[]{:S(2)}) copy-start(bf16[1,48,1152]{2,1,0:T(8,128)(2,1)} %shard_map.250) | copy-start | bytes 331780
  193.3 5.0 %collective-permute-start.28 = (bf16[1,48,1152]{2,1,0:T(8,128)(2,1)}, bf16[1,48,1152]{2,1,0:T(8,128)(2,1)S(1)}, u32[]{:S(2)}, u32[]{:S(2)}) collective-permute-start(bf16[1,48,1152]{2,1,0:T(8,128)(2,1)} %shard_map.250), channel_id=1, source_target_pairs={{0,1},{1,0},{2,3},{3,2},{4,5},{5,4},{6,7},{7,6},{8,9},{9,8},{10,11... | collective-permute-start | bytes 331784 | tf_op jit(solution)/shard_map/ppermute | solution.py:796
  198.4 3.4 %copy-start.12 = (f32[48,2304]{1,0:T(8,128)}, f32[48,2304]{1,0:T(8,128)S(1)}, u32[]{:S(2)}) copy-start(f32[48,2304]{1,0:T(8,128)S(1)} %slice_dynamic-update-slice_fusion) | copy-start | bytes 1327108
Sparse Core Ops, SparseCore 0:
  77.0 87.3 reduce-scatter.1

commit v5 on v4

--- a/solution.py
+++ b/solution.py
@@ -384,18 +384,18 @@
         for arrival in arrivals:
             arrival.start()
 
-    for index in range(attend_steps):
-
-        @pl.when(step == index)
-        def _(index=index):
-            own_arrivals[index].wait()
-            peer_arrivals[index].wait()
-            departures[index].start()
-
     @pl.when(step < attend_steps)
     def _():
         value = rotate_lanes(dot(normed1[...], query_weight[...]), cosine[...], sine[...])
         query[...] = (value * (LOG2E * HD ** (-0.5))).astype(jnp.bfloat16)
+        for index in range(attend_steps):
+
+            @pl.when(step == index)
+            def _(index=index):
+                own_arrivals[index].wait()
+                peer_arrivals[index].wait()
+                departures[index].start()
+
         pairs = own_pairs.at[step], peer_pairs.at[step]
         in_range, found = attend_heads(query, *pairs, log_total, False)
         attended[...] = found
@@ -705,7 +705,7 @@
 ):
     width = here.shape[1]
     sequences = (here.shape[0] - 8) // 8
-    own_columns = ada_grad.shape[1]
+    own_columns = ada_grad.shape[0]
     sums = here[8 * sequences :, :] + there[8 * sequences :, :]
     first_gain[...] = sums[0, :]
     second_gain[...] = sums[1, :]
@@ -729,13 +729,13 @@
         ada_bias[part * width : (part + 1) * width] = total[part, :]
     turned = pltpu.roll(every[...], places[0], 1)[:, : -(-own_columns // 128) * 128]
     grad = lax.dot_general(
+        turned,
         jnp.concatenate(conds, axis=0),
-        turned,
         (((0,), (0,)), ((), ())),
         precision=highest,
         preferred_element_type=jnp.float32,
     )
-    ada_grad[...] = grad[:, :own_columns]
+    ada_grad[...] = grad[:own_columns, :]
     own = jnp.where(places[1] == 1, here[:8, :], there[:8, :])
     products = ada_weight[:, :width].astype(jnp.float32) * own[0:1, :]
     for part in range(1, 6):
@@ -768,7 +768,7 @@
             shaped((hidden,), kind),
             shaped((width,), kind),
             shaped((all_columns,), kind),
-            shaped((ada_weight.shape[0], own_columns), kind),
+            shaped((own_columns, ada_weight.shape[0]), kind),
             shaped((1, ada_weight.shape[0]), kind),
         ],
         scratch_shapes=[pltpu.VMEM((2 * sequences, all_columns), kind)],
@@ -1063,7 +1063,7 @@
     d_query, away_keys, away_values = attend_back(query, peer_pair, d_attended, attended, log_total)
     after = ()
     if by_steps:
-        (down,), sent = stage(4, [([down], "half")], (away_keys,))
+        (down,), sent = stage(2, [([down], "half")], (away_keys,))
         after = (sent,)
     peer_keys, peer_values = swap_cores(away_keys), swap_cores(away_values)
     d_query, d_keys, d_values = attend_back(
@@ -1078,8 +1078,8 @@
             Flow(swap_cores(blocks(send)), blocks(keep))
             for keep, send in zip(qkv_parts[::2], qkv_parts[1::2])
         ]
-        (late,), *sent = stage(4, [(late, "half")])
-        (down, mixed), *sent = stage(4, [([down], (bits[1], 1))], sent, relay=mixed)
+        (late,), *sent = stage(2, [(late, "half")])
+        (down, mixed), *sent = stage(2, [([down], (bits[1], 1))], sent, relay=mixed)
     tokens_grad, small = tokens_back(
         d_projected, attn_qkv, tokens, d_middle, mods, sums2, up_bias_grad, sent
     )
@@ -1110,8 +1110,9 @@
         (late,) = next_stage([([late], "sum")], 1, 0)
         (
             first_gain_grad, second_gain_grad, all_up_bias_grad, down_bias_grad, ada_bias_grad,
-            ada_weight_grad, cond_grad,
+            ada_turned, cond_grad,
         ) = finish(small, last, own_embedded, ada_weight, hidden)
+        ada_weight_grad = ada_turned.T
         (down_rows,) = joined(down, (width // 2,))
         qkv_rows = jnp.concatenate(joined(late, (width // 2,) * 3), axis=1)
     else:

time: 210 us -> 210 us (level)
  Pallas kernels: 106 us -> 103 us
  waiting for transfers between devices: 27.1 us -> 29.5 us
    pallas_call x13, Pallas kernels: 105 us -> 101 us  [run(): return call(*placed)]
    ppermute x6, waiting for transfers between devices: 4.65 us -> 7.06 us  [swap_seq(): return lax.ppermute(block, 'seq', [(0, 1), (1, 0)])]
    reduce_scatter x1, waiting for transfers between devices: 6.1 us -> 8.36 us  [per_device(): up_rows = lax.psum_scatter(up_grad, 'dp', scatter_dimension=0, tiled=True)]
    ppermute x19, waiting for transfers between devices: 16.3 us -> 14.1 us  [swap_bit(): lax.ppermute(block, 'dp', [(i, i ^ bit) for i in range(lax.axis_size('dp'...]
  transfers between devices with their start and end apart: 31 -> 31, of which waited for: 14 -> 12; matrix products, arithmetic and copies ran while one was open for 6% -> 6% of each run, Pallas kernels for 30% -> 29%
where the time goes in v5:
time: 210 us; the launch traced here: 209 us
  Pallas kernels  103 us (49%)
  starting transfers between devices  43.4 us (21%)
  waiting for transfers between devices  29.5 us (14%)
  between operations  17.1 us (8%)
  other arithmetic  8.18 us (4%)
  local copies, waits for them, and re-layouts  6.53 us (3%)
    pallas_call x13, Pallas kernels, run(): return call(*placed)  101 us
    ppermute x19, starting transfers between devices, swap_bit(): lax.ppermute(block, 'dp', [(i, i ^ bit) for i in range(lax.axis_size('dp'...  21.7 us
    ppermute x5, starting transfers between devices, swap_halves(): return lax.ppermute(block, ('dp', 'seq'), perm)  14.8 us
    ppermute x19, waiting for transfers between devices, swap_bit(): lax.ppermute(block, 'dp', [(i, i ^ bit) for i in range(lax.axis_size('dp'...  14.1 us
    reduce_scatter x1, waiting for transfers between devices, per_device(): up_rows = lax.psum_scatter(up_grad, 'dp', scatter_dimension=0, tiled=True)  8.36 us
    ppermute x6, waiting for transfers between devices, swap_seq(): return lax.ppermute(block, 'seq', [(0, 1), (1, 0)])  7.06 us
    ppermute x6, starting transfers between devices, swap_seq(): return lax.ppermute(block, 'seq', [(0, 1), (1, 0)])  6.85 us
  transfers between devices with their start and end apart: 31, of which 12 were waited for; matrix products, arithmetic and copies ran while one was open for 6% of the time, Pallas kernels for 29%

profile of v5, /device:TPU:0, one launch (start us, length us, event | category | flops | bytes accessed | tf_op | source)
XLA Modules:
  0.0 208.5 jit_solution(1502265207666911045)
XLA Ops:
  7.2 2.0 collective-permute-start.1
  9.3 1.8 collective-permute-start
  11.0 1.8 collective-permute-start.5
  13.5 0.7 reshape.91
  14.2 0.7 reshape.92
  14.9 1.0 fusion.4
  15.9 1.3 pad_maximum_fusion.1
  19.3 0.8 constant_dynamic-slice_fusion
  20.0 0.6 convolution_reduce_fusion
  20.7 1.3 concatenate.15.mods
  22.0 6.8 %shard_map.237 = (bf16[512,768]{1,0:T(8,128)(2,1)}, bf16[512,1536]{1,0:T(8,128)(2,1)}, bf16[512,512]{1,0:T(8,128)(2,1)}, bf16[512,512]{1,0:T(8,128)(2,1)}, bf16[512,512]{1,0:T(8,128)(2,1)}) custom-call(bf16[512,768]{1,0:T(8,128)(2,1)S(1)} %collective-permute-done.tokens.refs_6_, f32[16,768]{1,0:T(8,128)} %concatenate.15.mods, bf16[768,2304]{1,0:T(8,128)(2,1)} %weight3.1, ...), custom_call_target="tpu_custom_call" | custom-call | flops 1 | bytes 1 | tf_op jit(solution)/shard_map/pallas_call | solution.py:93
  28.7 5.1 %collective-permute-start.2 = (bf16[512,512]{1,0:T(8,128)(2,1)}, bf16[512,512]{1,0:T(8,128)(2,1)S(1)}, u32[]{:S(2)}, u32[]{:S(2)}) collective-permute-start(bf16[512,512]{1,0:T(8,128)(2,1)} %get-tuple-element.75.refs_0_), channel_id=1, source_target_pairs={{0,2},{2,0},{4,6},{6,4},{8,10},{10,8},{12,14},{14,12},{16,18},{18,... | collective-permute-start | bytes 1572872 | tf_op jit(solution)/shard_map/ppermute | solution.py:788
  33.9 0.4 collective-permute-start.4
  34.4 0.6 broadcast_in_dim.55
  35.0 0.6 reshape.94.down_bias
  35.6 0.7 collective-permute-done.3.refs_4_
  36.3 0.7 collective-permute-done.4.refs_5_
  37.1 0.8 copy-done.10
  37.9 39.3 %shard_map.238 = (bf16[512,768]{1,0:T(8,128)(2,1)}, bf16[512,768]{1,0:T(8,128)(2,1)}, f32[3,4,512]{2,1,0:T(4,128)}, bf16[512,768]{1,0:T(8,128)(2,1)}, f32[512,76...) custom-call(s32[1]{0:T(128)} %bitcast.2.core, ...), custom_call_target="tpu_custom_call" | custom-call | flops 1 | bytes 1 | tf_op jit(solution)/shard_map/pallas_call | solution.py:93
  77.2 0.5 collective-permute-start.6
  77.7 11.1 %shard_map.239 = (f32[512,768]{1,0:T(8,128)}, bf16[512,768]{1,0:T(8,128)(2,1)}, bf16[512,768]{1,0:T(8,128)(2,1)}) custom-call(bf16[512,768]{1,0:T(8,128)(2,1)} %get-tuple-element.80.query, bf16[512,1536]{1,0:T(8,128)(2,1)} %get-tuple-element.81.pair, bf16[512,768]{1,0:T(8,128)(2,1)} %get-tuple-element.82.grad, bf16[512,768]{1,0:T(8,128)(2,1)} %get-tuple-element.83.attended, ...), custom_call_target="tpu_custom_call" | custom-call | flops 1 | bytes 1 | tf_op jit(solution)/shard_map/pallas_call | solution.py:93
  88.9 0.4 collective-permute-start.9
  89.3 4.0 %shard_map.240 = (bf16[8,192,384]{2,1,0:T(8,128)(2,1)}, bf16[8,192,384]{2,1,0:T(8,128)(2,1)}) custom-call(s32[1]{0:T(128)} %bitcast.1.mine, bf16[8,192,768]{2,1,0:T(8,128)(2,1)} %collective-permute-done.6.refs_0_, bf16[8,192,768]{2,1,0:T(8,128)(2,1)} %bitcast.41, bf16[512,768]{1,0:T(8,128)(2,1)} %get-tuple-element.85.refs_2_), custom_call_target="tpu_custom_call" | custom-call | flops 1 | bytes 1 | tf_op jit(solution)/shard_map/pallas_call | solution.py:93
  93.2 11.3 %shard_map.241 = (bf16[512,768]{1,0:T(8,128)(2,1)S(1)}, bf16[512,768]{1,0:T(8,128)(2,1)S(1)}, bf16[512,768]{1,0:T(8,128)(2,1)S(1)}) custom-call(bf16[512,768]{1,0:T(8,128)(2,1)} %get-tuple-element.80.query, bf16[512,1536]{1,0:T(8,128)(2,1)} %get-tuple-element.88.pair, bf16[512,768]{1,0:T(8,128)(2,1)} %get-tuple-element.82.grad, ...), custom_call_target="tpu_custom_call" | custom-call | flops 1 | bytes 1 | tf_op jit(solution)/shard_map/pallas_call | solution.py:93
  104.5 6.3 %shard_map.242 = (bf16[512,2304]{1,0:T(8,128)(2,1)}, bf16[384,768]{1,0:T(8,128)(2,1)}, bf16[384,768]{1,0:T(8,128)(2,1)}, bf16[384,768]{1,0:T(8,128)(2,1)}, bf16[...) custom-call(s32[1]{0:T(128)} %bitcast.2.core, ...), custom_call_target="tpu_custom_call" | custom-call | flops 1 | bytes 1 | tf_op jit(solution)/shard_map/pallas_call | solution.py:93
  110.8 0.5 collective-permute-start.11
  111.4 1.6 collective-permute-done.10.refs_0_
  113.0 0.8 collective-permute-done.11.refs_2_
  113.9 0.8 collective-permute-done.12.refs_4_
  114.7 2.6 %shard_map.243 = (bf16[8,48,1152]{2,1,0:T(8,128)(2,1)}, bf16[8,48,1152]{2,1,0:T(8,128)(2,1)}) custom-call(s32[1]{0:T(128)} %bitcast.1.mine, bf16[8,48,768]{2,1,0:T(8,128)(2,1)S(1)} %collective-permute-done.10.refs_0_, bf16[8,48,768]{2,1,0:T(8,128)(2,1)} %bitcast.43, bf16[8,48,768]{2,1,0:T(8,128)(2,1)S(1)} %collective-permute-done.11.refs_2_, ...), custom_call_target="tpu_custom_call" | custom-call | flops 1 | bytes 1 | tf_op jit(solution)/shard_map/pallas_call | solution.py:93
  117.3 2.0 collective-permute-start.15
  119.3 3.0 %collective-permute-done.7.refs_0_ = bf16[8,192,384]{2,1,0:T(8,128)(2,1)S(1)} collective-permute-done((bf16[8,192,384]{2,1,0:T(8,128)(2,1)}, bf16[8,192,384]{2,1,0:T(8,128)(2,1)S(1)}, u32[]{:S(2)}, u32[]{:S(2)}) %collective-permute-start.7) | collective-permute-done | bytes 1179680 | tf_op jit(solution)/shard_map/ppermute | solution.py:796
  122.3 2.9 %shard_map.244 = (bf16[4,192,384]{2,1,0:T(8,128)(2,1)}, bf16[4,192,384]{2,1,0:T(8,128)(2,1)}, bf16[512,768]{1,0:T(8,128)(2,1)}) custom-call(s32[1]{0:T(128)} %bitcast.mine, bf16[8,192,384]{2,1,0:T(8,128)(2,1)S(1)} %collective-permute-done.7.refs_0_, bf16[8,192,384]{2,1,0:T(8,128)(2,1)} %get-tuple-element.87.refs_1_, ...), custom_call_target="tpu_custom_call" | custom-call | flops 1 | bytes 1 | tf_op jit(solution)/shard_map/pallas_call | solution.py:93
  125.2 1.5 collective-permute-start.14
  126.7 8.0 %shard_map.245 = (bf16[512,768]{1,0:T(8,128)(2,1)}, f32[16,768]{1,0:T(8,128)}) custom-call(bf16[512,2304]{1,0:T(8,128)(2,1)} %get-tuple-element.106.d_projected, bf16[768,2304]{1,0:T(8,128)(2,1)} %weight3.1, bf16[768,2304]{1,0:T(8,128)(2,1)} %weight3.1, bf16[768,2304]{1,0:T(8,128)(2,1)} %weight3.1, bf16[512,768]{1,0:T(8,128)(2,1)} %copy-done, ...), custom_call_target="tpu_custom_call" | custom-call | flops 1 | bytes 1 | tf_op jit(solution)/shard_map/pallas_call | solution.py:93
  134.7 1.8 collective-permute-start.13
  136.5 0.8 add.65.refs_5_
  137.3 1.6 collective-permute-start.17
  139.0 2.6 %collective-permute-done.17.refs_6_ = f32[16,768]{1,0:T(8,128)S(1)} collective-permute-done((f32[16,768]{1,0:T(8,128)S(1)}, f32[16,768]{1,0:T(8,128)S(1)}, u32[]{:S(2)}, u32[]{:S(2)}) %collective-permute-start.17) | collective-permute-done | bytes 49184 | tf_op jit(solution)/shard_map/ppermute | solution.py:788
  141.7 3.4 %shard_map.246 = (bf16[2,192,384]{2,1,0:T(8,128)(2,1)}, bf16[2,192,384]{2,1,0:T(8,128)(2,1)}, bf16[4,48,1152]{2,1,0:T(8,128)(2,1)}, bf16[4,48,1152]{2,1,0:T(8,12...) custom-call(s32[2]{0:T(128)S(1)} %pad_add_fusion.mine, bf16[4,192,384]{2,1,0:T(8,128)(2,1)S(1)} %collective-permute-done.14.refs_0_, ...), custom_call_target="tpu_custom_call" | custom-call | flops 1 | bytes 1 | tf_op jit(solution)/shard_map/pallas_call | solution.py:93
  145.1 7.4 %collective-permute-start.18 = (bf16[512,768]{1,0:T(8,128)(2,1)}, bf16[512,768]{1,0:T(8,128)(2,1)}, u32[]{:S(2)}, u32[]{:S(2)}) collective-permute-start(bf16[512,768]{1,0:T(8,128)(2,1)} %get-tuple-element.112), channel_id=1, source_target_pairs={{0,0},{1,2},{2,1},{3,3},{4,4},{5,6},{6,5},{7,7},{8,8},{9,10},{10,9... | collective-permute-start | bytes 2359304 | tf_op jit(solution)/shard_map/ppermute | solution.py:784
  152.5 0.6 collective-permute-start.20
  153.1 1.5 collective-permute-start.19
  154.8 2.7 %collective-permute-start.21 = (f32[24,768]{1,0:T(8,128)}, f32[24,768]{1,0:T(8,128)S(1)}, u32[]{:S(2)}, u32[]{:S(2)}) collective-permute-start(f32[24,768]{1,0:T(8,128)} %get-tuple-element.117.refs_5_), channel_id=1, source_target_pairs={{0,16},{2,18},{4,20},{6,22},{8,24},{10,26},{12,28},{14,30},{16,0},... | collective-permute-start | bytes 221192 | tf_op jit(solution)/shard_map/ppermute | solution.py:788
  157.4 8.4 %reduce-scatter.2.cloned.1.call-done = bf16[48,3840]{1,0:T(8,128)(2,1)} async-done(((bf16[768,3840]{1,0:T(8,128)(2,1)}), bf16[48,3840]{1,0:T(8,128)(2,1)}) %reduce-scatter.2.cloned.1.call-update) | async-done | bytes 368656 | tf_op jit(solution)/shard_map/reduce_scatter | solution.py:1055
  165.8 1.9 collective-permute-start.24
  167.8 2.3 %shard_map.247 = (bf16[1,192,384]{2,1,0:T(8,128)(2,1)}, bf16[1,192,384]{2,1,0:T(8,128)(2,1)}, bf16[2,48,1152]{2,1,0:T(8,128)(2,1)}, bf16[2,48,1152]{2,1,0:T(8,128)(2,1)}, f32[40,768]{1,0:T(8,128)}) custom-call(s32[2]{0:T(128)S(1)} %pad_add_fusion.3.mine, bf16[2,192,384]{2,1,0:T(8,128)(2,1)S(1)} %collective-permute-done.19.refs_0_, ...), custom_call_target="tpu_custom_call" | custom-call | flops 1 | bytes 1 | tf_op jit(solution)/shard_map/pallas_call | solution.py:93
  170.0 3.1 %collective-permute-start.23 = (bf16[2,48,1152]{2,1,0:T(8,128)(2,1)}, bf16[2,48,1152]{2,1,0:T(8,128)(2,1)S(1)}, u32[]{:S(2)}, u32[]{:S(2)}) collective-permute-start(bf16[2,48,1152]{2,1,0:T(8,128)(2,1)} %get-tuple-element.120), channel_id=1, source_target_pairs={{0,8},{2,10},{4,12},{6,14},{8,0},{10,2},{12,4},{14,6},{16,24},{18,... | collective-permute-start | bytes 663560 | tf_op jit(solution)/shard_map/ppermute | solution.py:788
  173.2 0.8 collective-permute-start.22
  174.0 0.8 collective-permute-start.25
  174.8 2.4 %bitcast_convert_fusion = f32[1,512,768]{2,1,0:T(8,128)} fusion(bf16[512,768]{1,0:T(8,128)(2,1)} %collective-permute-done.18), kind=kLoop, calls=%fused_computation.1 | loop fusion | flops 393216 | bytes 2359296 | tf_op jit(solution)/shard_map/broadcast_in_dim | solution.py:1149
  177.2 1.9 collective-permute-done.25.refs_7_
  179.1 1.2 collective-permute-done.22.refs_0_
  180.3 2.0 shard_map.248
  182.4 2.9 %collective-permute-start.29 = (bf16[1,192,384]{2,1,0:T(8,128)(2,1)}, bf16[1,192,384]{2,1,0:T(8,128)(2,1)S(1)}, u32[]{:S(2)}, u32[]{:S(2)}) collective-permute-start(bf16[1,192,384]{2,1,0:T(8,128)(2,1)} %get-tuple-element.129.refs_2_), channel_id=1, source_target_pairs={{0,1},{1,0},{2,3},{3,2},{4,5},{5,4},{6,7},{7,6},{8,9},{9,8},{10,11... | collective-permute-start | bytes 442376 | tf_op jit(solution)/shard_map/ppermute | solution.py:796
  185.3 1.8 collective-permute-start.27
  187.2 0.9 slice.39
  188.0 0.7 slice.38
  188.8 3.5 %collective-permute-done.27.refs_0_ = bf16[1,48,1152]{2,1,0:T(8,128)(2,1)S(1)} collective-permute-done((bf16[1,48,1152]{2,1,0:T(8,128)(2,1)}, bf16[1,48,1152]{2,1,0:T(8,128)(2,1)S(1)}, u32[]{:S(2)}, u32[]{:S(2)}) %collective-permute-start.27) | collective-permute-done | bytes 110624 | tf_op jit(solution)/shard_map/ppermute | solution.py:788
  192.2 1.6 shard_map.250
  193.9 0.9 pad_maximum_fusion
  194.8 4.0 %collective-permute-done.28 = bf16[1,48,1152]{2,1,0:T(8,128)(2,1)S(1)} collective-permute-done((bf16[1,48,1152]{2,1,0:T(8,128)(2,1)}, bf16[1,48,1152]{2,1,0:T(8,128)(2,1)S(1)}, u32[]{:S(2)}, u32[]{:S(2)}) %collective-permute-start.28) | collective-permute-done | bytes 110624 | tf_op jit(solution)/shard_map/ppermute | solution.py:796
  198.9 1.8 shard_map.249
  200.8 0.9 copy.35
  (83 shorter events, 1.1 us)
Async XLA Ops:
  7.2 12.9 %copy-start.1 = (bf16[128,4608]{1,0:T(8,128)(2,1)S(1)}, bf16[128,4608]{1,0:T(8,128)(2,1)}, u32[]{:S(2)}) copy-start(bf16[128,4608]{1,0:T(8,128)(2,1)} %ada_weight.1) | copy-start | bytes 3538948
  7.2 158.6 %reduce-scatter.2.cloned.1.call-start = ((), (), s32[]{:S(2)}) async-start(), calls=%async_computation.1 | async-start | bytes 6266880 | tf_op jit(solution)/shard_map/reduce_scatter | solution.py:1055
  7.2 9.9 %collective-permute-start.1 = (s32[1]{0:T(128)}, s32[1]{0:T(128)}, u32[]{:S(2)}, u32[]{:S(2)}) collective-permute-start(s32[1]{0:T(128)} %param.16), channel_id=1, source_target_pairs={{0,0},{1,2},{2,1},{3,3},{4,4},{5,6},{6,5},{7,7},{8,8},{9,10},{10,9... | collective-permute-start | bytes 20 | tf_op jit(solution)/shard_map/ppermute | solution.py:784
  9.3 12.7 %collective-permute-start = (bf16[512,768]{1,0:T(8,128)(2,1)}, bf16[512,768]{1,0:T(8,128)(2,1)S(1)}, u32[]{:S(2)}, u32[]{:S(2)}) collective-permute-start(bf16[512,768]{1,0:T(8,128)(2,1)} %bitcast.47), channel_id=1, source_target_pairs={{0,0},{1,2},{2,1},{3,3},{4,4},{5,6},{6,5},{7,7},{8,8},{9,10},{10,9... | collective-permute-start | bytes 2359304 | tf_op jit(solution)/shard_map/ppermute | solution.py:784
  11.0 24.5 %collective-permute-start.5 = (bf16[512,768]{1,0:T(8,128)(2,1)}, bf16[512,768]{1,0:T(8,128)(2,1)S(1)}, u32[]{:S(2)}, u32[]{:S(2)}) collective-permute-start(bf16[512,768]{1,0:T(8,128)(2,1)} %bitcast.48), channel_id=1, source_target_pairs={{0,0},{1,2},{2,1},{3,3},{4,4},{5,6},{6,5},{7,7},{8,8},{9,10},{10,9... | collective-permute-start | bytes 2359304 | tf_op jit(solution)/shard_map/ppermute | solution.py:784
  14.9 5.7 %copy-start.15 = (bf16[4608]{0:T(1024)(128)(2,1)S(1)}, bf16[4608]{0:T(1024)(128)(2,1)}, u32[]{:S(2)}) copy-start(bf16[4608]{0:T(1024)(128)(2,1)} %param.27) | copy-start | bytes 27652
  21.9 6.8 %copy-start = (bf16[512,768]{1,0:T(8,128)(2,1)}, bf16[512,768]{1,0:T(8,128)(2,1)S(1)}, u32[]{:S(2)}) copy-start(bf16[512,768]{1,0:T(8,128)(2,1)S(1)} %collective-permute-done.tokens.refs_6_) | copy-start | bytes 2359300
  22.0 12.4 %copy-start.16 = (bf16[3072]{0:T(1024)(128)(2,1)S(1)}, bf16[3072]{0:T(1024)(128)(2,1)}, u32[]{:S(2)}) copy-start(bf16[3072]{0:T(1024)(128)(2,1)} %param.23) | copy-start | bytes 18436
  22.0 13.0 %copy-start.17 = (bf16[768]{0:T(1024)(128)(2,1)S(1)}, bf16[768]{0:T(1024)(128)(2,1)}, u32[]{:S(2)}) copy-start(bf16[768]{0:T(1024)(128)(2,1)} %param.25) | copy-start | bytes 4612
  28.7 6.9 %collective-permute-start.2 = (bf16[512,512]{1,0:T(8,128)(2,1)}, bf16[512,512]{1,0:T(8,128)(2,1)S(1)}, u32[]{:S(2)}, u32[]{:S(2)}) collective-permute-start(bf16[512,512]{1,0:T(8,128)(2,1)} %get-tuple-element.75.refs_0_), channel_id=1, source_target_pairs={{0,2},{2,0},{4,6},{6,4},{8,10},{10,8},{12,14},{14,12},{16,18},{18,... | collective-permute-start | bytes 1572872 | tf_op jit(solution)/shard_map/ppermute | solution.py:788
  33.8 2.5 %collective-permute-start.3 = (bf16[512,512]{1,0:T(8,128)(2,1)}, bf16[512,512]{1,0:T(8,128)(2,1)S(1)}, u32[]{:S(2)}, u32[]{:S(2)}) collective-permute-start(bf16[512,512]{1,0:T(8,128)(2,1)} %get-tuple-element.76.refs_1_), channel_id=1, source_target_pairs={{0,2},{2,0},{4,6},{6,4},{8,10},{10,8},{12,14},{14,12},{16,18},{18,... | collective-permute-start | bytes 1572872 | tf_op jit(solution)/shard_map/ppermute | solution.py:788
  33.9 3.2 %collective-permute-start.4 = (bf16[512,512]{1,0:T(8,128)(2,1)}, bf16[512,512]{1,0:T(8,128)(2,1)S(1)}, u32[]{:S(2)}, u32[]{:S(2)}) collective-permute-start(bf16[512,512]{1,0:T(8,128)(2,1)} %get-tuple-element.77.refs_2_), channel_id=1, source_target_pairs={{0,2},{2,0},{4,6},{6,4},{8,10},{10,8},{12,14},{14,12},{16,18},{18,... | collective-permute-start | bytes 1572872 | tf_op jit(solution)/shard_map/ppermute | solution.py:788
  35.5 1.5 copy-start.4
  35.6 1.5 copy-start.8
  36.3 0.8 copy-start.9
  37.1 0.8 copy-start.10
  77.2 12.1 %collective-permute-start.6 = (bf16[8,192,768]{2,1,0:T(8,128)(2,1)}, bf16[8,192,768]{2,1,0:T(8,128)(2,1)}, u32[]{:S(2)}, u32[]{:S(2)}) collective-permute-start(bf16[8,192,768]{2,1,0:T(8,128)(2,1)} %bitcast.9), channel_id=1, source_target_pairs={{0,2},{2,0},{4,6},{6,4},{8,10},{10,8},{12,14},{14,12},{16,18},{18,... | collective-permute-start | bytes 7077896 | tf_op jit(solution)/shard_map/ppermute | solution.py:788
  88.8 15.8 %collective-permute-start.8 = (bf16[512,768]{1,0:T(8,128)(2,1)}, bf16[512,768]{1,0:T(8,128)(2,1)S(1)}, u32[]{:S(2)}, u32[]{:S(2)}) collective-permute-start(bf16[512,768]{1,0:T(8,128)(2,1)} %get-tuple-element.85.refs_2_), channel_id=1, source_target_pairs={{0,2},{2,0},{4,6},{6,4},{8,10},{10,8},{12,14},{14,12},{16,18},{18,... | collective-permute-start | bytes 2359304 | tf_op jit(solution)/shard_map/ppermute | solution.py:788
  88.9 15.7 %collective-permute-start.9 = (bf16[512,768]{1,0:T(8,128)(2,1)}, bf16[512,768]{1,0:T(8,128)(2,1)}, u32[]{:S(2)}, u32[]{:S(2)}) collective-permute-start(bf16[512,768]{1,0:T(8,128)(2,1)} %get-tuple-element.93), channel_id=1, source_target_pairs={{0,2},{2,0},{4,6},{6,4},{8,10},{10,8},{12,14},{14,12},{16,18},{18,... | collective-permute-start | bytes 2359304 | tf_op jit(solution)/shard_map/ppermute | solution.py:788
  93.2 29.0 %collective-permute-start.7 = (bf16[8,192,384]{2,1,0:T(8,128)(2,1)}, bf16[8,192,384]{2,1,0:T(8,128)(2,1)S(1)}, u32[]{:S(2)}, u32[]{:S(2)}) collective-permute-start(bf16[8,192,384]{2,1,0:T(8,128)(2,1)} %get-tuple-element.86.refs_3_), channel_id=1, source_target_pairs={{0,1},{1,0},{2,3},{3,2},{4,5},{5,4},{6,7},{7,6},{8,9},{9,8},{10,11... | collective-permute-start | bytes 3538952 | tf_op jit(solution)/shard_map/ppermute | solution.py:796
  110.8 2.2 %collective-permute-start.10 = (bf16[8,48,768]{2,1,0:T(8,128)(2,1)}, bf16[8,48,768]{2,1,0:T(8,128)(2,1)S(1)}, u32[]{:S(2)}, u32[]{:S(2)}) collective-permute-start(bf16[8,48,768]{2,1,0:T(8,128)(2,1)} %bitcast.51), channel_id=1, source_target_pairs={{0,2},{2,0},{4,6},{6,4},{8,10},{10,8},{12,14},{14,12},{16,18},{18,... | collective-permute-start | bytes 1769480 | tf_op jit(solution)/shard_map/ppermute | solution.py:788
  110.8 3.1 %collective-permute-start.11 = (bf16[8,48,768]{2,1,0:T(8,128)(2,1)}, bf16[8,48,768]{2,1,0:T(8,128)(2,1)S(1)}, u32[]{:S(2)}, u32[]{:S(2)}) collective-permute-start(bf16[8,48,768]{2,1,0:T(8,128)(2,1)} %bitcast.50), channel_id=1, source_target_pairs={{0,2},{2,0},{4,6},{6,4},{8,10},{10,8},{12,14},{14,12},{16,18},{18,... | collective-permute-start | bytes 1769480 | tf_op jit(solution)/shard_map/ppermute | solution.py:788
  111.3 3.4 %collective-permute-start.12 = (bf16[8,48,768]{2,1,0:T(8,128)(2,1)}, bf16[8,48,768]{2,1,0:T(8,128)(2,1)S(1)}, u32[]{:S(2)}, u32[]{:S(2)}) collective-permute-start(bf16[8,48,768]{2,1,0:T(8,128)(2,1)} %bitcast.49), channel_id=1, source_target_pairs={{0,2},{2,0},{4,6},{6,4},{8,10},{10,8},{12,14},{14,12},{16,18},{18,... | collective-permute-start | bytes 1769480 | tf_op jit(solution)/shard_map/ppermute | solution.py:788
  117.3 24.4 %collective-permute-start.15 = (bf16[8,48,1152]{2,1,0:T(8,128)(2,1)}, bf16[8,48,1152]{2,1,0:T(8,128)(2,1)}, u32[]{:S(2)}, u32[]{:S(2)}) collective-permute-start(bf16[8,48,1152]{2,1,0:T(8,128)(2,1)} %get-tuple-element.100.refs_2_), channel_id=1, source_target_pairs={{0,1},{1,0},{2,3},{3,2},{4,5},{5,4},{6,7},{7,6},{8,9},{9,8},{10,11... | collective-permute-start | bytes 2654216 | tf_op jit(solution)/shard_map/ppermute | solution.py:796
  122.3 4.4 %copy-start.3 = (f32[1,3072]{1,0:T(1,128)S(1)}, f32[1,3072]{1,0:T(1,128)}, u32[]{:S(2)}) copy-start(f32[1,3072]{1,0:T(1,128)} %get-tuple-element.109.bias_grad) | copy-start | bytes 36868
  125.2 16.5 %collective-permute-start.14 = (bf16[4,192,384]{2,1,0:T(8,128)(2,1)}, bf16[4,192,384]{2,1,0:T(8,128)(2,1)S(1)}, u32[]{:S(2)}, u32[]{:S(2)}) collective-permute-start(bf16[4,192,384]{2,1,0:T(8,128)(2,1)} %get-tuple-element.103.refs_0_.refs_4_), channel_id=1, source_target_pairs={{0,4},{2,6},{4,0},{6,2},{8,12},{10,14},{12,8},{14,10},{16,20},{18,... | collective-permute-start | bytes 1769480 | tf_op jit(solution)/shard_map/ppermute | solution.py:788
  134.7 1.8 collective-permute-start.16
  134.7 22.7 %collective-permute-start.13 = (bf16[512,768]{1,0:T(8,128)(2,1)}, bf16[512,768]{1,0:T(8,128)(2,1)S(1)}, u32[]{:S(2)}, u32[]{:S(2)}) collective-permute-start(bf16[512,768]{1,0:T(8,128)(2,1)} %get-tuple-element.102), channel_id=1, source_target_pairs={{0,0},{1,2},{2,1},{3,3},{4,4},{5,6},{6,5},{7,7},{8,8},{9,10},{10,9... | collective-permute-start | bytes 2359304 | tf_op jit(solution)/shard_map/ppermute | solution.py:784
  137.3 4.3 %copy-start.13 = (f32[16,768]{1,0:T(8,128)}, f32[16,768]{1,0:T(8,128)S(1)}, u32[]{:S(2)}) copy-start(f32[16,768]{1,0:T(8,128)S(1)} %add.65.refs_5_) | copy-start | bytes 147460
  137.3 4.3 %collective-permute-start.17 = (f32[16,768]{1,0:T(8,128)S(1)}, f32[16,768]{1,0:T(8,128)S(1)}, u32[]{:S(2)}, u32[]{:S(2)}) collective-permute-start(f32[16,768]{1,0:T(8,128)S(1)} %add.65.refs_5_), channel_id=1, source_target_pairs={{0,8},{2,10},{4,12},{6,14},{8,0},{10,2},{12,4},{14,6},{16,24},{18,... | collective-permute-start | bytes 147464 | tf_op jit(solution)/shard_map/ppermute | solution.py:788
  145.1 29.7 %collective-permute-start.18 = (bf16[512,768]{1,0:T(8,128)(2,1)}, bf16[512,768]{1,0:T(8,128)(2,1)}, u32[]{:S(2)}, u32[]{:S(2)}) collective-permute-start(bf16[512,768]{1,0:T(8,128)(2,1)} %get-tuple-element.112), channel_id=1, source_target_pairs={{0,0},{1,2},{2,1},{3,3},{4,4},{5,6},{6,5},{7,7},{8,8},{9,10},{10,9... | collective-permute-start | bytes 2359304 | tf_op jit(solution)/shard_map/ppermute | solution.py:784
  152.5 15.2 %collective-permute-start.20 = (bf16[4,48,1152]{2,1,0:T(8,128)(2,1)}, bf16[4,48,1152]{2,1,0:T(8,128)(2,1)S(1)}, u32[]{:S(2)}, u32[]{:S(2)}) collective-permute-start(bf16[4,48,1152]{2,1,0:T(8,128)(2,1)} %get-tuple-element.115), channel_id=1, source_target_pairs={{0,4},{2,6},{4,0},{6,2},{8,12},{10,14},{12,8},{14,10},{16,20},{18,... | collective-permute-start | bytes 1327112 | tf_op jit(solution)/shard_map/ppermute | solution.py:788
  153.1 14.6 %collective-permute-start.19 = (bf16[2,192,384]{2,1,0:T(8,128)(2,1)}, bf16[2,192,384]{2,1,0:T(8,128)(2,1)S(1)}, u32[]{:S(2)}, u32[]{:S(2)}) collective-permute-start(bf16[2,192,384]{2,1,0:T(8,128)(2,1)} %get-tuple-element.113.refs_4_), channel_id=1, source_target_pairs={{0,8},{2,10},{4,12},{6,14},{8,0},{10,2},{12,4},{14,6},{16,24},{18,... | collective-permute-start | bytes 884744 | tf_op jit(solution)/shard_map/ppermute | solution.py:788
  154.8 13.0 %collective-permute-start.21 = (f32[24,768]{1,0:T(8,128)}, f32[24,768]{1,0:T(8,128)S(1)}, u32[]{:S(2)}, u32[]{:S(2)}) collective-permute-start(f32[24,768]{1,0:T(8,128)} %get-tuple-element.117.refs_5_), channel_id=1, source_target_pairs={{0,16},{2,18},{4,20},{6,22},{8,24},{10,26},{12,28},{14,30},{16,0},... | collective-permute-start | bytes 221192 | tf_op jit(solution)/shard_map/ppermute | solution.py:788
  157.4 19.8 %copy-start.5 = (bf16[512,768]{1,0:T(8,128)(2,1)}, bf16[512,768]{1,0:T(8,128)(2,1)S(1)}, u32[]{:S(2)}) copy-start(bf16[512,768]{1,0:T(8,128)(2,1)S(1)} %collective-permute-done.13) | copy-start | bytes 2359300
  165.8 14.5 %collective-permute-start.24 = (bf16[48,3840]{1,0:T(8,128)(2,1)}, bf16[48,3840]{1,0:T(8,128)(2,1)S(1)}, u32[]{:S(2)}, u32[]{:S(2)}) collective-permute-start(bf16[48,3840]{1,0:T(8,128)(2,1)} %reduce-scatter.2.cloned.1.call-done), channel_id=1, source_target_pairs={{0,1},{1,0},{2,3},{3,2},{4,5},{5,4},{6,7},{7,6},{8,9},{9,8},{10,11... | collective-permute-start | bytes 1105928 | tf_op jit(solution)/shard_map/ppermute | solution.py:796
  170.0 10.3 %collective-permute-start.23 = (bf16[2,48,1152]{2,1,0:T(8,128)(2,1)}, bf16[2,48,1152]{2,1,0:T(8,128)(2,1)S(1)}, u32[]{:S(2)}, u32[]{:S(2)}) collective-permute-start(bf16[2,48,1152]{2,1,0:T(8,128)(2,1)} %get-tuple-element.120), channel_id=1, source_target_pairs={{0,8},{2,10},{4,12},{6,14},{8,0},{10,2},{12,4},{14,6},{16,24},{18,... | collective-permute-start | bytes 663560 | tf_op jit(solution)/shard_map/ppermute | solution.py:788
  173.2 7.1 %collective-permute-start.22 = (bf16[1,192,384]{2,1,0:T(8,128)(2,1)}, bf16[1,192,384]{2,1,0:T(8,128)(2,1)S(1)}, u32[]{:S(2)}, u32[]{:S(2)}) collective-permute-start(bf16[1,192,384]{2,1,0:T(8,128)(2,1)} %get-tuple-element.118.refs_4_), channel_id=1, source_target_pairs={{0,16},{2,18},{4,20},{6,22},{8,24},{10,26},{12,28},{14,30},{16,0},... | collective-permute-start | bytes 442376 | tf_op jit(solution)/shard_map/ppermute | solution.py:788
  174.0 13.1 %copy-start.12 = (bf16[48,3840]{1,0:T(8,128)(2,1)S(1)}, bf16[48,3840]{1,0:T(8,128)(2,1)}, u32[]{:S(2)}) copy-start(bf16[48,3840]{1,0:T(8,128)(2,1)} %reduce-scatter.2.cloned.1.call-done) | copy-start | bytes 1105924
  174.0 5.1 %collective-permute-start.25 = (f32[40,768]{1,0:T(8,128)}, f32[40,768]{1,0:T(8,128)S(1)}, u32[]{:S(2)}, u32[]{:S(2)}) collective-permute-start(f32[40,768]{1,0:T(8,128)} %get-tuple-element.123.refs_6_), channel_id=1, source_target_pairs={{0,4},{2,6},{4,0},{6,2},{8,12},{10,14},{12,8},{14,10},{16,20},{18,... | collective-permute-start | bytes 368648 | tf_op jit(solution)/shard_map/ppermute | solution.py:788
  182.4 6.4 %copy-start.2 = (f32[72,768]{1,0:T(8,128)S(1)}, f32[72,768]{1,0:T(8,128)}, u32[]{:S(2)}) copy-start(f32[72,768]{1,0:T(8,128)} %get-tuple-element.124.here) | copy-start | bytes 663556
  182.4 11.5 %collective-permute-start.29 = (bf16[1,192,384]{2,1,0:T(8,128)(2,1)}, bf16[1,192,384]{2,1,0:T(8,128)(2,1)S(1)}, u32[]{:S(2)}, u32[]{:S(2)}) collective-permute-start(bf16[1,192,384]{2,1,0:T(8,128)(2,1)} %get-tuple-element.129.refs_2_), channel_id=1, source_target_pairs={{0,1},{1,0},{2,3},{3,2},{4,5},{5,4},{6,7},{7,6},{8,9},{9,8},{10,11... | collective-permute-start | bytes 442376 | tf_op jit(solution)/shard_map/ppermute | solution.py:796
  185.3 8.6 %copy-start.7 = (bf16[1,192,384]{2,1,0:T(8,128)(2,1)S(1)}, bf16[1,192,384]{2,1,0:T(8,128)(2,1)}, u32[]{:S(2)}) copy-start(bf16[1,192,384]{2,1,0:T(8,128)(2,1)} %get-tuple-element.129.refs_2_) | copy-start | bytes 442372
  185.3 7.0 %collective-permute-start.27 = (bf16[1,48,1152]{2,1,0:T(8,128)(2,1)}, bf16[1,48,1152]{2,1,0:T(8,128)(2,1)S(1)}, u32[]{:S(2)}, u32[]{:S(2)}) collective-permute-start(bf16[1,48,1152]{2,1,0:T(8,128)(2,1)} %get-tuple-element.127), channel_id=1, source_target_pairs={{0,16},{2,18},{4,20},{6,22},{8,24},{10,26},{12,28},{14,30},{16,0},... | collective-permute-start | bytes 331784 | tf_op jit(solution)/shard_map/ppermute | solution.py:788
  188.7 10.2 %collective-permute-start.26 = (f32[72,768]{1,0:T(8,128)S(1)}, f32[72,768]{1,0:T(8,128)S(1)}, u32[]{:S(2)}, u32[]{:S(2)}) collective-permute-start(f32[72,768]{1,0:T(8,128)S(1)} %copy-done.2), channel_id=1, source_target_pairs={{0,1},{1,0},{2,3},{3,2},{4,5},{5,4},{6,7},{7,6},{8,9},{9,8},{10,11... | collective-permute-start | bytes 663560 | tf_op jit(solution)/shard_map/ppermute | solution.py:796
  193.8 5.0 %copy-start.11 = (bf16[1,48,1152]{2,1,0:T(8,128)(2,1)S(1)}, bf16[1,48,1152]{2,1,0:T(8,128)(2,1)}, u32[]{:S(2)}) copy-start(bf16[1,48,1152]{2,1,0:T(8,128)(2,1)} %shard_map.250) | copy-start | bytes 331780
  193.8 5.0 %collective-permute-start.28 = (bf16[1,48,1152]{2,1,0:T(8,128)(2,1)}, bf16[1,48,1152]{2,1,0:T(8,128)(2,1)S(1)}, u32[]{:S(2)}, u32[]{:S(2)}) collective-permute-start(bf16[1,48,1152]{2,1,0:T(8,128)(2,1)} %shard_map.250), channel_id=1, source_target_pairs={{0,1},{1,0},{2,3},{3,2},{4,5},{5,4},{6,7},{7,6},{8,9},{9,8},{10,11... | collective-permute-start | bytes 331784 | tf_op jit(solution)/shard_map/ppermute | solution.py:796
  194.7 6.0 %copy-start.6 = (bf16[512,768]{1,0:T(8,128)(2,1)S(1)}, bf16[512,768]{1,0:T(8,128)(2,1)}, u32[]{:S(2)}) copy-start(bf16[512,768]{1,0:T(8,128)(2,1)} %copy-done.5) | copy-start | bytes 2359300
  198.9 2.8 %copy-start.14 = (f32[48,2304]{1,0:T(8,128)}, f32[48,2304]{1,0:T(8,128)S(1)}, u32[]{:S(2)}) copy-start(f32[48,2304]{1,0:T(8,128)S(1)} %slice_dynamic-update-slice_fusion) | copy-start | bytes 1327108
Sparse Core Ops, SparseCore 0:
  77.3 88.4 reduce-scatter.1

commit v6 on v5

--- a/solution.py
+++ b/solution.py
@@ -145,7 +145,7 @@
 
 
 def key_value_body(
-    tokens, mods, key_weight, value_weight, cosine, sine, normed, every, *parts
+    tokens, mods, key_weight, value_weight, cosine, sine, normed, *parts
 ):
     step = pl.program_id(0)
 
@@ -158,7 +158,6 @@
     keys = rotate_lanes(dot(normed[...], key_weight[...]), cosine[...], sine[...])
     values = dot(normed[...], value_weight[...])
     both = jnp.concatenate([keys, values], axis=1).astype(jnp.bfloat16)
-    every[...] = both
     for index, part in enumerate(parts):
 
         @pl.when(step == index)
@@ -182,9 +181,8 @@
             full((rows, 128)),
             full((rows, 128)),
         ],
-        [full((rows, width)), columns(rows, 2 * lanes)] + [full((rows, 2 * lanes))] * steps,
-        [far((rows, width), low), far((rows, 2 * width), low)]
-        + [far((rows, 2 * lanes), low)] * steps,
+        [full((rows, width))] + [full((rows, 2 * lanes))] * steps,
+        [far((rows, width), low)] + [far((rows, 2 * lanes), low)] * steps,
         [],
         24,
     )(tokens, mods, weight, weight, cosine, sine, free=(tokens,))
@@ -253,7 +251,27 @@
     )
 
 
-def attend_back_body(second, query, pair, grad, attended, log_total, *refs):
+def attend_back_body(second, parts, query, grad, attended, log_total, *refs):
+    step = pl.program_id(0)
+    pairs, arrived = refs[-2:]
+    arrivals = [
+        pltpu.make_async_copy(refs[index], pairs.at[index], arrived.at[index])
+        for index in range(parts)
+    ]
+    refs = refs[parts:-2]
+
+    @pl.when(step == 0)
+    def _():
+        for arrival in arrivals:
+            arrival.start()
+
+    for index in range(parts):
+
+        @pl.when(step == index)
+        def _(index=index):
+            arrivals[index].wait()
+
+    pair = pairs.at[step]
     if second:
         before, cosine, sine = refs[:3]
     d_query, d_keys, d_values = refs[-3:]
@@ -295,7 +313,7 @@
         d_values[:, lanes] = (one[2] + two[2]).astype(jnp.bfloat16)
 
 
-def attend_back(query, pair, grad, attended, log_total, before=None, after=(), free=()):
+def attend_back(query, parts, grad, attended, log_total, before=None, after=(), free=()):
     rows, width = query.shape
     lanes = HEADS * HD
     steps = width // lanes
@@ -304,15 +322,15 @@
     extra = list(before) if second else []
     extra_specs = [block, full((rows, 128)), full((rows, 128))] if second else []
     return kernel_call(
-        functools.partial(attend_back_body, second),
+        functools.partial(attend_back_body, second, steps),
         steps,
         [
             block,
-            columns(rows, 2 * lanes),
             block,
             block,
             pl.BlockSpec((1, HEADS, rows), lambda step: (step, 0, 0)),
         ]
+        + [pl.BlockSpec(memory_space=pl.ANY)] * steps
         + extra_specs
         + [pl.BlockSpec(memory_space=pl.ANY)] * len(after),
         [block, block, block],
@@ -323,9 +341,12 @@
             far((rows, width), jnp.bfloat16),
             far((rows, width), jnp.bfloat16),
         ],
-        [],
-        28,
-    )(query, pair, grad, attended, log_total, *extra, *after, free=free)
+        [
+            pltpu.VMEM((steps, rows, 2 * lanes), jnp.bfloat16),
+            pltpu.SemaphoreType.DMA((steps,)),
+        ],
+        30,
+    )(query, grad, attended, log_total, *parts, *extra, *after, free=free)
 
 
 def block_body(
@@ -334,17 +355,16 @@
 ):
     pairs_far, refs = refs[: 2 * attend_steps], refs[2 * attend_steps :]
     (
-        tokens_far, cotangent_far, out_far, up_far, down_far,
+        tokens_far, cotangent_far, out_far, up_far, down_far, cotangent_own,
         query, attended, log_total, mixed, d_middle, d_attended, up_grad,
-        down_keep, down_send, bias_grad, sums, peer_far,
+        down_keep, down_send, bias_grad, sums,
         tokens, cotangent, out_weight, up_weight, down_weight, arrived,
-        own_pairs, peer_pairs, pair_arrived, left,
+        own_pairs, peer_pairs, pair_arrived,
         all_attended, normed, d_ffn, branch, middle, forward, back,
     ) = refs
     step = pl.program_id(0)
     tile = up_bias.shape[1]
-    lanes = 2 * HEADS * HD
-    own_arrivals, peer_arrivals, departures = [], [], []
+    own_arrivals, peer_arrivals = [], []
     for index in range(attend_steps):
         own_arrivals.append(
             pltpu.make_async_copy(
@@ -354,13 +374,6 @@
         peer_arrivals.append(
             pltpu.make_async_copy(
                 pairs_far[attend_steps + index], peer_pairs.at[index], pair_arrived.at[1, index]
-            )
-        )
-        departures.append(
-            pltpu.make_async_copy(
-                peer_pairs.at[index],
-                peer_far.at[:, pl.ds(index * lanes, lanes)],
-                left.at[index],
             )
         )
     arrivals = [
@@ -381,8 +394,17 @@
         for index in range(attend_steps):
             own_arrivals[index].start()
             peer_arrivals[index].start()
-        for arrival in arrivals:
-            arrival.start()
+        for index, arrival in enumerate(arrivals):
+            if index != 1:
+                arrival.start()
+
+        @pl.when(core[1] == 0)
+        def _():
+            arrivals[1].start()
+
+        @pl.when(core[1] == 1)
+        def _():
+            pltpu.make_async_copy(cotangent_own, cotangent, arrived.at[1]).start()
 
     @pl.when(step < attend_steps)
     def _():
@@ -394,7 +416,6 @@
             def _(index=index):
                 own_arrivals[index].wait()
                 peer_arrivals[index].wait()
-                departures[index].start()
 
         pairs = own_pairs.at[step], peer_pairs.at[step]
         in_range, found = attend_heads(query, *pairs, log_total, False)
@@ -415,8 +436,6 @@
     def _():
         for arrival in arrivals:
             arrival.wait()
-        for departure in departures:
-            departure.wait()
         turned = dot(all_attended[...], out_weight[...])
         branch[...] = turned.astype(jnp.bfloat16)
         value = tokens[...].astype(jnp.float32) + row(mods, GATE1) * turned
@@ -478,7 +497,7 @@
 
 def block_layer(
     core, normed1, qkv_weight, cosine, sine, mods, up_bias, down_bias, own, peer,
-    tokens, cotangent, out_weight, up_weight, down_weight,
+    tokens, cotangent, out_weight, up_weight, down_weight, cotangent_own,
 ):
     rows, width = tokens.shape
     hidden = up_weight.shape[1]
@@ -519,7 +538,7 @@
             pl.BlockSpec((1, tile), lambda step: (0, tiles(step))),
             full((1, width)),
         ]
-        + [far_spec] * (2 * attend_steps + 5),
+        + [far_spec] * (2 * attend_steps + 6),
         [
             heads(),
             heads(),
@@ -534,7 +553,6 @@
             down_spec,
             pl.BlockSpec((1, tile), lambda step: (0, tiles(step))),
             full((8, width)),
-            far_spec,
         ],
         [
             far((rows, width), low),
@@ -548,7 +566,6 @@
             far((hidden // 2, width), low),
             far((1, hidden), jnp.float32),
             far((8, width), jnp.float32),
-            far((rows, 2 * width), low),
         ],
         [
             pltpu.VMEM((rows, width), low),
@@ -560,7 +577,6 @@
             pltpu.VMEM((attend_steps, rows, 2 * lanes), low),
             pltpu.VMEM((attend_steps, rows, 2 * lanes), low),
             pltpu.SemaphoreType.DMA((2, attend_steps)),
-            pltpu.SemaphoreType.DMA((attend_steps,)),
             pltpu.VMEM((rows, width), low),
             pltpu.VMEM((rows, width), low),
             pltpu.VMEM((rows, width), low),
@@ -572,8 +588,8 @@
         58,
     )(
         core, normed1, qkv_weight, cosine, sine, mods, up_bias, down_bias, *own, *peer,
-        tokens, cotangent, out_weight, up_weight, down_weight,
-        free=(*peer, cotangent, tokens),
+        tokens, cotangent, out_weight, up_weight, down_weight, cotangent_own,
+        free=(cotangent, tokens),
     )
 
 
@@ -777,10 +793,12 @@
     )(jnp.stack([turn, same]), here, there, embedded, ada_weight)
 
 
-def swap_halves(block):
+def swap_halves(block, alone=True):
     count = lax.axis_size("dp") * lax.axis_size("seq")
     target = {1: 2, 2: 1}
     perm = [(i, i - i % 4 + target.get(i % 4, i % 4)) for i in range(count)]
+    if not alone:
+        perm = [(source, partner) for source, partner in perm if source != partner]
     return lax.ppermute(block, ("dp", "seq"), perm)
 
 
@@ -1026,7 +1044,8 @@
     cosine, sine = tables(positions)
     tokens = swap_halves(tokens[0])
     time_index = swap_halves(time_index)
-    cotangent = swap_halves(cotangent[0])
+    cotangent_own = cotangent[0]
+    cotangent = swap_halves(cotangent_own, alone=False)
     cond = jax.nn.silu(lax.dynamic_slice_in_dim(step_table, time_index[0], 1, axis=0))
     ada_float = ada_weight.astype(jnp.float32)
     modulation = jnp.dot(cond, ada_float, precision=highest) + ada_bias.astype(jnp.float32)
@@ -1036,17 +1055,17 @@
     mods = jnp.concatenate(
         [modulation.reshape(6, width), gain1[None], gain2[None], cond_row, jnp.zeros((7, width))]
     )
-    normed1, own_pair, *own_parts = project_key_value(tokens, mods, attn_qkv, cosine, sine)
+    normed1, *own_parts = project_key_value(tokens, mods, attn_qkv, cosine, sine)
     peer_parts = [swap_cores(part) for part in own_parts]
-    core_ref = core[None]
+    core_ref = jnp.stack([core, (lax.axis_index("seq") == core).astype(jnp.int32)])
     (
         query, attended, log_total, mixed, d_middle, d_attended, up_grad,
-        down_keep, down_send, up_bias_grad, sums2, peer_pair,
+        down_keep, down_send, up_bias_grad, sums2,
     ) = block_layer(
         core_ref, normed1, attn_qkv, cosine, sine, mods,
         up_bias.astype(jnp.float32)[None], down_bias.astype(jnp.float32)[None],
         own_parts, peer_parts,
-        tokens, cotangent, attn_out, mlp_up, mlp_down,
+        tokens, cotangent, attn_out, mlp_up, mlp_down, cotangent_own,
     )
     hidden = mlp_up.shape[1]
     dp_size = lax.axis_size("dp")
@@ -1060,14 +1079,14 @@
 
     if by_steps:
         down = Flow(swap_cores(blocks(down_send)), blocks(down_keep))
-    d_query, away_keys, away_values = attend_back(query, peer_pair, d_attended, attended, log_total)
+    d_query, away_keys, away_values = attend_back(query, peer_parts, d_attended, attended, log_total)
     after = ()
     if by_steps:
         (down,), sent = stage(2, [([down], "half")], (away_keys,))
         after = (sent,)
     peer_keys, peer_values = swap_cores(away_keys), swap_cores(away_values)
     d_query, d_keys, d_values = attend_back(
-        query, own_pair, d_attended, attended, log_total, (d_query, cosine, sine), after
+        query, own_parts, d_attended, attended, log_total, (d_query, cosine, sine), after
     )
     d_projected, *qkv_parts = projected_back(
         core_ref, d_query, d_keys, d_values, peer_keys, peer_values, normed1, cosine, sine

time: 210 us -> 209 us (level)
  waiting for transfers between devices: 29.5 us -> 22.5 us
  starting transfers between devices: 43.4 us -> 46.8 us
    reduce_scatter x1, waiting for transfers between devices: 8.36 us -> 4.45 us  [per_device(): up_rows = lax.psum_scatter(up_grad, 'dp', scatter_dimension=0, tiled=True)]
    ppermute x6, waiting for transfers between devices: 7.06 us -> 3.41 us  [swap_seq(): return lax.ppermute(block, 'seq', [(0, 1), (1, 0)])]
    ppermute x6, starting transfers between devices: 6.85 us -> 10.5 us  [swap_seq(): return lax.ppermute(block, 'seq', [(0, 1), (1, 0)])]
  transfers between devices with their start and end apart: 31 -> 31, of which waited for: 12 -> 13; matrix products, arithmetic and copies ran while one was open for 6% -> 7% of each run, Pallas kernels for 29% -> 29%
where the time goes in v6:
time: 209 us; the launch traced here: 208 us
  Pallas kernels  104 us (50%)
  starting transfers between devices  46.8 us (22%)
  waiting for transfers between devices  22.5 us (11%)
  between operations  16.7 us (8%)
  other arithmetic  8.87 us (4%)
  local copies, waits for them, and re-layouts  8.16 us (4%)
    pallas_call x13, Pallas kernels, run(): return call(*placed)  102 us
    ppermute x19, starting transfers between devices, swap_bit(): lax.ppermute(block, 'dp', [(i, i ^ bit) for i in range(lax.axis_size('dp'...  21.5 us
    ppermute x5, starting transfers between devices, swap_halves(): return lax.ppermute(block, ('dp', 'seq'), perm)  14.8 us
    ppermute x19, waiting for transfers between devices, swap_bit(): lax.ppermute(block, 'dp', [(i, i ^ bit) for i in range(lax.axis_size('dp'...  14.6 us
    ppermute x6, starting transfers between devices, swap_seq(): return lax.ppermute(block, 'seq', [(0, 1), (1, 0)])  10.5 us
    reduce_scatter x1, waiting for transfers between devices, per_device(): up_rows = lax.psum_scatter(up_grad, 'dp', scatter_dimension=0, tiled=True)  4.45 us
  transfers between devices with their start and end apart: 31, of which 13 were waited for; matrix products, arithmetic and copies ran while one was open for 7% of the time, Pallas kernels for 29%

profile of v6, /device:TPU:0, one launch (start us, length us, event | category | flops | bytes accessed | tf_op | source)
XLA Modules:
  0.0 207.8 jit_solution(7454833046080707417)
XLA Ops:
  7.2 1.9 collective-permute-start.1
  9.2 1.8 collective-permute-start
  10.9 1.6 collective-permute-start.5
  13.2 0.7 reshape.92
  13.9 0.7 reshape.93
  14.6 1.0 fusion.4
  15.6 1.3 pad_maximum_fusion.1
  18.6 0.8 constant_dynamic-slice_fusion
  19.3 0.6 convolution_reduce_fusion
  20.0 1.3 concatenate.15.mods
  21.3 6.5 %shard_map.237 = (bf16[512,768]{1,0:T(8,128)(2,1)}, bf16[512,512]{1,0:T(8,128)(2,1)}, bf16[512,512]{1,0:T(8,128)(2,1)}, bf16[512,512]{1,0:T(8,128)(2,1)}) custom-call(bf16[512,768]{1,0:T(8,128)(2,1)S(1)} %collective-permute-done.tokens.refs_6_, f32[16,768]{1,0:T(8,128)} %concatenate.15.mods, bf16[768,2304]{1,0:T(8,128)(2,1)} %weight3.1, ...), custom_call_target="tpu_custom_call" | custom-call | flops 1 | bytes 1 | tf_op jit(solution)/shard_map/pallas_call | solution.py:93
  27.7 5.4 %collective-permute-start.2 = (bf16[512,512]{1,0:T(8,128)(2,1)}, bf16[512,512]{1,0:T(8,128)(2,1)S(1)}, u32[]{:S(2)}, u32[]{:S(2)}) collective-permute-start(bf16[512,512]{1,0:T(8,128)(2,1)} %get-tuple-element.73.refs_0_), channel_id=1, source_target_pairs={{0,2},{2,0},{4,6},{6,4},{8,10},{10,8},{12,14},{14,12},{16,18},{18,... | collective-permute-start | bytes 1572872 | tf_op jit(solution)/shard_map/ppermute | solution.py:806
  33.6 0.6 reshape.95.down_bias
  34.2 0.6 broadcast_in_dim.51
  34.8 0.7 pad_add_fusion.core
  35.6 0.7 collective-permute-done.4.refs_5_.refs_2_
  36.5 0.7 copy-done.7
  37.1 39.2 %shard_map.238 = (bf16[512,768]{1,0:T(8,128)(2,1)}, bf16[512,768]{1,0:T(8,128)(2,1)}, f32[3,4,512]{2,1,0:T(4,128)}, bf16[512,768]{1,0:T(8,128)(2,1)}, f32[512,76...) custom-call(s32[2]{0:T(128)} %pad_add_fusion.core, ...), custom_call_target="tpu_custom_call" | custom-call | flops 1 | bytes 1 | tf_op jit(solution)/shard_map/pallas_call | solution.py:93
  76.4 1.6 copy-done.18
  78.4 12.1 %shard_map.239 = (f32[512,768]{1,0:T(8,128)}, bf16[512,768]{1,0:T(8,128)(2,1)}, bf16[512,768]{1,0:T(8,128)(2,1)}) custom-call(bf16[512,768]{1,0:T(8,128)(2,1)} %get-tuple-element.78.query, bf16[512,768]{1,0:T(8,128)(2,1)} %get-tuple-element.79.grad, bf16[512,768]{1,0:T(8,128)(2,1)} %get-tuple-element.80.attended, f32[3,4,512]{2,1,0:T(4,128)} %get-tuple-element.81.log_total, ...), custom_call_target="tpu_custom_call" | custom-call | flops 1 | bytes 1 | tf_op jit(solution)/shard_map/pallas_call | solution.py:93
  91.1 3.1 %shard_map.240 = (bf16[8,192,384]{2,1,0:T(8,128)(2,1)}, bf16[8,192,384]{2,1,0:T(8,128)(2,1)}) custom-call(s32[1]{0:T(128)} %bitcast.1.mine, bf16[8,192,768]{2,1,0:T(8,128)(2,1)S(1)} %collective-permute-done.6.refs_0_, bf16[8,192,768]{2,1,0:T(8,128)(2,1)} %bitcast.41, bf16[512,768]{1,0:T(8,128)(2,1)} %get-tuple-element.82.refs_2_), custom_call_target="tpu_custom_call" | custom-call | flops 1 | bytes 1 | tf_op jit(solution)/shard_map/pallas_call | solution.py:93
  94.2 12.2 %shard_map.241 = (bf16[512,768]{1,0:T(8,128)(2,1)S(1)}, bf16[512,768]{1,0:T(8,128)(2,1)S(1)}, bf16[512,768]{1,0:T(8,128)(2,1)S(1)}) custom-call(bf16[512,768]{1,0:T(8,128)(2,1)} %get-tuple-element.78.query, bf16[512,768]{1,0:T(8,128)(2,1)} %get-tuple-element.79.grad, bf16[512,768]{1,0:T(8,128)(2,1)} %get-tuple-element.80.attended, ...), custom_call_target="tpu_custom_call" | custom-call | flops 1 | bytes 1 | tf_op jit(solution)/shard_map/pallas_call | solution.py:93
  106.5 6.4 %shard_map.242 = (bf16[512,2304]{1,0:T(8,128)(2,1)}, bf16[384,768]{1,0:T(8,128)(2,1)}, bf16[384,768]{1,0:T(8,128)(2,1)}, bf16[384,768]{1,0:T(8,128)(2,1)}, bf16[...) custom-call(s32[2]{0:T(128)S(1)} %copy-done.4, ...), custom_call_target="tpu_custom_call" | custom-call | flops 1 | bytes 1 | tf_op jit(solution)/shard_map/pallas_call | solution.py:93
  112.9 0.5 collective-permute-start.11
  113.4 1.6 collective-permute-done.10.refs_0_
  115.0 0.8 collective-permute-done.11.refs_2_
  115.9 0.8 collective-permute-done.12.refs_4_
  116.7 2.6 %shard_map.243 = (bf16[8,48,1152]{2,1,0:T(8,128)(2,1)}, bf16[8,48,1152]{2,1,0:T(8,128)(2,1)}) custom-call(s32[1]{0:T(128)} %bitcast.1.mine, bf16[8,48,768]{2,1,0:T(8,128)(2,1)S(1)} %collective-permute-done.10.refs_0_, bf16[8,48,768]{2,1,0:T(8,128)(2,1)} %bitcast.45, bf16[8,48,768]{2,1,0:T(8,128)(2,1)S(1)} %collective-permute-done.11.refs_2_, ...), custom_call_target="tpu_custom_call" | custom-call | flops 1 | bytes 1 | tf_op jit(solution)/shard_map/pallas_call | solution.py:93
  119.3 2.2 %collective-permute-start.15 = (bf16[8,48,1152]{2,1,0:T(8,128)(2,1)}, bf16[8,48,1152]{2,1,0:T(8,128)(2,1)}, u32[]{:S(2)}, u32[]{:S(2)}) collective-permute-start(bf16[8,48,1152]{2,1,0:T(8,128)(2,1)} %get-tuple-element.96.refs_2_), channel_id=1, source_target_pairs={{0,1},{1,0},{2,3},{3,2},{4,5},{5,4},{6,7},{7,6},{8,9},{9,8},{10,11... | collective-permute-start | bytes 2654216 | tf_op jit(solution)/shard_map/ppermute | solution.py:814
  121.5 0.9 collective-permute-done.7.refs_0_
  122.4 2.9 %shard_map.244 = (bf16[4,192,384]{2,1,0:T(8,128)(2,1)}, bf16[4,192,384]{2,1,0:T(8,128)(2,1)}, bf16[512,768]{1,0:T(8,128)(2,1)}) custom-call(s32[1]{0:T(128)} %bitcast.mine, bf16[8,192,384]{2,1,0:T(8,128)(2,1)S(1)} %collective-permute-done.7.refs_0_, bf16[8,192,384]{2,1,0:T(8,128)(2,1)} %get-tuple-element.84.refs_1_, ...), custom_call_target="tpu_custom_call" | custom-call | flops 1 | bytes 1 | tf_op jit(solution)/shard_map/pallas_call | solution.py:93
  125.3 1.6 collective-permute-start.14
  126.9 8.1 %shard_map.245 = (bf16[512,768]{1,0:T(8,128)(2,1)}, f32[16,768]{1,0:T(8,128)}) custom-call(bf16[512,2304]{1,0:T(8,128)(2,1)} %get-tuple-element.102.d_projected, bf16[768,2304]{1,0:T(8,128)(2,1)} %weight3.1, bf16[768,2304]{1,0:T(8,128)(2,1)} %weight3.1, bf16[768,2304]{1,0:T(8,128)(2,1)} %weight3.1, bf16[512,768]{1,0:T(8,128)(2,1)} %copy-done, ...), custom_call_target="tpu_custom_call" | custom-call | flops 1 | bytes 1 | tf_op jit(solution)/shard_map/pallas_call | solution.py:93
  135.0 1.8 collective-permute-start.13
  136.8 0.8 add.65.refs_5_
  137.6 1.6 collective-permute-start.17
  139.4 2.6 %collective-permute-done.17.refs_6_ = f32[16,768]{1,0:T(8,128)S(1)} collective-permute-done((f32[16,768]{1,0:T(8,128)S(1)}, f32[16,768]{1,0:T(8,128)S(1)}, u32[]{:S(2)}, u32[]{:S(2)}) %collective-permute-start.17) | collective-permute-done | bytes 49184 | tf_op jit(solution)/shard_map/ppermute | solution.py:806
  142.0 3.4 %shard_map.246 = (bf16[2,192,384]{2,1,0:T(8,128)(2,1)}, bf16[2,192,384]{2,1,0:T(8,128)(2,1)}, bf16[4,48,1152]{2,1,0:T(8,128)(2,1)}, bf16[4,48,1152]{2,1,0:T(8,12...) custom-call(s32[2]{0:T(128)S(1)} %pad_add_fusion.1.mine, bf16[4,192,384]{2,1,0:T(8,128)(2,1)S(1)} %collective-permute-done.14.refs_0_, ...), custom_call_target="tpu_custom_call" | custom-call | flops 1 | bytes 1 | tf_op jit(solution)/shard_map/pallas_call | solution.py:93
  145.4 7.7 %collective-permute-start.18 = (bf16[512,768]{1,0:T(8,128)(2,1)}, bf16[512,768]{1,0:T(8,128)(2,1)}, u32[]{:S(2)}, u32[]{:S(2)}) collective-permute-start(bf16[512,768]{1,0:T(8,128)(2,1)} %get-tuple-element.108), channel_id=1, source_target_pairs={{0,0},{1,2},{2,1},{3,3},{4,4},{5,6},{6,5},{7,7},{8,8},{9,10},{10,9... | collective-permute-start | bytes 2359304 | tf_op jit(solution)/shard_map/ppermute | solution.py:802
  153.1 1.3 collective-permute-start.20
  154.5 1.7 collective-permute-start.19
  156.3 2.7 %collective-permute-start.21 = (f32[24,768]{1,0:T(8,128)}, f32[24,768]{1,0:T(8,128)S(1)}, u32[]{:S(2)}, u32[]{:S(2)}) collective-permute-start(f32[24,768]{1,0:T(8,128)} %get-tuple-element.113.refs_5_), channel_id=1, source_target_pairs={{0,16},{2,18},{4,20},{6,22},{8,24},{10,26},{12,28},{14,30},{16,0},... | collective-permute-start | bytes 221192 | tf_op jit(solution)/shard_map/ppermute | solution.py:806
  158.9 4.5 %reduce-scatter.2.cloned.1.call-done = bf16[48,3840]{1,0:T(8,128)(2,1)} async-done(((bf16[768,3840]{1,0:T(8,128)(2,1)}), bf16[48,3840]{1,0:T(8,128)(2,1)}) %reduce-scatter.2.cloned.1.call-update) | async-done | bytes 368656 | tf_op jit(solution)/shard_map/reduce_scatter | solution.py:1074
  163.4 2.0 collective-permute-start.24
  165.4 1.4 collective-permute-done.19.refs_0_
  166.8 2.3 %shard_map.247 = (bf16[1,192,384]{2,1,0:T(8,128)(2,1)}, bf16[1,192,384]{2,1,0:T(8,128)(2,1)}, bf16[2,48,1152]{2,1,0:T(8,128)(2,1)}, bf16[2,48,1152]{2,1,0:T(8,128)(2,1)}, f32[40,768]{1,0:T(8,128)}) custom-call(s32[2]{0:T(128)S(1)} %pad_add_fusion.4.mine, bf16[2,192,384]{2,1,0:T(8,128)(2,1)S(1)} %collective-permute-done.19.refs_0_, ...), custom_call_target="tpu_custom_call" | custom-call | flops 1 | bytes 1 | tf_op jit(solution)/shard_map/pallas_call | solution.py:93
  169.1 1.4 collective-permute-start.25
  170.5 1.0 collective-permute-start.22
  171.5 1.4 collective-permute-start.23
  173.0 2.4 %bitcast_convert_fusion = f32[1,512,768]{2,1,0:T(8,128)} fusion(bf16[512,768]{1,0:T(8,128)(2,1)} %collective-permute-done.18), kind=kLoop, calls=%fused_computation.1 | loop fusion | flops 393216 | bytes 2359296 | tf_op jit(solution)/shard_map/broadcast_in_dim | solution.py:1168
  175.4 4.4 %collective-permute-done.22.refs_0_ = bf16[1,192,384]{2,1,0:T(8,128)(2,1)S(1)} collective-permute-done((bf16[1,192,384]{2,1,0:T(8,128)(2,1)}, bf16[1,192,384]{2,1,0:T(8,128)(2,1)S(1)}, u32[]{:S(2)}, u32[]{:S(2)}) %collective-permute-start.22) | collective-permute-done | bytes 147488 | tf_op jit(solution)/shard_map/ppermute | solution.py:806
  179.7 1.2 collective-permute-done.23.refs_2_
  180.9 2.0 shard_map.248
  182.9 1.3 collective-permute-start.27
  184.2 2.8 %collective-permute-start.29 = (bf16[1,192,384]{2,1,0:T(8,128)(2,1)}, bf16[1,192,384]{2,1,0:T(8,128)(2,1)S(1)}, u32[]{:S(2)}, u32[]{:S(2)}) collective-permute-start(bf16[1,192,384]{2,1,0:T(8,128)(2,1)} %get-tuple-element.125.refs_2_), channel_id=1, source_target_pairs={{0,1},{1,0},{2,3},{3,2},{4,5},{5,4},{6,7},{7,6},{8,9},{9,8},{10,11... | collective-permute-start | bytes 442376 | tf_op jit(solution)/shard_map/ppermute | solution.py:814
  187.1 0.7 slice.38
  187.8 0.9 slice.39
  188.7 0.9 collective-permute-done.27.refs_0_
  189.6 1.6 shard_map.250
  191.1 3.5 %collective-permute-start.28 = (bf16[1,48,1152]{2,1,0:T(8,128)(2,1)}, bf16[1,48,1152]{2,1,0:T(8,128)(2,1)S(1)}, u32[]{:S(2)}, u32[]{:S(2)}) collective-permute-start(bf16[1,48,1152]{2,1,0:T(8,128)(2,1)} %shard_map.250), channel_id=1, source_target_pairs={{0,1},{1,0},{2,3},{3,2},{4,5},{5,4},{6,7},{7,6},{8,9},{9,8},{10,11... | collective-permute-start | bytes 331784 | tf_op jit(solution)/shard_map/ppermute | solution.py:814
  194.7 0.9 pad_maximum_fusion
  195.5 2.5 %collective-permute-done.28 = bf16[1,48,1152]{2,1,0:T(8,128)(2,1)S(1)} collective-permute-done((bf16[1,48,1152]{2,1,0:T(8,128)(2,1)}, bf16[1,48,1152]{2,1,0:T(8,128)(2,1)S(1)}, u32[]{:S(2)}, u32[]{:S(2)}) %collective-permute-start.28) | collective-permute-done | bytes 110624 | tf_op jit(solution)/shard_map/ppermute | solution.py:814
  198.2 1.8 shard_map.249
  200.1 0.9 copy.35
  (86 shorter events, 2.6 us)
Async XLA Ops:
  7.2 12.2 %copy-start.1 = (bf16[128,4608]{1,0:T(8,128)(2,1)S(1)}, bf16[128,4608]{1,0:T(8,128)(2,1)}, u32[]{:S(2)}) copy-start(bf16[128,4608]{1,0:T(8,128)(2,1)} %ada_weight.1) | copy-start | bytes 3538948
  7.2 156.2 %reduce-scatter.2.cloned.1.call-start = ((), (), s32[]{:S(2)}) async-start(), calls=%async_computation.1 | async-start | bytes 6266880 | tf_op jit(solution)/shard_map/reduce_scatter | solution.py:1074
  7.2 9.6 %collective-permute-start.1 = (s32[1]{0:T(128)}, s32[1]{0:T(128)}, u32[]{:S(2)}, u32[]{:S(2)}) collective-permute-start(s32[1]{0:T(128)} %param.16), channel_id=1, source_target_pairs={{0,0},{1,2},{2,1},{3,3},{4,4},{5,6},{6,5},{7,7},{8,8},{9,10},{10,9... | collective-permute-start | bytes 20 | tf_op jit(solution)/shard_map/ppermute | solution.py:802
  9.2 12.1 %collective-permute-start = (bf16[512,768]{1,0:T(8,128)(2,1)}, bf16[512,768]{1,0:T(8,128)(2,1)S(1)}, u32[]{:S(2)}, u32[]{:S(2)}) collective-permute-start(bf16[512,768]{1,0:T(8,128)(2,1)} %bitcast.50), channel_id=1, source_target_pairs={{0,0},{1,2},{2,1},{3,3},{4,4},{5,6},{6,5},{7,7},{8,8},{9,10},{10,9... | collective-permute-start | bytes 2359304 | tf_op jit(solution)/shard_map/ppermute | solution.py:802
  10.9 24.5 %collective-permute-start.5 = (bf16[512,768]{1,0:T(8,128)(2,1)}, bf16[512,768]{1,0:T(8,128)(2,1)}, u32[]{:S(2)}, u32[]{:S(2)}) collective-permute-start(bf16[512,768]{1,0:T(8,128)(2,1)} %bitcast.42), channel_id=1, source_target_pairs={{1,2},{2,1},{5,6},{6,5},{9,10},{10,9},{13,14},{14,13},{17,18},{18,... | collective-permute-start | bytes 2359304 | tf_op jit(solution)/shard_map/ppermute | solution.py:802
  14.6 5.4 %copy-start.15 = (bf16[4608]{0:T(1024)(128)(2,1)S(1)}, bf16[4608]{0:T(1024)(128)(2,1)}, u32[]{:S(2)}) copy-start(bf16[4608]{0:T(1024)(128)(2,1)} %param.27) | copy-start | bytes 27652
  21.3 6.5 %copy-start = (bf16[512,768]{1,0:T(8,128)(2,1)}, bf16[512,768]{1,0:T(8,128)(2,1)S(1)}, u32[]{:S(2)}) copy-start(bf16[512,768]{1,0:T(8,128)(2,1)S(1)} %collective-permute-done.tokens.refs_6_) | copy-start | bytes 2359300
  21.3 12.3 %copy-start.17 = (bf16[768]{0:T(1024)(128)(2,1)S(1)}, bf16[768]{0:T(1024)(128)(2,1)}, u32[]{:S(2)}) copy-start(bf16[768]{0:T(1024)(128)(2,1)} %param.25) | copy-start | bytes 4612
  21.3 12.9 %copy-start.16 = (bf16[3072]{0:T(1024)(128)(2,1)S(1)}, bf16[3072]{0:T(1024)(128)(2,1)}, u32[]{:S(2)}) copy-start(bf16[3072]{0:T(1024)(128)(2,1)} %param.23) | copy-start | bytes 18436
  27.7 7.7 %collective-permute-start.2 = (bf16[512,512]{1,0:T(8,128)(2,1)}, bf16[512,512]{1,0:T(8,128)(2,1)S(1)}, u32[]{:S(2)}, u32[]{:S(2)}) collective-permute-start(bf16[512,512]{1,0:T(8,128)(2,1)} %get-tuple-element.73.refs_0_), channel_id=1, source_target_pairs={{0,2},{2,0},{4,6},{6,4},{8,10},{10,8},{12,14},{14,12},{16,18},{18,... | collective-permute-start | bytes 1572872 | tf_op jit(solution)/shard_map/ppermute | solution.py:806
  33.1 2.5 %collective-permute-start.3 = (bf16[512,512]{1,0:T(8,128)(2,1)}, bf16[512,512]{1,0:T(8,128)(2,1)S(1)}, u32[]{:S(2)}, u32[]{:S(2)}) collective-permute-start(bf16[512,512]{1,0:T(8,128)(2,1)} %get-tuple-element.74.refs_1_), channel_id=1, source_target_pairs={{0,2},{2,0},{4,6},{6,4},{8,10},{10,8},{12,14},{14,12},{16,18},{18,... | collective-permute-start | bytes 1572872 | tf_op jit(solution)/shard_map/ppermute | solution.py:806
  33.2 3.2 %collective-permute-start.4 = (bf16[512,512]{1,0:T(8,128)(2,1)}, bf16[512,512]{1,0:T(8,128)(2,1)S(1)}, u32[]{:S(2)}, u32[]{:S(2)}) collective-permute-start(bf16[512,512]{1,0:T(8,128)(2,1)} %get-tuple-element.75.refs_2_), channel_id=1, source_target_pairs={{0,2},{2,0},{4,6},{6,4},{8,10},{10,8},{12,14},{14,12},{16,18},{18,... | collective-permute-start | bytes 1572872 | tf_op jit(solution)/shard_map/ppermute | solution.py:806
  35.5 0.9 copy-start.5
  35.6 0.9 copy-start.6
  36.3 0.8 copy-start.7
  76.4 1.7 copy-start.18
  78.0 13.1 %collective-permute-start.6 = (bf16[8,192,768]{2,1,0:T(8,128)(2,1)S(1)}, bf16[8,192,768]{2,1,0:T(8,128)(2,1)S(1)}, u32[]{:S(2)}, u32[]{:S(2)}) collective-permute-start(bf16[8,192,768]{2,1,0:T(8,128)(2,1)S(1)} %bitcast.49), channel_id=1, source_target_pairs={{0,2},{2,0},{4,6},{6,4},{8,10},{10,8},{12,14},{14,12},{16,18},{18,... | collective-permute-start | bytes 7077896 | tf_op jit(solution)/shard_map/ppermute | solution.py:806
  90.5 15.9 %collective-permute-start.9 = (bf16[512,768]{1,0:T(8,128)(2,1)}, bf16[512,768]{1,0:T(8,128)(2,1)S(1)}, u32[]{:S(2)}, u32[]{:S(2)}) collective-permute-start(bf16[512,768]{1,0:T(8,128)(2,1)} %get-tuple-element.89), channel_id=1, source_target_pairs={{0,2},{2,0},{4,6},{6,4},{8,10},{10,8},{12,14},{14,12},{16,18},{18,... | collective-permute-start | bytes 2359304 | tf_op jit(solution)/shard_map/ppermute | solution.py:806
  90.7 15.8 %collective-permute-start.8 = (bf16[512,768]{1,0:T(8,128)(2,1)}, bf16[512,768]{1,0:T(8,128)(2,1)S(1)}, u32[]{:S(2)}, u32[]{:S(2)}) collective-permute-start(bf16[512,768]{1,0:T(8,128)(2,1)} %get-tuple-element.82.refs_2_), channel_id=1, source_target_pairs={{0,2},{2,0},{4,6},{6,4},{8,10},{10,8},{12,14},{14,12},{16,18},{18,... | collective-permute-start | bytes 2359304 | tf_op jit(solution)/shard_map/ppermute | solution.py:806
  94.2 28.2 %collective-permute-start.7 = (bf16[8,192,384]{2,1,0:T(8,128)(2,1)}, bf16[8,192,384]{2,1,0:T(8,128)(2,1)S(1)}, u32[]{:S(2)}, u32[]{:S(2)}) collective-permute-start(bf16[8,192,384]{2,1,0:T(8,128)(2,1)} %get-tuple-element.83.refs_6_), channel_id=1, source_target_pairs={{0,1},{1,0},{2,3},{3,2},{4,5},{5,4},{6,7},{7,6},{8,9},{9,8},{10,11... | collective-permute-start | bytes 3538952 | tf_op jit(solution)/shard_map/ppermute | solution.py:814
  94.2 12.2 %copy-start.4 = (s32[2]{0:T(128)S(1)}, s32[2]{0:T(128)}, u32[]{:S(2)}) copy-start(s32[2]{0:T(128)} %pad_add_fusion.core) | copy-start | bytes 28
  112.8 2.2 %collective-permute-start.10 = (bf16[8,48,768]{2,1,0:T(8,128)(2,1)}, bf16[8,48,768]{2,1,0:T(8,128)(2,1)S(1)}, u32[]{:S(2)}, u32[]{:S(2)}) collective-permute-start(bf16[8,48,768]{2,1,0:T(8,128)(2,1)} %bitcast.53), channel_id=1, source_target_pairs={{0,2},{2,0},{4,6},{6,4},{8,10},{10,8},{12,14},{14,12},{16,18},{18,... | collective-permute-start | bytes 1769480 | tf_op jit(solution)/shard_map/ppermute | solution.py:806
  112.9 3.0 %collective-permute-start.11 = (bf16[8,48,768]{2,1,0:T(8,128)(2,1)}, bf16[8,48,768]{2,1,0:T(8,128)(2,1)S(1)}, u32[]{:S(2)}, u32[]{:S(2)}) collective-permute-start(bf16[8,48,768]{2,1,0:T(8,128)(2,1)} %bitcast.52), channel_id=1, source_target_pairs={{0,2},{2,0},{4,6},{6,4},{8,10},{10,8},{12,14},{14,12},{16,18},{18,... | collective-permute-start | bytes 1769480 | tf_op jit(solution)/shard_map/ppermute | solution.py:806
  113.3 3.4 %collective-permute-start.12 = (bf16[8,48,768]{2,1,0:T(8,128)(2,1)}, bf16[8,48,768]{2,1,0:T(8,128)(2,1)S(1)}, u32[]{:S(2)}, u32[]{:S(2)}) collective-permute-start(bf16[8,48,768]{2,1,0:T(8,128)(2,1)} %bitcast.51), channel_id=1, source_target_pairs={{0,2},{2,0},{4,6},{6,4},{8,10},{10,8},{12,14},{14,12},{16,18},{18,... | collective-permute-start | bytes 1769480 | tf_op jit(solution)/shard_map/ppermute | solution.py:806
  119.3 22.7 %collective-permute-start.15 = (bf16[8,48,1152]{2,1,0:T(8,128)(2,1)}, bf16[8,48,1152]{2,1,0:T(8,128)(2,1)}, u32[]{:S(2)}, u32[]{:S(2)}) collective-permute-start(bf16[8,48,1152]{2,1,0:T(8,128)(2,1)} %get-tuple-element.96.refs_2_), channel_id=1, source_target_pairs={{0,1},{1,0},{2,3},{3,2},{4,5},{5,4},{6,7},{7,6},{8,9},{9,8},{10,11... | collective-permute-start | bytes 2654216 | tf_op jit(solution)/shard_map/ppermute | solution.py:814
  122.4 4.5 %copy-start.3 = (f32[1,3072]{1,0:T(1,128)S(1)}, f32[1,3072]{1,0:T(1,128)}, u32[]{:S(2)}) copy-start(f32[1,3072]{1,0:T(1,128)} %get-tuple-element.105.bias_grad) | copy-start | bytes 36868
  125.3 16.7 %collective-permute-start.14 = (bf16[4,192,384]{2,1,0:T(8,128)(2,1)}, bf16[4,192,384]{2,1,0:T(8,128)(2,1)S(1)}, u32[]{:S(2)}, u32[]{:S(2)}) collective-permute-start(bf16[4,192,384]{2,1,0:T(8,128)(2,1)} %get-tuple-element.99.refs_0_.refs_4_), channel_id=1, source_target_pairs={{0,4},{2,6},{4,0},{6,2},{8,12},{10,14},{12,8},{14,10},{16,20},{18,... | collective-permute-start | bytes 1769480 | tf_op jit(solution)/shard_map/ppermute | solution.py:806
  135.0 1.8 collective-permute-start.16
  135.0 23.9 %collective-permute-start.13 = (bf16[512,768]{1,0:T(8,128)(2,1)}, bf16[512,768]{1,0:T(8,128)(2,1)S(1)}, u32[]{:S(2)}, u32[]{:S(2)}) collective-permute-start(bf16[512,768]{1,0:T(8,128)(2,1)} %get-tuple-element.98), channel_id=1, source_target_pairs={{0,0},{1,2},{2,1},{3,3},{4,4},{5,6},{6,5},{7,7},{8,8},{9,10},{10,9... | collective-permute-start | bytes 2359304 | tf_op jit(solution)/shard_map/ppermute | solution.py:802
  137.6 4.3 %copy-start.13 = (f32[16,768]{1,0:T(8,128)}, f32[16,768]{1,0:T(8,128)S(1)}, u32[]{:S(2)}) copy-start(f32[16,768]{1,0:T(8,128)S(1)} %add.65.refs_5_) | copy-start | bytes 147460
  137.6 4.3 %collective-permute-start.17 = (f32[16,768]{1,0:T(8,128)S(1)}, f32[16,768]{1,0:T(8,128)S(1)}, u32[]{:S(2)}, u32[]{:S(2)}) collective-permute-start(f32[16,768]{1,0:T(8,128)S(1)} %add.65.refs_5_), channel_id=1, source_target_pairs={{0,8},{2,10},{4,12},{6,14},{8,0},{10,2},{12,4},{14,6},{16,24},{18,... | collective-permute-start | bytes 147464 | tf_op jit(solution)/shard_map/ppermute | solution.py:806
  145.4 27.6 %collective-permute-start.18 = (bf16[512,768]{1,0:T(8,128)(2,1)}, bf16[512,768]{1,0:T(8,128)(2,1)}, u32[]{:S(2)}, u32[]{:S(2)}) collective-permute-start(bf16[512,768]{1,0:T(8,128)(2,1)} %get-tuple-element.108), channel_id=1, source_target_pairs={{0,0},{1,2},{2,1},{3,3},{4,4},{5,6},{6,5},{7,7},{8,8},{9,10},{10,9... | collective-permute-start | bytes 2359304 | tf_op jit(solution)/shard_map/ppermute | solution.py:802
  153.1 13.7 %collective-permute-start.20 = (bf16[4,48,1152]{2,1,0:T(8,128)(2,1)}, bf16[4,48,1152]{2,1,0:T(8,128)(2,1)S(1)}, u32[]{:S(2)}, u32[]{:S(2)}) collective-permute-start(bf16[4,48,1152]{2,1,0:T(8,128)(2,1)} %get-tuple-element.111), channel_id=1, source_target_pairs={{0,4},{2,6},{4,0},{6,2},{8,12},{10,14},{12,8},{14,10},{16,20},{18,... | collective-permute-start | bytes 1327112 | tf_op jit(solution)/shard_map/ppermute | solution.py:806
  154.5 12.3 %collective-permute-start.19 = (bf16[2,192,384]{2,1,0:T(8,128)(2,1)}, bf16[2,192,384]{2,1,0:T(8,128)(2,1)S(1)}, u32[]{:S(2)}, u32[]{:S(2)}) collective-permute-start(bf16[2,192,384]{2,1,0:T(8,128)(2,1)} %get-tuple-element.109.refs_4_), channel_id=1, source_target_pairs={{0,8},{2,10},{4,12},{6,14},{8,0},{10,2},{12,4},{14,6},{16,24},{18,... | collective-permute-start | bytes 884744 | tf_op jit(solution)/shard_map/ppermute | solution.py:806
  156.3 9.2 %collective-permute-start.21 = (f32[24,768]{1,0:T(8,128)}, f32[24,768]{1,0:T(8,128)S(1)}, u32[]{:S(2)}, u32[]{:S(2)}) collective-permute-start(f32[24,768]{1,0:T(8,128)} %get-tuple-element.113.refs_5_), channel_id=1, source_target_pairs={{0,16},{2,18},{4,20},{6,22},{8,24},{10,26},{12,28},{14,30},{16,0},... | collective-permute-start | bytes 221192 | tf_op jit(solution)/shard_map/ppermute | solution.py:806
  158.9 16.4 %copy-start.8 = (bf16[512,768]{1,0:T(8,128)(2,1)}, bf16[512,768]{1,0:T(8,128)(2,1)S(1)}, u32[]{:S(2)}) copy-start(bf16[512,768]{1,0:T(8,128)(2,1)S(1)} %collective-permute-done.13) | copy-start | bytes 2359300
  163.4 17.5 %collective-permute-start.24 = (bf16[48,3840]{1,0:T(8,128)(2,1)}, bf16[48,3840]{1,0:T(8,128)(2,1)S(1)}, u32[]{:S(2)}, u32[]{:S(2)}) collective-permute-start(bf16[48,3840]{1,0:T(8,128)(2,1)} %reduce-scatter.2.cloned.1.call-done), channel_id=1, source_target_pairs={{0,1},{1,0},{2,3},{3,2},{4,5},{5,4},{6,7},{7,6},{8,9},{9,8},{10,11... | collective-permute-start | bytes 1105928 | tf_op jit(solution)/shard_map/ppermute | solution.py:814
  169.1 6.3 %collective-permute-start.25 = (f32[40,768]{1,0:T(8,128)}, f32[40,768]{1,0:T(8,128)S(1)}, u32[]{:S(2)}, u32[]{:S(2)}) collective-permute-start(f32[40,768]{1,0:T(8,128)} %get-tuple-element.119.refs_6_), channel_id=1, source_target_pairs={{0,4},{2,6},{4,0},{6,2},{8,12},{10,14},{12,8},{14,10},{16,20},{18,... | collective-permute-start | bytes 368648 | tf_op jit(solution)/shard_map/ppermute | solution.py:806
  170.5 9.2 %collective-permute-start.22 = (bf16[1,192,384]{2,1,0:T(8,128)(2,1)}, bf16[1,192,384]{2,1,0:T(8,128)(2,1)S(1)}, u32[]{:S(2)}, u32[]{:S(2)}) collective-permute-start(bf16[1,192,384]{2,1,0:T(8,128)(2,1)} %get-tuple-element.114.refs_4_), channel_id=1, source_target_pairs={{0,16},{2,18},{4,20},{6,22},{8,24},{10,26},{12,28},{14,30},{16,0},... | collective-permute-start | bytes 442376 | tf_op jit(solution)/shard_map/ppermute | solution.py:806
  171.5 15.5 %copy-start.12 = (bf16[48,3840]{1,0:T(8,128)(2,1)S(1)}, bf16[48,3840]{1,0:T(8,128)(2,1)}, u32[]{:S(2)}) copy-start(bf16[48,3840]{1,0:T(8,128)(2,1)} %reduce-scatter.2.cloned.1.call-done) | copy-start | bytes 1105924
  171.5 9.4 %collective-permute-start.23 = (bf16[2,48,1152]{2,1,0:T(8,128)(2,1)}, bf16[2,48,1152]{2,1,0:T(8,128)(2,1)S(1)}, u32[]{:S(2)}, u32[]{:S(2)}) collective-permute-start(bf16[2,48,1152]{2,1,0:T(8,128)(2,1)} %get-tuple-element.116), channel_id=1, source_target_pairs={{0,8},{2,10},{4,12},{6,14},{8,0},{10,2},{12,4},{14,6},{16,24},{18,... | collective-permute-start | bytes 663560 | tf_op jit(solution)/shard_map/ppermute | solution.py:806
  182.9 5.7 %copy-start.2 = (f32[72,768]{1,0:T(8,128)S(1)}, f32[72,768]{1,0:T(8,128)}, u32[]{:S(2)}) copy-start(f32[72,768]{1,0:T(8,128)} %get-tuple-element.120.here) | copy-start | bytes 663556
  182.9 6.6 %collective-permute-start.27 = (bf16[1,48,1152]{2,1,0:T(8,128)(2,1)}, bf16[1,48,1152]{2,1,0:T(8,128)(2,1)S(1)}, u32[]{:S(2)}, u32[]{:S(2)}) collective-permute-start(bf16[1,48,1152]{2,1,0:T(8,128)(2,1)} %get-tuple-element.123), channel_id=1, source_target_pairs={{0,16},{2,18},{4,20},{6,22},{8,24},{10,26},{12,28},{14,30},{16,0},... | collective-permute-start | bytes 331784 | tf_op jit(solution)/shard_map/ppermute | solution.py:806
  184.2 10.4 %copy-start.10 = (bf16[1,192,384]{2,1,0:T(8,128)(2,1)S(1)}, bf16[1,192,384]{2,1,0:T(8,128)(2,1)}, u32[]{:S(2)}) copy-start(bf16[1,192,384]{2,1,0:T(8,128)(2,1)} %get-tuple-element.125.refs_2_) | copy-start | bytes 442372
  184.2 10.4 %collective-permute-start.29 = (bf16[1,192,384]{2,1,0:T(8,128)(2,1)}, bf16[1,192,384]{2,1,0:T(8,128)(2,1)S(1)}, u32[]{:S(2)}, u32[]{:S(2)}) collective-permute-start(bf16[1,192,384]{2,1,0:T(8,128)(2,1)} %get-tuple-element.125.refs_2_), channel_id=1, source_target_pairs={{0,1},{1,0},{2,3},{3,2},{4,5},{5,4},{6,7},{7,6},{8,9},{9,8},{10,11... | collective-permute-start | bytes 442376 | tf_op jit(solution)/shard_map/ppermute | solution.py:814
  188.7 9.5 %collective-permute-start.26 = (f32[72,768]{1,0:T(8,128)S(1)}, f32[72,768]{1,0:T(8,128)S(1)}, u32[]{:S(2)}, u32[]{:S(2)}) collective-permute-start(f32[72,768]{1,0:T(8,128)S(1)} %copy-done.2), channel_id=1, source_target_pairs={{0,1},{1,0},{2,3},{3,2},{4,5},{5,4},{6,7},{7,6},{8,9},{9,8},{10,11... | collective-permute-start | bytes 663560 | tf_op jit(solution)/shard_map/ppermute | solution.py:814
  191.1 6.9 %copy-start.11 = (bf16[1,48,1152]{2,1,0:T(8,128)(2,1)S(1)}, bf16[1,48,1152]{2,1,0:T(8,128)(2,1)}, u32[]{:S(2)}) copy-start(bf16[1,48,1152]{2,1,0:T(8,128)(2,1)} %shard_map.250) | copy-start | bytes 331780
  191.1 6.9 %collective-permute-start.28 = (bf16[1,48,1152]{2,1,0:T(8,128)(2,1)}, bf16[1,48,1152]{2,1,0:T(8,128)(2,1)S(1)}, u32[]{:S(2)}, u32[]{:S(2)}) collective-permute-start(bf16[1,48,1152]{2,1,0:T(8,128)(2,1)} %shard_map.250), channel_id=1, source_target_pairs={{0,1},{1,0},{2,3},{3,2},{4,5},{5,4},{6,7},{7,6},{8,9},{9,8},{10,11... | collective-permute-start | bytes 331784 | tf_op jit(solution)/shard_map/ppermute | solution.py:814
  195.5 4.5 %copy-start.9 = (bf16[512,768]{1,0:T(8,128)(2,1)S(1)}, bf16[512,768]{1,0:T(8,128)(2,1)}, u32[]{:S(2)}) copy-start(bf16[512,768]{1,0:T(8,128)(2,1)} %copy-done.8) | copy-start | bytes 2359300
  198.2 2.8 %copy-start.14 = (f32[48,2304]{1,0:T(8,128)}, f32[48,2304]{1,0:T(8,128)S(1)}, u32[]{:S(2)}) copy-start(f32[48,2304]{1,0:T(8,128)S(1)} %slice_dynamic-update-slice_fusion) | copy-start | bytes 1327108
Sparse Core Ops, SparseCore 0:
  76.5 86.8 reduce-scatter.1
